TPU v7x, 128 devices: a whole 4x4x4 slice. The times are simulated.
128 devices in a mesh: grp: 4 (over x_lo, core), blk: 32 (over x_hi, y, z).
Axes of the slice: x: 4 (x_hi: 2, x_lo: 2; x = x_hi * 2 + x_lo), y: 4, z: 4, core: 2. Of those that a mesh axis runs over, the one named last changes fastest.
Arguments:
- resid: bfloat16 [2, 3072, 4096], P(None, ('grp', 'blk'))
- attn: bfloat16 [2, 3072, 4096], P(None, ('grp', 'blk')), may hold values from -5 to 5
- out_proj: bfloat16 [4096, 4096], P(None, 'grp'), may hold values from -0.09375 to 0.09375
- out_bias: float32 [4096], replicated, may hold values from -2 to 2
- gain: float32 [4096], replicated, may hold values from 0.5 to 1.5
- task_bias: float32 [8, 4096], replicated, may hold values from -1 to 1
- task_ids: int32 [4], P('grp'), may hold values from 0 to 7
- neg_owner: int32 [3072, 7], P(('grp', 'blk')), may hold values from 0 to 127, as said below
- neg_row: int32 [3072, 7], P(('grp', 'blk')), may hold values from 0 to 23
Outputs:
- losses: float32 [3072], P(('grp', 'blk'))
- grad_attn: float32 [2, 3072, 4096], P(None, ('grp', 'blk'))
- grad_gain: float32 [4096], replicated
- grad_task_bias: float32 [8, 4096], replicated
- grad_out_bias: float32 [4096], replicated
Inputs may be any that keep to these rules, and one draw needn't show every extreme that they name: `neg_owner`: within one device's 24 x 7 entries each owner is named at most 2 times, and one owner is named exactly 2 times by every device. Owners number the devices of grp and blk together, grp the slower.
All inputs are finite; a program needn't handle non-finite values.
Results may differ from a plain program's by a relative error of at most 0.014.
Values may be sent and summed in bfloat16 or wider, within the bound.
No kernel may reach another device: no remote copies, remote signals or barrier semaphores. Data moves between devices by JAX's collectives and lax.ppermute only.
A program may use at most 128 MiB of HBM per device.

v0:
```python
import jax
import jax.numpy as jnp
from jax import lax
from jax.sharding import PartitionSpec as P

TAU = 0.02
LOSS_SCALE = 256.0


def rounded(values):
    return lax.optimization_barrier(values.astype(jnp.bfloat16)).astype(jnp.float32)


def embed_rows(pooled, gain, bias_rows):
    normed = pooled * lax.rsqrt(jnp.mean(pooled * pooled, axis=-1, keepdims=True) + 1e-05)
    mixture = normed * gain + bias_rows
    return mixture * lax.rsqrt(jnp.sum(mixture * mixture, axis=-1, keepdims=True) + 1e-06)


def local(resid, attn, out_proj, out_bias, gain, task_bias, task_ids, neg_owner, neg_row):
    tok_rows = resid.shape[1]
    feat_width = resid.shape[2]
    hard_count = neg_owner.shape[1]
    row_count = 2 * tok_rows
    attn_rows = attn.reshape(row_count, feat_width)
    column_part = jnp.dot(
        lax.all_gather(attn_rows, "grp", axis=0, tiled=True),
        out_proj,
        preferred_element_type=jnp.float32,
    ).astype(jnp.bfloat16)
    projected = lax.all_to_all(column_part, "grp", split_axis=0, concat_axis=1, tiled=True)
    pooled = (
        resid.reshape(row_count, feat_width).astype(jnp.float32)
        + projected.astype(jnp.float32)
        + out_bias
    )
    task_onehot = (jnp.arange(task_bias.shape[0]) == task_ids[0]).astype(jnp.float32)

    def embed_local(pooled, gain, task_bias):
        bias_row = jnp.sum(task_onehot[:, None] * task_bias, axis=0)
        return embed_rows(pooled, gain, bias_row[None, :])

    embedded, pullback = jax.vjp(embed_local, pooled, gain, task_bias)
    emb = embedded.astype(jnp.bfloat16)
    query_emb = emb[:tok_rows]
    passage_emb = emb[tok_rows:]
    dev_count = lax.axis_size(("grp", "blk"))
    slot_cap = max(2, 2 * tok_rows * hard_count // dev_count)
    owner_flat = neg_owner.reshape(-1)
    row_flat = neg_row.reshape(-1)
    owner_onehot = (owner_flat[:, None] == jnp.arange(dev_count)[None, :]).astype(jnp.int32)
    slot_index = jnp.sum(owner_onehot * (jnp.cumsum(owner_onehot, 0) - 1), 1)
    request = jnp.zeros((dev_count, slot_cap), jnp.int32).at[owner_flat, slot_index].set(row_flat)
    incoming = lax.all_to_all(request, ("grp", "blk"), split_axis=0, concat_axis=0, tiled=True)
    served = passage_emb[incoming]
    returned_vectors = lax.all_to_all(
        served, ("grp", "blk"), split_axis=0, concat_axis=0, tiled=True
    )
    negatives = returned_vectors[owner_flat, slot_index].reshape(tok_rows, hard_count, feat_width)
    block_rows = lax.all_gather(passage_emb, "blk", axis=0, tiled=True)
    score_block = jnp.dot(query_emb, block_rows.T, preferred_element_type=jnp.float32) / TAU
    weights = jnp.exp(score_block)
    totals = jnp.sum(weights, 1)
    numerator = jnp.dot(
        weights.astype(jnp.bfloat16), block_rows, preferred_element_type=jnp.float32
    )
    scores = score_block
    totals, numerator, scores = (totals, numerator, scores)
    hard_scores = (
        jnp.einsum("td,tkd->tk", query_emb, negatives, preferred_element_type=jnp.float32) / TAU
    )
    hard_weights = jnp.exp(hard_scores)
    totals = totals + jnp.sum(hard_weights, 1)
    numerator = numerator + jnp.einsum(
        "tk,tkd->td",
        hard_weights.astype(jnp.bfloat16),
        negatives,
        preferred_element_type=jnp.float32,
    )
    own_offset = lax.axis_index("blk") * tok_rows
    own_block = lax.dynamic_slice_in_dim(scores, own_offset, tok_rows, 1)
    losses = jnp.log(totals) - jnp.diagonal(own_block)
    grad_q = numerator / (TAU * totals[:, None]) - passage_emb.astype(jnp.float32) / TAU
    probs = (jnp.exp(scores) / totals[:, None]).astype(jnp.bfloat16)
    summed = lax.psum_scatter(
        jnp.dot(probs.T, query_emb, preferred_element_type=jnp.float32).astype(jnp.bfloat16),
        "blk",
        scatter_dimension=0,
        tiled=True,
    ).astype(jnp.float32)
    grad_p = summed / TAU - query_emb.astype(jnp.float32) / TAU
    hard_probs = rounded(hard_weights / totals[:, None])
    slot_grads = (hard_probs[:, :, None] * query_emb.astype(jnp.float32)[:, None, :] / TAU).astype(
        jnp.bfloat16
    )
    outgoing = (
        jnp.zeros((dev_count, slot_cap, feat_width), jnp.bfloat16)
        .at[owner_flat, slot_index]
        .set(slot_grads.reshape(-1, feat_width))
    )
    returned_grads = lax.all_to_all(
        outgoing, ("grp", "blk"), split_axis=0, concat_axis=0, tiled=True
    )
    grad_p = grad_p.at[incoming.reshape(-1)].add(
        returned_grads.reshape(-1, feat_width).astype(jnp.float32)
    )
    d_pooled, grad_gain, grad_task_bias = pullback(jnp.concatenate([grad_q, grad_p], 0))
    grad_out_bias = jnp.sum(d_pooled, 0)
    grad_gain, grad_task_bias, grad_out_bias = lax.psum(
        (grad_gain, grad_task_bias, grad_out_bias), ("grp", "blk")
    )
    scaled = (LOSS_SCALE * d_pooled).astype(jnp.bfloat16)
    scaled_columns = lax.all_to_all(scaled, "grp", split_axis=1, concat_axis=0, tiled=True)
    grad_attn = lax.psum_scatter(
        jnp.dot(scaled_columns, out_proj.T, preferred_element_type=jnp.float32).astype(
            jnp.bfloat16
        ),
        "grp",
        scatter_dimension=0,
        tiled=True,
    ).astype(jnp.float32)
    return (
        losses,
        grad_attn.reshape(2, tok_rows, feat_width),
        grad_gain,
        grad_task_bias,
        grad_out_bias,
    )


def solution(mesh):
    in_specs = (
        P(None, ("grp", "blk"), None),
        P(None, ("grp", "blk"), None),
        P(None, "grp"),
        P(),
        P(),
        P(),
        P("grp"),
        P(("grp", "blk"), None),
        P(("grp", "blk"), None),
    )
    out_specs = (P(("grp", "blk")), P(None, ("grp", "blk"), None), P(), P(), P())
    return jax.shard_map(local, mesh=mesh, in_specs=in_specs, out_specs=out_specs, check_vma=False)
```

profile of v0, /device:TPU:1, one launch (start us, length us, event | category | flops | bytes accessed | tf_op | source)
XLA Modules:
  0.0 642.5 jit_solution(15834689028549073858)
XLA Ops:
  7.9 30.2 %all-gather.3.cloned.1.call-done = bf16[192,4096]{1,0:T(8,128)(2,1)} async-done(((bf16[48,4096]{1,0:T(8,128)(2,1)}), bf16[192,4096]{1,0:T(8,128)(2,1)}) %all-gather.3.cloned.1.call-update) | async-done | bytes 1572880 | tf_op jit(solution)/shard_map/all_gather | solution.py:27
  38.1 6.4 convolution_convert_fusion.2
  44.5 3.6 all-to-all-start
  49.0 5.8 all-to-all-done
  61.3 8.6 %scatter_fusion = s32[128,2]{0,1:T(2,128)S(1)} fusion(s32[128,2]{0,1:T(2,128)S(1)} %broadcast.344, s32[168]{0:T(256)S(1)} %bitcast.74, s32[168]{0:T(256)S(1)} %reshape.491), kind=kCustom, calls=%fused_computation.3 | custom fusion | bytes 3360 | tf_op jit(solution)/shard_map/scatter | solution.py:53
  70.0 18.8 %all_to_all.51 = s32[128,1,2]{2,1,0:T(1,128)S(1)} all-to-all(s32[128,1,2]{2,1,0:T(1,128)S(1)} %copy.38), channel_id=1, replica_groups=mesh['grp'=4,'blk'=32] {'grp','blk'}, dimensions={0} | all-to-all | bytes 2048 | tf_op jit(solution)/shard_map/all_to_all | solution.py:54
  89.4 1.8 gather_fusion
  91.3 2.7 reshape.470
  94.0 35.2 %all_to_all.52 = bf16[128,2,4096]{2,1,0:T(2,128)(2,1)S(1)} all-to-all(bf16[128,2,4096]{2,1,0:T(2,128)(2,1)} %reshape.470), channel_id=1, replica_groups=mesh['grp'=4,'blk'=32] {'grp','blk'}, dimensions={0} | all-to-all | bytes 4194304 | tf_op jit(solution)/shard_map/all_to_all | solution.py:56
  129.2 6.4 gather_fusion.1
  135.6 1.7 reshape.456
  138.6 35.8 %all-gather.5.cloned.1.call-done = bf16[768,4096]{1,0:T(8,128)(2,1)} async-done(((bf16[24,4096]{1,0:T(8,128)(2,1)}), bf16[768,4096]{1,0:T(8,128)(2,1)}) %all-gather.5.cloned.1.call-update) | async-done | bytes 6291472 | tf_op jit(solution)/shard_map/all_gather | solution.py:60
  174.4 4.6 exponential_reduce_fusion
  179.6 4.6 convolution_convert_fusion
  185.2 2.0 mul.244
  187.2 2.0 mul.245
  192.8 3.4 broadcast_in_dim.14
  196.2 41.2 %scatter_fusion.1 = bf16[128,2,4096]{2,1,0:T(2,128)(2,1)} fusion(bf16[128,2,4096]{2,1,0:T(2,128)(2,1)} %broadcast_in_dim.14, s32[168]{0:T(256)S(1)} %bitcast.75, bf16[168,4096]{1,0:T(8,128)(2,1)S(1)} %copy-done.4), kind=kCustom, calls=%fused_computation.4 | custom fusion | bytes 4130112 | tf_op jit(solution)/shard_map/scatter | solution.py:99
  237.4 6.6 %all-to-all-start.3 = ((bf16[128,2,4096]{2,1,0:T(2,128)(2,1)}), bf16[128,2,4096]{2,1,0:T(2,128)(2,1)S(1)}, u32[]{:S(2)}, u32[]{:S(2)}) async-start(bf16[128,2,4096]{2,1,0:T(2,128)(2,1)} %scatter_fusion.1), calls=%async_computation.4 | async-start | bytes 4194304 | tf_op jit(solution)/shard_map/all_to_all | solution.py:101
  244.8 2.5 reshape.466
  249.9 2.0 fusion.23
  251.9 4.6 fusion.1
  256.4 17.4 %all-to-all-done.3 = bf16[128,2,4096]{2,1,0:T(2,128)(2,1)S(1)} async-done(((bf16[128,2,4096]{2,1,0:T(2,128)(2,1)}), bf16[128,2,4096]{2,1,0:T(2,128)(2,1)S(1)}, u32[]{:S(2)}, u32[]{:S(2)}) %all-to-all-start.3) | async-done | bytes 2097184 | tf_op jit(solution)/shard_map/all_to_all | solution.py:101
  273.8 2.7 reshape.505
  276.5 151.6 %reduce-scatter.3.cloned.1.call-done = bf16[24,4096]{1,0:T(8,128)(2,1)} async-done(((bf16[768,4096]{1,0:T(8,128)(2,1)}), bf16[24,4096]{1,0:T(8,128)(2,1)}) %reduce-scatter.3.cloned.1.call-update) | async-done | bytes 196624 | tf_op jit(solution)/shard_map/reduce_scatter | solution.py:85
  429.0 7.7 %scatter_fusion.2 = f32[24,4096]{1,0:T(8,128)S(1)} fusion(f32[24,4096]{1,0:T(8,128)S(1)} %multiply_subtract_fusion, s32[256]{0:T(256)S(1)} %bitcast.93, f32[256,4096]{1,0:T(8,128)} %reshape.505), kind=kCustom, calls=%fused_computation.5 | custom fusion | flops 1048576 | bytes 12583936 | tf_op jit(solution)/shard_map/scatter-add | solution.py:104
  441.7 1.7 multiply_reduce_fusion.1
  446.8 11.6 %all_to_all.53 = bf16[48,4,1024]{2,0,1:T(8,128)(2,1)S(1)} all-to-all(bf16[48,4,1024]{2,0,1:T(8,128)(2,1)S(1)} %fusion.5), channel_id=1, replica_groups=mesh['grp'=4,'blk'=32] {'grp'}, dimensions={1} | all-to-all | bytes 786432 | tf_op jit(solution)/shard_map/all_to_all | solution.py:113
  458.5 7.5 %convolution_convert_fusion.1 = bf16[192,4096]{1,0:T(8,128)(2,1)} fusion(bf16[192,1024]{1,0:T(8,128)(2,1)S(1)} %bitcast.87, bf16[4096,1024]{1,0:T(8,128)(2,1)} %param.11), kind=kOutput, calls=%fused_computation.7 | convolution fusion | flops 1611399168 | bytes 10354688 | tf_op jit(solution)/shard_map/dot_general | solution.py:115
  469.6 63.2 %all-reduce.1 = (f32[4096]{0:T(1024)}, f32[4096]{0:T(1024)}) all-reduce(f32[4096]{0:T(1024)S(1)} %get-tuple-element.7, f32[4096]{0:T(1024)S(1)} %get-tuple-element.5), channel_id=1, replica_groups=mesh['grp'=4,'blk'=32] {'grp','blk'}, use_global_device_ids=true, to_apply=%region_16.17 | all-reduce | flops 8192 | bytes 65536 | tf_op jit(solution)/shard_map/psum | solution.py:109
  532.8 1.9 convert.17
  534.7 99.5 %all-reduce.4.cloned.1.call-done = f32[8,4096]{1,0:T(8,128)} async-done(((f32[8,4096]{1,0:T(8,128)}), f32[8,4096]{1,0:T(8,128)}) %all-reduce.4.cloned.1.call-update) | async-done | bytes 131088 | tf_op jit(solution)/shard_map/psum | solution.py:109
  (171 shorter events, 32.0 us)
Async XLA Ops:
  7.2 30.9 %all-gather.3.cloned.1.call-start = ((), (), s32[]{:S(2)}) async-start(), calls=%async_computation.7 | async-start | bytes 1966080 | tf_op jit(solution)/shard_map/all_gather | solution.py:27
  7.9 40.9 %copy-start.23 = (f32[8,4096]{1,0:T(8,128)S(1)}, f32[8,4096]{1,0:T(8,128)}, u32[]{:S(2)}) copy-start(f32[8,4096]{1,0:T(8,128)} %param.14) | copy-start | bytes 393220
  44.5 10.2 %all-to-all-start = ((bf16[4,48,1024]{2,1,0:T(8,128)(2,1)}), bf16[4,48,1024]{2,1,0:T(8,128)(2,1)S(1)}, u32[]{:S(2)}, u32[]{:S(2)}) async-start(bf16[4,48,1024]{2,1,0:T(8,128)(2,1)} %bitcast.2), calls=%async_computation | async-start | bytes 786432 | tf_op jit(solution)/shard_map/all_to_all | solution.py:31
  48.1 126.3 %all-gather.5.cloned.1.call-start = ((), (), s32[]{:S(2)}) async-start(), calls=%async_computation.8 | async-start | bytes 6488064 | tf_op jit(solution)/shard_map/all_gather | solution.py:60
  48.8 6.6 %copy-start.39 = (f32[8]{0:T(128)}, f32[8]{0:T(128)S(1)}, u32[]{:S(2)}) copy-start(f32[8]{0:T(128)S(1)} %compare_convert_fusion) | copy-start | bytes 100
  48.9 10.0 %copy-start.13 = (f32[4096]{0:T(1024)}, f32[4096]{0:T(1024)S(1)}, u32[]{:S(2)}) copy-start(f32[4096]{0:T(1024)S(1)} %multiply_reduce_fusion.5) | copy-start | bytes 49156
  48.9 7.1 %copy-start.6 = (bf16[2,24,4096]{2,1,0:T(8,128)(2,1)S(1)}, bf16[2,24,4096]{2,1,0:T(8,128)(2,1)}, u32[]{:S(2)}) copy-start(bf16[2,24,4096]{2,1,0:T(8,128)(2,1)} %param.9) | copy-start | bytes 1179652
  56.0 2.9 copy-start.15
  57.0 3.1 copy-start.27
  57.0 3.1 copy-start.25
  59.2 120.5 %copy-start.2 = (bf16[48,4096]{1,0:T(8,128)(2,1)}, bf16[48,4096]{1,0:T(8,128)(2,1)S(1)}, u32[]{:S(2)}) copy-start(bf16[48,4096]{1,0:T(8,128)(2,1)S(1)} %fusion.12) | copy-start | bytes 1179652
  60.2 29.3 %copy-start = (bf16[24,4096]{1,0:T(8,128)(2,1)S(1)}, bf16[24,4096]{1,0:T(8,128)(2,1)}, u32[]{:S(2)}) copy-start(bf16[24,4096]{1,0:T(8,128)(2,1)} %get-tuple-element.18) | copy-start | bytes 589828
  60.2 367.8 %reduce-scatter.3.cloned.1.call-start = ((), (), s32[]{:S(2)}) async-start(), calls=%async_computation.9 | async-start | bytes 6488064 | tf_op jit(solution)/shard_map/reduce_scatter | solution.py:85
  137.3 41.8 %copy-start.1 = (bf16[24,7,4096]{2,1,0:T(8,128)(2,1)}, bf16[24,7,4096]{2,1,0:T(8,128)(2,1)S(1)}, u32[]{:S(2)}) copy-start(bf16[24,7,4096]{2,1,0:T(8,128)(2,1)S(1)} %reshape.456) | copy-start | bytes 4128772
  179.1 5.1 copy-start.11
  179.6 4.6 copy-start.33
  192.8 3.4 copy-start.4
  237.4 6.7 %copy-start.14 = (f32[4096]{0:T(1024)S(1)}, f32[4096]{0:T(1024)}, u32[]{:S(2)}) copy-start(f32[4096]{0:T(1024)} %copy-done.13) | copy-start | bytes 49156
  237.4 9.9 %copy-start.22 = (f32[4096]{0:T(1024)S(1)}, f32[4096]{0:T(1024)}, u32[]{:S(2)}) copy-start(f32[4096]{0:T(1024)} %param.12) | copy-start | bytes 49156
  237.4 10.5 %copy-start.16 = (f32[4096]{0:T(1024)S(1)}, f32[4096]{0:T(1024)}, u32[]{:S(2)}) copy-start(f32[4096]{0:T(1024)} %param.13) | copy-start | bytes 49156
  237.4 11.6 %copy-start.19 = (s32[128,1,2]{2,1,0:T(1,128)S(1)}, s32[128,1,2]{2,1,0:T(1,128)}, u32[]{:S(2)}) copy-start(s32[128,1,2]{2,1,0:T(1,128)} %copy-done.18) | copy-start | bytes 3076
  237.4 12.4 %copy-start.24 = (bf16[24,7,1]{1,0,2:T(8,128)(2,1)S(1)}, bf16[24,7,1]{1,0,2:T(8,128)(2,1)}, u32[]{:S(2)}) copy-start(bf16[24,7,1]{1,0,2:T(8,128)(2,1)} %get-tuple-element.21) | copy-start | bytes 1012
  237.4 36.4 %all-to-all-start.3 = ((bf16[128,2,4096]{2,1,0:T(2,128)(2,1)}), bf16[128,2,4096]{2,1,0:T(2,128)(2,1)S(1)}, u32[]{:S(2)}, u32[]{:S(2)}) async-start(bf16[128,2,4096]{2,1,0:T(2,128)(2,1)} %scatter_fusion.1), calls=%async_computation.4 | async-start | bytes 4194304 | tf_op jit(solution)/shard_map/all_to_all | solution.py:101
  244.1 7.8 %copy-start.3 = (bf16[48,4096]{1,0:T(8,128)(2,1)S(1)}, bf16[48,4096]{1,0:T(8,128)(2,1)}, u32[]{:S(2)}) copy-start(bf16[48,4096]{1,0:T(8,128)(2,1)} %copy-done.2) | copy-start | bytes 1179652
  244.1 7.8 %copy-start.12 = (f32[24,768]{1,0:T(8,128)S(1)}, f32[24,768]{1,0:T(8,128)}, u32[]{:S(2)}) copy-start(f32[24,768]{1,0:T(8,128)} %copy-done.11) | copy-start | bytes 221188
  244.1 7.8 %copy-start.41 = (f32[24]{0:T(128)S(1)}, f32[24]{0:T(128)}, u32[]{:S(2)}) copy-start(f32[24]{0:T(128)} %get-tuple-element.10) | copy-start | bytes 292
  244.1 288.7 %reduce-scatter.5.cloned.1.call-start = ((), (), s32[]{:S(2)}) async-start(), calls=%async_computation.10 | async-start | bytes 1966080 | tf_op jit(solution)/shard_map/reduce_scatter | solution.py:114
  429.0 7.7 %copy-start.5 = (f32[24,4096]{1,0:T(8,128)S(1)}, f32[24,4096]{1,0:T(8,128)}, u32[]{:S(2)}) copy-start(f32[24,4096]{1,0:T(8,128)} %fusion.1) | copy-start | bytes 1179652
  436.8 8.5 %copy-start.8 = (bf16[4,48,1024]{2,1,0:T(8,128)(2,1)S(1)}, bf16[4,48,1024]{2,1,0:T(8,128)(2,1)}, u32[]{:S(2)}) copy-start(bf16[4,48,1024]{2,1,0:T(8,128)(2,1)} %copy-done.7) | copy-start | bytes 1179652
  436.9 8.5 %copy-start.9 = (f32[48,4,1024]{2,1,0:T(4,128)S(1)}, f32[48,4,1024]{2,1,0:T(4,128)}, u32[]{:S(2)}) copy-start(f32[48,4,1024]{2,1,0:T(4,128)} %reshape.466) | copy-start | bytes 2359300
  466.0 3.1 copy-start.34
  466.0 168.2 %all-reduce.4.cloned.1.call-start = ((), (), s32[]{:S(2)}) async-start(), calls=%async_computation.11 | async-start | bytes 262144 | tf_op jit(solution)/shard_map/psum | solution.py:109
  (21 other events, 33.2 us)
Sparse Core Ops, SparseCore 0:
  9.7 28.3 all-gather.2
  60.3 114.0 all-gather.4
  184.4 243.6 reduce-scatter.2
  466.1 22.1 reduce-scatter.4
  493.5 140.6 all-reduce.3
where the time goes:
time: 651 us; the launch traced here: 643 us
  waiting for transfers between devices  341 us (52%)
  blocking collectives  129 us (20%)
  local copies, waits for them, and re-layouts  88.8 us (14%)
  matrix products  30.8 us (5%)
  other arithmetic  27.5 us (4%)
  between operations  15.3 us (2%)
  starting transfers between devices  10.4 us (2%)
    reduce_scatter x1, waiting for transfers between devices, local(): lax.psum_scatter(jnp.dot(probs.T, query_emb, preferred_element_type=jnp.f...  152 us
    psum x1, waiting for transfers between devices, local(): lax.psum((grad_gain, grad_task_bias, grad_out_bias), ('grp', 'blk'))  99.5 us
    psum x1, blocking collectives, local(): lax.psum((grad_gain, grad_task_bias, grad_out_bias), ('grp', 'blk'))  63.2 us
    scatter x1, local copies, waits for them, and re-layouts, local(): outgoing = jnp.zeros((dev_count, slot_cap, feat_width), jnp.bfloat16).at[...  41.2 us
    all_gather x1, waiting for transfers between devices, local(): block_rows = lax.all_gather(passage_emb, 'blk', axis=0, tiled=True)  35.8 us
    all_to_all x1, blocking collectives, local(): lax.all_to_all(served, ('grp', 'blk'), split_axis=0, concat_axis=0, tiled...  35.2 us
    all_gather x1, waiting for transfers between devices, local(): lax.all_gather(attn_rows, 'grp', axis=0, tiled=True)  30.2 us
    all_to_all x1, blocking collectives, local(): lax.all_to_all(request, ('grp', 'blk'), split_axis=0, concat_axis=0, tile...  18.8 us
  transfers between devices with their start and end apart: 7, of which 6 were waited for; matrix products, arithmetic and copies ran while one was open for 15% of the time, Pallas kernels for 0%

commit v1 on v0

v1 whole, which is shorter than its diff:
```python
import jax
import jax.numpy as jnp
from jax import lax
from jax.experimental import pallas as pl
from jax.experimental.pallas import tpu as pltpu
from jax.sharding import Mesh, PartitionSpec as P

TAU = 0.02
LOSS_SCALE = 256.0
GRP = ("xl", "co")
BLK = ("xh", "y", "z")
ALL = GRP + BLK
SWAP = [(0, 1), (1, 0)]
LANES = 128
F32 = jnp.float32
BF16 = jnp.bfloat16
SEND = jnp.float16


def swap_core(values):
    return lax.ppermute(values, "co", SWAP)


def swap_chip(values):
    return lax.ppermute(values, "xl", SWAP)


def exchange(values, axes):
    return lax.all_to_all(values, axes, split_axis=0, concat_axis=0, tiled=True)


def embed_rows(pooled, gain, bias_rows):
    normed = pooled * lax.rsqrt(jnp.mean(pooled * pooled, axis=-1, keepdims=True) + 1e-05)
    mixture = normed * gain + bias_rows
    return mixture * lax.rsqrt(jnp.sum(mixture * mixture, axis=-1, keepdims=True) + 1e-06)


def gather_kernel(hard_count, ids, q_ref, p_ref, neg_ref, hard_ref, wide, picked):
    rows = q_ref.shape[0]
    wide[...] = p_ref[...].astype(F32)

    def pick(i, carry):
        for k in range(hard_count):
            source = ids[i * hard_count + k]
            picked[k, pl.ds(i, 1), :] = wide[pl.ds(source, 1), :]
        return carry

    lax.fori_loop(0, rows, pick, 0, unroll=8)
    q = q_ref[...].astype(F32)
    lane = lax.broadcasted_iota(jnp.int32, (rows, LANES), 1)
    hard = jnp.zeros((rows, LANES), F32)
    for k in range(hard_count):
        chosen = picked[k]
        neg_ref[k] = chosen.astype(BF16)
        hard = jnp.where(lane == k, jnp.sum(q * chosen, axis=1, keepdims=True), hard)
    hard_ref[...] = hard


def scatter_kernel(hard_count, ids, w_ref, q_ref, neg_ref, add_ref, sum_ref, slot, *parts):
    rows = q_ref.shape[0]
    q = q_ref[...].astype(F32)
    total = jnp.zeros((rows, LANES), F32)
    for k in range(hard_count):
        weight = w_ref[:, k : k + 1].astype(F32)
        slot[k] = weight * q
        total = total + weight * neg_ref[k].astype(F32)
        parts[k][...] = jnp.zeros_like(parts[k])
    sum_ref[...] = total

    def place(i, carry):
        for k in range(hard_count):
            target = pl.ds(ids[i * hard_count + k], 1)
            parts[k][target, :] = parts[k][target, :] + slot[k, pl.ds(i, 1), :]
        return carry

    lax.fori_loop(0, rows, place, 0, unroll=4)
    added = parts[0][...]
    for k in range(1, hard_count):
        added = added + parts[k][...]
    add_ref[...] = added.astype(BF16)


def local(resid, attn, out_proj, out_bias, gain, task_bias, task_ids, neg_owner, neg_row):
    tok_rows = resid.shape[1]
    width = resid.shape[2]
    hard_count = neg_owner.shape[1]
    row_count = 2 * tok_rows
    blocks = lax.axis_size(BLK)
    pairs = blocks * tok_rows
    me = lax.axis_index(GRP)
    core = lax.axis_index("co")
    chip = lax.axis_index("xl")
    vmem = pl.BlockSpec(memory_space=pltpu.VMEM)
    smem = pl.BlockSpec(memory_space=pltpu.SMEM)
    params = pltpu.CompilerParams(vmem_limit_bytes=40 * 1024 * 1024)

    attn_rows = attn.reshape(row_count, width)
    far_rows = swap_chip(attn_rows)
    near_rows = swap_core(attn_rows)

    owner_group = (neg_owner // blocks) ^ me
    own_ids = (owner_group * pairs + (neg_owner % blocks) * tok_rows + neg_row).reshape(1, -1)
    ids = exchange(jnp.broadcast_to(own_ids, (blocks, tok_rows * hard_count)), BLK).reshape(-1)
    near_task = swap_core(task_ids)
    tasks = jnp.concatenate([task_ids, near_task])
    tasks = jnp.concatenate([tasks, swap_chip(tasks)])

    def project(rows):
        return jnp.dot(rows, out_proj, preferred_element_type=F32).astype(BF16)

    chip_columns = project(jnp.concatenate([attn_rows, near_rows]))
    far_columns = project(jnp.concatenate([far_rows, swap_core(far_rows)]))
    parts = [
        chip_columns[:row_count],
        swap_core(chip_columns[row_count:]),
        swap_chip(far_columns[:row_count]),
        lax.ppermute(far_columns[row_count:], GRP, [(0, 3), (1, 2), (2, 1), (3, 0)]),
    ]

    def by_group(items):
        items = [jnp.where(core == 1, items[i ^ 1], items[i]) for i in range(4)]
        return [jnp.where(chip == 1, items[i ^ 2], items[i]) for i in range(4)]

    projected = jnp.concatenate(by_group(parts), axis=1)
    pooled = resid.reshape(row_count, width).astype(F32) + projected.astype(F32) + out_bias
    task_onehot = (jnp.arange(task_bias.shape[0]) == task_ids[0]).astype(F32)
    bias_row = jnp.sum(task_onehot[:, None] * task_bias, axis=0)

    embedded, pullback = jax.vjp(
        lambda a, b, c: embed_rows(a, b, c[None, :]), pooled, gain, bias_row
    )
    emb = embedded.astype(BF16)

    spread = exchange(
        emb.reshape(2, tok_rows, blocks, LANES).transpose(2, 0, 1, 3), BLK
    )
    q_all = spread[:, 0].reshape(pairs, LANES)
    p_own = spread[:, 1].reshape(pairs, LANES)
    p_far = swap_chip(p_own)
    p_all = jnp.concatenate([p_own, swap_core(p_own), p_far, swap_core(p_far)])

    score_part = lax.dot_general(
        q_all, p_own, (((1,), (1,)), ((), ())), preferred_element_type=F32
    )
    negatives, hard_part = pl.pallas_call(
        lambda *refs: gather_kernel(hard_count, *refs),
        out_shape=(
            jax.ShapeDtypeStruct((hard_count, pairs, LANES), BF16),
            jax.ShapeDtypeStruct((pairs, LANES), F32),
        ),
        in_specs=[smem, vmem, vmem],
        out_specs=(vmem, vmem),
        scratch_shapes=[
            pltpu.VMEM((4 * pairs, LANES), F32),
            pltpu.VMEM((hard_count, pairs, LANES), F32),
        ],
        compiler_params=params,
    )(ids, q_all, p_all)
    part = jnp.concatenate([score_part, hard_part], axis=1).astype(SEND)
    part = exchange(part.reshape(blocks, tok_rows, pairs + LANES), BLK)
    scores = jnp.sum(part.astype(F32), axis=0) / TAU

    column = lax.broadcasted_iota(jnp.int32, scores.shape, 1)
    row = lax.broadcasted_iota(jnp.int32, scores.shape, 0)
    weights = jnp.where(column < pairs + hard_count, jnp.exp(scores), 0.0)
    totals = jnp.sum(weights, axis=1, keepdims=True)
    own_column = lax.axis_index(BLK) * tok_rows + row
    own_score = jnp.sum(jnp.where(column == own_column, scores, 0.0), axis=1)
    losses = jnp.log(totals[:, 0]) - own_score
    probs = (weights / totals).astype(BF16)
    probs = exchange(
        jnp.broadcast_to(probs[None], (blocks, tok_rows, pairs + LANES)), BLK
    ).reshape(pairs, pairs + LANES)

    group_probs = probs[:, :pairs]
    hard_add, hard_sum = pl.pallas_call(
        lambda *refs: scatter_kernel(hard_count, *refs),
        out_shape=(
            jax.ShapeDtypeStruct((4 * pairs, LANES), BF16),
            jax.ShapeDtypeStruct((pairs, LANES), F32),
        ),
        in_specs=[smem, vmem, vmem, vmem],
        out_specs=(vmem, vmem),
        scratch_shapes=[pltpu.VMEM((hard_count, pairs, LANES), F32)]
        + [pltpu.VMEM((4 * pairs, LANES), F32)] * hard_count,
        compiler_params=params,
    )(ids, probs[:, pairs:], q_all, negatives)
    hard_add = hard_add.reshape(4, pairs, LANES)
    crossed = swap_core(jnp.stack([hard_add[1], hard_add[3]])).astype(F32)
    over_chip = swap_chip((hard_add[2].astype(F32) + crossed[1]).astype(BF16)).astype(F32)
    sum_q = jnp.dot(group_probs, p_own, preferred_element_type=F32) + hard_sum
    sum_p = lax.dot_general(
        group_probs, q_all, (((0,), (0,)), ((), ())), preferred_element_type=F32
    )
    sum_p = sum_p + (hard_add[0].astype(F32) + crossed[0] + over_chip)
    sums = jnp.stack(
        [sum_q.reshape(blocks, tok_rows, LANES), sum_p.reshape(blocks, tok_rows, LANES)], axis=1
    ).astype(BF16)
    sums = exchange(sums, BLK).transpose(1, 2, 0, 3).reshape(2, tok_rows, width).astype(F32)
    other = jnp.stack([emb[tok_rows:], emb[:tok_rows]]).astype(F32)
    cotangent = ((sums - other) / TAU).reshape(row_count, width)

    d_pooled, d_gain, d_bias = pullback(cotangent)
    d_out_bias = jnp.sum(d_pooled, 0)
    scaled = (LOSS_SCALE * d_pooled).astype(BF16)

    cols = [scaled[:, i * (width // 4) : (i + 1) * (width // 4)] for i in range(4)]
    cols = by_group(cols)
    far_cols = swap_chip(cols[2])
    diag_cols = lax.ppermute(cols[3], GRP, [(0, 3), (1, 2), (2, 1), (3, 0)])
    near_cols = swap_core(cols[1])

    def back(rows):
        return lax.dot_general(
            rows, out_proj, (((1,), (1,)), ((), ())), preferred_element_type=F32
        )

    far_part = back(jnp.concatenate([far_cols, diag_cols]))
    near_part = back(jnp.concatenate([cols[0], near_cols]))
    far_sum = far_part[:row_count] + swap_core(far_part[row_count:].astype(BF16)).astype(F32)
    far_sum = swap_chip(far_sum.astype(BF16)).astype(F32)
    near_sum = near_part[:row_count] + swap_core(near_part[row_count:].astype(BF16)).astype(F32)
    grad_attn = near_sum + far_sum

    vectors = jnp.stack([d_gain, d_out_bias, d_bias]).reshape(3, blocks, LANES).transpose(1, 0, 2)
    vectors = jnp.sum(exchange(vectors, BLK), axis=0)
    pair = jnp.stack([vectors, swap_core(vectors)])
    four = jnp.concatenate([pair, swap_chip(pair)])
    onehot = (tasks[:, None] == jnp.arange(task_bias.shape[0])[None, :]).astype(F32)
    placed = jnp.concatenate(
        [four[:, :2], onehot[:, :, None] * four[:, 2:3]], axis=1
    )
    placed = (placed[0] + placed[1]) + (placed[2] + placed[3])
    whole = exchange(jnp.broadcast_to(placed[None], (blocks,) + placed.shape), BLK)
    whole = whole.transpose(1, 0, 2).reshape(placed.shape[0], width)
    return (
        losses,
        grad_attn.reshape(2, tok_rows, width),
        whole[0],
        whole[2:],
        whole[1],
    )


def solution(mesh):
    fine = Mesh(mesh.devices.reshape(2, 2, 2, 4, 4), ALL)
    in_specs = (
        P(None, ALL, None),
        P(None, ALL, None),
        P(None, GRP),
        P(),
        P(),
        P(),
        P(GRP),
        P(ALL, None),
        P(ALL, None),
    )
    out_specs = (P(ALL), P(None, ALL, None), P(), P(), P())
    return jax.shard_map(local, mesh=fine, in_specs=in_specs, out_specs=out_specs, check_vma=False)
```

time: 651 us -> 225 us (0.35); the launches traced: 643 us -> 224 us
  waiting for transfers between devices: 341 us -> 88.3 us
  blocking collectives: 129 us -> 13.3 us
  local copies, waits for them, and re-layouts: 88.8 us -> 6.42 us
  starting transfers between devices: 10.4 us -> 60.1 us
  Pallas kernels: 0 us -> 14.5 us
  between operations: 15.3 us -> 1.84 us
  other arithmetic: 27.5 us -> 16.6 us
  matrix products: 30.8 us -> 22.6 us
    reduce_scatter x2 -> x0, waiting for transfers between devices: 152 us -> none  [the longest x1 152 us: local(): lax.psum_scatter(jnp.dot(probs.T, query_emb, preferred_element_type=jnp.f...]
    psum x1 -> x0, waiting for transfers between devices: 99.5 us -> none  [local(): lax.psum((grad_gain, grad_task_bias, grad_out_bias), ('grp', 'blk'))]
    all_gather x2 -> x0, waiting for transfers between devices: 66 us -> none  [the longest x1 35.8 us: local(): block_rows = lax.all_gather(passage_emb, 'blk', axis=0, tiled=True)]
    psum x1 -> x0, blocking collectives: 63.2 us -> none  [local(): lax.psum((grad_gain, grad_task_bias, grad_out_bias), ('grp', 'blk'))]
    all_to_all x3 -> x1, blocking collectives: 65.6 us -> 13.3 us  [exchange(): return lax.all_to_all(values, axes, split_axis=0, concat_axis=0, tiled=True)]
    scatter x2 -> x0, local copies, waits for them, and re-layouts: 49.7 us -> none  [the longest x1 41.2 us: local(): outgoing = jnp.zeros((dev_count, slot_cap, feat_width), jnp.bfloat16).at[...]
    ppermute x0 -> x21, waiting for transfers between devices: none -> 39.7 us  [the longest x8 35.6 us: swap_chip(): return lax.ppermute(values, 'xl', SWAP)]
    all_to_all x2 -> x6, starting transfers between devices: 10.2 us -> 37.4 us  [exchange(): return lax.all_to_all(values, axes, split_axis=0, concat_axis=0, tiled=True)]
  transfers between devices with their start and end apart: 7 -> 27, of which waited for: 6 -> 14; matrix products, arithmetic and copies ran while one was open for 15% -> 16% of each run, Pallas kernels for 0% -> 0%
where the time goes in v1:
time: 225 us; the launch traced here: 224 us
  waiting for transfers between devices  88.3 us (39%)
  starting transfers between devices  60.1 us (27%)
  matrix products  22.6 us (10%)
  other arithmetic  16.6 us (7%)
  Pallas kernels  14.5 us (6%)
  blocking collectives  13.3 us (6%)
  local copies, waits for them, and re-layouts  6.42 us (3%)
    all_to_all x6, waiting for transfers between devices, exchange(): return lax.all_to_all(values, axes, split_axis=0, concat_axis=0, tiled=True)  48.6 us
    all_to_all x6, starting transfers between devices, exchange(): return lax.all_to_all(values, axes, split_axis=0, concat_axis=0, tiled=True)  37.4 us
    ppermute x8, waiting for transfers between devices, swap_chip(): return lax.ppermute(values, 'xl', SWAP)  35.6 us
    ppermute x11, starting transfers between devices, swap_core(): return lax.ppermute(values, 'co', SWAP)  14.5 us
    all_to_all x1, blocking collectives, exchange(): return lax.all_to_all(values, axes, split_axis=0, concat_axis=0, tiled=True)  13.3 us
    dot_general x2, matrix products, back(): lax.dot_general(rows, out_proj, (((1,), (1,)), ((), ())), preferred_eleme...  12.1 us
    pallas_call x1, Pallas kernels, local(): pl.pallas_call(lambda *refs: scatter_kernel(hard_count, *refs), out_shape...  7.97 us
    pallas_call x1, Pallas kernels, local(): pl.pallas_call(lambda *refs: gather_kernel(hard_count, *refs), out_shape=...  6.57 us
  transfers between devices with their start and end apart: 27, of which 14 were waited for; matrix products, arithmetic and copies ran while one was open for 16% of the time, Pallas kernels for 0%

profile of v1, /device:TPU:1, one launch (start us, length us, event | category | flops | bytes accessed | tf_op | source)
XLA Modules:
  0.0 223.7 jit_solution(1813176288878953030)
XLA Ops:
  0.6 2.1 collective-permute-start
  4.4 6.9 %collective-permute-done = bf16[48,4096]{1,0:T(8,128)(2,1)S(1)} collective-permute-done((bf16[48,4096]{1,0:T(8,128)(2,1)}, bf16[48,4096]{1,0:T(8,128)(2,1)S(1)}, u32[]{:S(2)}, u32[]{:S(2)}) %collective-permute-start) | collective-permute-done | bytes 393248 | tf_op jit(solution)/shard_map/ppermute | solution.py:25
  11.3 1.7 collective-permute-start.1
  13.0 5.0 %convolution_convert_fusion.1 = bf16[96,1024]{1,0:T(8,128)(2,1)S(1)} fusion(bf16[4096,1024]{1,0:T(8,128)(2,1)} %param.11, bf16[48,4096]{1,0:T(8,128)(2,1)S(1)} %collective-permute-done.4, bf16[48,4096]{1,0:T(8,128)(2,1)} %bitcast.177), kind=kOutput, calls=%fused_computation.10 | convolution fusion | flops 806977536 | bytes 9371648 | tf_op jit(solution)/shard_map/dot_general | solution.py:109
  19.8 1.9 collective-permute-start.2
  21.8 3.2 %collective-permute-done.2 = bf16[48,1024]{1,0:T(8,128)(2,1)S(1)} collective-permute-done((bf16[48,1024]{1,0:T(8,128)(2,1)S(1)}, bf16[48,1024]{1,0:T(8,128)(2,1)S(1)}, u32[]{:S(2)}, u32[]{:S(2)}) %collective-permute-start.2) | collective-permute-done | bytes 98336 | tf_op jit(solution)/shard_map/ppermute | solution.py:117
  25.0 1.8 collective-permute-done.3
  29.1 10.8 %all-to-all-start = ((bf16[32,2,24,128]{3,2,1,0:T(8,128)(2,1)}), bf16[32,2,24,128]{3,2,1,0:T(8,128)(2,1)S(1)}, u32[]{:S(2)}, u32[]{:S(2)}) async-start(bf16[32,2,24,128]{3,2,1,0:T(8,128)(2,1)} %get-tuple-element.17), calls=%async_computation | async-start | bytes 786432 | tf_op jit(solution)/shard_map/all_to_all | solution.py:29
  40.0 10.4 %all-to-all-done = bf16[32,2,24,128]{3,2,1,0:T(8,128)(2,1)S(1)} async-done(((bf16[32,2,24,128]{3,2,1,0:T(8,128)(2,1)}), bf16[32,2,24,128]{3,2,1,0:T(8,128)(2,1)S(1)}, u32[]{:S(2)}, u32[]{:S(2)}) %all-to-all-start) | async-done | bytes 393248 | tf_op jit(solution)/shard_map/all_to_all | solution.py:29
  51.1 13.3 %all_to_all.36 = s32[32,1,168]{2,1,0:T(1,128)S(1)} all-to-all(s32[32,1,168]{2,1,0:T(1,128)S(1)} %broadcast_in_dim.49), channel_id=1, replica_groups=mesh['xl'=2,'co'=2,'xh'=2,'y'=4,'z'=4] {'xh','y','z'}, dimensions={0} | all-to-all | bytes 43008 | tf_op jit(solution)/shard_map/all_to_all | solution.py:29
  64.5 3.7 %collective-permute-start.6 = (bf16[768,128]{1,0:T(8,128)(2,1)S(1)}, bf16[768,128]{1,0:T(8,128)(2,1)S(1)}, u32[]{:S(2)}, u32[]{:S(2)}) collective-permute-start(bf16[768,128]{1,0:T(8,128)(2,1)S(1)} %bitcast.159), channel_id=1, source_target_pairs={{0,32},{32,0},{1,33},{33,1},{2,34},{34,2},{3,35},{35,3},{4,36},{36... | collective-permute-start | bytes 589832 | tf_op jit(solution)/shard_map/ppermute | solution.py:21
  69.7 6.6 %shard_map.128 = (bf16[7,768,128]{2,1,0:T(8,128)(2,1)S(1)}, f32[768,128]{1,0:T(8,128)S(1)}) custom-call(s32[5376]{0:T(1024)S(1)} %reshape.416.refs_0_, bf16[768,128]{1,0:T(8,128)(2,1)S(1)} %bitcast.131, bf16[3072,128]{1,0:T(8,128)(2,1)S(1)} %pad_maximum_fusion.1.refs_2_), custom_call_target="tpu_custom_call" | custom-call | tf_op jit(solution)/shard_map/pallas_call | solution.py:145
  77.7 4.7 %all-to-all-start.2 = ((f16[32,24,896]{2,1,0:T(8,128)(2,1)}), f16[32,24,896]{2,1,0:T(8,128)(2,1)}, u32[]{:S(2)}, u32[]{:S(2)}) async-start(f16[32,24,896]{2,1,0:T(8,128)(2,1)} %pad_maximum_fusion), calls=%async_computation.2 | async-start | bytes 2752512 | tf_op jit(solution)/shard_map/all_to_all | solution.py:29
  82.8 19.9 %all-to-all-done.2 = f16[32,24,896]{2,1,0:T(8,128)(2,1)} async-done(((f16[32,24,896]{2,1,0:T(8,128)(2,1)}), f16[32,24,896]{2,1,0:T(8,128)(2,1)}, u32[]{:S(2)}, u32[]{:S(2)}) %all-to-all-start.2) | async-done | bytes 1376288 | tf_op jit(solution)/shard_map/all_to_all | solution.py:29
  105.7 6.5 %all-to-all-start.3 = ((bf16[32,24,896]{2,1,0:T(8,128)(2,1)}), bf16[32,24,896]{2,1,0:T(8,128)(2,1)}, u32[]{:S(2)}, u32[]{:S(2)}) async-start(bf16[32,24,896]{2,1,0:T(8,128)(2,1)} %broadcast_in_dim.51), calls=%async_computation.3 | async-start | bytes 2752512 | tf_op jit(solution)/shard_map/all_to_all | solution.py:29
  113.6 14.0 %collective-permute-done.20 = s32[2]{0:T(128)S(1)} collective-permute-done((s32[2]{0:T(128)S(1)}, s32[2]{0:T(128)S(1)}, u32[]{:S(2)}, u32[]{:S(2)}) %collective-permute-start.20) | collective-permute-done | bytes 40 | tf_op jit(solution)/shard_map/ppermute | solution.py:25
  129.6 2.3 %all-to-all-done.3 = bf16[32,24,896]{2,1,0:T(8,128)(2,1)} async-done(((bf16[32,24,896]{2,1,0:T(8,128)(2,1)}), bf16[32,24,896]{2,1,0:T(8,128)(2,1)}, u32[]{:S(2)}, u32[]{:S(2)}) %all-to-all-start.3) | async-done | bytes 1376288 | tf_op jit(solution)/shard_map/all_to_all | solution.py:29
  132.9 8.0 %shard_map.129 = (bf16[3072,128]{1,0:T(8,128)(2,1)S(1)}, f32[768,128]{1,0:T(8,128)S(1)}) custom-call(s32[5376]{0:T(1024)S(1)} %reshape.416.refs_0_, bf16[768,128]{1,0:T(8,128)(2,1)S(1)} %slice.157.refs_1_, bf16[768,128]{1,0:T(8,128)(2,1)S(1)} %bitcast.132, bf16[7,768,128]{2,1,0:T(8,128)(2,1)S(1)} %get-tuple-element.10.refs_3_), custom_call_target="tpu_custom_call" | custom-call | tf_op jit(solution)/shard_map/pallas_call | solution.py:176
  140.9 2.4 %collective-permute-start.9 = (bf16[2,768,128]{2,1,0:T(8,128)(2,1)S(1)}, bf16[2,768,128]{2,1,0:T(8,128)(2,1)S(1)}, u32[]{:S(2)}, u32[]{:S(2)}) collective-permute-start(bf16[2,768,128]{2,1,0:T(8,128)(2,1)S(1)} %pad_maximum_fusion.4), channel_id=1, source_target_pairs={{0,32},{32,0},{1,33},{33,1},{2,34},{34,2},{3,35},{35,3},{4,36},{36... | collective-permute-start | bytes 1179656 | tf_op jit(solution)/shard_map/ppermute | solution.py:21
  143.5 1.7 fusion
  145.9 1.8 fusion.1
  147.6 4.3 %collective-permute-done.10 = bf16[768,128]{1,0:T(8,128)(2,1)S(1)} collective-permute-done((bf16[768,128]{1,0:T(8,128)(2,1)S(1)}, bf16[768,128]{1,0:T(8,128)(2,1)S(1)}, u32[]{:S(2)}, u32[]{:S(2)}) %collective-permute-start.10) | collective-permute-done | bytes 196640 | tf_op jit(solution)/shard_map/ppermute | solution.py:25
  152.8 6.6 %all-to-all-start.4 = ((bf16[32,2,24,128]{3,2,1,0:T(8,128)(2,1)}), bf16[32,2,24,128]{3,2,1,0:T(8,128)(2,1)S(1)}, u32[]{:S(2)}, u32[]{:S(2)}) async-start(bf16[32,2,24,128]{3,2,1,0:T(8,128)(2,1)} %pad_maximum_fusion.5), calls=%async_computation.4 | async-start | bytes 786432 | tf_op jit(solution)/shard_map/all_to_all | solution.py:29
  161.8 7.6 %all-to-all-done.4 = bf16[32,2,24,128]{3,2,1,0:T(8,128)(2,1)S(1)} async-done(((bf16[32,2,24,128]{3,2,1,0:T(8,128)(2,1)}), bf16[32,2,24,128]{3,2,1,0:T(8,128)(2,1)S(1)}, u32[]{:S(2)}, u32[]{:S(2)}) %all-to-all-start.4) | async-done | bytes 393248 | tf_op jit(solution)/shard_map/all_to_all | solution.py:29
  171.2 1.6 fusion.9
  173.4 4.7 %all-to-all-start.5 = ((f32[32,3,128]{2,1,0:T(4,128)}), f32[32,3,128]{2,1,0:T(4,128)S(1)}, u32[]{:S(2)}, u32[]{:S(2)}) async-start(f32[32,3,128]{2,1,0:T(4,128)} %maximum_bitcast_fusion), calls=%async_computation.5 | async-start | bytes 131072 | tf_op jit(solution)/shard_map/all_to_all | solution.py:29
  178.4 8.4 %all-to-all-done.5 = f32[32,3,128]{2,1,0:T(4,128)S(1)} async-done(((f32[32,3,128]{2,1,0:T(4,128)}), f32[32,3,128]{2,1,0:T(4,128)S(1)}, u32[]{:S(2)}, u32[]{:S(2)}) %all-to-all-start.5) | async-done | bytes 49184 | tf_op jit(solution)/shard_map/all_to_all | solution.py:29
  186.9 3.3 %collective-permute-start.17 = (f32[3,128]{1,0:T(4,128)S(1)}, f32[3,128]{1,0:T(4,128)S(1)}, u32[]{:S(2)}, u32[]{:S(2)}) collective-permute-start(f32[3,128]{1,0:T(4,128)S(1)} %reduce_sum.141), channel_id=1, source_target_pairs={{0,32},{32,0},{1,33},{33,1},{2,34},{34,2},{3,35},{35,3},{4,36},{36... | collective-permute-start | bytes 4616 | tf_op jit(solution)/shard_map/ppermute | solution.py:21
  194.5 4.1 %all-to-all-start.6 = ((f32[32,10,128]{2,1,0:T(8,128)}), f32[32,10,128]{2,1,0:T(8,128)S(1)}, u32[]{:S(2)}, u32[]{:S(2)}) async-start(f32[32,10,128]{2,1,0:T(8,128)} %broadcast_in_dim.58), calls=%async_computation.6 | async-start | bytes 524288 | tf_op jit(solution)/shard_map/all_to_all | solution.py:29
  198.6 6.1 %fusion.32 = f32[96,4096]{1,0:T(8,128)S(1)} fusion(bf16[4096,1024]{1,0:T(8,128)(2,1)} %param.11, bf16[48,1024]{1,0:T(8,128)(2,1)S(1)} %collective-permute-done.14, bf16[48,1024]{1,0:T(8,128)(2,1)S(1)} %collective-permute-done.13), kind=kOutput, calls=%fused_computation.74 | convolution fusion | flops 805699584 | bytes 10158080 | tf_op jit(solution)/shard_map/dot_general | solution.py:214
  206.1 6.0 %fusion.28 = f32[96,4096]{1,0:T(8,128)S(1)} fusion(bf16[4096,1024]{1,0:T(8,128)(2,1)} %param.11, bf16[48,1024]{1,0:T(8,128)(2,1)S(1)} %collective-permute-done.11, bf16[48,1024]{1,0:T(8,128)(2,1)S(1)} %get-tuple-element.30), kind=kOutput, calls=%fused_computation.70 | convolution fusion | flops 805699584 | bytes 10158080 | tf_op jit(solution)/shard_map/dot_general | solution.py:214
  214.2 8.5 %collective-permute-done.16 = bf16[48,4096]{1,0:T(8,128)(2,1)S(1)} collective-permute-done((bf16[48,4096]{1,0:T(8,128)(2,1)S(1)}, bf16[48,4096]{1,0:T(8,128)(2,1)S(1)}, u32[]{:S(2)}, u32[]{:S(2)}) %collective-permute-start.16) | collective-permute-done | bytes 393248 | tf_op jit(solution)/shard_map/ppermute | solution.py:25
  (131 shorter events, 32.0 us)
Async XLA Ops:
  0.6 10.7 %collective-permute-start = (bf16[48,4096]{1,0:T(8,128)(2,1)}, bf16[48,4096]{1,0:T(8,128)(2,1)S(1)}, u32[]{:S(2)}, u32[]{:S(2)}) collective-permute-start(bf16[48,4096]{1,0:T(8,128)(2,1)} %bitcast.175), channel_id=1, source_target_pairs={{0,64},{64,0},{1,65},{65,1},{2,66},{66,2},{3,67},{67,3},{4,68},{68... | collective-permute-start | bytes 1179656 | tf_op jit(solution)/shard_map/ppermute | solution.py:25
  2.8 10.3 %collective-permute-start.4 = (bf16[48,4096]{1,0:T(8,128)(2,1)}, bf16[48,4096]{1,0:T(8,128)(2,1)S(1)}, u32[]{:S(2)}, u32[]{:S(2)}) collective-permute-start(bf16[48,4096]{1,0:T(8,128)(2,1)} %bitcast.176), channel_id=1, source_target_pairs={{0,32},{32,0},{1,33},{33,1},{2,34},{34,2},{3,35},{35,3},{4,36},{36... | collective-permute-start | bytes 1179656 | tf_op jit(solution)/shard_map/ppermute | solution.py:21
  4.4 13.8 %slice-start = ((s8[8388608]{0:T(1024)(128)(4,1)}), s8[4194304]{0:T(1024)(128)(4,1)S(1)}, s32[]{:S(2)}) async-start(s8[8388608]{0:T(1024)(128)(4,1)} %bitcast.134), calls=%async_computation.7 | async-start | bytes 8388608
  4.4 13.8 %slice-start.1 = ((s8[8388608]{0:T(1024)(128)(4,1)}), s8[4194304]{0:T(1024)(128)(4,1)S(1)}, s32[]{:S(2)}) async-start(s8[8388608]{0:T(1024)(128)(4,1)} %bitcast.134), calls=%async_computation.8 | async-start | bytes 8388608
  11.3 6.8 %collective-permute-start.1 = (bf16[48,4096]{1,0:T(8,128)(2,1)S(1)}, bf16[48,4096]{1,0:T(8,128)(2,1)S(1)}, u32[]{:S(2)}, u32[]{:S(2)}) collective-permute-start(bf16[48,4096]{1,0:T(8,128)(2,1)S(1)} %collective-permute-done), channel_id=1, source_target_pairs={{0,32},{32,0},{1,33},{33,1},{2,34},{34,2},{3,35},{35,3},{4,36},{36... | collective-permute-start | bytes 1179656 | tf_op jit(solution)/shard_map/ppermute | solution.py:21
  18.1 3.8 %collective-permute-start.5 = (bf16[48,1024]{1,0:T(8,128)(2,1)S(1)}, bf16[48,1024]{1,0:T(8,128)(2,1)S(1)}, u32[]{:S(2)}, u32[]{:S(2)}) collective-permute-start(bf16[48,1024]{1,0:T(8,128)(2,1)S(1)} %slice.152), channel_id=1, source_target_pairs={{0,32},{32,0},{1,33},{33,1},{2,34},{34,2},{3,35},{35,3},{4,36},{36... | collective-permute-start | bytes 294920 | tf_op jit(solution)/shard_map/ppermute | solution.py:21
  19.8 5.3 %collective-permute-start.2 = (bf16[48,1024]{1,0:T(8,128)(2,1)S(1)}, bf16[48,1024]{1,0:T(8,128)(2,1)S(1)}, u32[]{:S(2)}, u32[]{:S(2)}) collective-permute-start(bf16[48,1024]{1,0:T(8,128)(2,1)S(1)} %get-tuple-element.39), channel_id=1, source_target_pairs={{0,96},{32,64},{64,32},{96,0},{1,97},{33,65},{65,33},{97,1},{2,98}... | collective-permute-start | bytes 294920 | tf_op jit(solution)/shard_map/ppermute | solution.py:117
  21.7 5.2 %collective-permute-start.3 = (bf16[48,1024]{1,0:T(8,128)(2,1)S(1)}, bf16[48,1024]{1,0:T(8,128)(2,1)S(1)}, u32[]{:S(2)}, u32[]{:S(2)}) collective-permute-start(bf16[48,1024]{1,0:T(8,128)(2,1)S(1)} %get-tuple-element.40), channel_id=1, source_target_pairs={{0,64},{64,0},{1,65},{65,1},{2,66},{66,2},{3,67},{67,3},{4,68},{68... | collective-permute-start | bytes 294920 | tf_op jit(solution)/shard_map/ppermute | solution.py:25
  27.7 23.1 %copy-start.6 = (s32[24,7]{0,1:T(8,128)S(1)}, s32[24,7]{0,1:T(8,128)}, u32[]{:S(2)}) copy-start(s32[24,7]{0,1:T(8,128)} %param.17) | copy-start | bytes 2020
  27.7 23.1 %copy-start.7 = (s32[24,7]{0,1:T(8,128)S(1)}, s32[24,7]{0,1:T(8,128)}, u32[]{:S(2)}) copy-start(s32[24,7]{0,1:T(8,128)} %param.16) | copy-start | bytes 2020
  29.1 21.3 %all-to-all-start = ((bf16[32,2,24,128]{3,2,1,0:T(8,128)(2,1)}), bf16[32,2,24,128]{3,2,1,0:T(8,128)(2,1)S(1)}, u32[]{:S(2)}, u32[]{:S(2)}) async-start(bf16[32,2,24,128]{3,2,1,0:T(8,128)(2,1)} %get-tuple-element.17), calls=%async_computation | async-start | bytes 786432 | tf_op jit(solution)/shard_map/all_to_all | solution.py:29
  50.4 17.8 %collective-permute-start.7 = (bf16[768,128]{1,0:T(8,128)(2,1)S(1)}, bf16[768,128]{1,0:T(8,128)(2,1)S(1)}, u32[]{:S(2)}, u32[]{:S(2)}) collective-permute-start(bf16[768,128]{1,0:T(8,128)(2,1)S(1)} %bitcast.158), channel_id=1, source_target_pairs={{0,64},{64,0},{1,65},{65,1},{2,66},{66,2},{3,67},{67,3},{4,68},{68... | collective-permute-start | bytes 589832 | tf_op jit(solution)/shard_map/ppermute | solution.py:25
  64.5 4.8 %collective-permute-start.6 = (bf16[768,128]{1,0:T(8,128)(2,1)S(1)}, bf16[768,128]{1,0:T(8,128)(2,1)S(1)}, u32[]{:S(2)}, u32[]{:S(2)}) collective-permute-start(bf16[768,128]{1,0:T(8,128)(2,1)S(1)} %bitcast.159), channel_id=1, source_target_pairs={{0,32},{32,0},{1,33},{33,1},{2,34},{34,2},{3,35},{35,3},{4,36},{36... | collective-permute-start | bytes 589832 | tf_op jit(solution)/shard_map/ppermute | solution.py:21
  68.2 1.4 collective-permute-start.8
  77.7 25.0 %all-to-all-start.2 = ((f16[32,24,896]{2,1,0:T(8,128)(2,1)}), f16[32,24,896]{2,1,0:T(8,128)(2,1)}, u32[]{:S(2)}, u32[]{:S(2)}) async-start(f16[32,24,896]{2,1,0:T(8,128)(2,1)} %pad_maximum_fusion), calls=%async_computation.2 | async-start | bytes 2752512 | tf_op jit(solution)/shard_map/all_to_all | solution.py:29
  82.4 29.8 %collective-permute-start.19 = (s32[1]{0:T(128)}, s32[1]{0:T(128)}, u32[]{:S(2)}, u32[]{:S(2)}) collective-permute-start(s32[1]{0:T(128)} %param.15), channel_id=1, source_target_pairs={{0,32},{32,0},{1,33},{33,1},{2,34},{34,2},{3,35},{35,3},{4,36},{36... | collective-permute-start | bytes 20 | tf_op jit(solution)/shard_map/ppermute | solution.py:21
  105.7 26.2 %all-to-all-start.3 = ((bf16[32,24,896]{2,1,0:T(8,128)(2,1)}), bf16[32,24,896]{2,1,0:T(8,128)(2,1)}, u32[]{:S(2)}, u32[]{:S(2)}) async-start(bf16[32,24,896]{2,1,0:T(8,128)(2,1)} %broadcast_in_dim.51), calls=%async_computation.3 | async-start | bytes 2752512 | tf_op jit(solution)/shard_map/all_to_all | solution.py:29
  112.9 14.7 %collective-permute-start.20 = (s32[2]{0:T(128)S(1)}, s32[2]{0:T(128)S(1)}, u32[]{:S(2)}, u32[]{:S(2)}) collective-permute-start(s32[2]{0:T(128)S(1)} %pad_add_fusion), channel_id=1, source_target_pairs={{0,64},{64,0},{1,65},{65,1},{2,66},{66,2},{3,67},{67,3},{4,68},{68... | collective-permute-start | bytes 32 | tf_op jit(solution)/shard_map/ppermute | solution.py:25
  140.9 4.3 %collective-permute-start.9 = (bf16[2,768,128]{2,1,0:T(8,128)(2,1)S(1)}, bf16[2,768,128]{2,1,0:T(8,128)(2,1)S(1)}, u32[]{:S(2)}, u32[]{:S(2)}) collective-permute-start(bf16[2,768,128]{2,1,0:T(8,128)(2,1)S(1)} %pad_maximum_fusion.4), channel_id=1, source_target_pairs={{0,32},{32,0},{1,33},{33,1},{2,34},{34,2},{3,35},{35,3},{4,36},{36... | collective-permute-start | bytes 1179656 | tf_op jit(solution)/shard_map/ppermute | solution.py:21
  145.3 6.6 %collective-permute-start.10 = (bf16[768,128]{1,0:T(8,128)(2,1)S(1)}, bf16[768,128]{1,0:T(8,128)(2,1)S(1)}, u32[]{:S(2)}, u32[]{:S(2)}) collective-permute-start(bf16[768,128]{1,0:T(8,128)(2,1)S(1)} %fusion.22), channel_id=1, source_target_pairs={{0,64},{64,0},{1,65},{65,1},{2,66},{66,2},{3,67},{67,3},{4,68},{68... | collective-permute-start | bytes 589832 | tf_op jit(solution)/shard_map/ppermute | solution.py:25
  152.8 16.5 %all-to-all-start.4 = ((bf16[32,2,24,128]{3,2,1,0:T(8,128)(2,1)}), bf16[32,2,24,128]{3,2,1,0:T(8,128)(2,1)S(1)}, u32[]{:S(2)}, u32[]{:S(2)}) async-start(bf16[32,2,24,128]{3,2,1,0:T(8,128)(2,1)} %pad_maximum_fusion.5), calls=%async_computation.4 | async-start | bytes 786432 | tf_op jit(solution)/shard_map/all_to_all | solution.py:29
  172.7 17.5 %copy-start.1 = (f32[2,24,4096]{2,1,0:T(8,128)S(1)}, f32[2,24,4096]{2,1,0:T(8,128)}, u32[]{:S(2)}) copy-start(f32[2,24,4096]{2,1,0:T(8,128)} %maximum_convert_fusion) | copy-start | bytes 2359300
  173.4 13.4 %all-to-all-start.5 = ((f32[32,3,128]{2,1,0:T(4,128)}), f32[32,3,128]{2,1,0:T(4,128)S(1)}, u32[]{:S(2)}, u32[]{:S(2)}) async-start(f32[32,3,128]{2,1,0:T(4,128)} %maximum_bitcast_fusion), calls=%async_computation.5 | async-start | bytes 131072 | tf_op jit(solution)/shard_map/all_to_all | solution.py:29
  186.9 4.2 %collective-permute-start.17 = (f32[3,128]{1,0:T(4,128)S(1)}, f32[3,128]{1,0:T(4,128)S(1)}, u32[]{:S(2)}, u32[]{:S(2)}) collective-permute-start(f32[3,128]{1,0:T(4,128)S(1)} %reduce_sum.141), channel_id=1, source_target_pairs={{0,32},{32,0},{1,33},{33,1},{2,34},{34,2},{3,35},{35,3},{4,36},{36... | collective-permute-start | bytes 4616 | tf_op jit(solution)/shard_map/ppermute | solution.py:21
  191.1 2.5 %collective-permute-start.18 = (f32[2,3,128]{2,1,0:T(4,128)S(1)}, f32[2,3,128]{2,1,0:T(4,128)S(1)}, u32[]{:S(2)}, u32[]{:S(2)}) collective-permute-start(f32[2,3,128]{2,1,0:T(4,128)S(1)} %pad_maximum_fusion.8), channel_id=1, source_target_pairs={{0,64},{64,0},{1,65},{65,1},{2,66},{66,2},{3,67},{67,3},{4,68},{68... | collective-permute-start | bytes 9224 | tf_op jit(solution)/shard_map/ppermute | solution.py:25
  191.2 7.3 %collective-permute-start.13 = (bf16[48,1024]{1,0:T(8,128)(2,1)S(1)}, bf16[48,1024]{1,0:T(8,128)(2,1)S(1)}, u32[]{:S(2)}, u32[]{:S(2)}) collective-permute-start(bf16[48,1024]{1,0:T(8,128)(2,1)S(1)} %get-tuple-element.29), channel_id=1, source_target_pairs={{0,64},{64,0},{1,65},{65,1},{2,66},{66,2},{3,67},{67,3},{4,68},{68... | collective-permute-start | bytes 294920 | tf_op jit(solution)/shard_map/ppermute | solution.py:25
  192.7 5.8 %collective-permute-start.14 = (bf16[48,1024]{1,0:T(8,128)(2,1)S(1)}, bf16[48,1024]{1,0:T(8,128)(2,1)S(1)}, u32[]{:S(2)}, u32[]{:S(2)}) collective-permute-start(bf16[48,1024]{1,0:T(8,128)(2,1)S(1)} %get-tuple-element.32), channel_id=1, source_target_pairs={{0,96},{32,64},{64,32},{96,0},{1,97},{33,65},{65,33},{97,1},{2,98}... | collective-permute-start | bytes 294920 | tf_op jit(solution)/shard_map/ppermute | solution.py:210
  193.2 12.9 %collective-permute-start.11 = (bf16[48,1024]{1,0:T(8,128)(2,1)S(1)}, bf16[48,1024]{1,0:T(8,128)(2,1)S(1)}, u32[]{:S(2)}, u32[]{:S(2)}) collective-permute-start(bf16[48,1024]{1,0:T(8,128)(2,1)S(1)} %get-tuple-element.31), channel_id=1, source_target_pairs={{0,32},{32,0},{1,33},{33,1},{2,34},{34,2},{3,35},{35,3},{4,36},{36... | collective-permute-start | bytes 294920 | tf_op jit(solution)/shard_map/ppermute | solution.py:21
  194.5 18.5 %all-to-all-start.6 = ((f32[32,10,128]{2,1,0:T(8,128)}), f32[32,10,128]{2,1,0:T(8,128)S(1)}, u32[]{:S(2)}, u32[]{:S(2)}) async-start(f32[32,10,128]{2,1,0:T(8,128)} %broadcast_in_dim.58), calls=%async_computation.6 | async-start | bytes 524288 | tf_op jit(solution)/shard_map/all_to_all | solution.py:29
  204.7 7.7 %collective-permute-start.15 = (bf16[48,4096]{1,0:T(8,128)(2,1)S(1)}, bf16[48,4096]{1,0:T(8,128)(2,1)S(1)}, u32[]{:S(2)}, u32[]{:S(2)}) collective-permute-start(bf16[48,4096]{1,0:T(8,128)(2,1)S(1)} %slice.299), channel_id=1, source_target_pairs={{0,32},{32,0},{1,33},{33,1},{2,34},{34,2},{3,35},{35,3},{4,36},{36... | collective-permute-start | bytes 1179656 | tf_op jit(solution)/shard_map/ppermute | solution.py:21
  212.2 2.0 collective-permute-start.12
  212.4 10.3 %collective-permute-start.16 = (bf16[48,4096]{1,0:T(8,128)(2,1)S(1)}, bf16[48,4096]{1,0:T(8,128)(2,1)S(1)}, u32[]{:S(2)}, u32[]{:S(2)}) collective-permute-start(bf16[48,4096]{1,0:T(8,128)(2,1)S(1)} %fusion.12), channel_id=1, source_target_pairs={{0,64},{64,0},{1,65},{65,1},{2,66},{66,2},{3,67},{67,3},{4,68},{68... | collective-permute-start | bytes 1179656 | tf_op jit(solution)/shard_map/ppermute | solution.py:25
  (5 other events, 36.1 us)

commit v2 on v1

--- a/solution.py
+++ b/solution.py
@@ -35,17 +35,18 @@
     return mixture * lax.rsqrt(jnp.sum(mixture * mixture, axis=-1, keepdims=True) + 1e-06)
 
 
-def gather_kernel(hard_count, ids, q_ref, p_ref, neg_ref, hard_ref, wide, picked):
+def gather_kernel(hard_count, tok_rows, ids, q_ref, p_ref, neg_ref, hard_ref, wide, picked):
     rows = q_ref.shape[0]
     wide[...] = p_ref[...].astype(F32)
 
-    def pick(i, carry):
-        for k in range(hard_count):
-            source = ids[i * hard_count + k]
-            picked[k, pl.ds(i, 1), :] = wide[pl.ds(source, 1), :]
+    def pick(block, carry):
+        for i in range(tok_rows):
+            for k in range(hard_count):
+                source = ids[(block * hard_count + k) * tok_rows + i]
+                picked[k, pl.ds(block * tok_rows + i, 1), :] = wide[pl.ds(source, 1), :]
         return carry
 
-    lax.fori_loop(0, rows, pick, 0, unroll=8)
+    lax.fori_loop(0, rows // tok_rows, pick, 0)
     q = q_ref[...].astype(F32)
     lane = lax.broadcasted_iota(jnp.int32, (rows, LANES), 1)
     hard = jnp.zeros((rows, LANES), F32)
@@ -56,7 +57,7 @@
     hard_ref[...] = hard
 
 
-def scatter_kernel(hard_count, ids, w_ref, q_ref, neg_ref, add_ref, sum_ref, slot, *parts):
+def scatter_kernel(hard_count, tok_rows, ids, w_ref, q_ref, neg_ref, add_ref, sum_ref, slot, *parts):
     rows = q_ref.shape[0]
     q = q_ref[...].astype(F32)
     total = jnp.zeros((rows, LANES), F32)
@@ -67,13 +68,14 @@
         parts[k][...] = jnp.zeros_like(parts[k])
     sum_ref[...] = total
 
-    def place(i, carry):
-        for k in range(hard_count):
-            target = pl.ds(ids[i * hard_count + k], 1)
-            parts[k][target, :] = parts[k][target, :] + slot[k, pl.ds(i, 1), :]
+    def place(block, carry):
+        for i in range(tok_rows):
+            for k in range(hard_count):
+                target = pl.ds(ids[(block * hard_count + k) * tok_rows + i], 1)
+                parts[k][target, :] += slot[k, pl.ds(block * tok_rows + i, 1), :]
         return carry
 
-    lax.fori_loop(0, rows, place, 0, unroll=4)
+    lax.fori_loop(0, rows // tok_rows, place, 0)
     added = parts[0][...]
     for k in range(1, hard_count):
         added = added + parts[k][...]
@@ -98,9 +100,7 @@
     far_rows = swap_chip(attn_rows)
     near_rows = swap_core(attn_rows)
 
-    owner_group = (neg_owner // blocks) ^ me
-    own_ids = (owner_group * pairs + (neg_owner % blocks) * tok_rows + neg_row).reshape(1, -1)
-    ids = exchange(jnp.broadcast_to(own_ids, (blocks, tok_rows * hard_count)), BLK).reshape(-1)
+    out_proj_t = lax.optimization_barrier(out_proj.T)
     near_task = swap_core(task_ids)
     tasks = jnp.concatenate([task_ids, near_task])
     tasks = jnp.concatenate([tasks, swap_chip(tasks)])
@@ -109,6 +109,7 @@
         return jnp.dot(rows, out_proj, preferred_element_type=F32).astype(BF16)
 
     chip_columns = project(jnp.concatenate([attn_rows, near_rows]))
+    far_rows, chip_columns = lax.optimization_barrier((far_rows, chip_columns))
     far_columns = project(jnp.concatenate([far_rows, swap_core(far_rows)]))
     parts = [
         chip_columns[:row_count],
@@ -131,11 +132,26 @@
     )
     emb = embedded.astype(BF16)
 
-    spread = exchange(
-        emb.reshape(2, tok_rows, blocks, LANES).transpose(2, 0, 1, 3), BLK
-    )
-    q_all = spread[:, 0].reshape(pairs, LANES)
-    p_own = spread[:, 1].reshape(pairs, LANES)
+    half = LANES // 2
+    fill = ((0, 1), (0, half - tok_rows))
+    requests = jnp.concatenate(
+        [jnp.pad(neg_owner.T, fill), jnp.pad(neg_row.T, fill)], axis=1
+    ).astype(BF16)
+    spread = emb.reshape(2, tok_rows, blocks, LANES).transpose(2, 0, 1, 3)
+    spread = jnp.concatenate(
+        [
+            spread.reshape(blocks, row_count, LANES),
+            jnp.broadcast_to(requests[None], (blocks,) + requests.shape),
+        ],
+        axis=1,
+    )
+    spread = exchange(spread, BLK)
+    q_all = spread[:, :tok_rows].reshape(pairs, LANES)
+    p_own = spread[:, tok_rows:row_count].reshape(pairs, LANES)
+    requests = spread[:, row_count : row_count + hard_count].astype(jnp.int32)
+    owner = requests[:, :, :tok_rows]
+    ids = ((owner // blocks) ^ me) * pairs + (owner % blocks) * tok_rows
+    ids = (ids + requests[:, :, half : half + tok_rows]).reshape(-1)
     p_far = swap_chip(p_own)
     p_all = jnp.concatenate([p_own, swap_core(p_own), p_far, swap_core(p_far)])
 
@@ -143,7 +159,7 @@
         q_all, p_own, (((1,), (1,)), ((), ())), preferred_element_type=F32
     )
     negatives, hard_part = pl.pallas_call(
-        lambda *refs: gather_kernel(hard_count, *refs),
+        lambda *refs: gather_kernel(hard_count, tok_rows, *refs),
         out_shape=(
             jax.ShapeDtypeStruct((hard_count, pairs, LANES), BF16),
             jax.ShapeDtypeStruct((pairs, LANES), F32),
@@ -156,25 +172,32 @@
         ],
         compiler_params=params,
     )(ids, q_all, p_all)
-    part = jnp.concatenate([score_part, hard_part], axis=1).astype(SEND)
-    part = exchange(part.reshape(blocks, tok_rows, pairs + LANES), BLK)
-    scores = jnp.sum(part.astype(F32), axis=0) / TAU
+    score_part = exchange(score_part.astype(SEND).reshape(blocks, tok_rows, pairs), BLK)
+    score_part, hard_part = lax.optimization_barrier((score_part, hard_part))
+    hard_part = exchange(hard_part.astype(SEND).reshape(blocks, tok_rows, LANES), BLK)
+    scores = jnp.sum(score_part.astype(F32), axis=0) / TAU
+    hard = jnp.sum(hard_part.astype(F32), axis=0) / TAU
 
     column = lax.broadcasted_iota(jnp.int32, scores.shape, 1)
     row = lax.broadcasted_iota(jnp.int32, scores.shape, 0)
-    weights = jnp.where(column < pairs + hard_count, jnp.exp(scores), 0.0)
-    totals = jnp.sum(weights, axis=1, keepdims=True)
+    weights = jnp.exp(scores)
+    slot = lax.broadcasted_iota(jnp.int32, hard.shape, 1)
+    hard_weights = jnp.where(slot < hard_count, jnp.exp(hard), 0.0)
+    totals = jnp.sum(weights, axis=1, keepdims=True) + jnp.sum(hard_weights, axis=1, keepdims=True)
     own_column = lax.axis_index(BLK) * tok_rows + row
     own_score = jnp.sum(jnp.where(column == own_column, scores, 0.0), axis=1)
     losses = jnp.log(totals[:, 0]) - own_score
-    probs = (weights / totals).astype(BF16)
-    probs = exchange(
-        jnp.broadcast_to(probs[None], (blocks, tok_rows, pairs + LANES)), BLK
-    ).reshape(pairs, pairs + LANES)
-
-    group_probs = probs[:, :pairs]
+
+    def spread_rows(values):
+        values = values.astype(BF16)
+        values = exchange(jnp.broadcast_to(values[None], (blocks,) + values.shape), BLK)
+        return values.reshape((pairs,) + values.shape[2:])
+
+    group_probs = spread_rows(weights / totals)
+    hard_probs = spread_rows(hard_weights / totals)
+
     hard_add, hard_sum = pl.pallas_call(
-        lambda *refs: scatter_kernel(hard_count, *refs),
+        lambda *refs: scatter_kernel(hard_count, tok_rows, *refs),
         out_shape=(
             jax.ShapeDtypeStruct((4 * pairs, LANES), BF16),
             jax.ShapeDtypeStruct((pairs, LANES), F32),
@@ -184,7 +207,7 @@
         scratch_shapes=[pltpu.VMEM((hard_count, pairs, LANES), F32)]
         + [pltpu.VMEM((4 * pairs, LANES), F32)] * hard_count,
         compiler_params=params,
-    )(ids, probs[:, pairs:], q_all, negatives)
+    )(ids, hard_probs, q_all, negatives)
     hard_add = hard_add.reshape(4, pairs, LANES)
     crossed = swap_core(jnp.stack([hard_add[1], hard_add[3]])).astype(F32)
     over_chip = swap_chip((hard_add[2].astype(F32) + crossed[1]).astype(BF16)).astype(F32)
@@ -204,26 +227,34 @@
     d_out_bias = jnp.sum(d_pooled, 0)
     scaled = (LOSS_SCALE * d_pooled).astype(BF16)
 
+
     cols = [scaled[:, i * (width // 4) : (i + 1) * (width // 4)] for i in range(4)]
     cols = by_group(cols)
     far_cols = swap_chip(cols[2])
     diag_cols = lax.ppermute(cols[3], GRP, [(0, 3), (1, 2), (2, 1), (3, 0)])
     near_cols = swap_core(cols[1])
+    d_gain, d_out_bias, d_bias, near_cols = lax.optimization_barrier(
+        (d_gain, d_out_bias, d_bias, near_cols)
+    )
 
     def back(rows):
         return lax.dot_general(
-            rows, out_proj, (((1,), (1,)), ((), ())), preferred_element_type=F32
+            rows, out_proj_t, (((1,), (0,)), ((), ())), preferred_element_type=F32
         )
 
+    vectors = jnp.stack([d_gain, d_out_bias, d_bias]).reshape(3, blocks, LANES).transpose(1, 0, 2)
+    vectors, far_cols, diag_cols = lax.optimization_barrier(
+        (exchange(vectors, BLK), far_cols, diag_cols)
+    )
+    vectors = jnp.sum(vectors, axis=0)
     far_part = back(jnp.concatenate([far_cols, diag_cols]))
+    far_sum = far_part[:row_count] + swap_core(far_part[row_count:].astype(BF16)).astype(F32)
+    far_sum, near_cols = lax.optimization_barrier((far_sum.astype(BF16), near_cols))
+    far_sum = swap_chip(far_sum).astype(F32)
     near_part = back(jnp.concatenate([cols[0], near_cols]))
-    far_sum = far_part[:row_count] + swap_core(far_part[row_count:].astype(BF16)).astype(F32)
-    far_sum = swap_chip(far_sum.astype(BF16)).astype(F32)
     near_sum = near_part[:row_count] + swap_core(near_part[row_count:].astype(BF16)).astype(F32)
     grad_attn = near_sum + far_sum
 
-    vectors = jnp.stack([d_gain, d_out_bias, d_bias]).reshape(3, blocks, LANES).transpose(1, 0, 2)
-    vectors = jnp.sum(exchange(vectors, BLK), axis=0)
     pair = jnp.stack([vectors, swap_core(vectors)])
     four = jnp.concatenate([pair, swap_chip(pair)])
     onehot = (tasks[:, None] == jnp.arange(task_bias.shape[0])[None, :]).astype(F32)

time: 225 us -> 221 us (0.982)
  starting transfers between devices: 60.1 us -> 76.9 us
  blocking collectives: 13.3 us -> 0 us
  waiting for transfers between devices: 88.3 us -> 76.2 us
  matrix products: 22.6 us -> 27 us
    all_to_all x6 -> x8, starting transfers between devices: 37.4 us -> 51 us  [exchange(): return lax.all_to_all(values, axes, split_axis=0, concat_axis=0, tiled=True)]
    all_to_all x1 -> x0, blocking collectives: 13.3 us -> none  [exchange(): return lax.all_to_all(values, axes, split_axis=0, concat_axis=0, tiled=True)]
    ppermute x8, waiting for transfers between devices: 35.6 us -> 22.4 us  [swap_chip(): return lax.ppermute(values, 'xl', SWAP)]
    ppermute x11, starting transfers between devices: 14.5 us -> 18.3 us  [swap_core(): return lax.ppermute(values, 'co', SWAP)]
    dot_general x2, matrix products: 6.49 us -> 9.86 us  [project(): return jnp.dot(rows, out_proj, preferred_element_type=F32).astype(BF16)]
    all_to_all x6 -> x8, waiting for transfers between devices: 48.6 us -> 47.8 us  [exchange(): return lax.all_to_all(values, axes, split_axis=0, concat_axis=0, tiled=True)]
  transfers between devices with their start and end apart: 27 -> 29, of which waited for: 14 -> 16; matrix products, arithmetic and copies ran while one was open for 16% -> 21% of each run, Pallas kernels for 0% -> 6%
where the time goes in v2:
time: 221 us; the launch traced here: 220 us
  starting transfers between devices  76.9 us (35%)
  waiting for transfers between devices  76.2 us (34%)
  matrix products  27 us (12%)
  other arithmetic  17.8 us (8%)
  Pallas kernels  13.4 us (6%)
  local copies, waits for them, and re-layouts  6.33 us (3%)
    all_to_all x8, starting transfers between devices, exchange(): return lax.all_to_all(values, axes, split_axis=0, concat_axis=0, tiled=True)  51 us
    all_to_all x8, waiting for transfers between devices, exchange(): return lax.all_to_all(values, axes, split_axis=0, concat_axis=0, tiled=True)  47.8 us
    ppermute x8, waiting for transfers between devices, swap_chip(): return lax.ppermute(values, 'xl', SWAP)  22.4 us
    ppermute x11, starting transfers between devices, swap_core(): return lax.ppermute(values, 'co', SWAP)  18.3 us
    dot_general x2, matrix products, back(): lax.dot_general(rows, out_proj_t, (((1,), (0,)), ((), ())), preferred_ele...  12.1 us
    dot_general x2, matrix products, project(): return jnp.dot(rows, out_proj, preferred_element_type=F32).astype(BF16)  9.86 us
    pallas_call x1, Pallas kernels, local(): pl.pallas_call(lambda *refs: scatter_kernel(hard_count, tok_rows, *refs),...  7.21 us
    pallas_call x1, Pallas kernels, local(): pl.pallas_call(lambda *refs: gather_kernel(hard_count, tok_rows, *refs),...  6.24 us
  transfers between devices with their start and end apart: 29, of which 16 were waited for; matrix products, arithmetic and copies ran while one was open for 21% of the time, Pallas kernels for 6%

profile of v2, /device:TPU:1, one launch (start us, length us, event | category | flops | bytes accessed | tf_op | source)
XLA Modules:
  0.0 219.6 jit_solution(17704861751950839275)
XLA Ops:
  4.1 5.0 %convolution_convert_fusion.2 = bf16[96,1024]{1,0:T(8,128)(2,1)S(1)} fusion(bf16[4096,1024]{1,0:T(8,128)(2,1)} %param.11, bf16[48,4096]{1,0:T(8,128)(2,1)S(1)} %collective-permute-done.1, bf16[48,4096]{1,0:T(8,128)(2,1)} %bitcast.185), kind=kOutput, calls=%fused_computation.11 | convolution fusion | flops 806977536 | bytes 9371648 | tf_op jit(solution)/shard_map/dot_general | solution.py:109
  9.2 3.8 %collective-permute-done = bf16[48,4096]{1,0:T(8,128)(2,1)S(1)} collective-permute-done((bf16[48,4096]{1,0:T(8,128)(2,1)}, bf16[48,4096]{1,0:T(8,128)(2,1)S(1)}, u32[]{:S(2)}, u32[]{:S(2)}) %collective-permute-start) | collective-permute-done | bytes 393248 | tf_op jit(solution)/shard_map/ppermute | solution.py:25
  15.2 4.8 %convolution_convert_fusion.1 = bf16[96,1024]{1,0:T(8,128)(2,1)S(1)} fusion(bf16[4096,1024]{1,0:T(8,128)(2,1)} %param.11, bf16[48,4096]{1,0:T(8,128)(2,1)S(1)} %collective-permute-done.2, bf16[48,4096]{1,0:T(8,128)(2,1)S(1)} %collective-permute-done), kind=kOutput, calls=%fused_computation.10 | convolution fusion | flops 806977536 | bytes 9371648 | tf_op jit(solution)/shard_map/dot_general | solution.py:109
  22.0 3.3 %collective-permute-done.3 = bf16[48,1024]{1,0:T(8,128)(2,1)S(1)} collective-permute-done((bf16[48,1024]{1,0:T(8,128)(2,1)S(1)}, bf16[48,1024]{1,0:T(8,128)(2,1)S(1)}, u32[]{:S(2)}, u32[]{:S(2)}) %collective-permute-start.3) | collective-permute-done | bytes 98336 | tf_op jit(solution)/shard_map/ppermute | solution.py:118
  25.3 1.8 collective-permute-done.4
  30.4 10.6 %all-to-all-start = ((bf16[32,56,128]{2,1,0:T(8,128)(2,1)}), bf16[32,56,128]{2,1,0:T(8,128)(2,1)S(1)}, u32[]{:S(2)}, u32[]{:S(2)}) async-start(bf16[32,56,128]{2,1,0:T(8,128)(2,1)} %pad_maximum_fusion.1), calls=%async_computation | async-start | bytes 917504 | tf_op jit(solution)/shard_map/all_to_all | solution.py:29
  42.0 9.8 %all-to-all-done = bf16[32,56,128]{2,1,0:T(8,128)(2,1)S(1)} async-done(((bf16[32,56,128]{2,1,0:T(8,128)(2,1)}), bf16[32,56,128]{2,1,0:T(8,128)(2,1)S(1)}, u32[]{:S(2)}, u32[]{:S(2)}) %all-to-all-start) | async-done | bytes 458784 | tf_op jit(solution)/shard_map/all_to_all | solution.py:29
  53.4 4.7 %all-to-all-start.1 = ((f16[32,24,768]{2,1,0:T(8,128)(2,1)}), f16[32,24,768]{2,1,0:T(8,128)(2,1)}, u32[]{:S(2)}, u32[]{:S(2)}) async-start(f16[32,24,768]{2,1,0:T(8,128)(2,1)} %bitcast.15), calls=%async_computation.1 | async-start | bytes 2359296 | tf_op jit(solution)/shard_map/all_to_all | solution.py:29
  60.5 3.1 %collective-permute-start.6 = (bf16[768,128]{1,0:T(8,128)(2,1)S(1)}, bf16[768,128]{1,0:T(8,128)(2,1)S(1)}, u32[]{:S(2)}, u32[]{:S(2)}) collective-permute-start(bf16[768,128]{1,0:T(8,128)(2,1)S(1)} %bitcast.167), channel_id=1, source_target_pairs={{0,32},{32,0},{1,33},{33,1},{2,34},{34,2},{3,35},{35,3},{4,36},{36... | collective-permute-start | bytes 589832 | tf_op jit(solution)/shard_map/ppermute | solution.py:21
  63.6 10.1 %collective-permute-done.7 = bf16[768,128]{1,0:T(8,128)(2,1)S(1)} collective-permute-done((bf16[768,128]{1,0:T(8,128)(2,1)S(1)}, bf16[768,128]{1,0:T(8,128)(2,1)S(1)}, u32[]{:S(2)}, u32[]{:S(2)}) %collective-permute-start.7) | collective-permute-done | bytes 196640 | tf_op jit(solution)/shard_map/ppermute | solution.py:25
  73.7 3.1 %collective-permute-start.8 = (bf16[768,128]{1,0:T(8,128)(2,1)S(1)}, bf16[768,128]{1,0:T(8,128)(2,1)S(1)}, u32[]{:S(2)}, u32[]{:S(2)}) collective-permute-start(bf16[768,128]{1,0:T(8,128)(2,1)S(1)} %collective-permute-done.7), channel_id=1, source_target_pairs={{0,32},{32,0},{1,33},{33,1},{2,34},{34,2},{3,35},{35,3},{4,36},{36... | collective-permute-start | bytes 589832 | tf_op jit(solution)/shard_map/ppermute | solution.py:21
  77.8 6.2 %shard_map.128 = (bf16[7,768,128]{2,1,0:T(8,128)(2,1)S(1)}, f32[768,128]{1,0:T(8,128)S(1)}) custom-call(s32[5376]{0:T(1024)S(1)} %reshape.461.refs_0_, bf16[768,128]{1,0:T(8,128)(2,1)S(1)} %bitcast.138, bf16[3072,128]{1,0:T(8,128)(2,1)S(1)} %pad_maximum_fusion.refs_2_), custom_call_target="tpu_custom_call" | custom-call | tf_op jit(solution)/shard_map/pallas_call | solution.py:161
  84.8 10.0 %all-to-all-start.2 = ((f16[32,24,128]{2,1,0:T(8,128)(2,1)}), f16[32,24,128]{2,1,0:T(8,128)(2,1)S(1)}, u32[]{:S(2)}, u32[]{:S(2)}) async-start(f16[32,24,128]{2,1,0:T(8,128)(2,1)} %bitcast.16), calls=%async_computation.2 | async-start | bytes 393216 | tf_op jit(solution)/shard_map/all_to_all | solution.py:29
  96.4 7.5 %all-to-all-done.2 = f16[32,24,128]{2,1,0:T(8,128)(2,1)S(1)} async-done(((f16[32,24,128]{2,1,0:T(8,128)(2,1)}), f16[32,24,128]{2,1,0:T(8,128)(2,1)S(1)}, u32[]{:S(2)}, u32[]{:S(2)}) %all-to-all-start.2) | async-done | bytes 196640 | tf_op jit(solution)/shard_map/all_to_all | solution.py:29
  105.4 3.9 %all-to-all-start.4 = ((bf16[32,24,128]{2,1,0:T(8,128)(2,1)}), bf16[32,24,128]{2,1,0:T(8,128)(2,1)S(1)}, u32[]{:S(2)}, u32[]{:S(2)}) async-start(bf16[32,24,128]{2,1,0:T(8,128)(2,1)} %broadcast_in_dim.32), calls=%async_computation.4 | async-start | bytes 393216 | tf_op jit(solution)/shard_map/all_to_all | solution.py:29
  109.4 9.1 %all-to-all-done.4 = bf16[32,24,128]{2,1,0:T(8,128)(2,1)S(1)} async-done(((bf16[32,24,128]{2,1,0:T(8,128)(2,1)}), bf16[32,24,128]{2,1,0:T(8,128)(2,1)S(1)}, u32[]{:S(2)}, u32[]{:S(2)}) %all-to-all-start.4) | async-done | bytes 196640 | tf_op jit(solution)/shard_map/all_to_all | solution.py:29
  119.6 4.9 %all-to-all-start.3 = ((bf16[32,24,768]{2,1,0:T(8,128)(2,1)}), bf16[32,24,768]{2,1,0:T(8,128)(2,1)}, u32[]{:S(2)}, u32[]{:S(2)}) async-start(bf16[32,24,768]{2,1,0:T(8,128)(2,1)} %broadcast_in_dim.31), calls=%async_computation.3 | async-start | bytes 2359296 | tf_op jit(solution)/shard_map/all_to_all | solution.py:29
  124.5 7.2 %shard_map.129 = (bf16[3072,128]{1,0:T(8,128)(2,1)S(1)}, f32[768,128]{1,0:T(8,128)S(1)}) custom-call(s32[5376]{0:T(1024)S(1)} %reshape.461.refs_0_, bf16[768,128]{1,0:T(8,128)(2,1)S(1)} %bitcast.140, bf16[768,128]{1,0:T(8,128)(2,1)S(1)} %bitcast.139, bf16[7,768,128]{2,1,0:T(8,128)(2,1)S(1)} %get-tuple-element.27.refs_3_), custom_call_target="tpu_custom_call" | custom-call | tf_op jit(solution)/shard_map/pallas_call | solution.py:199
  131.8 3.0 %collective-permute-start.9 = (bf16[2,768,128]{2,1,0:T(8,128)(2,1)S(1)}, bf16[2,768,128]{2,1,0:T(8,128)(2,1)S(1)}, u32[]{:S(2)}, u32[]{:S(2)}) collective-permute-start(bf16[2,768,128]{2,1,0:T(8,128)(2,1)S(1)} %pad_maximum_fusion.4), channel_id=1, source_target_pairs={{0,32},{32,0},{1,33},{33,1},{2,34},{34,2},{3,35},{35,3},{4,36},{36... | collective-permute-start | bytes 1179656 | tf_op jit(solution)/shard_map/ppermute | solution.py:21
  136.9 3.0 %all-to-all-done.3 = bf16[32,24,768]{2,1,0:T(8,128)(2,1)} async-done(((bf16[32,24,768]{2,1,0:T(8,128)(2,1)}), bf16[32,24,768]{2,1,0:T(8,128)(2,1)}, u32[]{:S(2)}, u32[]{:S(2)}) %all-to-all-start.3) | async-done | bytes 1179680 | tf_op jit(solution)/shard_map/all_to_all | solution.py:29
  139.9 1.8 convolution_bitcast_fusion
  141.7 1.7 fusion
  145.3 9.2 %all-to-all-start.5 = ((bf16[32,2,24,128]{3,2,1,0:T(8,128)(2,1)}), bf16[32,2,24,128]{3,2,1,0:T(8,128)(2,1)S(1)}, u32[]{:S(2)}, u32[]{:S(2)}) async-start(bf16[32,2,24,128]{3,2,1,0:T(8,128)(2,1)} %pad_maximum_fusion.5), calls=%async_computation.5 | async-start | bytes 786432 | tf_op jit(solution)/shard_map/all_to_all | solution.py:29
  155.5 9.0 %all-to-all-done.5 = bf16[32,2,24,128]{3,2,1,0:T(8,128)(2,1)S(1)} async-done(((bf16[32,2,24,128]{3,2,1,0:T(8,128)(2,1)}), bf16[32,2,24,128]{3,2,1,0:T(8,128)(2,1)S(1)}, u32[]{:S(2)}, u32[]{:S(2)}) %all-to-all-start.5) | async-done | bytes 393248 | tf_op jit(solution)/shard_map/all_to_all | solution.py:29
  167.9 2.8 %collective-permute-start.11 = (bf16[48,1024]{1,0:T(8,128)(2,1)S(1)}, bf16[48,1024]{1,0:T(8,128)(2,1)S(1)}, u32[]{:S(2)}, u32[]{:S(2)}) collective-permute-start(bf16[48,1024]{1,0:T(8,128)(2,1)S(1)} %get-tuple-element.56), channel_id=1, source_target_pairs={{0,32},{32,0},{1,33},{33,1},{2,34},{34,2},{3,35},{35,3},{4,36},{36... | collective-permute-start | bytes 294920 | tf_op jit(solution)/shard_map/ppermute | solution.py:21
  170.7 1.7 collective-permute-start.13
  173.8 3.9 %all-to-all-start.6 = ((f32[32,3,128]{2,1,0:T(4,128)}), f32[32,3,128]{2,1,0:T(4,128)S(1)}, u32[]{:S(2)}, u32[]{:S(2)}) async-start(f32[32,3,128]{2,1,0:T(4,128)} %maximum_bitcast_fusion), calls=%async_computation.6 | async-start | bytes 131072 | tf_op jit(solution)/shard_map/all_to_all | solution.py:29
  178.4 7.9 %all-to-all-done.6 = f32[32,3,128]{2,1,0:T(4,128)S(1)} async-done(((f32[32,3,128]{2,1,0:T(4,128)}), f32[32,3,128]{2,1,0:T(4,128)S(1)}, u32[]{:S(2)}, u32[]{:S(2)}) %all-to-all-start.6) | async-done | bytes 49184 | tf_op jit(solution)/shard_map/all_to_all | solution.py:29
  188.8 6.1 %fusion.24 = f32[96,4096]{1,0:T(8,128)S(1)} fusion(bf16[1024,4096]{0,1:T(8,128)(2,1)} %bitcast.141, bf16[48,1024]{1,0:T(8,128)(2,1)S(1)} %collective-permute-done.13, bf16[48,1024]{1,0:T(8,128)(2,1)S(1)} %collective-permute-done.12), kind=kOutput, calls=%fused_computation.68 | convolution fusion | flops 805699584 | bytes 10158080 | tf_op jit(solution)/shard_map/dot_general | solution.py:241
  196.6 4.0 %all-to-all-start.7 = ((f32[32,10,128]{2,1,0:T(8,128)}), f32[32,10,128]{2,1,0:T(8,128)S(1)}, u32[]{:S(2)}, u32[]{:S(2)}) async-start(f32[32,10,128]{2,1,0:T(8,128)} %broadcast_in_dim.68), calls=%async_computation.7 | async-start | bytes 524288 | tf_op jit(solution)/shard_map/all_to_all | solution.py:29
  201.4 6.1 %fusion.28 = f32[96,4096]{1,0:T(8,128)S(1)} fusion(bf16[1024,4096]{0,1:T(8,128)(2,1)} %bitcast.142, bf16[48,1024]{1,0:T(8,128)(2,1)S(1)} %collective-permute-done.11, bf16[48,1024]{1,0:T(8,128)(2,1)S(1)} %get-tuple-element.55), kind=kOutput, calls=%fused_computation.72 | convolution fusion | flops 805699584 | bytes 10158080 | tf_op jit(solution)/shard_map/dot_general | solution.py:241
  211.9 6.7 %collective-permute-done.16 = bf16[48,4096]{1,0:T(8,128)(2,1)S(1)} collective-permute-done((bf16[48,4096]{1,0:T(8,128)(2,1)}, bf16[48,4096]{1,0:T(8,128)(2,1)S(1)}, u32[]{:S(2)}, u32[]{:S(2)}) %collective-permute-start.16) | collective-permute-done | bytes 393248 | tf_op jit(solution)/shard_map/ppermute | solution.py:25
  (159 shorter events, 42.1 us)
Async XLA Ops:
  0.6 3.5 %collective-permute-start.1 = (bf16[48,4096]{1,0:T(8,128)(2,1)}, bf16[48,4096]{1,0:T(8,128)(2,1)S(1)}, u32[]{:S(2)}, u32[]{:S(2)}) collective-permute-start(bf16[48,4096]{1,0:T(8,128)(2,1)} %bitcast.183), channel_id=1, source_target_pairs={{0,32},{32,0},{1,33},{33,1},{2,34},{34,2},{3,35},{35,3},{4,36},{36... | collective-permute-start | bytes 1179656 | tf_op jit(solution)/shard_map/ppermute | solution.py:21
  2.1 10.9 %collective-permute-start = (bf16[48,4096]{1,0:T(8,128)(2,1)}, bf16[48,4096]{1,0:T(8,128)(2,1)S(1)}, u32[]{:S(2)}, u32[]{:S(2)}) collective-permute-start(bf16[48,4096]{1,0:T(8,128)(2,1)} %bitcast.184), channel_id=1, source_target_pairs={{0,64},{64,0},{1,65},{65,1},{2,66},{66,2},{3,67},{67,3},{4,68},{68... | collective-permute-start | bytes 1179656 | tf_op jit(solution)/shard_map/ppermute | solution.py:25
  13.0 2.2 %collective-permute-start.2 = (bf16[48,4096]{1,0:T(8,128)(2,1)S(1)}, bf16[48,4096]{1,0:T(8,128)(2,1)S(1)}, u32[]{:S(2)}, u32[]{:S(2)}) collective-permute-start(bf16[48,4096]{1,0:T(8,128)(2,1)S(1)} %collective-permute-done), channel_id=1, source_target_pairs={{0,32},{32,0},{1,33},{33,1},{2,34},{34,2},{3,35},{35,3},{4,36},{36... | collective-permute-start | bytes 1179656 | tf_op jit(solution)/shard_map/ppermute | solution.py:21
  14.1 8.0 %collective-permute-start.5 = (bf16[48,1024]{1,0:T(8,128)(2,1)S(1)}, bf16[48,1024]{1,0:T(8,128)(2,1)S(1)}, u32[]{:S(2)}, u32[]{:S(2)}) collective-permute-start(bf16[48,1024]{1,0:T(8,128)(2,1)S(1)} %slice.119), channel_id=1, source_target_pairs={{0,32},{32,0},{1,33},{33,1},{2,34},{34,2},{3,35},{35,3},{4,36},{36... | collective-permute-start | bytes 294920 | tf_op jit(solution)/shard_map/ppermute | solution.py:21
  20.1 5.2 %collective-permute-start.3 = (bf16[48,1024]{1,0:T(8,128)(2,1)S(1)}, bf16[48,1024]{1,0:T(8,128)(2,1)S(1)}, u32[]{:S(2)}, u32[]{:S(2)}) collective-permute-start(bf16[48,1024]{1,0:T(8,128)(2,1)S(1)} %get-tuple-element.67), channel_id=1, source_target_pairs={{0,96},{32,64},{64,32},{96,0},{1,97},{33,65},{65,33},{97,1},{2,98}... | collective-permute-start | bytes 294920 | tf_op jit(solution)/shard_map/ppermute | solution.py:118
  21.8 5.3 %collective-permute-start.4 = (bf16[48,1024]{1,0:T(8,128)(2,1)S(1)}, bf16[48,1024]{1,0:T(8,128)(2,1)S(1)}, u32[]{:S(2)}, u32[]{:S(2)}) collective-permute-start(bf16[48,1024]{1,0:T(8,128)(2,1)S(1)} %get-tuple-element.68), channel_id=1, source_target_pairs={{0,64},{64,0},{1,65},{65,1},{2,66},{66,2},{3,67},{67,3},{4,68},{68... | collective-permute-start | bytes 294920 | tf_op jit(solution)/shard_map/ppermute | solution.py:25
  30.4 21.4 %all-to-all-start = ((bf16[32,56,128]{2,1,0:T(8,128)(2,1)}), bf16[32,56,128]{2,1,0:T(8,128)(2,1)S(1)}, u32[]{:S(2)}, u32[]{:S(2)}) async-start(bf16[32,56,128]{2,1,0:T(8,128)(2,1)} %pad_maximum_fusion.1), calls=%async_computation | async-start | bytes 917504 | tf_op jit(solution)/shard_map/all_to_all | solution.py:29
  41.0 17.1 %collective-permute-start.19 = (s32[1]{0:T(128)}, s32[1]{0:T(128)}, u32[]{:S(2)}, u32[]{:S(2)}) collective-permute-start(s32[1]{0:T(128)} %param.15), channel_id=1, source_target_pairs={{0,32},{32,0},{1,33},{33,1},{2,34},{34,2},{3,35},{35,3},{4,36},{36... | collective-permute-start | bytes 20 | tf_op jit(solution)/shard_map/ppermute | solution.py:21
  51.8 11.8 %copy-start.14 = (bf16[32,56,128]{2,1,0:T(8,128)(2,1)}, bf16[32,56,128]{2,1,0:T(8,128)(2,1)S(1)}, u32[]{:S(2)}) copy-start(bf16[32,56,128]{2,1,0:T(8,128)(2,1)S(1)} %all-to-all-done) | copy-start | bytes 1376260
  51.8 25.9 %copy-start.12 = (bf16[32,24,128]{2,1,0:T(8,128)(2,1)}, bf16[32,24,128]{2,1,0:T(8,128)(2,1)S(1)}, u32[]{:S(2)}) copy-start(bf16[32,24,128]{2,1,0:T(8,128)(2,1)S(1)} %get-tuple-element.53) | copy-start | bytes 589828
  53.4 30.7 %all-to-all-start.1 = ((f16[32,24,768]{2,1,0:T(8,128)(2,1)}), f16[32,24,768]{2,1,0:T(8,128)(2,1)}, u32[]{:S(2)}, u32[]{:S(2)}) async-start(f16[32,24,768]{2,1,0:T(8,128)(2,1)} %bitcast.15), calls=%async_computation.1 | async-start | bytes 2359296 | tf_op jit(solution)/shard_map/all_to_all | solution.py:29
  58.8 118.8 %collective-permute-start.20 = (s32[2]{0:T(128)S(1)}, s32[2]{0:T(128)S(1)}, u32[]{:S(2)}, u32[]{:S(2)}) collective-permute-start(s32[2]{0:T(128)S(1)} %pad_add_fusion), channel_id=1, source_target_pairs={{0,64},{64,0},{1,65},{65,1},{2,66},{66,2},{3,67},{67,3},{4,68},{68... | collective-permute-start | bytes 32 | tf_op jit(solution)/shard_map/ppermute | solution.py:25
  59.3 14.3 %collective-permute-start.7 = (bf16[768,128]{1,0:T(8,128)(2,1)S(1)}, bf16[768,128]{1,0:T(8,128)(2,1)S(1)}, u32[]{:S(2)}, u32[]{:S(2)}) collective-permute-start(bf16[768,128]{1,0:T(8,128)(2,1)S(1)} %bitcast.166), channel_id=1, source_target_pairs={{0,64},{64,0},{1,65},{65,1},{2,66},{66,2},{3,67},{67,3},{4,68},{68... | collective-permute-start | bytes 589832 | tf_op jit(solution)/shard_map/ppermute | solution.py:25
  60.5 16.5 %collective-permute-start.6 = (bf16[768,128]{1,0:T(8,128)(2,1)S(1)}, bf16[768,128]{1,0:T(8,128)(2,1)S(1)}, u32[]{:S(2)}, u32[]{:S(2)}) collective-permute-start(bf16[768,128]{1,0:T(8,128)(2,1)S(1)} %bitcast.167), channel_id=1, source_target_pairs={{0,32},{32,0},{1,33},{33,1},{2,34},{34,2},{3,35},{35,3},{4,36},{36... | collective-permute-start | bytes 589832 | tf_op jit(solution)/shard_map/ppermute | solution.py:21
  73.7 4.1 %collective-permute-start.8 = (bf16[768,128]{1,0:T(8,128)(2,1)S(1)}, bf16[768,128]{1,0:T(8,128)(2,1)S(1)}, u32[]{:S(2)}, u32[]{:S(2)}) collective-permute-start(bf16[768,128]{1,0:T(8,128)(2,1)S(1)} %collective-permute-done.7), channel_id=1, source_target_pairs={{0,32},{32,0},{1,33},{33,1},{2,34},{34,2},{3,35},{35,3},{4,36},{36... | collective-permute-start | bytes 589832 | tf_op jit(solution)/shard_map/ppermute | solution.py:21
  84.8 19.2 %all-to-all-start.2 = ((f16[32,24,128]{2,1,0:T(8,128)(2,1)}), f16[32,24,128]{2,1,0:T(8,128)(2,1)S(1)}, u32[]{:S(2)}, u32[]{:S(2)}) async-start(f16[32,24,128]{2,1,0:T(8,128)(2,1)} %bitcast.16), calls=%async_computation.2 | async-start | bytes 393216 | tf_op jit(solution)/shard_map/all_to_all | solution.py:29
  105.4 13.0 %all-to-all-start.4 = ((bf16[32,24,128]{2,1,0:T(8,128)(2,1)}), bf16[32,24,128]{2,1,0:T(8,128)(2,1)S(1)}, u32[]{:S(2)}, u32[]{:S(2)}) async-start(bf16[32,24,128]{2,1,0:T(8,128)(2,1)} %broadcast_in_dim.32), calls=%async_computation.4 | async-start | bytes 393216 | tf_op jit(solution)/shard_map/all_to_all | solution.py:29
  119.6 20.3 %all-to-all-start.3 = ((bf16[32,24,768]{2,1,0:T(8,128)(2,1)}), bf16[32,24,768]{2,1,0:T(8,128)(2,1)}, u32[]{:S(2)}, u32[]{:S(2)}) async-start(bf16[32,24,768]{2,1,0:T(8,128)(2,1)} %broadcast_in_dim.31), calls=%async_computation.3 | async-start | bytes 2359296 | tf_op jit(solution)/shard_map/all_to_all | solution.py:29
  124.4 10.3 %copy-start.2 = (bf16[48,1024]{1,0:T(8,128)(2,1)S(1)}, bf16[48,1024]{1,0:T(8,128)(2,1)}, u32[]{:S(2)}) copy-start(bf16[48,1024]{1,0:T(8,128)(2,1)} %copy-done.1) | copy-start | bytes 294916
  131.8 4.4 %collective-permute-start.9 = (bf16[2,768,128]{2,1,0:T(8,128)(2,1)S(1)}, bf16[2,768,128]{2,1,0:T(8,128)(2,1)S(1)}, u32[]{:S(2)}, u32[]{:S(2)}) collective-permute-start(bf16[2,768,128]{2,1,0:T(8,128)(2,1)S(1)} %pad_maximum_fusion.4), channel_id=1, source_target_pairs={{0,32},{32,0},{1,33},{33,1},{2,34},{34,2},{3,35},{35,3},{4,36},{36... | collective-permute-start | bytes 1179656 | tf_op jit(solution)/shard_map/ppermute | solution.py:21
  136.9 6.6 %collective-permute-start.10 = (bf16[768,128]{1,0:T(8,128)(2,1)}, bf16[768,128]{1,0:T(8,128)(2,1)}, u32[]{:S(2)}, u32[]{:S(2)}) collective-permute-start(bf16[768,128]{1,0:T(8,128)(2,1)} %fusion.18), channel_id=1, source_target_pairs={{0,64},{64,0},{1,65},{65,1},{2,66},{66,2},{3,67},{67,3},{4,68},{68... | collective-permute-start | bytes 589832 | tf_op jit(solution)/shard_map/ppermute | solution.py:25
  145.3 19.2 %all-to-all-start.5 = ((bf16[32,2,24,128]{3,2,1,0:T(8,128)(2,1)}), bf16[32,2,24,128]{3,2,1,0:T(8,128)(2,1)S(1)}, u32[]{:S(2)}, u32[]{:S(2)}) async-start(bf16[32,2,24,128]{3,2,1,0:T(8,128)(2,1)} %pad_maximum_fusion.5), calls=%async_computation.5 | async-start | bytes 786432 | tf_op jit(solution)/shard_map/all_to_all | solution.py:29
  167.9 5.2 %collective-permute-start.11 = (bf16[48,1024]{1,0:T(8,128)(2,1)S(1)}, bf16[48,1024]{1,0:T(8,128)(2,1)S(1)}, u32[]{:S(2)}, u32[]{:S(2)}) collective-permute-start(bf16[48,1024]{1,0:T(8,128)(2,1)S(1)} %get-tuple-element.56), channel_id=1, source_target_pairs={{0,32},{32,0},{1,33},{33,1},{2,34},{34,2},{3,35},{35,3},{4,36},{36... | collective-permute-start | bytes 294920 | tf_op jit(solution)/shard_map/ppermute | solution.py:21
  170.7 7.7 %collective-permute-start.12 = (bf16[48,1024]{1,0:T(8,128)(2,1)S(1)}, bf16[48,1024]{1,0:T(8,128)(2,1)S(1)}, u32[]{:S(2)}, u32[]{:S(2)}) collective-permute-start(bf16[48,1024]{1,0:T(8,128)(2,1)S(1)} %get-tuple-element.57), channel_id=1, source_target_pairs={{0,64},{64,0},{1,65},{65,1},{2,66},{66,2},{3,67},{67,3},{4,68},{68... | collective-permute-start | bytes 294920 | tf_op jit(solution)/shard_map/ppermute | solution.py:25
  170.7 7.7 %collective-permute-start.13 = (bf16[48,1024]{1,0:T(8,128)(2,1)S(1)}, bf16[48,1024]{1,0:T(8,128)(2,1)S(1)}, u32[]{:S(2)}, u32[]{:S(2)}) collective-permute-start(bf16[48,1024]{1,0:T(8,128)(2,1)S(1)} %get-tuple-element.58), channel_id=1, source_target_pairs={{0,96},{32,64},{64,32},{96,0},{1,97},{33,65},{65,33},{97,1},{2,98}... | collective-permute-start | bytes 294920 | tf_op jit(solution)/shard_map/ppermute | solution.py:234
  173.8 12.6 %all-to-all-start.6 = ((f32[32,3,128]{2,1,0:T(4,128)}), f32[32,3,128]{2,1,0:T(4,128)S(1)}, u32[]{:S(2)}, u32[]{:S(2)}) async-start(f32[32,3,128]{2,1,0:T(4,128)} %maximum_bitcast_fusion), calls=%async_computation.6 | async-start | bytes 131072 | tf_op jit(solution)/shard_map/all_to_all | solution.py:29
  186.4 2.4 %collective-permute-start.17 = (f32[3,128]{1,0:T(4,128)S(1)}, f32[3,128]{1,0:T(4,128)S(1)}, u32[]{:S(2)}, u32[]{:S(2)}) collective-permute-start(f32[3,128]{1,0:T(4,128)S(1)} %reduce_sum.167), channel_id=1, source_target_pairs={{0,32},{32,0},{1,33},{33,1},{2,34},{34,2},{3,35},{35,3},{4,36},{36... | collective-permute-start | bytes 4616 | tf_op jit(solution)/shard_map/ppermute | solution.py:21
  188.8 7.0 %collective-permute-start.18 = (f32[2,3,128]{2,1,0:T(4,128)S(1)}, f32[2,3,128]{2,1,0:T(4,128)S(1)}, u32[]{:S(2)}, u32[]{:S(2)}) collective-permute-start(f32[2,3,128]{2,1,0:T(4,128)S(1)} %pad_maximum_fusion.8), channel_id=1, source_target_pairs={{0,64},{64,0},{1,65},{65,1},{2,66},{66,2},{3,67},{67,3},{4,68},{68... | collective-permute-start | bytes 9224 | tf_op jit(solution)/shard_map/ppermute | solution.py:25
  194.9 5.7 %collective-permute-start.14 = (bf16[48,4096]{1,0:T(8,128)(2,1)S(1)}, bf16[48,4096]{1,0:T(8,128)(2,1)S(1)}, u32[]{:S(2)}, u32[]{:S(2)}) collective-permute-start(bf16[48,4096]{1,0:T(8,128)(2,1)S(1)} %slice.300), channel_id=1, source_target_pairs={{0,32},{32,0},{1,33},{33,1},{2,34},{34,2},{3,35},{35,3},{4,36},{36... | collective-permute-start | bytes 1179656 | tf_op jit(solution)/shard_map/ppermute | solution.py:21
  196.6 14.0 %all-to-all-start.7 = ((f32[32,10,128]{2,1,0:T(8,128)}), f32[32,10,128]{2,1,0:T(8,128)S(1)}, u32[]{:S(2)}, u32[]{:S(2)}) async-start(f32[32,10,128]{2,1,0:T(8,128)} %broadcast_in_dim.68), calls=%async_computation.7 | async-start | bytes 524288 | tf_op jit(solution)/shard_map/all_to_all | solution.py:29
  207.5 4.4 %collective-permute-start.15 = (bf16[48,4096]{1,0:T(8,128)(2,1)S(1)}, bf16[48,4096]{1,0:T(8,128)(2,1)S(1)}, u32[]{:S(2)}, u32[]{:S(2)}) collective-permute-start(bf16[48,4096]{1,0:T(8,128)(2,1)S(1)} %slice.299), channel_id=1, source_target_pairs={{0,32},{32,0},{1,33},{33,1},{2,34},{34,2},{3,35},{35,3},{4,36},{36... | collective-permute-start | bytes 1179656 | tf_op jit(solution)/shard_map/ppermute | solution.py:21
  207.9 10.7 %collective-permute-start.16 = (bf16[48,4096]{1,0:T(8,128)(2,1)}, bf16[48,4096]{1,0:T(8,128)(2,1)S(1)}, u32[]{:S(2)}, u32[]{:S(2)}) collective-permute-start(bf16[48,4096]{1,0:T(8,128)(2,1)} %fusion.10), channel_id=1, source_target_pairs={{0,64},{64,0},{1,65},{65,1},{2,66},{66,2},{3,67},{67,3},{4,68},{68... | collective-permute-start | bytes 1179656 | tf_op jit(solution)/shard_map/ppermute | solution.py:25
  (18 other events, 121.8 us)

commit v3 on v2

--- a/solution.py
+++ b/solution.py
@@ -25,6 +25,24 @@
     return lax.ppermute(values, "xl", SWAP)
 
 
+def from_ahead(values, axis, step):
+    size = lax.axis_size(axis)
+    return lax.ppermute(values, axis, [((i + step) % size, i) for i in range(size)])
+
+
+def sum_over(values, axis):
+    if lax.axis_size(axis) == 2:
+        return values + from_ahead(values, axis, 1)
+    one, two, three = [from_ahead(values, axis, step) for step in (1, 2, 3)]
+    return (values + two) + (one + three)
+
+
+def gather_ahead(values, axis):
+    return jnp.stack(
+        [values] + [from_ahead(values, axis, step) for step in range(1, lax.axis_size(axis))]
+    )
+
+
 def exchange(values, axes):
     return lax.all_to_all(values, axes, split_axis=0, concat_axis=0, tiled=True)
 
@@ -57,16 +75,26 @@
     hard_ref[...] = hard
 
 
-def scatter_kernel(hard_count, tok_rows, ids, w_ref, q_ref, neg_ref, add_ref, sum_ref, slot, *parts):
+def scatter_kernel(hard_count, tok_rows, ids, place_ref, w_ref, q_ref, neg_ref, add_ref, sum_ref, slot, negf, *parts):
     rows = q_ref.shape[0]
+    for k in range(hard_count):
+        negf[k] = neg_ref[k].astype(F32)
+    for part in parts:
+        part[...] = jnp.zeros_like(part)
     q = q_ref[...].astype(F32)
-    total = jnp.zeros((rows, LANES), F32)
-    for k in range(hard_count):
-        weight = w_ref[:, k : k + 1].astype(F32)
-        slot[k] = weight * q
-        total = total + weight * neg_ref[k].astype(F32)
-        parts[k][...] = jnp.zeros_like(parts[k])
-    sum_ref[...] = total
+    for block in range(rows // tok_rows):
+        ahead_z = lax.rem(block % 4 + 4 - place_ref[2], 4)
+        ahead_y = lax.rem(block // 4 % 4 + 4 - place_ref[1], 4)
+        ahead_x = lax.rem(block // 16 + 2 - place_ref[0], 2)
+        source = pl.multiple_of((ahead_z * 8 + ahead_y * 2 + ahead_x) * tok_rows, 8)
+        weight = w_ref[pl.ds(source, tok_rows), :]
+        here = slice(block * tok_rows, (block + 1) * tok_rows)
+        total = jnp.zeros((tok_rows, LANES), F32)
+        for k in range(hard_count):
+            one = weight[:, k : k + 1]
+            slot[k, here, :] = one * q[here]
+            total = total + one * negf[k, here, :]
+        sum_ref[here, :] = total
 
     def place(block, carry):
         for i in range(tok_rows):
@@ -94,7 +122,7 @@
     chip = lax.axis_index("xl")
     vmem = pl.BlockSpec(memory_space=pltpu.VMEM)
     smem = pl.BlockSpec(memory_space=pltpu.SMEM)
-    params = pltpu.CompilerParams(vmem_limit_bytes=40 * 1024 * 1024)
+    params = pltpu.CompilerParams(vmem_limit_bytes=24 * 1024 * 1024)
 
     attn_rows = attn.reshape(row_count, width)
     far_rows = swap_chip(attn_rows)
@@ -111,6 +139,7 @@
     chip_columns = project(jnp.concatenate([attn_rows, near_rows]))
     far_rows, chip_columns = lax.optimization_barrier((far_rows, chip_columns))
     far_columns = project(jnp.concatenate([far_rows, swap_core(far_rows)]))
+    tasks, far_columns = lax.optimization_barrier((tasks, far_columns))
     parts = [
         chip_columns[:row_count],
         swap_core(chip_columns[row_count:]),
@@ -172,11 +201,11 @@
         ],
         compiler_params=params,
     )(ids, q_all, p_all)
-    score_part = exchange(score_part.astype(SEND).reshape(blocks, tok_rows, pairs), BLK)
-    score_part, hard_part = lax.optimization_barrier((score_part, hard_part))
-    hard_part = exchange(hard_part.astype(SEND).reshape(blocks, tok_rows, LANES), BLK)
-    scores = jnp.sum(score_part.astype(F32), axis=0) / TAU
-    hard = jnp.sum(hard_part.astype(F32), axis=0) / TAU
+    part = jnp.concatenate([score_part, hard_part], axis=1).astype(SEND)
+    part = exchange(part.reshape(blocks, tok_rows, pairs + LANES), BLK)
+    part = jnp.sum(part.astype(F32), axis=0) / TAU
+    scores = part[:, :pairs]
+    hard = part[:, pairs:]
 
     column = lax.broadcasted_iota(jnp.int32, scores.shape, 1)
     row = lax.broadcasted_iota(jnp.int32, scores.shape, 0)
@@ -193,8 +222,13 @@
         values = exchange(jnp.broadcast_to(values[None], (blocks,) + values.shape), BLK)
         return values.reshape((pairs,) + values.shape[2:])
 
-    group_probs = spread_rows(weights / totals)
-    hard_probs = spread_rows(hard_weights / totals)
+    hard_probs = (hard_weights / totals).astype(BF16)
+    for axis in BLK:
+        hard_probs = gather_ahead(hard_probs, axis)
+    hard_probs = hard_probs.astype(F32).reshape(pairs, LANES)
+    hard_probs, probs = lax.optimization_barrier((hard_probs, weights / totals))
+    group_probs = spread_rows(probs)
+    place = jnp.stack([lax.axis_index(axis) for axis in BLK]).astype(jnp.int32)
 
     hard_add, hard_sum = pl.pallas_call(
         lambda *refs: scatter_kernel(hard_count, tok_rows, *refs),
@@ -202,12 +236,12 @@
             jax.ShapeDtypeStruct((4 * pairs, LANES), BF16),
             jax.ShapeDtypeStruct((pairs, LANES), F32),
         ),
-        in_specs=[smem, vmem, vmem, vmem],
+        in_specs=[smem, smem, vmem, vmem, vmem],
         out_specs=(vmem, vmem),
-        scratch_shapes=[pltpu.VMEM((hard_count, pairs, LANES), F32)]
+        scratch_shapes=[pltpu.VMEM((hard_count, pairs, LANES), F32)] * 2
         + [pltpu.VMEM((4 * pairs, LANES), F32)] * hard_count,
         compiler_params=params,
-    )(ids, hard_probs, q_all, negatives)
+    )(ids, place, hard_probs, q_all, negatives)
     hard_add = hard_add.reshape(4, pairs, LANES)
     crossed = swap_core(jnp.stack([hard_add[1], hard_add[3]])).astype(F32)
     over_chip = swap_chip((hard_add[2].astype(F32) + crossed[1]).astype(BF16)).astype(F32)
@@ -229,47 +263,49 @@
 
 
     cols = [scaled[:, i * (width // 4) : (i + 1) * (width // 4)] for i in range(4)]
+    lines = width // LANES
+    vectors = jnp.concatenate([d_gain, d_out_bias, d_bias]).reshape(3 * lines, LANES)
     cols = by_group(cols)
     far_cols = swap_chip(cols[2])
     diag_cols = lax.ppermute(cols[3], GRP, [(0, 3), (1, 2), (2, 1), (3, 0)])
     near_cols = swap_core(cols[1])
-    d_gain, d_out_bias, d_bias, near_cols = lax.optimization_barrier(
-        (d_gain, d_out_bias, d_bias, near_cols)
-    )
 
     def back(rows):
         return lax.dot_general(
             rows, out_proj_t, (((1,), (0,)), ((), ())), preferred_element_type=F32
         )
 
-    vectors = jnp.stack([d_gain, d_out_bias, d_bias]).reshape(3, blocks, LANES).transpose(1, 0, 2)
-    vectors, far_cols, diag_cols = lax.optimization_barrier(
-        (exchange(vectors, BLK), far_cols, diag_cols)
-    )
-    vectors = jnp.sum(vectors, axis=0)
+    vectors, near_cols = lax.optimization_barrier((vectors, near_cols))
+    vectors = sum_over(sum_over(vectors, "z"), "y")
+    near_part = back(jnp.concatenate([cols[0], near_cols]))
+    far_cols, diag_cols, near_part, vectors = lax.optimization_barrier(
+        (far_cols, diag_cols, near_part, vectors)
+    )
     far_part = back(jnp.concatenate([far_cols, diag_cols]))
+    vectors = sum_over(vectors, "xh")
+    far_part, vectors = lax.optimization_barrier((far_part, vectors))
     far_sum = far_part[:row_count] + swap_core(far_part[row_count:].astype(BF16)).astype(F32)
-    far_sum, near_cols = lax.optimization_barrier((far_sum.astype(BF16), near_cols))
+    near = swap_core(vectors)
+    far_sum, near = lax.optimization_barrier((far_sum.astype(BF16), near))
     far_sum = swap_chip(far_sum).astype(F32)
-    near_part = back(jnp.concatenate([cols[0], near_cols]))
     near_sum = near_part[:row_count] + swap_core(near_part[row_count:].astype(BF16)).astype(F32)
     grad_attn = near_sum + far_sum
 
-    pair = jnp.stack([vectors, swap_core(vectors)])
-    four = jnp.concatenate([pair, swap_chip(pair)])
+    vectors = jnp.concatenate(
+        [vectors[: 2 * lines] + near[: 2 * lines], vectors[2 * lines :], near[2 * lines :]]
+    )
+    far = swap_chip(vectors)
+    both = (vectors + far)[: 2 * lines].reshape(2, width)
+    task_rows = jnp.concatenate([vectors[2 * lines :], far[2 * lines :]]).reshape(4, 1, width)
     onehot = (tasks[:, None] == jnp.arange(task_bias.shape[0])[None, :]).astype(F32)
-    placed = jnp.concatenate(
-        [four[:, :2], onehot[:, :, None] * four[:, 2:3]], axis=1
-    )
+    placed = onehot[:, :, None] * task_rows
     placed = (placed[0] + placed[1]) + (placed[2] + placed[3])
-    whole = exchange(jnp.broadcast_to(placed[None], (blocks,) + placed.shape), BLK)
-    whole = whole.transpose(1, 0, 2).reshape(placed.shape[0], width)
     return (
         losses,
         grad_attn.reshape(2, tok_rows, width),
-        whole[0],
-        whole[2:],
-        whole[1],
+        both[0],
+        placed,
+        both[1],
     )
 
 

time: 221 us -> 211 us (0.955)
  matrix products: 27 us -> 22.8 us
  waiting for transfers between devices: 76.2 us -> 73.7 us
  local copies, waits for them, and re-layouts: 6.33 us -> 3.85 us
    all_to_all x8 -> x4, starting transfers between devices: 51 us -> 29.6 us  [exchange(): return lax.all_to_all(values, axes, split_axis=0, concat_axis=0, tiled=True)]
    ppermute x0 -> x14, starting transfers between devices: none -> 13.1 us  [from_ahead(): lax.ppermute(values, axis, [((i + step) % size, i) for i in range(size)])]
    ppermute x0 -> x14, waiting for transfers between devices: none -> 11.1 us  [from_ahead(): lax.ppermute(values, axis, [((i + step) % size, i) for i in range(size)])]
    all_to_all x8 -> x4, waiting for transfers between devices: 47.8 us -> 40.1 us  [exchange(): return lax.all_to_all(values, axes, split_axis=0, concat_axis=0, tiled=True)]
    ppermute x11, starting transfers between devices: 18.3 us -> 25.4 us  [swap_core(): return lax.ppermute(values, 'co', SWAP)]
    ppermute x8, waiting for transfers between devices: 22.4 us -> 16.7 us  [swap_chip(): return lax.ppermute(values, 'xl', SWAP)]
    dot_general x2, matrix products: 12.1 us -> 8.88 us  [back(): lax.dot_general(rows, out_proj_t, (((1,), (0,)), ((), ())), preferred_ele...]
  transfers between devices with their start and end apart: 29 -> 39, of which waited for: 16 -> 22; matrix products, arithmetic and copies ran while one was open for 21% -> 14% of each run, Pallas kernels for 6% -> 4%
where the time goes in v3:
time: 211 us; the launch traced here: 210 us
  starting transfers between devices  77.3 us (37%)
  waiting for transfers between devices  73.7 us (35%)
  matrix products  22.8 us (11%)
  other arithmetic  16.4 us (8%)
  Pallas kernels  13.9 us (7%)
  local copies, waits for them, and re-layouts  3.85 us (2%)
    all_to_all x4, waiting for transfers between devices, exchange(): return lax.all_to_all(values, axes, split_axis=0, concat_axis=0, tiled=True)  40.1 us
    all_to_all x4, starting transfers between devices, exchange(): return lax.all_to_all(values, axes, split_axis=0, concat_axis=0, tiled=True)  29.6 us
    ppermute x11, starting transfers between devices, swap_core(): return lax.ppermute(values, 'co', SWAP)  25.4 us
    ppermute x8, waiting for transfers between devices, swap_chip(): return lax.ppermute(values, 'xl', SWAP)  16.7 us
    ppermute x14, starting transfers between devices, from_ahead(): lax.ppermute(values, axis, [((i + step) % size, i) for i in range(size)])  13.1 us
    ppermute x14, waiting for transfers between devices, from_ahead(): lax.ppermute(values, axis, [((i + step) % size, i) for i in range(size)])  11.1 us
    dot_general x2, matrix products, project(): return jnp.dot(rows, out_proj, preferred_element_type=F32).astype(BF16)  9.84 us
    dot_general x2, matrix products, back(): lax.dot_general(rows, out_proj_t, (((1,), (0,)), ((), ())), preferred_ele...  8.88 us
  transfers between devices with their start and end apart: 39, of which 22 were waited for; matrix products, arithmetic and copies ran while one was open for 14% of the time, Pallas kernels for 4%

profile of v3, /device:TPU:1, one launch (start us, length us, event | category | flops | bytes accessed | tf_op | source)
XLA Modules:
  0.0 209.9 jit_solution(1376509976755980178)
XLA Ops:
  0.6 1.5 collective-permute-start.3
  5.2 5.0 %convolution_convert_fusion.2 = bf16[96,1024]{1,0:T(8,128)(2,1)S(1)} fusion(bf16[4096,1024]{1,0:T(8,128)(2,1)} %param.11, bf16[48,4096]{1,0:T(8,128)(2,1)S(1)} %collective-permute-done.3, bf16[48,4096]{1,0:T(8,128)(2,1)} %bitcast.192), kind=kOutput, calls=%fused_computation.12 | convolution fusion | flops 806977536 | bytes 9371648 | tf_op jit(solution)/shard_map/dot_general | solution.py:137
  10.2 2.8 %collective-permute-done.2 = bf16[48,4096]{1,0:T(8,128)(2,1)S(1)} collective-permute-done((bf16[48,4096]{1,0:T(8,128)(2,1)}, bf16[48,4096]{1,0:T(8,128)(2,1)S(1)}, u32[]{:S(2)}, u32[]{:S(2)}) %collective-permute-start.2) | collective-permute-done | bytes 393248 | tf_op jit(solution)/shard_map/ppermute | solution.py:25
  18.9 4.8 %convolution_convert_fusion.1 = bf16[96,1024]{1,0:T(8,128)(2,1)S(1)} fusion(bf16[4096,1024]{1,0:T(8,128)(2,1)} %param.11, bf16[48,4096]{1,0:T(8,128)(2,1)S(1)} %collective-permute-done.4, bf16[48,4096]{1,0:T(8,128)(2,1)S(1)} %collective-permute-done.2), kind=kOutput, calls=%fused_computation.11 | convolution fusion | flops 806977536 | bytes 9371648 | tf_op jit(solution)/shard_map/dot_general | solution.py:137
  25.4 3.6 %collective-permute-done.5 = bf16[48,1024]{1,0:T(8,128)(2,1)S(1)} collective-permute-done((bf16[48,1024]{1,0:T(8,128)(2,1)S(1)}, bf16[48,1024]{1,0:T(8,128)(2,1)S(1)}, u32[]{:S(2)}, u32[]{:S(2)}) %collective-permute-start.5) | collective-permute-done | bytes 98336 | tf_op jit(solution)/shard_map/ppermute | solution.py:147
  31.0 1.5 multiply_convert_fusion.1
  33.3 10.6 %all-to-all-start = ((bf16[32,56,128]{2,1,0:T(8,128)(2,1)}), bf16[32,56,128]{2,1,0:T(8,128)(2,1)S(1)}, u32[]{:S(2)}, u32[]{:S(2)}) async-start(bf16[32,56,128]{2,1,0:T(8,128)(2,1)} %pad_maximum_fusion.2), calls=%async_computation | async-start | bytes 917504 | tf_op jit(solution)/shard_map/all_to_all | solution.py:47
  43.9 10.2 %all-to-all-done = bf16[32,56,128]{2,1,0:T(8,128)(2,1)S(1)} async-done(((bf16[32,56,128]{2,1,0:T(8,128)(2,1)}), bf16[32,56,128]{2,1,0:T(8,128)(2,1)S(1)}, u32[]{:S(2)}, u32[]{:S(2)}) %all-to-all-start) | async-done | bytes 458784 | tf_op jit(solution)/shard_map/all_to_all | solution.py:47
  54.6 3.4 %collective-permute-start.8 = (bf16[768,128]{1,0:T(8,128)(2,1)S(1)}, bf16[768,128]{1,0:T(8,128)(2,1)S(1)}, u32[]{:S(2)}, u32[]{:S(2)}) collective-permute-start(bf16[768,128]{1,0:T(8,128)(2,1)S(1)} %bitcast.174), channel_id=1, source_target_pairs={{0,32},{32,0},{1,33},{33,1},{2,34},{34,2},{3,35},{35,3},{4,36},{36... | collective-permute-start | bytes 589832 | tf_op jit(solution)/shard_map/ppermute | solution.py:21
  58.8 4.3 %collective-permute-start.10 = (bf16[768,128]{1,0:T(8,128)(2,1)S(1)}, bf16[768,128]{1,0:T(8,128)(2,1)S(1)}, u32[]{:S(2)}, u32[]{:S(2)}) collective-permute-start(bf16[768,128]{1,0:T(8,128)(2,1)S(1)} %collective-permute-done.9), channel_id=1, source_target_pairs={{0,32},{32,0},{1,33},{33,1},{2,34},{34,2},{3,35},{35,3},{4,36},{36... | collective-permute-start | bytes 589832 | tf_op jit(solution)/shard_map/ppermute | solution.py:21
  64.2 6.2 %shard_map.128 = (bf16[7,768,128]{2,1,0:T(8,128)(2,1)S(1)}, f32[768,128]{1,0:T(8,128)S(1)}) custom-call(s32[5376]{0:T(1024)S(1)} %reshape.415.refs_0_, bf16[768,128]{1,0:T(8,128)(2,1)S(1)} %bitcast.145, bf16[3072,128]{1,0:T(8,128)(2,1)S(1)} %pad_maximum_fusion.1.refs_2_), custom_call_target="tpu_custom_call" | custom-call | tf_op jit(solution)/shard_map/pallas_call | solution.py:190
  72.0 4.0 %all-to-all-start.1 = ((f16[32,24,896]{2,1,0:T(8,128)(2,1)}), f16[32,24,896]{2,1,0:T(8,128)(2,1)S(1)}, u32[]{:S(2)}, u32[]{:S(2)}) async-start(f16[32,24,896]{2,1,0:T(8,128)(2,1)} %pad_maximum_fusion), calls=%async_computation.1 | async-start | bytes 2752512 | tf_op jit(solution)/shard_map/all_to_all | solution.py:47
  76.0 19.9 %all-to-all-done.1 = f16[32,24,896]{2,1,0:T(8,128)(2,1)S(1)} async-done(((f16[32,24,896]{2,1,0:T(8,128)(2,1)}), f16[32,24,896]{2,1,0:T(8,128)(2,1)S(1)}, u32[]{:S(2)}, u32[]{:S(2)}) %all-to-all-start.1) | async-done | bytes 1376288 | tf_op jit(solution)/shard_map/all_to_all | solution.py:47
  97.0 1.9 collective-permute-start.11
  99.0 2.1 collective-permute-done.11
  101.1 2.4 %collective-permute-start.12 = (bf16[2,24,128]{2,1,0:T(8,128)(2,1)S(1)}, bf16[2,24,128]{2,1,0:T(8,128)(2,1)S(1)}, u32[]{:S(2)}, u32[]{:S(2)}) collective-permute-start(bf16[2,24,128]{2,1,0:T(8,128)(2,1)S(1)} %get-tuple-element.80), channel_id=1, source_target_pairs={{4,0},{8,4},{12,8},{0,12},{5,1},{9,5},{13,9},{1,13},{6,2},{10,6},{... | collective-permute-start | bytes 36872 | tf_op jit(solution)/shard_map/ppermute | solution.py:30
  104.3 3.2 %collective-permute-done.13 = bf16[2,24,128]{2,1,0:T(8,128)(2,1)S(1)} collective-permute-done((bf16[2,24,128]{2,1,0:T(8,128)(2,1)S(1)}, bf16[2,24,128]{2,1,0:T(8,128)(2,1)S(1)}, u32[]{:S(2)}, u32[]{:S(2)}) %collective-permute-start.13) | collective-permute-done | bytes 12320 | tf_op jit(solution)/shard_map/ppermute | solution.py:30
  110.9 1.7 collective-permute-done.16
  114.4 5.6 %all-to-all-start.2 = ((bf16[32,24,768]{2,1,0:T(8,128)(2,1)}), bf16[32,24,768]{2,1,0:T(8,128)(2,1)}, u32[]{:S(2)}, u32[]{:S(2)}) async-start(bf16[32,24,768]{2,1,0:T(8,128)(2,1)} %broadcast_in_dim.46), calls=%async_computation.2 | async-start | bytes 2359296 | tf_op jit(solution)/shard_map/all_to_all | solution.py:47
  120.0 7.7 %shard_map.129 = (bf16[3072,128]{1,0:T(8,128)(2,1)S(1)}, f32[768,128]{1,0:T(8,128)S(1)}) custom-call(s32[5376]{0:T(1024)S(1)} %reshape.415.refs_0_, s32[3]{0:T(128)S(1)} %pad_add_fusion.2.refs_1_, f32[768,128]{1,0:T(8,128)S(1)} %bitcast_convert_fusion.refs_2_, bf16[768,128]{1,0:T(8,128)(2,1)S(1)} %bitcast.146, bf16[7,768,128]{2,1,0:T(8,128)(2,1)S(1)} %get-tuple-element.31.refs_4_), custom_call_target="tpu_custom_call" | custom-call | tf_op jit(solution)/shard_map/pallas_call | solution.py:233
  127.8 6.0 %collective-permute-start.18 = (bf16[2,768,128]{2,1,0:T(8,128)(2,1)S(1)}, bf16[2,768,128]{2,1,0:T(8,128)(2,1)S(1)}, u32[]{:S(2)}, u32[]{:S(2)}) collective-permute-start(bf16[2,768,128]{2,1,0:T(8,128)(2,1)S(1)} %pad_maximum_fusion.5), channel_id=1, source_target_pairs={{0,32},{32,0},{1,33},{33,1},{2,34},{34,2},{3,35},{35,3},{4,36},{36... | collective-permute-start | bytes 1179656 | tf_op jit(solution)/shard_map/ppermute | solution.py:21
  136.3 1.8 convolution_bitcast_fusion
  138.1 1.7 fusion
  139.8 2.6 %collective-permute-done.19 = bf16[768,128]{1,0:T(8,128)(2,1)} collective-permute-done((bf16[768,128]{1,0:T(8,128)(2,1)}, bf16[768,128]{1,0:T(8,128)(2,1)}, u32[]{:S(2)}, u32[]{:S(2)}) %collective-permute-start.19) | collective-permute-done | bytes 196640 | tf_op jit(solution)/shard_map/ppermute | solution.py:25
  144.2 9.5 %all-to-all-start.3 = ((bf16[32,2,24,128]{3,2,1,0:T(8,128)(2,1)}), bf16[32,2,24,128]{3,2,1,0:T(8,128)(2,1)S(1)}, u32[]{:S(2)}, u32[]{:S(2)}) async-start(bf16[32,2,24,128]{3,2,1,0:T(8,128)(2,1)} %pad_maximum_fusion.6), calls=%async_computation.3 | async-start | bytes 786432 | tf_op jit(solution)/shard_map/all_to_all | solution.py:47
  153.8 9.9 %all-to-all-done.3 = bf16[32,2,24,128]{3,2,1,0:T(8,128)(2,1)S(1)} async-done(((bf16[32,2,24,128]{3,2,1,0:T(8,128)(2,1)}), bf16[32,2,24,128]{3,2,1,0:T(8,128)(2,1)S(1)}, u32[]{:S(2)}, u32[]{:S(2)}) %all-to-all-start.3) | async-done | bytes 393248 | tf_op jit(solution)/shard_map/all_to_all | solution.py:47
  166.7 2.8 %collective-permute-start.22 = (bf16[48,1024]{1,0:T(8,128)(2,1)S(1)}, bf16[48,1024]{1,0:T(8,128)(2,1)S(1)}, u32[]{:S(2)}, u32[]{:S(2)}) collective-permute-start(bf16[48,1024]{1,0:T(8,128)(2,1)S(1)} %get-tuple-element.64), channel_id=1, source_target_pairs={{0,32},{32,0},{1,33},{33,1},{2,34},{34,2},{3,35},{35,3},{4,36},{36... | collective-permute-start | bytes 294920 | tf_op jit(solution)/shard_map/ppermute | solution.py:21
  173.6 2.5 %collective-permute-start.21 = (bf16[48,1024]{1,0:T(8,128)(2,1)S(1)}, bf16[48,1024]{1,0:T(8,128)(2,1)S(1)}, u32[]{:S(2)}, u32[]{:S(2)}) collective-permute-start(bf16[48,1024]{1,0:T(8,128)(2,1)S(1)} %get-tuple-element.63), channel_id=1, source_target_pairs={{0,96},{32,64},{64,32},{96,0},{1,97},{33,65},{65,33},{97,1},{2,98}... | collective-permute-start | bytes 294920 | tf_op jit(solution)/shard_map/ppermute | solution.py:270
  180.0 6.2 %fusion.22 = f32[96,4096]{1,0:T(8,128)S(1)} fusion(bf16[1024,4096]{0,1:T(8,128)(2,1)} %bitcast.147, bf16[48,1024]{1,0:T(8,128)(2,1)S(1)} %collective-permute-done.22, bf16[48,1024]{1,0:T(8,128)(2,1)S(1)} %get-tuple-element.61), kind=kOutput, calls=%fused_computation.68 | convolution fusion | flops 805699584 | bytes 10158080 | tf_op jit(solution)/shard_map/dot_general | solution.py:274
  187.1 2.7 %fusion.26 = f32[96,4096]{1,0:T(8,128)S(1)} fusion(bf16[1024,4096]{0,1:T(8,128)(2,1)S(1)} %bitcast.150, bf16[48,1024]{1,0:T(8,128)(2,1)S(1)} %collective-permute-done.21, bf16[48,1024]{1,0:T(8,128)(2,1)S(1)} %collective-permute-done.20), kind=kOutput, calls=%fused_computation.72 | convolution fusion | flops 805699584 | bytes 10158080 | tf_op jit(solution)/shard_map/dot_general | solution.py:274
  190.9 4.1 %collective-permute-start.31 = (bf16[48,4096]{1,0:T(8,128)(2,1)S(1)}, bf16[48,4096]{1,0:T(8,128)(2,1)S(1)}, u32[]{:S(2)}, u32[]{:S(2)}) collective-permute-start(bf16[48,4096]{1,0:T(8,128)(2,1)S(1)} %slice.305), channel_id=1, source_target_pairs={{0,32},{32,0},{1,33},{33,1},{2,34},{34,2},{3,35},{35,3},{4,36},{36... | collective-permute-start | bytes 1179656 | tf_op jit(solution)/shard_map/ppermute | solution.py:21
  201.1 7.7 %collective-permute-done.33 = bf16[48,4096]{1,0:T(8,128)(2,1)S(1)} collective-permute-done((bf16[48,4096]{1,0:T(8,128)(2,1)S(1)}, bf16[48,4096]{1,0:T(8,128)(2,1)S(1)}, u32[]{:S(2)}, u32[]{:S(2)}) %collective-permute-start.33) | collective-permute-done | bytes 393248 | tf_op jit(solution)/shard_map/ppermute | solution.py:25
  (179 shorter events, 48.0 us)
Async XLA Ops:
  0.6 4.5 %collective-permute-start.3 = (bf16[48,4096]{1,0:T(8,128)(2,1)}, bf16[48,4096]{1,0:T(8,128)(2,1)S(1)}, u32[]{:S(2)}, u32[]{:S(2)}) collective-permute-start(bf16[48,4096]{1,0:T(8,128)(2,1)} %bitcast.190), channel_id=1, source_target_pairs={{0,32},{32,0},{1,33},{33,1},{2,34},{34,2},{3,35},{35,3},{4,36},{36... | collective-permute-start | bytes 1179656 | tf_op jit(solution)/shard_map/ppermute | solution.py:21
  2.1 10.9 %collective-permute-start.2 = (bf16[48,4096]{1,0:T(8,128)(2,1)}, bf16[48,4096]{1,0:T(8,128)(2,1)S(1)}, u32[]{:S(2)}, u32[]{:S(2)}) collective-permute-start(bf16[48,4096]{1,0:T(8,128)(2,1)} %bitcast.191), channel_id=1, source_target_pairs={{0,64},{64,0},{1,65},{65,1},{2,66},{66,2},{3,67},{67,3},{4,68},{68... | collective-permute-start | bytes 1179656 | tf_op jit(solution)/shard_map/ppermute | solution.py:25
  3.4 10.6 %collective-permute-start = (s32[1]{0:T(128)}, s32[1]{0:T(128)}, u32[]{:S(2)}, u32[]{:S(2)}) collective-permute-start(s32[1]{0:T(128)} %param.15), channel_id=1, source_target_pairs={{0,32},{32,0},{1,33},{33,1},{2,34},{34,2},{3,35},{35,3},{4,36},{36... | collective-permute-start | bytes 20 | tf_op jit(solution)/shard_map/ppermute | solution.py:21
  13.0 5.9 %collective-permute-start.4 = (bf16[48,4096]{1,0:T(8,128)(2,1)S(1)}, bf16[48,4096]{1,0:T(8,128)(2,1)S(1)}, u32[]{:S(2)}, u32[]{:S(2)}) collective-permute-start(bf16[48,4096]{1,0:T(8,128)(2,1)S(1)} %collective-permute-done.2), channel_id=1, source_target_pairs={{0,32},{32,0},{1,33},{33,1},{2,34},{34,2},{3,35},{35,3},{4,36},{36... | collective-permute-start | bytes 1179656 | tf_op jit(solution)/shard_map/ppermute | solution.py:21
  17.7 7.7 %collective-permute-start.7 = (bf16[48,1024]{1,0:T(8,128)(2,1)S(1)}, bf16[48,1024]{1,0:T(8,128)(2,1)S(1)}, u32[]{:S(2)}, u32[]{:S(2)}) collective-permute-start(bf16[48,1024]{1,0:T(8,128)(2,1)S(1)} %slice.133), channel_id=1, source_target_pairs={{0,32},{32,0},{1,33},{33,1},{2,34},{34,2},{3,35},{35,3},{4,36},{36... | collective-permute-start | bytes 294920 | tf_op jit(solution)/shard_map/ppermute | solution.py:21
  23.8 5.1 %collective-permute-start.5 = (bf16[48,1024]{1,0:T(8,128)(2,1)S(1)}, bf16[48,1024]{1,0:T(8,128)(2,1)S(1)}, u32[]{:S(2)}, u32[]{:S(2)}) collective-permute-start(bf16[48,1024]{1,0:T(8,128)(2,1)S(1)} %get-tuple-element.71), channel_id=1, source_target_pairs={{0,96},{32,64},{64,32},{96,0},{1,97},{33,65},{65,33},{97,1},{2,98}... | collective-permute-start | bytes 294920 | tf_op jit(solution)/shard_map/ppermute | solution.py:147
  25.1 5.0 %collective-permute-start.6 = (bf16[48,1024]{1,0:T(8,128)(2,1)S(1)}, bf16[48,1024]{1,0:T(8,128)(2,1)S(1)}, u32[]{:S(2)}, u32[]{:S(2)}) collective-permute-start(bf16[48,1024]{1,0:T(8,128)(2,1)S(1)} %get-tuple-element.72), channel_id=1, source_target_pairs={{0,64},{64,0},{1,65},{65,1},{2,66},{66,2},{3,67},{67,3},{4,68},{68... | collective-permute-start | bytes 294920 | tf_op jit(solution)/shard_map/ppermute | solution.py:25
  33.3 20.8 %all-to-all-start = ((bf16[32,56,128]{2,1,0:T(8,128)(2,1)}), bf16[32,56,128]{2,1,0:T(8,128)(2,1)S(1)}, u32[]{:S(2)}, u32[]{:S(2)}) async-start(bf16[32,56,128]{2,1,0:T(8,128)(2,1)} %pad_maximum_fusion.2), calls=%async_computation | async-start | bytes 917504 | tf_op jit(solution)/shard_map/all_to_all | solution.py:47
  54.2 4.6 %collective-permute-start.9 = (bf16[768,128]{1,0:T(8,128)(2,1)S(1)}, bf16[768,128]{1,0:T(8,128)(2,1)S(1)}, u32[]{:S(2)}, u32[]{:S(2)}) collective-permute-start(bf16[768,128]{1,0:T(8,128)(2,1)S(1)} %bitcast.173), channel_id=1, source_target_pairs={{0,64},{64,0},{1,65},{65,1},{2,66},{66,2},{3,67},{67,3},{4,68},{68... | collective-permute-start | bytes 589832 | tf_op jit(solution)/shard_map/ppermute | solution.py:25
  54.6 9.0 %collective-permute-start.8 = (bf16[768,128]{1,0:T(8,128)(2,1)S(1)}, bf16[768,128]{1,0:T(8,128)(2,1)S(1)}, u32[]{:S(2)}, u32[]{:S(2)}) collective-permute-start(bf16[768,128]{1,0:T(8,128)(2,1)S(1)} %bitcast.174), channel_id=1, source_target_pairs={{0,32},{32,0},{1,33},{33,1},{2,34},{34,2},{3,35},{35,3},{4,36},{36... | collective-permute-start | bytes 589832 | tf_op jit(solution)/shard_map/ppermute | solution.py:21
  58.8 5.3 %collective-permute-start.10 = (bf16[768,128]{1,0:T(8,128)(2,1)S(1)}, bf16[768,128]{1,0:T(8,128)(2,1)S(1)}, u32[]{:S(2)}, u32[]{:S(2)}) collective-permute-start(bf16[768,128]{1,0:T(8,128)(2,1)S(1)} %collective-permute-done.9), channel_id=1, source_target_pairs={{0,32},{32,0},{1,33},{33,1},{2,34},{34,2},{3,35},{35,3},{4,36},{36... | collective-permute-start | bytes 589832 | tf_op jit(solution)/shard_map/ppermute | solution.py:21
  72.0 23.9 %all-to-all-start.1 = ((f16[32,24,896]{2,1,0:T(8,128)(2,1)}), f16[32,24,896]{2,1,0:T(8,128)(2,1)S(1)}, u32[]{:S(2)}, u32[]{:S(2)}) async-start(f16[32,24,896]{2,1,0:T(8,128)(2,1)} %pad_maximum_fusion), calls=%async_computation.1 | async-start | bytes 2752512 | tf_op jit(solution)/shard_map/all_to_all | solution.py:47
  97.0 4.0 %collective-permute-start.11 = (bf16[24,128]{1,0:T(8,128)(2,1)S(1)}, bf16[24,128]{1,0:T(8,128)(2,1)S(1)}, u32[]{:S(2)}, u32[]{:S(2)}) collective-permute-start(bf16[24,128]{1,0:T(8,128)(2,1)S(1)} %divide_convert_fusion), channel_id=1, source_target_pairs={{16,0},{0,16},{17,1},{1,17},{18,2},{2,18},{19,3},{3,19},{20,4},{4,... | collective-permute-start | bytes 18440 | tf_op jit(solution)/shard_map/ppermute | solution.py:30
  103.4 4.1 %collective-permute-start.13 = (bf16[2,24,128]{2,1,0:T(8,128)(2,1)S(1)}, bf16[2,24,128]{2,1,0:T(8,128)(2,1)S(1)}, u32[]{:S(2)}, u32[]{:S(2)}) collective-permute-start(bf16[2,24,128]{2,1,0:T(8,128)(2,1)S(1)} %get-tuple-element.80), channel_id=1, source_target_pairs={{8,0},{12,4},{0,8},{4,12},{9,1},{13,5},{1,9},{5,13},{10,2},{14,6},... | collective-permute-start | bytes 36872 | tf_op jit(solution)/shard_map/ppermute | solution.py:30
  108.1 4.4 %collective-permute-start.16 = (bf16[4,2,24,128]{3,2,1,0:T(8,128)(2,1)S(1)}, bf16[4,2,24,128]{3,2,1,0:T(8,128)(2,1)S(1)}, u32[]{:S(2)}, u32[]{:S(2)}) collective-permute-start(bf16[4,2,24,128]{3,2,1,0:T(8,128)(2,1)S(1)} %get-tuple-element.76), channel_id=1, source_target_pairs={{2,0},{3,1},{0,2},{1,3},{6,4},{7,5},{4,6},{5,7},{10,8},{11,9},{8,1... | collective-permute-start | bytes 147464 | tf_op jit(solution)/shard_map/ppermute | solution.py:30
  109.1 4.2 %collective-permute-start.17 = (bf16[4,2,24,128]{3,2,1,0:T(8,128)(2,1)S(1)}, bf16[4,2,24,128]{3,2,1,0:T(8,128)(2,1)S(1)}, u32[]{:S(2)}, u32[]{:S(2)}) collective-permute-start(bf16[4,2,24,128]{3,2,1,0:T(8,128)(2,1)S(1)} %get-tuple-element.76), channel_id=1, source_target_pairs={{3,0},{0,1},{1,2},{2,3},{7,4},{4,5},{5,6},{6,7},{11,8},{8,9},{9,10... | collective-permute-start | bytes 147464 | tf_op jit(solution)/shard_map/ppermute | solution.py:30
  114.4 21.9 %all-to-all-start.2 = ((bf16[32,24,768]{2,1,0:T(8,128)(2,1)}), bf16[32,24,768]{2,1,0:T(8,128)(2,1)}, u32[]{:S(2)}, u32[]{:S(2)}) async-start(bf16[32,24,768]{2,1,0:T(8,128)(2,1)} %broadcast_in_dim.46), calls=%async_computation.2 | async-start | bytes 2359296 | tf_op jit(solution)/shard_map/all_to_all | solution.py:47
  127.8 7.3 %collective-permute-start.18 = (bf16[2,768,128]{2,1,0:T(8,128)(2,1)S(1)}, bf16[2,768,128]{2,1,0:T(8,128)(2,1)S(1)}, u32[]{:S(2)}, u32[]{:S(2)}) collective-permute-start(bf16[2,768,128]{2,1,0:T(8,128)(2,1)S(1)} %pad_maximum_fusion.5), channel_id=1, source_target_pairs={{0,32},{32,0},{1,33},{33,1},{2,34},{34,2},{3,35},{35,3},{4,36},{36... | collective-permute-start | bytes 1179656 | tf_op jit(solution)/shard_map/ppermute | solution.py:21
  135.9 6.4 %collective-permute-start.19 = (bf16[768,128]{1,0:T(8,128)(2,1)}, bf16[768,128]{1,0:T(8,128)(2,1)}, u32[]{:S(2)}, u32[]{:S(2)}) collective-permute-start(bf16[768,128]{1,0:T(8,128)(2,1)} %fusion.16), channel_id=1, source_target_pairs={{0,64},{64,0},{1,65},{65,1},{2,66},{66,2},{3,67},{67,3},{4,68},{68... | collective-permute-start | bytes 589832 | tf_op jit(solution)/shard_map/ppermute | solution.py:25
  144.2 19.5 %all-to-all-start.3 = ((bf16[32,2,24,128]{3,2,1,0:T(8,128)(2,1)}), bf16[32,2,24,128]{3,2,1,0:T(8,128)(2,1)S(1)}, u32[]{:S(2)}, u32[]{:S(2)}) async-start(bf16[32,2,24,128]{3,2,1,0:T(8,128)(2,1)} %pad_maximum_fusion.6), calls=%async_computation.3 | async-start | bytes 786432 | tf_op jit(solution)/shard_map/all_to_all | solution.py:47
  170.5 5.6 %collective-permute-start.23 = (f32[96,128]{1,0:T(8,128)S(1)}, f32[96,128]{1,0:T(8,128)S(1)}, u32[]{:S(2)}, u32[]{:S(2)}) collective-permute-start(f32[96,128]{1,0:T(8,128)S(1)} %pad_maximum_fusion.11), channel_id=1, source_target_pairs={{2,0},{3,1},{0,2},{1,3},{6,4},{7,5},{4,6},{5,7},{10,8},{11,9},{8,1... | collective-permute-start | bytes 147464 | tf_op jit(solution)/shard_map/ppermute | solution.py:30
  171.8 4.3 %collective-permute-start.24 = (f32[96,128]{1,0:T(8,128)S(1)}, f32[96,128]{1,0:T(8,128)S(1)}, u32[]{:S(2)}, u32[]{:S(2)}) collective-permute-start(f32[96,128]{1,0:T(8,128)S(1)} %pad_maximum_fusion.11), channel_id=1, source_target_pairs={{1,0},{2,1},{3,2},{0,3},{5,4},{6,5},{7,6},{4,7},{9,8},{10,9},{11,1... | collective-permute-start | bytes 147464 | tf_op jit(solution)/shard_map/ppermute | solution.py:30
  173.0 4.2 %collective-permute-start.25 = (f32[96,128]{1,0:T(8,128)S(1)}, f32[96,128]{1,0:T(8,128)S(1)}, u32[]{:S(2)}, u32[]{:S(2)}) collective-permute-start(f32[96,128]{1,0:T(8,128)S(1)} %pad_maximum_fusion.11), channel_id=1, source_target_pairs={{3,0},{0,1},{1,2},{2,3},{7,4},{4,5},{5,6},{6,7},{11,8},{8,9},{9,10... | collective-permute-start | bytes 147464 | tf_op jit(solution)/shard_map/ppermute | solution.py:30
  173.3 13.0 %collective-permute-start.20 = (bf16[48,1024]{1,0:T(8,128)(2,1)S(1)}, bf16[48,1024]{1,0:T(8,128)(2,1)S(1)}, u32[]{:S(2)}, u32[]{:S(2)}) collective-permute-start(bf16[48,1024]{1,0:T(8,128)(2,1)S(1)} %get-tuple-element.62), channel_id=1, source_target_pairs={{0,64},{64,0},{1,65},{65,1},{2,66},{66,2},{3,67},{67,3},{4,68},{68... | collective-permute-start | bytes 294920 | tf_op jit(solution)/shard_map/ppermute | solution.py:25
  173.6 12.7 %collective-permute-start.21 = (bf16[48,1024]{1,0:T(8,128)(2,1)S(1)}, bf16[48,1024]{1,0:T(8,128)(2,1)S(1)}, u32[]{:S(2)}, u32[]{:S(2)}) collective-permute-start(bf16[48,1024]{1,0:T(8,128)(2,1)S(1)} %get-tuple-element.63), channel_id=1, source_target_pairs={{0,96},{32,64},{64,32},{96,0},{1,97},{33,65},{65,33},{97,1},{2,98}... | collective-permute-start | bytes 294920 | tf_op jit(solution)/shard_map/ppermute | solution.py:270
  177.2 9.0 %collective-permute-start.26 = (f32[96,128]{1,0:T(8,128)S(1)}, f32[96,128]{1,0:T(8,128)S(1)}, u32[]{:S(2)}, u32[]{:S(2)}) collective-permute-start(f32[96,128]{1,0:T(8,128)S(1)} %add_add_fusion.7), channel_id=1, source_target_pairs={{8,0},{12,4},{0,8},{4,12},{9,1},{13,5},{1,9},{5,13},{10,2},{14,6},... | collective-permute-start | bytes 147464 | tf_op jit(solution)/shard_map/ppermute | solution.py:30
  178.5 7.7 %collective-permute-start.27 = (f32[96,128]{1,0:T(8,128)S(1)}, f32[96,128]{1,0:T(8,128)S(1)}, u32[]{:S(2)}, u32[]{:S(2)}) collective-permute-start(f32[96,128]{1,0:T(8,128)S(1)} %add_add_fusion.7), channel_id=1, source_target_pairs={{4,0},{8,4},{12,8},{0,12},{5,1},{9,5},{13,9},{1,13},{6,2},{10,6},{... | collective-permute-start | bytes 147464 | tf_op jit(solution)/shard_map/ppermute | solution.py:30
  179.7 6.5 %collective-permute-start.28 = (f32[96,128]{1,0:T(8,128)S(1)}, f32[96,128]{1,0:T(8,128)S(1)}, u32[]{:S(2)}, u32[]{:S(2)}) collective-permute-start(f32[96,128]{1,0:T(8,128)S(1)} %add_add_fusion.7), channel_id=1, source_target_pairs={{12,0},{0,4},{4,8},{8,12},{13,1},{1,5},{5,9},{9,13},{14,2},{2,6},{... | collective-permute-start | bytes 147464 | tf_op jit(solution)/shard_map/ppermute | solution.py:30
  186.3 4.5 %collective-permute-start.30 = (f32[96,128]{1,0:T(8,128)S(1)}, f32[96,128]{1,0:T(8,128)S(1)}, u32[]{:S(2)}, u32[]{:S(2)}) collective-permute-start(f32[96,128]{1,0:T(8,128)S(1)} %add_add_fusion.6), channel_id=1, source_target_pairs={{16,0},{0,16},{17,1},{1,17},{18,2},{2,18},{19,3},{3,19},{20,4},{4,... | collective-permute-start | bytes 147464 | tf_op jit(solution)/shard_map/ppermute | solution.py:30
  190.9 5.5 %collective-permute-start.31 = (bf16[48,4096]{1,0:T(8,128)(2,1)S(1)}, bf16[48,4096]{1,0:T(8,128)(2,1)S(1)}, u32[]{:S(2)}, u32[]{:S(2)}) collective-permute-start(bf16[48,4096]{1,0:T(8,128)(2,1)S(1)} %slice.305), channel_id=1, source_target_pairs={{0,32},{32,0},{1,33},{33,1},{2,34},{34,2},{3,35},{35,3},{4,36},{36... | collective-permute-start | bytes 1179656 | tf_op jit(solution)/shard_map/ppermute | solution.py:21
  197.0 4.2 %collective-permute-start.29 = (bf16[48,4096]{1,0:T(8,128)(2,1)S(1)}, bf16[48,4096]{1,0:T(8,128)(2,1)S(1)}, u32[]{:S(2)}, u32[]{:S(2)}) collective-permute-start(bf16[48,4096]{1,0:T(8,128)(2,1)S(1)} %slice.306), channel_id=1, source_target_pairs={{0,32},{32,0},{1,33},{33,1},{2,34},{34,2},{3,35},{35,3},{4,36},{36... | collective-permute-start | bytes 1179656 | tf_op jit(solution)/shard_map/ppermute | solution.py:21
  197.7 11.1 %collective-permute-start.33 = (bf16[48,4096]{1,0:T(8,128)(2,1)S(1)}, bf16[48,4096]{1,0:T(8,128)(2,1)S(1)}, u32[]{:S(2)}, u32[]{:S(2)}) collective-permute-start(bf16[48,4096]{1,0:T(8,128)(2,1)S(1)} %add_convert_fusion), channel_id=1, source_target_pairs={{0,64},{64,0},{1,65},{65,1},{2,66},{66,2},{3,67},{67,3},{4,68},{68... | collective-permute-start | bytes 1179656 | tf_op jit(solution)/shard_map/ppermute | solution.py:25
  (23 other events, 157.0 us)

commit v4 on v2

--- a/solution.py
+++ b/solution.py
@@ -11,6 +11,7 @@
 BLK = ("xh", "y", "z")
 ALL = GRP + BLK
 SWAP = [(0, 1), (1, 0)]
+DIAGONAL = [(0, 3), (1, 2), (2, 1), (3, 0)]
 LANES = 128
 F32 = jnp.float32
 BF16 = jnp.bfloat16
@@ -23,6 +24,24 @@
 
 def swap_chip(values):
     return lax.ppermute(values, "xl", SWAP)
+
+
+def from_ahead(values, axis, step):
+    size = lax.axis_size(axis)
+    return lax.ppermute(values, axis, [((i + step) % size, i) for i in range(size)])
+
+
+def sum_over(values, axis):
+    if lax.axis_size(axis) == 2:
+        return values + from_ahead(values, axis, 1)
+    one, two, three = [from_ahead(values, axis, step) for step in (1, 2, 3)]
+    return (values + two) + (one + three)
+
+
+def gather_ahead(values, axis):
+    return jnp.stack(
+        [values] + [from_ahead(values, axis, step) for step in range(1, lax.axis_size(axis))]
+    )
 
 
 def exchange(values, axes):
@@ -59,13 +78,14 @@
 
 def scatter_kernel(hard_count, tok_rows, ids, w_ref, q_ref, neg_ref, add_ref, sum_ref, slot, *parts):
     rows = q_ref.shape[0]
+    for part in parts:
+        part[...] = jnp.zeros_like(part)
     q = q_ref[...].astype(F32)
     total = jnp.zeros((rows, LANES), F32)
     for k in range(hard_count):
         weight = w_ref[:, k : k + 1].astype(F32)
         slot[k] = weight * q
         total = total + weight * neg_ref[k].astype(F32)
-        parts[k][...] = jnp.zeros_like(parts[k])
     sum_ref[...] = total
 
     def place(block, carry):
@@ -80,6 +100,42 @@
     for k in range(1, hard_count):
         added = added + parts[k][...]
     add_ref[...] = added.astype(BF16)
+
+
+def stream_chunks(w_ref, held, sems):
+    chunks, depth = held.shape[0], held.shape[1]
+    copies = [
+        pltpu.make_async_copy(w_ref.at[pl.ds(c * depth, depth), :], held.at[c], sems.at[c])
+        for c in range(chunks)
+    ]
+    for copy in copies:
+        copy.start()
+    return copies
+
+
+def forward_kernel(x0, x1, x2, x3, w_ref, y0, y1, y2, y3, held, total, sems):
+    depth = held.shape[1]
+    rows = y0.shape[0]
+    for c, copy in enumerate(stream_chunks(w_ref, held, sems)):
+        copy.wait()
+        here = slice(c * depth, (c + 1) * depth)
+        x = jnp.concatenate([x_ref[:, here] for x_ref in (x0, x1, x2, x3)])
+        term = jnp.dot(x, held[c], preferred_element_type=F32)
+        total[...] = term if c == 0 else total[...] + term
+    for i, y_ref in enumerate((y0, y1, y2, y3)):
+        y_ref[...] = total[i * rows : (i + 1) * rows, :].astype(BF16)
+
+
+def backward_kernel(x0, x1, x2, x3, w_ref, y0, y1, y2, y3, held, sems):
+    depth = held.shape[1]
+    rows = y0.shape[0]
+    copies = stream_chunks(w_ref, held, sems)
+    x = jnp.concatenate([x_ref[:rows, :] for x_ref in (x0, x1, x2, x3)])
+    for c, copy in enumerate(copies):
+        copy.wait()
+        term = lax.dot_general(x, held[c], (((1,), (1,)), ((), ())), preferred_element_type=F32)
+        for i, y_ref in enumerate((y0, y1, y2, y3)):
+            y_ref[:, c * depth : (c + 1) * depth] = term[i * rows : (i + 1) * rows].astype(BF16)
 
 
 def local(resid, attn, out_proj, out_bias, gain, task_bias, task_ids, neg_owner, neg_row):
@@ -94,28 +150,32 @@
     chip = lax.axis_index("xl")
     vmem = pl.BlockSpec(memory_space=pltpu.VMEM)
     smem = pl.BlockSpec(memory_space=pltpu.SMEM)
-    params = pltpu.CompilerParams(vmem_limit_bytes=40 * 1024 * 1024)
+    params = pltpu.CompilerParams(vmem_limit_bytes=24 * 1024 * 1024)
 
     attn_rows = attn.reshape(row_count, width)
     far_rows = swap_chip(attn_rows)
     near_rows = swap_core(attn_rows)
 
-    out_proj_t = lax.optimization_barrier(out_proj.T)
-    near_task = swap_core(task_ids)
-    tasks = jnp.concatenate([task_ids, near_task])
-    tasks = jnp.concatenate([tasks, swap_chip(tasks)])
-
-    def project(rows):
-        return jnp.dot(rows, out_proj, preferred_element_type=F32).astype(BF16)
-
-    chip_columns = project(jnp.concatenate([attn_rows, near_rows]))
-    far_rows, chip_columns = lax.optimization_barrier((far_rows, chip_columns))
-    far_columns = project(jnp.concatenate([far_rows, swap_core(far_rows)]))
+
+    chunks = 8
+    held = [
+        pltpu.VMEM((chunks, out_proj.shape[0] // chunks, out_proj.shape[1]), BF16),
+        pltpu.SemaphoreType.DMA((chunks,)),
+    ]
+    hbm = pl.BlockSpec(memory_space=pl.ANY)
+    columns = pl.pallas_call(
+        forward_kernel,
+        out_shape=[jax.ShapeDtypeStruct((row_count, out_proj.shape[1]), BF16)] * 4,
+        in_specs=[vmem] * 4 + [hbm],
+        out_specs=[vmem] * 4,
+        scratch_shapes=[held[0], pltpu.VMEM((4 * row_count, out_proj.shape[1]), F32), held[1]],
+        compiler_params=params,
+    )(attn_rows, near_rows, far_rows, swap_core(far_rows), out_proj)
     parts = [
-        chip_columns[:row_count],
-        swap_core(chip_columns[row_count:]),
-        swap_chip(far_columns[:row_count]),
-        lax.ppermute(far_columns[row_count:], GRP, [(0, 3), (1, 2), (2, 1), (3, 0)]),
+        columns[0],
+        swap_core(columns[1]),
+        swap_chip(columns[2]),
+        lax.ppermute(columns[3], GRP, DIAGONAL),
     ]
 
     def by_group(items):
@@ -172,11 +232,11 @@
         ],
         compiler_params=params,
     )(ids, q_all, p_all)
-    score_part = exchange(score_part.astype(SEND).reshape(blocks, tok_rows, pairs), BLK)
-    score_part, hard_part = lax.optimization_barrier((score_part, hard_part))
-    hard_part = exchange(hard_part.astype(SEND).reshape(blocks, tok_rows, LANES), BLK)
-    scores = jnp.sum(score_part.astype(F32), axis=0) / TAU
-    hard = jnp.sum(hard_part.astype(F32), axis=0) / TAU
+    part = jnp.concatenate([score_part, hard_part], axis=1).astype(SEND)
+    part = exchange(part.reshape(blocks, tok_rows, pairs + LANES), BLK)
+    part = jnp.sum(part.astype(F32), axis=0) / TAU
+    scores = part[:, :pairs]
+    hard = part[:, pairs:]
 
     column = lax.broadcasted_iota(jnp.int32, scores.shape, 1)
     row = lax.broadcasted_iota(jnp.int32, scores.shape, 0)
@@ -193,8 +253,8 @@
         values = exchange(jnp.broadcast_to(values[None], (blocks,) + values.shape), BLK)
         return values.reshape((pairs,) + values.shape[2:])
 
+    hard_probs = spread_rows(hard_weights / totals)
     group_probs = spread_rows(weights / totals)
-    hard_probs = spread_rows(hard_weights / totals)
 
     hard_add, hard_sum = pl.pallas_call(
         lambda *refs: scatter_kernel(hard_count, tok_rows, *refs),
@@ -228,42 +288,49 @@
     scaled = (LOSS_SCALE * d_pooled).astype(BF16)
 
 
-    cols = [scaled[:, i * (width // 4) : (i + 1) * (width // 4)] for i in range(4)]
-    cols = by_group(cols)
-    far_cols = swap_chip(cols[2])
-    diag_cols = lax.ppermute(cols[3], GRP, [(0, 3), (1, 2), (2, 1), (3, 0)])
-    near_cols = swap_core(cols[1])
-    d_gain, d_out_bias, d_bias, near_cols = lax.optimization_barrier(
-        (d_gain, d_out_bias, d_bias, near_cols)
-    )
-
-    def back(rows):
-        return lax.dot_general(
-            rows, out_proj_t, (((1,), (0,)), ((), ())), preferred_element_type=F32
-        )
-
-    vectors = jnp.stack([d_gain, d_out_bias, d_bias]).reshape(3, blocks, LANES).transpose(1, 0, 2)
-    vectors, far_cols, diag_cols = lax.optimization_barrier(
-        (exchange(vectors, BLK), far_cols, diag_cols)
-    )
-    vectors = jnp.sum(vectors, axis=0)
-    far_part = back(jnp.concatenate([far_cols, diag_cols]))
-    far_sum = far_part[:row_count] + swap_core(far_part[row_count:].astype(BF16)).astype(F32)
-    far_sum, near_cols = lax.optimization_barrier((far_sum.astype(BF16), near_cols))
+    vectors = jnp.stack([d_gain, d_out_bias, d_bias])
+    high = vectors.astype(BF16)
+    low = (vectors - high.astype(F32)).astype(BF16)
+    task = jnp.broadcast_to(task_ids.astype(BF16)[:, None], (2, width))
+    cols = jnp.concatenate([scaled, high, low, task])
+    cols = by_group(jnp.split(cols, 4, axis=1))
+    cols = [
+        cols[0],
+        swap_core(cols[1]),
+        swap_chip(cols[2]),
+        lax.ppermute(cols[3], GRP, DIAGONAL),
+    ]
+    extra = jnp.stack([part[row_count:] for part in cols])
+    vectors = extra[:, :3].astype(F32) + extra[:, 3:6].astype(F32)
+    tasks = extra[:, 6, :1].astype(jnp.int32)
+    both = (vectors[0, :2] + vectors[1, :2]) + (vectors[2, :2] + vectors[3, :2])
+    vectors = jnp.concatenate([both, vectors[:, 2]]).reshape(-1, LANES)
+    back = pl.pallas_call(
+        backward_kernel,
+        out_shape=[jax.ShapeDtypeStruct((row_count, width), BF16)] * 4,
+        in_specs=[vmem] * 4 + [hbm],
+        out_specs=[vmem] * 4,
+        scratch_shapes=held,
+        compiler_params=params,
+    )(*cols, out_proj)
+    vectors = sum_over(vectors, "z")
+    vectors, *back = lax.optimization_barrier((vectors, *back))
+    vectors = sum_over(vectors, "y")
+    far_sum = back[2].astype(F32) + swap_core(back[3]).astype(F32)
+    far_sum, vectors = lax.optimization_barrier((far_sum.astype(BF16), vectors))
     far_sum = swap_chip(far_sum).astype(F32)
-    near_part = back(jnp.concatenate([cols[0], near_cols]))
-    near_sum = near_part[:row_count] + swap_core(near_part[row_count:].astype(BF16)).astype(F32)
-    grad_attn = near_sum + far_sum
-
-    pair = jnp.stack([vectors, swap_core(vectors)])
-    four = jnp.concatenate([pair, swap_chip(pair)])
-    onehot = (tasks[:, None] == jnp.arange(task_bias.shape[0])[None, :]).astype(F32)
-    placed = jnp.concatenate(
-        [four[:, :2], onehot[:, :, None] * four[:, 2:3]], axis=1
-    )
+    grad_attn = back[0].astype(F32) + swap_core(back[1]).astype(F32) + far_sum
+
+    vectors = sum_over(vectors, "xh")
+    vectors = vectors.reshape(6, -1)
+    onehot = (tasks == jnp.arange(task_bias.shape[0])[None, :]).astype(F32)
+    placed = onehot[:, :, None] * vectors[2:, None, :]
     placed = (placed[0] + placed[1]) + (placed[2] + placed[3])
-    whole = exchange(jnp.broadcast_to(placed[None], (blocks,) + placed.shape), BLK)
-    whole = whole.transpose(1, 0, 2).reshape(placed.shape[0], width)
+    placed = jnp.concatenate([vectors[:2], placed])
+    pair = jnp.stack([placed, swap_core(placed)])
+    pair, grad_attn = lax.optimization_barrier((pair, grad_attn))
+    far = swap_chip(pair)
+    whole = jnp.concatenate(by_group([pair[0], pair[1], far[0], far[1]]), axis=1)
     return (
         losses,
         grad_attn.reshape(2, tok_rows, width),

time: 221 us -> 211 us (0.955)
  matrix products: 27 us -> 4.05 us
  starting transfers between devices: 76.9 us -> 67.7 us
  local copies, waits for them, and re-layouts: 6.33 us -> 14.5 us
  waiting for transfers between devices: 76.2 us -> 83.9 us
  Pallas kernels: 13.4 us -> 21 us
    dot_general x4 -> x0, matrix products: 22 us -> none  [the longest x2 12.1 us: back(): lax.dot_general(rows, out_proj_t, (((1,), (0,)), ((), ())), preferred_ele...]
    all_to_all x8 -> x5, starting transfers between devices: 51 us -> 33 us  [exchange(): return lax.all_to_all(values, axes, split_axis=0, concat_axis=0, tiled=True)]
    unnamed x46 -> x47, local copies, waits for them, and re-layouts: 0.78 us -> 9.1 us
    pallas_call x0 -> x2, Pallas kernels: none -> 7.6 us  [the longest x1 4.7 us: local(): pl.pallas_call(backward_kernel, out_shape=[jax.ShapeDtypeStruct((row_coun...]
    ppermute x2 -> x9, starting transfers between devices: 3.35 us -> 10.8 us  [the longest x7 6.37 us: from_ahead(): lax.ppermute(values, axis, [((i + step) % size, i) for i in range(size)])]
    ppermute x2 -> x9, waiting for transfers between devices: 3.29 us -> 8.78 us  [the longest x7 3.97 us: from_ahead(): lax.ppermute(values, axis, [((i + step) % size, i) for i in range(size)])]
    all_to_all x8 -> x5, waiting for transfers between devices: 47.8 us -> 51.9 us  [exchange(): return lax.all_to_all(values, axes, split_axis=0, concat_axis=0, tiled=True)]
    ppermute x11 -> x10, starting transfers between devices: 18.3 us -> 19 us  [swap_core(): return lax.ppermute(values, 'co', SWAP)]
  transfers between devices with their start and end apart: 29 -> 31, of which waited for: 16 -> 20; matrix products, arithmetic and copies ran while one was open for 21% -> 5% of each run, Pallas kernels for 6% -> 6%
where the time goes in v4:
time: 211 us; the launch traced here: 210 us
  waiting for transfers between devices  83.9 us (40%)
  starting transfers between devices  67.7 us (32%)
  Pallas kernels  21 us (10%)
  other arithmetic  16.3 us (8%)
  local copies, waits for them, and re-layouts  14.5 us (7%)
  matrix products  4.05 us (2%)
    all_to_all x5, waiting for transfers between devices, exchange(): return lax.all_to_all(values, axes, split_axis=0, concat_axis=0, tiled=True)  51.9 us
    all_to_all x5, starting transfers between devices, exchange(): return lax.all_to_all(values, axes, split_axis=0, concat_axis=0, tiled=True)  33 us
    ppermute x7, waiting for transfers between devices, swap_chip(): return lax.ppermute(values, 'xl', SWAP)  21.7 us
    ppermute x10, starting transfers between devices, swap_core(): return lax.ppermute(values, 'co', SWAP)  19 us
    unnamed x47, local copies, waits for them, and re-layouts  9.1 us
    pallas_call x1, Pallas kernels, local(): pl.pallas_call(lambda *refs: scatter_kernel(hard_count, tok_rows, *refs),...  7.21 us
    ppermute x7, starting transfers between devices, from_ahead(): lax.ppermute(values, axis, [((i + step) % size, i) for i in range(size)])  6.37 us
    pallas_call x1, Pallas kernels, local(): pl.pallas_call(lambda *refs: gather_kernel(hard_count, tok_rows, *refs),...  6.24 us
  transfers between devices with their start and end apart: 31, of which 20 were waited for; matrix products, arithmetic and copies ran while one was open for 5% of the time, Pallas kernels for 6%

profile of v4, /device:TPU:1, one launch (start us, length us, event | category | flops | bytes accessed | tf_op | source)
XLA Modules:
  0.0 209.5 jit_solution(10454813701963229987)
XLA Ops:
  0.6 2.1 %collective-permute-start.1 = (bf16[48,4096]{1,0:T(8,128)(2,1)}, bf16[48,4096]{1,0:T(8,128)(2,1)S(1)}, u32[]{:S(2)}, u32[]{:S(2)}) collective-permute-start(bf16[48,4096]{1,0:T(8,128)(2,1)} %bitcast.150), channel_id=1, source_target_pairs={{0,64},{64,0},{1,65},{65,1},{2,66},{66,2},{3,67},{67,3},{4,68},{68... | collective-permute-start | bytes 1179656 | tf_op jit(solution)/shard_map/ppermute | solution.py:26
  4.4 6.9 %collective-permute-done.1.x2 = bf16[48,4096]{1,0:T(8,128)(2,1)S(1)} collective-permute-done((bf16[48,4096]{1,0:T(8,128)(2,1)}, bf16[48,4096]{1,0:T(8,128)(2,1)S(1)}, u32[]{:S(2)}, u32[]{:S(2)}) %collective-permute-start.1) | collective-permute-done | bytes 393248 | tf_op jit(solution)/shard_map/ppermute | solution.py:26
  14.8 3.4 %copy-done = bf16[4096,1024]{1,0:T(8,128)(2,1)S(1)} copy-done((bf16[4096,1024]{1,0:T(8,128)(2,1)S(1)}, bf16[4096,1024]{1,0:T(8,128)(2,1)}, u32[]{:S(2)}) %copy-start) | copy-done | bytes 8388632
  19.1 2.9 %shard_map.128 = (bf16[48,1024]{1,0:T(8,128)(2,1)S(1)}, bf16[48,1024]{1,0:T(8,128)(2,1)S(1)}, bf16[48,1024]{1,0:T(8,128)(2,1)S(1)}, bf16[48,1024]{1,0:T(8,128)(2,1)S(1)}) custom-call(bf16[48,4096]{1,0:T(8,128)(2,1)S(1)} %bitcast.152, bf16[48,4096]{1,0:T(8,128)(2,1)S(1)} %collective-permute-done.x1, bf16[48,4096]{1,0:T(8,128)(2,1)S(1)} %collective-permute-done.1.x2, ...), custom_call_target="tpu_custom_call" | custom-call | tf_op jit(solution)/shard_map/pallas_call | solution.py:166
  24.4 2.8 %collective-permute-done.3 = bf16[48,1024]{1,0:T(8,128)(2,1)S(1)} collective-permute-done((bf16[48,1024]{1,0:T(8,128)(2,1)S(1)}, bf16[48,1024]{1,0:T(8,128)(2,1)S(1)}, u32[]{:S(2)}, u32[]{:S(2)}) %collective-permute-start.3) | collective-permute-done | bytes 98336 | tf_op jit(solution)/shard_map/ppermute | solution.py:178
  32.1 10.5 %all-to-all-start = ((bf16[32,56,128]{2,1,0:T(8,128)(2,1)}), bf16[32,56,128]{2,1,0:T(8,128)(2,1)S(1)}, u32[]{:S(2)}, u32[]{:S(2)}) async-start(bf16[32,56,128]{2,1,0:T(8,128)(2,1)} %pad_maximum_fusion.2), calls=%async_computation | async-start | bytes 917504 | tf_op jit(solution)/shard_map/all_to_all | solution.py:48
  42.7 10.2 %all-to-all-done = bf16[32,56,128]{2,1,0:T(8,128)(2,1)S(1)} async-done(((bf16[32,56,128]{2,1,0:T(8,128)(2,1)}), bf16[32,56,128]{2,1,0:T(8,128)(2,1)S(1)}, u32[]{:S(2)}, u32[]{:S(2)}) %all-to-all-start) | async-done | bytes 458784 | tf_op jit(solution)/shard_map/all_to_all | solution.py:48
  53.3 3.4 %collective-permute-start.6 = (bf16[768,128]{1,0:T(8,128)(2,1)S(1)}, bf16[768,128]{1,0:T(8,128)(2,1)S(1)}, u32[]{:S(2)}, u32[]{:S(2)}) collective-permute-start(bf16[768,128]{1,0:T(8,128)(2,1)S(1)} %bitcast.176), channel_id=1, source_target_pairs={{0,32},{32,0},{1,33},{33,1},{2,34},{34,2},{3,35},{35,3},{4,36},{36... | collective-permute-start | bytes 589832 | tf_op jit(solution)/shard_map/ppermute | solution.py:22
  57.5 4.3 %collective-permute-start.8 = (bf16[768,128]{1,0:T(8,128)(2,1)S(1)}, bf16[768,128]{1,0:T(8,128)(2,1)S(1)}, u32[]{:S(2)}, u32[]{:S(2)}) collective-permute-start(bf16[768,128]{1,0:T(8,128)(2,1)S(1)} %collective-permute-done.7), channel_id=1, source_target_pairs={{0,32},{32,0},{1,33},{33,1},{2,34},{34,2},{3,35},{35,3},{4,36},{36... | collective-permute-start | bytes 589832 | tf_op jit(solution)/shard_map/ppermute | solution.py:22
  63.0 6.2 %shard_map.129 = (bf16[7,768,128]{2,1,0:T(8,128)(2,1)S(1)}, f32[768,128]{1,0:T(8,128)S(1)}) custom-call(s32[5376]{0:T(1024)S(1)} %reshape.442.refs_0_, bf16[768,128]{1,0:T(8,128)(2,1)S(1)} %bitcast.147, bf16[3072,128]{1,0:T(8,128)(2,1)S(1)} %pad_maximum_fusion.1.refs_2_), custom_call_target="tpu_custom_call" | custom-call | tf_op jit(solution)/shard_map/pallas_call | solution.py:221
  70.7 4.0 %all-to-all-start.1 = ((f16[32,24,896]{2,1,0:T(8,128)(2,1)}), f16[32,24,896]{2,1,0:T(8,128)(2,1)S(1)}, u32[]{:S(2)}, u32[]{:S(2)}) async-start(f16[32,24,896]{2,1,0:T(8,128)(2,1)} %pad_maximum_fusion), calls=%async_computation.1 | async-start | bytes 2752512 | tf_op jit(solution)/shard_map/all_to_all | solution.py:48
  76.1 18.5 %all-to-all-done.1 = f16[32,24,896]{2,1,0:T(8,128)(2,1)S(1)} async-done(((f16[32,24,896]{2,1,0:T(8,128)(2,1)}), f16[32,24,896]{2,1,0:T(8,128)(2,1)S(1)}, u32[]{:S(2)}, u32[]{:S(2)}) %all-to-all-start.1) | async-done | bytes 1376288 | tf_op jit(solution)/shard_map/all_to_all | solution.py:48
  96.5 6.0 %all-to-all-start.3 = ((bf16[32,24,128]{2,1,0:T(8,128)(2,1)}), bf16[32,24,128]{2,1,0:T(8,128)(2,1)S(1)}, u32[]{:S(2)}, u32[]{:S(2)}) async-start(bf16[32,24,128]{2,1,0:T(8,128)(2,1)} %broadcast_in_dim.32), calls=%async_computation.3 | async-start | bytes 393216 | tf_op jit(solution)/shard_map/all_to_all | solution.py:48
  102.6 9.1 %all-to-all-done.3 = bf16[32,24,128]{2,1,0:T(8,128)(2,1)S(1)} async-done(((bf16[32,24,128]{2,1,0:T(8,128)(2,1)}), bf16[32,24,128]{2,1,0:T(8,128)(2,1)S(1)}, u32[]{:S(2)}, u32[]{:S(2)}) %all-to-all-start.3) | async-done | bytes 196640 | tf_op jit(solution)/shard_map/all_to_all | solution.py:48
  112.7 4.8 %all-to-all-start.2 = ((bf16[32,24,768]{2,1,0:T(8,128)(2,1)}), bf16[32,24,768]{2,1,0:T(8,128)(2,1)}, u32[]{:S(2)}, u32[]{:S(2)}) async-start(bf16[32,24,768]{2,1,0:T(8,128)(2,1)} %broadcast_in_dim.31), calls=%async_computation.2 | async-start | bytes 2359296 | tf_op jit(solution)/shard_map/all_to_all | solution.py:48
  117.6 7.2 %shard_map.130 = (bf16[3072,128]{1,0:T(8,128)(2,1)S(1)}, f32[768,128]{1,0:T(8,128)S(1)}) custom-call(s32[5376]{0:T(1024)S(1)} %reshape.442.refs_0_, bf16[768,128]{1,0:T(8,128)(2,1)S(1)} %bitcast.149, bf16[768,128]{1,0:T(8,128)(2,1)S(1)} %bitcast.148, bf16[7,768,128]{2,1,0:T(8,128)(2,1)S(1)} %get-tuple-element.31.refs_3_), custom_call_target="tpu_custom_call" | custom-call | tf_op jit(solution)/shard_map/pallas_call | solution.py:259
  124.9 2.3 %collective-permute-start.9 = (bf16[2,768,128]{2,1,0:T(8,128)(2,1)S(1)}, bf16[2,768,128]{2,1,0:T(8,128)(2,1)S(1)}, u32[]{:S(2)}, u32[]{:S(2)}) collective-permute-start(bf16[2,768,128]{2,1,0:T(8,128)(2,1)S(1)} %pad_maximum_fusion.5), channel_id=1, source_target_pairs={{0,32},{32,0},{1,33},{33,1},{2,34},{34,2},{3,35},{35,3},{4,36},{36... | collective-permute-start | bytes 1179656 | tf_op jit(solution)/shard_map/ppermute | solution.py:22
  129.7 4.2 %all-to-all-done.2 = bf16[32,24,768]{2,1,0:T(8,128)(2,1)} async-done(((bf16[32,24,768]{2,1,0:T(8,128)(2,1)}), bf16[32,24,768]{2,1,0:T(8,128)(2,1)}, u32[]{:S(2)}, u32[]{:S(2)}) %all-to-all-start.2) | async-done | bytes 1179680 | tf_op jit(solution)/shard_map/all_to_all | solution.py:48
  133.9 1.8 convolution_bitcast_fusion
  135.7 1.7 fusion
  139.2 7.7 %all-to-all-start.4 = ((bf16[32,2,24,128]{3,2,1,0:T(8,128)(2,1)}), bf16[32,2,24,128]{3,2,1,0:T(8,128)(2,1)S(1)}, u32[]{:S(2)}, u32[]{:S(2)}) async-start(bf16[32,2,24,128]{3,2,1,0:T(8,128)(2,1)} %pad_maximum_fusion.6), calls=%async_computation.4 | async-start | bytes 786432 | tf_op jit(solution)/shard_map/all_to_all | solution.py:48
  147.0 9.9 %all-to-all-done.4 = bf16[32,2,24,128]{3,2,1,0:T(8,128)(2,1)S(1)} async-done(((bf16[32,2,24,128]{3,2,1,0:T(8,128)(2,1)}), bf16[32,2,24,128]{3,2,1,0:T(8,128)(2,1)S(1)}, u32[]{:S(2)}, u32[]{:S(2)}) %all-to-all-start.4) | async-done | bytes 393248 | tf_op jit(solution)/shard_map/all_to_all | solution.py:48
  161.6 3.0 %collective-permute-start.13 = (bf16[56,1024]{1,0:T(8,128)(2,1)S(1)}, bf16[56,1024]{1,0:T(8,128)(2,1)S(1)}, u32[]{:S(2)}, u32[]{:S(2)}) collective-permute-start(bf16[56,1024]{1,0:T(8,128)(2,1)S(1)} %get-tuple-element.60), channel_id=1, source_target_pairs={{0,96},{32,64},{64,32},{96,0},{1,97},{33,65},{65,33},{97,1},{2,98}... | collective-permute-start | bytes 344072 | tf_op jit(solution)/shard_map/ppermute | solution.py:301
  165.8 2.0 collective-permute-done.13.x3
  167.8 3.0 %collective-permute-done.12.x2 = bf16[56,1024]{1,0:T(8,128)(2,1)S(1)} collective-permute-done((bf16[56,1024]{1,0:T(8,128)(2,1)S(1)}, bf16[56,1024]{1,0:T(8,128)(2,1)S(1)}, u32[]{:S(2)}, u32[]{:S(2)}) %collective-permute-start.12) | collective-permute-done | bytes 114720 | tf_op jit(solution)/shard_map/ppermute | solution.py:26
  173.8 3.4 %copy-done.1 = bf16[4096,1024]{1,0:T(8,128)(2,1)S(1)} copy-done((bf16[4096,1024]{1,0:T(8,128)(2,1)S(1)}, bf16[4096,1024]{1,0:T(8,128)(2,1)}, u32[]{:S(2)}) %copy-start.1) | copy-done | bytes 8388632
  177.2 4.7 %shard_map.131 = (bf16[48,4096]{1,0:T(8,128)(2,1)S(1)}, bf16[48,4096]{1,0:T(8,128)(2,1)S(1)}, bf16[48,4096]{1,0:T(8,128)(2,1)S(1)}, bf16[48,4096]{1,0:T(8,128)(2,1)S(1)}) custom-call(bf16[56,1024]{1,0:T(8,128)(2,1)S(1)} %get-tuple-element.57.x0, bf16[56,1024]{1,0:T(8,128)(2,1)S(1)} %collective-permute-done.11.x1, ...), custom_call_target="tpu_custom_call" | custom-call | tf_op jit(solution)/shard_map/pallas_call | solution.py:308
  185.4 1.9 collective-permute-done.20
  190.2 1.9 collective-permute-start.23
  193.0 3.0 %collective-permute-start.22 = (f32[10,1024]{1,0:T(8,128)S(1)}, f32[10,1024]{1,0:T(8,128)S(1)}, u32[]{:S(2)}, u32[]{:S(2)}) collective-permute-start(f32[10,1024]{1,0:T(8,128)S(1)} %get-tuple-element.80), channel_id=1, source_target_pairs={{0,32},{32,0},{1,33},{33,1},{2,34},{34,2},{3,35},{35,3},{4,36},{36... | collective-permute-start | bytes 122888 | tf_op jit(solution)/shard_map/ppermute | solution.py:22
  196.9 6.0 %collective-permute-done.24 = bf16[48,4096]{1,0:T(8,128)(2,1)S(1)} collective-permute-done((bf16[48,4096]{1,0:T(8,128)(2,1)S(1)}, bf16[48,4096]{1,0:T(8,128)(2,1)S(1)}, u32[]{:S(2)}, u32[]{:S(2)}) %collective-permute-start.24) | collective-permute-done | bytes 393248 | tf_op jit(solution)/shard_map/ppermute | solution.py:26
  204.3 3.8 %collective-permute-done.25 = f32[2,10,1024]{2,1,0:T(8,128)S(1)} collective-permute-done((f32[2,10,1024]{2,1,0:T(8,128)S(1)}, f32[2,10,1024]{2,1,0:T(8,128)S(1)}, u32[]{:S(2)}, u32[]{:S(2)}) %collective-permute-start.25) | collective-permute-done | bytes 81952 | tf_op jit(solution)/shard_map/ppermute | solution.py:26
  (177 shorter events, 44.6 us)
Async XLA Ops:
  0.6 10.7 %collective-permute-start.1 = (bf16[48,4096]{1,0:T(8,128)(2,1)}, bf16[48,4096]{1,0:T(8,128)(2,1)S(1)}, u32[]{:S(2)}, u32[]{:S(2)}) collective-permute-start(bf16[48,4096]{1,0:T(8,128)(2,1)} %bitcast.150), channel_id=1, source_target_pairs={{0,64},{64,0},{1,65},{65,1},{2,66},{66,2},{3,67},{67,3},{4,68},{68... | collective-permute-start | bytes 1179656 | tf_op jit(solution)/shard_map/ppermute | solution.py:26
  2.8 12.0 %collective-permute-start = (bf16[48,4096]{1,0:T(8,128)(2,1)}, bf16[48,4096]{1,0:T(8,128)(2,1)S(1)}, u32[]{:S(2)}, u32[]{:S(2)}) collective-permute-start(bf16[48,4096]{1,0:T(8,128)(2,1)} %bitcast.151), channel_id=1, source_target_pairs={{0,32},{32,0},{1,33},{33,1},{2,34},{34,2},{3,35},{35,3},{4,36},{36... | collective-permute-start | bytes 1179656 | tf_op jit(solution)/shard_map/ppermute | solution.py:22
  11.3 3.5 %collective-permute-start.2 = (bf16[48,4096]{1,0:T(8,128)(2,1)S(1)}, bf16[48,4096]{1,0:T(8,128)(2,1)S(1)}, u32[]{:S(2)}, u32[]{:S(2)}) collective-permute-start(bf16[48,4096]{1,0:T(8,128)(2,1)S(1)} %collective-permute-done.1.x2), channel_id=1, source_target_pairs={{0,32},{32,0},{1,33},{33,1},{2,34},{34,2},{3,35},{35,3},{4,36},{36... | collective-permute-start | bytes 1179656 | tf_op jit(solution)/shard_map/ppermute | solution.py:22
  22.1 5.1 %collective-permute-start.3 = (bf16[48,1024]{1,0:T(8,128)(2,1)S(1)}, bf16[48,1024]{1,0:T(8,128)(2,1)S(1)}, u32[]{:S(2)}, u32[]{:S(2)}) collective-permute-start(bf16[48,1024]{1,0:T(8,128)(2,1)S(1)} %get-tuple-element.26), channel_id=1, source_target_pairs={{0,96},{32,64},{64,32},{96,0},{1,97},{33,65},{65,33},{97,1},{2,98}... | collective-permute-start | bytes 294920 | tf_op jit(solution)/shard_map/ppermute | solution.py:178
  23.5 5.1 %collective-permute-start.4 = (bf16[48,1024]{1,0:T(8,128)(2,1)S(1)}, bf16[48,1024]{1,0:T(8,128)(2,1)S(1)}, u32[]{:S(2)}, u32[]{:S(2)}) collective-permute-start(bf16[48,1024]{1,0:T(8,128)(2,1)S(1)} %get-tuple-element.27), channel_id=1, source_target_pairs={{0,64},{64,0},{1,65},{65,1},{2,66},{66,2},{3,67},{67,3},{4,68},{68... | collective-permute-start | bytes 294920 | tf_op jit(solution)/shard_map/ppermute | solution.py:26
  23.7 4.9 %collective-permute-start.5 = (bf16[48,1024]{1,0:T(8,128)(2,1)S(1)}, bf16[48,1024]{1,0:T(8,128)(2,1)S(1)}, u32[]{:S(2)}, u32[]{:S(2)}) collective-permute-start(bf16[48,1024]{1,0:T(8,128)(2,1)S(1)} %get-tuple-element.28), channel_id=1, source_target_pairs={{0,32},{32,0},{1,33},{33,1},{2,34},{34,2},{3,35},{35,3},{4,36},{36... | collective-permute-start | bytes 294920 | tf_op jit(solution)/shard_map/ppermute | solution.py:22
  32.1 20.7 %all-to-all-start = ((bf16[32,56,128]{2,1,0:T(8,128)(2,1)}), bf16[32,56,128]{2,1,0:T(8,128)(2,1)S(1)}, u32[]{:S(2)}, u32[]{:S(2)}) async-start(bf16[32,56,128]{2,1,0:T(8,128)(2,1)} %pad_maximum_fusion.2), calls=%async_computation | async-start | bytes 917504 | tf_op jit(solution)/shard_map/all_to_all | solution.py:48
  52.9 4.6 %collective-permute-start.7 = (bf16[768,128]{1,0:T(8,128)(2,1)S(1)}, bf16[768,128]{1,0:T(8,128)(2,1)S(1)}, u32[]{:S(2)}, u32[]{:S(2)}) collective-permute-start(bf16[768,128]{1,0:T(8,128)(2,1)S(1)} %bitcast.175), channel_id=1, source_target_pairs={{0,64},{64,0},{1,65},{65,1},{2,66},{66,2},{3,67},{67,3},{4,68},{68... | collective-permute-start | bytes 589832 | tf_op jit(solution)/shard_map/ppermute | solution.py:26
  53.3 9.0 %collective-permute-start.6 = (bf16[768,128]{1,0:T(8,128)(2,1)S(1)}, bf16[768,128]{1,0:T(8,128)(2,1)S(1)}, u32[]{:S(2)}, u32[]{:S(2)}) collective-permute-start(bf16[768,128]{1,0:T(8,128)(2,1)S(1)} %bitcast.176), channel_id=1, source_target_pairs={{0,32},{32,0},{1,33},{33,1},{2,34},{34,2},{3,35},{35,3},{4,36},{36... | collective-permute-start | bytes 589832 | tf_op jit(solution)/shard_map/ppermute | solution.py:22
  57.5 5.4 %collective-permute-start.8 = (bf16[768,128]{1,0:T(8,128)(2,1)S(1)}, bf16[768,128]{1,0:T(8,128)(2,1)S(1)}, u32[]{:S(2)}, u32[]{:S(2)}) collective-permute-start(bf16[768,128]{1,0:T(8,128)(2,1)S(1)} %collective-permute-done.7), channel_id=1, source_target_pairs={{0,32},{32,0},{1,33},{33,1},{2,34},{34,2},{3,35},{35,3},{4,36},{36... | collective-permute-start | bytes 589832 | tf_op jit(solution)/shard_map/ppermute | solution.py:22
  70.7 23.9 %all-to-all-start.1 = ((f16[32,24,896]{2,1,0:T(8,128)(2,1)}), f16[32,24,896]{2,1,0:T(8,128)(2,1)S(1)}, u32[]{:S(2)}, u32[]{:S(2)}) async-start(f16[32,24,896]{2,1,0:T(8,128)(2,1)} %pad_maximum_fusion), calls=%async_computation.1 | async-start | bytes 2752512 | tf_op jit(solution)/shard_map/all_to_all | solution.py:48
  96.5 15.2 %all-to-all-start.3 = ((bf16[32,24,128]{2,1,0:T(8,128)(2,1)}), bf16[32,24,128]{2,1,0:T(8,128)(2,1)S(1)}, u32[]{:S(2)}, u32[]{:S(2)}) async-start(bf16[32,24,128]{2,1,0:T(8,128)(2,1)} %broadcast_in_dim.32), calls=%async_computation.3 | async-start | bytes 393216 | tf_op jit(solution)/shard_map/all_to_all | solution.py:48
  112.7 21.1 %all-to-all-start.2 = ((bf16[32,24,768]{2,1,0:T(8,128)(2,1)}), bf16[32,24,768]{2,1,0:T(8,128)(2,1)}, u32[]{:S(2)}, u32[]{:S(2)}) async-start(bf16[32,24,768]{2,1,0:T(8,128)(2,1)} %broadcast_in_dim.31), calls=%async_computation.2 | async-start | bytes 2359296 | tf_op jit(solution)/shard_map/all_to_all | solution.py:48
  124.9 3.7 %collective-permute-start.9 = (bf16[2,768,128]{2,1,0:T(8,128)(2,1)S(1)}, bf16[2,768,128]{2,1,0:T(8,128)(2,1)S(1)}, u32[]{:S(2)}, u32[]{:S(2)}) collective-permute-start(bf16[2,768,128]{2,1,0:T(8,128)(2,1)S(1)} %pad_maximum_fusion.5), channel_id=1, source_target_pairs={{0,32},{32,0},{1,33},{33,1},{2,34},{34,2},{3,35},{35,3},{4,36},{36... | collective-permute-start | bytes 1179656 | tf_op jit(solution)/shard_map/ppermute | solution.py:22
  129.4 8.1 %collective-permute-start.10 = (bf16[768,128]{1,0:T(8,128)(2,1)}, bf16[768,128]{1,0:T(8,128)(2,1)}, u32[]{:S(2)}, u32[]{:S(2)}) collective-permute-start(bf16[768,128]{1,0:T(8,128)(2,1)} %fusion.10), channel_id=1, source_target_pairs={{0,64},{64,0},{1,65},{65,1},{2,66},{66,2},{3,67},{67,3},{4,68},{68... | collective-permute-start | bytes 589832 | tf_op jit(solution)/shard_map/ppermute | solution.py:26
  139.2 17.7 %all-to-all-start.4 = ((bf16[32,2,24,128]{3,2,1,0:T(8,128)(2,1)}), bf16[32,2,24,128]{3,2,1,0:T(8,128)(2,1)S(1)}, u32[]{:S(2)}, u32[]{:S(2)}) async-start(bf16[32,2,24,128]{3,2,1,0:T(8,128)(2,1)} %pad_maximum_fusion.6), calls=%async_computation.4 | async-start | bytes 786432 | tf_op jit(solution)/shard_map/all_to_all | solution.py:48
  146.9 10.1 %copy-start.6 = (bf16[48,1024]{1,0:T(8,128)(2,1)S(1)}, bf16[48,1024]{1,0:T(8,128)(2,1)}, u32[]{:S(2)}) copy-start(bf16[48,1024]{1,0:T(8,128)(2,1)} %copy-done.4) | copy-start | bytes 294916
  161.6 6.2 %collective-permute-start.13 = (bf16[56,1024]{1,0:T(8,128)(2,1)S(1)}, bf16[56,1024]{1,0:T(8,128)(2,1)S(1)}, u32[]{:S(2)}, u32[]{:S(2)}) collective-permute-start(bf16[56,1024]{1,0:T(8,128)(2,1)S(1)} %get-tuple-element.60), channel_id=1, source_target_pairs={{0,96},{32,64},{64,32},{96,0},{1,97},{33,65},{65,33},{97,1},{2,98}... | collective-permute-start | bytes 344072 | tf_op jit(solution)/shard_map/ppermute | solution.py:301
  164.6 6.2 %collective-permute-start.12 = (bf16[56,1024]{1,0:T(8,128)(2,1)S(1)}, bf16[56,1024]{1,0:T(8,128)(2,1)S(1)}, u32[]{:S(2)}, u32[]{:S(2)}) collective-permute-start(bf16[56,1024]{1,0:T(8,128)(2,1)S(1)} %get-tuple-element.59), channel_id=1, source_target_pairs={{0,64},{64,0},{1,65},{65,1},{2,66},{66,2},{3,67},{67,3},{4,68},{68... | collective-permute-start | bytes 344072 | tf_op jit(solution)/shard_map/ppermute | solution.py:26
  165.8 5.0 %collective-permute-start.11 = (bf16[56,1024]{1,0:T(8,128)(2,1)S(1)}, bf16[56,1024]{1,0:T(8,128)(2,1)S(1)}, u32[]{:S(2)}, u32[]{:S(2)}) collective-permute-start(bf16[56,1024]{1,0:T(8,128)(2,1)S(1)} %get-tuple-element.58), channel_id=1, source_target_pairs={{0,32},{32,0},{1,33},{33,1},{2,34},{34,2},{3,35},{35,3},{4,36},{36... | collective-permute-start | bytes 344072 | tf_op jit(solution)/shard_map/ppermute | solution.py:22
  171.0 10.9 %collective-permute-start.15 = (f32[48,128]{1,0:T(8,128)S(1)}, f32[48,128]{1,0:T(8,128)S(1)}, u32[]{:S(2)}, u32[]{:S(2)}) collective-permute-start(f32[48,128]{1,0:T(8,128)S(1)} %reshape.448), channel_id=1, source_target_pairs={{1,0},{2,1},{3,2},{0,3},{5,4},{6,5},{7,6},{4,7},{9,8},{10,9},{11,1... | collective-permute-start | bytes 73736 | tf_op jit(solution)/shard_map/ppermute | solution.py:31
  172.1 9.8 %collective-permute-start.16 = (f32[48,128]{1,0:T(8,128)S(1)}, f32[48,128]{1,0:T(8,128)S(1)}, u32[]{:S(2)}, u32[]{:S(2)}) collective-permute-start(f32[48,128]{1,0:T(8,128)S(1)} %reshape.448), channel_id=1, source_target_pairs={{3,0},{0,1},{1,2},{2,3},{7,4},{4,5},{5,6},{6,7},{11,8},{8,9},{9,10... | collective-permute-start | bytes 73736 | tf_op jit(solution)/shard_map/ppermute | solution.py:31
  172.5 9.4 %collective-permute-start.14 = (f32[48,128]{1,0:T(8,128)S(1)}, f32[48,128]{1,0:T(8,128)S(1)}, u32[]{:S(2)}, u32[]{:S(2)}) collective-permute-start(f32[48,128]{1,0:T(8,128)S(1)} %reshape.448), channel_id=1, source_target_pairs={{2,0},{3,1},{0,2},{1,3},{6,4},{7,5},{4,6},{5,7},{10,8},{11,9},{8,1... | collective-permute-start | bytes 73736 | tf_op jit(solution)/shard_map/ppermute | solution.py:31
  181.9 6.5 %collective-permute-start.17 = (bf16[48,4096]{1,0:T(8,128)(2,1)S(1)}, bf16[48,4096]{1,0:T(8,128)(2,1)S(1)}, u32[]{:S(2)}, u32[]{:S(2)}) collective-permute-start(bf16[48,4096]{1,0:T(8,128)(2,1)S(1)} %get-tuple-element.39), channel_id=1, source_target_pairs={{0,32},{32,0},{1,33},{33,1},{2,34},{34,2},{3,35},{35,3},{4,36},{36... | collective-permute-start | bytes 1179656 | tf_op jit(solution)/shard_map/ppermute | solution.py:22
  182.7 2.7 %collective-permute-start.19 = (f32[48,128]{1,0:T(8,128)S(1)}, f32[48,128]{1,0:T(8,128)S(1)}, u32[]{:S(2)}, u32[]{:S(2)}) collective-permute-start(f32[48,128]{1,0:T(8,128)S(1)} %add_add_fusion.7), channel_id=1, source_target_pairs={{4,0},{8,4},{12,8},{0,12},{5,1},{9,5},{13,9},{1,13},{6,2},{10,6},{... | collective-permute-start | bytes 73736 | tf_op jit(solution)/shard_map/ppermute | solution.py:31
  183.5 3.9 %collective-permute-start.20 = (f32[48,128]{1,0:T(8,128)S(1)}, f32[48,128]{1,0:T(8,128)S(1)}, u32[]{:S(2)}, u32[]{:S(2)}) collective-permute-start(f32[48,128]{1,0:T(8,128)S(1)} %add_add_fusion.7), channel_id=1, source_target_pairs={{12,0},{0,4},{4,8},{8,12},{13,1},{1,5},{5,9},{9,13},{14,2},{2,6},{... | collective-permute-start | bytes 73736 | tf_op jit(solution)/shard_map/ppermute | solution.py:31
  184.2 4.2 %collective-permute-start.18 = (f32[48,128]{1,0:T(8,128)S(1)}, f32[48,128]{1,0:T(8,128)S(1)}, u32[]{:S(2)}, u32[]{:S(2)}) collective-permute-start(f32[48,128]{1,0:T(8,128)S(1)} %add_add_fusion.7), channel_id=1, source_target_pairs={{8,0},{12,4},{0,8},{4,12},{9,1},{13,5},{1,9},{5,13},{10,2},{14,6},... | collective-permute-start | bytes 73736 | tf_op jit(solution)/shard_map/ppermute | solution.py:31
  188.5 4.3 %collective-permute-start.21 = (f32[48,128]{1,0:T(8,128)S(1)}, f32[48,128]{1,0:T(8,128)S(1)}, u32[]{:S(2)}, u32[]{:S(2)}) collective-permute-start(f32[48,128]{1,0:T(8,128)S(1)} %add_add_fusion.6), channel_id=1, source_target_pairs={{16,0},{0,16},{17,1},{1,17},{18,2},{2,18},{19,3},{3,19},{20,4},{4,... | collective-permute-start | bytes 73736 | tf_op jit(solution)/shard_map/ppermute | solution.py:31
  190.2 6.6 %collective-permute-start.23 = (bf16[48,4096]{1,0:T(8,128)(2,1)S(1)}, bf16[48,4096]{1,0:T(8,128)(2,1)S(1)}, u32[]{:S(2)}, u32[]{:S(2)}) collective-permute-start(bf16[48,4096]{1,0:T(8,128)(2,1)S(1)} %get-tuple-element.43), channel_id=1, source_target_pairs={{0,32},{32,0},{1,33},{33,1},{2,34},{34,2},{3,35},{35,3},{4,36},{36... | collective-permute-start | bytes 1179656 | tf_op jit(solution)/shard_map/ppermute | solution.py:22
  192.2 10.7 %collective-permute-start.24 = (bf16[48,4096]{1,0:T(8,128)(2,1)S(1)}, bf16[48,4096]{1,0:T(8,128)(2,1)S(1)}, u32[]{:S(2)}, u32[]{:S(2)}) collective-permute-start(bf16[48,4096]{1,0:T(8,128)(2,1)S(1)} %add_convert_fusion), channel_id=1, source_target_pairs={{0,64},{64,0},{1,65},{65,1},{2,66},{66,2},{3,67},{67,3},{4,68},{68... | collective-permute-start | bytes 1179656 | tf_op jit(solution)/shard_map/ppermute | solution.py:26
  193.0 3.9 %collective-permute-start.22 = (f32[10,1024]{1,0:T(8,128)S(1)}, f32[10,1024]{1,0:T(8,128)S(1)}, u32[]{:S(2)}, u32[]{:S(2)}) collective-permute-start(f32[10,1024]{1,0:T(8,128)S(1)} %get-tuple-element.80), channel_id=1, source_target_pairs={{0,32},{32,0},{1,33},{33,1},{2,34},{34,2},{3,35},{35,3},{4,36},{36... | collective-permute-start | bytes 122888 | tf_op jit(solution)/shard_map/ppermute | solution.py:22
  203.9 4.2 %collective-permute-start.25 = (f32[2,10,1024]{2,1,0:T(8,128)S(1)}, f32[2,10,1024]{2,1,0:T(8,128)S(1)}, u32[]{:S(2)}, u32[]{:S(2)}) collective-permute-start(f32[2,10,1024]{2,1,0:T(8,128)S(1)} %pad_maximum_fusion.8), channel_id=1, source_target_pairs={{0,64},{64,0},{1,65},{65,1},{2,66},{66,2},{3,67},{67,3},{4,68},{68... | collective-permute-start | bytes 245768 | tf_op jit(solution)/shard_map/ppermute | solution.py:26
  (20 other events, 103.3 us)

commit v5 on v4

--- a/solution.py
+++ b/solution.py
@@ -48,10 +48,99 @@
     return lax.all_to_all(values, axes, split_axis=0, concat_axis=0, tiled=True)
 
 
-def embed_rows(pooled, gain, bias_rows):
-    normed = pooled * lax.rsqrt(jnp.mean(pooled * pooled, axis=-1, keepdims=True) + 1e-05)
-    mixture = normed * gain + bias_rows
-    return mixture * lax.rsqrt(jnp.sum(mixture * mixture, axis=-1, keepdims=True) + 1e-06)
+def embed_kernel(
+    me, x0, x1, x2, x3, resid, out_bias, gain, bias_row, requests,
+    spread, pooled, inv_rms, inv_norm, held,
+):
+    rows, width = resid.shape
+    quarter = width // 4
+    for i, x_ref in enumerate((x0, x1, x2, x3)):
+        held[i] = x_ref[...]
+    squares = jnp.zeros((rows, LANES), F32)
+    for b in range(width // LANES):
+        here = slice(b * LANES, (b + 1) * LANES)
+        start = b * LANES % quarter
+        projected = held[me[0] ^ (b * LANES // quarter), :, start : start + LANES]
+        value = resid[:, here].astype(F32) + projected.astype(F32) + out_bias[:, here]
+        pooled[:, here] = value
+        squares = squares + value * value
+    mean = jnp.sum(squares, axis=1, keepdims=True) / width
+    rms = jnp.broadcast_to(lax.rsqrt(mean + 1e-05), (rows, LANES))
+    inv_rms[...] = rms
+
+    def mixture(b):
+        here = slice(b * LANES, (b + 1) * LANES)
+        return pooled[:, here] * rms * gain[:, here] + bias_row[:, here]
+
+    squares = jnp.zeros((rows, LANES), F32)
+    for b in range(width // LANES):
+        value = mixture(b)
+        squares = squares + value * value
+    total = jnp.sum(squares, axis=1, keepdims=True)
+    norm = jnp.broadcast_to(lax.rsqrt(total + 1e-06), (rows, LANES))
+    inv_norm[...] = norm
+    wanted = requests[...].astype(F32)
+    for b in range(width // LANES):
+        spread[b] = jnp.concatenate([mixture(b) * norm, wanted]).astype(BF16)
+
+
+def pullback_kernel(
+    me, task, sums, spread, pooled, inv_rms, inv_norm, gain, bias_row,
+    y0, y1, y2, y3, grad, vectors, held,
+):
+    rows, width = pooled.shape
+    half = rows // 2
+    quarter = width // 4
+    rms, norm = inv_rms[...], inv_norm[...]
+
+    def across(values):
+        return jnp.broadcast_to(jnp.sum(values, axis=1, keepdims=True), values.shape)
+
+    def embedded(b):
+        here = slice(b * LANES, (b + 1) * LANES)
+        normed = pooled[:, here] * rms
+        return normed, (normed * gain[:, here] + bias_row[:, here]) * norm
+
+    along = jnp.zeros((rows, LANES), F32)
+    for b in range(width // LANES):
+        own = spread[b].astype(F32)
+        other = jnp.concatenate([own[half:rows], own[:half]])
+        both = jnp.concatenate([sums[b, 0].astype(F32), sums[b, 1].astype(F32)])
+        cotangent = (both - other) / TAU
+        grad[:, b * LANES : (b + 1) * LANES] = cotangent
+        along = along + embedded(b)[1] * cotangent
+    along = across(along)
+    inner = jnp.zeros((rows, LANES), F32)
+    for b in range(width // LANES):
+        here = slice(b * LANES, (b + 1) * LANES)
+        normed, unit = embedded(b)
+        d_mixture = norm * (grad[:, here] - unit * along)
+        vectors[0:1, here] = jnp.sum(d_mixture * normed, axis=0, keepdims=True)
+        vectors[2:3, here] = jnp.sum(d_mixture, axis=0, keepdims=True)
+        d_normed = d_mixture * gain[:, here]
+        grad[:, here] = d_normed
+        inner = inner + d_normed * normed
+    inner = across(inner) / width
+    line = lax.broadcasted_iota(jnp.int32, (8, LANES), 0)
+    for b in range(width // LANES):
+        here = slice(b * LANES, (b + 1) * LANES)
+        d_pooled = rms * (grad[:, here] - pooled[:, here] * rms * inner)
+        three = [
+            vectors[0:1, here],
+            jnp.sum(d_pooled, axis=0, keepdims=True),
+            vectors[2:3, here],
+        ]
+        extra = jnp.full((8, LANES), task[0].astype(F32))
+        for i, value in enumerate(three):
+            high = value.astype(BF16).astype(F32)
+            extra = jnp.where(line == i, high, extra)
+            extra = jnp.where(line == i + 3, value - high, extra)
+        start = b * LANES % quarter
+        held[b * LANES // quarter, :, start : start + LANES] = jnp.concatenate(
+            [LOSS_SCALE * d_pooled, extra]
+        ).astype(BF16)
+    for i, y_ref in enumerate((y0, y1, y2, y3)):
+        y_ref[...] = held[me[0] ^ i]
 
 
 def gather_kernel(hard_count, tok_rows, ids, q_ref, p_ref, neg_ref, hard_ref, wide, picked):
@@ -126,16 +215,18 @@
         y_ref[...] = total[i * rows : (i + 1) * rows, :].astype(BF16)
 
 
-def backward_kernel(x0, x1, x2, x3, w_ref, y0, y1, y2, y3, held, sems):
+def backward_kernel(x0, x1, x2, x3, w_ref, keep_ref, send_ref, held, sems):
     depth = held.shape[1]
-    rows = y0.shape[0]
+    rows = keep_ref.shape[1]
     copies = stream_chunks(w_ref, held, sems)
     x = jnp.concatenate([x_ref[:rows, :] for x_ref in (x0, x1, x2, x3)])
     for c, copy in enumerate(copies):
         copy.wait()
         term = lax.dot_general(x, held[c], (((1,), (1,)), ((), ())), preferred_element_type=F32)
-        for i, y_ref in enumerate((y0, y1, y2, y3)):
-            y_ref[:, c * depth : (c + 1) * depth] = term[i * rows : (i + 1) * rows].astype(BF16)
+        here = slice(c * depth, (c + 1) * depth)
+        for i in range(4):
+            out_ref = send_ref if i % 2 else keep_ref
+            out_ref[i // 2, :, here] = term[i * rows : (i + 1) * rows].astype(BF16)
 
 
 def local(resid, attn, out_proj, out_bias, gain, task_bias, task_ids, neg_owner, neg_row):
@@ -152,6 +243,8 @@
     smem = pl.BlockSpec(memory_space=pltpu.SMEM)
     params = pltpu.CompilerParams(vmem_limit_bytes=24 * 1024 * 1024)
 
+    stream = pltpu.CompilerParams(vmem_limit_bytes=52 * 1024 * 1024)
+
     attn_rows = attn.reshape(row_count, width)
     far_rows = swap_chip(attn_rows)
     near_rows = swap_core(attn_rows)
@@ -162,14 +255,14 @@
         pltpu.VMEM((chunks, out_proj.shape[0] // chunks, out_proj.shape[1]), BF16),
         pltpu.SemaphoreType.DMA((chunks,)),
     ]
-    hbm = pl.BlockSpec(memory_space=pl.ANY)
+    hbm = pl.BlockSpec(memory_space=pltpu.HBM)
     columns = pl.pallas_call(
         forward_kernel,
         out_shape=[jax.ShapeDtypeStruct((row_count, out_proj.shape[1]), BF16)] * 4,
         in_specs=[vmem] * 4 + [hbm],
         out_specs=[vmem] * 4,
         scratch_shapes=[held[0], pltpu.VMEM((4 * row_count, out_proj.shape[1]), F32), held[1]],
-        compiler_params=params,
+        compiler_params=stream,
     )(attn_rows, near_rows, far_rows, swap_core(far_rows), out_proj)
     parts = [
         columns[0],
@@ -182,30 +275,37 @@
         items = [jnp.where(core == 1, items[i ^ 1], items[i]) for i in range(4)]
         return [jnp.where(chip == 1, items[i ^ 2], items[i]) for i in range(4)]
 
-    projected = jnp.concatenate(by_group(parts), axis=1)
-    pooled = resid.reshape(row_count, width).astype(F32) + projected.astype(F32) + out_bias
-    task_onehot = (jnp.arange(task_bias.shape[0]) == task_ids[0]).astype(F32)
-    bias_row = jnp.sum(task_onehot[:, None] * task_bias, axis=0)
-
-    embedded, pullback = jax.vjp(
-        lambda a, b, c: embed_rows(a, b, c[None, :]), pooled, gain, bias_row
-    )
-    emb = embedded.astype(BF16)
-
     half = LANES // 2
     fill = ((0, 1), (0, half - tok_rows))
     requests = jnp.concatenate(
         [jnp.pad(neg_owner.T, fill), jnp.pad(neg_row.T, fill)], axis=1
     ).astype(BF16)
-    spread = emb.reshape(2, tok_rows, blocks, LANES).transpose(2, 0, 1, 3)
-    spread = jnp.concatenate(
-        [
-            spread.reshape(blocks, row_count, LANES),
-            jnp.broadcast_to(requests[None], (blocks,) + requests.shape),
-        ],
-        axis=1,
-    )
-    spread = exchange(spread, BLK)
+    task_onehot = (jnp.arange(task_bias.shape[0]) == task_ids[0]).astype(F32)
+    bias_row = jnp.sum(task_onehot[:, None] * task_bias, axis=0, keepdims=True)
+    place = me.astype(jnp.int32).reshape(1)
+    rows_f32 = jax.ShapeDtypeStruct((row_count, LANES), F32)
+    own_spread, pooled, inv_rms, inv_norm = pl.pallas_call(
+        embed_kernel,
+        out_shape=(
+            jax.ShapeDtypeStruct((blocks, row_count + 8, LANES), BF16),
+            jax.ShapeDtypeStruct((row_count, width), F32),
+            rows_f32,
+            rows_f32,
+        ),
+        in_specs=[smem] + [vmem] * 9,
+        out_specs=(vmem,) * 4,
+        scratch_shapes=[pltpu.VMEM((4, row_count, width // 4), BF16)],
+        compiler_params=params,
+    )(
+        place,
+        *parts,
+        resid.reshape(row_count, width),
+        out_bias[None],
+        gain[None],
+        bias_row,
+        requests,
+    )
+    spread = exchange(own_spread, BLK)
     q_all = spread[:, :tok_rows].reshape(pairs, LANES)
     p_own = spread[:, tok_rows:row_count].reshape(pairs, LANES)
     requests = spread[:, row_count : row_count + hard_count].astype(jnp.int32)
@@ -279,21 +379,21 @@
     sums = jnp.stack(
         [sum_q.reshape(blocks, tok_rows, LANES), sum_p.reshape(blocks, tok_rows, LANES)], axis=1
     ).astype(BF16)
-    sums = exchange(sums, BLK).transpose(1, 2, 0, 3).reshape(2, tok_rows, width).astype(F32)
-    other = jnp.stack([emb[tok_rows:], emb[:tok_rows]]).astype(F32)
-    cotangent = ((sums - other) / TAU).reshape(row_count, width)
-
-    d_pooled, d_gain, d_bias = pullback(cotangent)
-    d_out_bias = jnp.sum(d_pooled, 0)
-    scaled = (LOSS_SCALE * d_pooled).astype(BF16)
-
-
-    vectors = jnp.stack([d_gain, d_out_bias, d_bias])
-    high = vectors.astype(BF16)
-    low = (vectors - high.astype(F32)).astype(BF16)
-    task = jnp.broadcast_to(task_ids.astype(BF16)[:, None], (2, width))
-    cols = jnp.concatenate([scaled, high, low, task])
-    cols = by_group(jnp.split(cols, 4, axis=1))
+    sums = exchange(sums, BLK)
+
+    part_shape = jax.ShapeDtypeStruct((row_count + 8, width // 4), BF16)
+    cols = pl.pallas_call(
+        pullback_kernel,
+        out_shape=[part_shape] * 4,
+        in_specs=[smem] * 2 + [vmem] * 7,
+        out_specs=[vmem] * 4,
+        scratch_shapes=[
+            pltpu.VMEM((row_count, width), F32),
+            pltpu.VMEM((8, width), F32),
+            pltpu.VMEM((4, row_count + 8, width // 4), BF16),
+        ],
+        compiler_params=params,
+    )(place, task_ids, sums, own_spread, pooled, inv_rms, inv_norm, gain[None], bias_row)
     cols = [
         cols[0],
         swap_core(cols[1]),
@@ -305,21 +405,23 @@
     tasks = extra[:, 6, :1].astype(jnp.int32)
     both = (vectors[0, :2] + vectors[1, :2]) + (vectors[2, :2] + vectors[3, :2])
     vectors = jnp.concatenate([both, vectors[:, 2]]).reshape(-1, LANES)
-    back = pl.pallas_call(
+    keep, send = pl.pallas_call(
         backward_kernel,
-        out_shape=[jax.ShapeDtypeStruct((row_count, width), BF16)] * 4,
+        out_shape=[jax.ShapeDtypeStruct((2, row_count, width), BF16)] * 2,
         in_specs=[vmem] * 4 + [hbm],
-        out_specs=[vmem] * 4,
+        out_specs=[vmem] * 2,
         scratch_shapes=held,
-        compiler_params=params,
+        compiler_params=stream,
     )(*cols, out_proj)
-    vectors = sum_over(vectors, "z")
-    vectors, *back = lax.optimization_barrier((vectors, *back))
-    vectors = sum_over(vectors, "y")
-    far_sum = back[2].astype(F32) + swap_core(back[3]).astype(F32)
-    far_sum, vectors = lax.optimization_barrier((far_sum.astype(BF16), vectors))
-    far_sum = swap_chip(far_sum).astype(F32)
-    grad_attn = back[0].astype(F32) + swap_core(back[1]).astype(F32) + far_sum
+    crossed = swap_core(send)
+    far_sum = (keep[1].astype(F32) + crossed[1].astype(F32)).astype(BF16)
+    far_sum, vectors = lax.optimization_barrier((far_sum, vectors))
+    first = swap_chip(far_sum[:, : width // 2])
+    vectors, first = lax.optimization_barrier((sum_over(vectors, "z"), first))
+    second = swap_chip(far_sum[:, width // 2 :])
+    vectors, second = lax.optimization_barrier((sum_over(vectors, "y"), second))
+    far_sum = jnp.concatenate([first, second], axis=1).astype(F32)
+    grad_attn = keep[0].astype(F32) + crossed[0].astype(F32) + far_sum
 
     vectors = sum_over(vectors, "xh")
     vectors = vectors.reshape(6, -1)
@@ -327,10 +429,13 @@
     placed = onehot[:, :, None] * vectors[2:, None, :]
     placed = (placed[0] + placed[1]) + (placed[2] + placed[3])
     placed = jnp.concatenate([vectors[:2], placed])
-    pair = jnp.stack([placed, swap_core(placed)])
-    pair, grad_attn = lax.optimization_barrier((pair, grad_attn))
-    far = swap_chip(pair)
-    whole = jnp.concatenate(by_group([pair[0], pair[1], far[0], far[1]]), axis=1)
+    whole = [
+        placed,
+        swap_core(placed),
+        swap_chip(placed),
+        lax.ppermute(placed, GRP, DIAGONAL),
+    ]
+    whole = jnp.concatenate(by_group(whole), axis=1)
     return (
         losses,
         grad_attn.reshape(2, tok_rows, width),

time: 211 us -> 204 us (0.967)
  blocking collectives: 0 us -> 40.9 us
  starting transfers between devices: 67.7 us -> 51.2 us
  waiting for transfers between devices: 83.9 us -> 69.4 us
  local copies, waits for them, and re-layouts: 14.5 us -> 3.76 us
  other arithmetic: 16.3 us -> 8.4 us
  Pallas kernels: 21 us -> 24.2 us
    all_to_all x0 -> x2, blocking collectives: none -> 40.9 us  [exchange(): return lax.all_to_all(values, axes, split_axis=0, concat_axis=0, tiled=True)]
    all_to_all x5 -> x3, waiting for transfers between devices: 51.9 us -> 33.9 us  [exchange(): return lax.all_to_all(values, axes, split_axis=0, concat_axis=0, tiled=True)]
    all_to_all x5 -> x3, starting transfers between devices: 33 us -> 15.4 us  [exchange(): return lax.all_to_all(values, axes, split_axis=0, concat_axis=0, tiled=True)]
    ppermute x10 -> x9, starting transfers between devices: 19 us -> 10.3 us  [swap_core(): return lax.ppermute(values, 'co', SWAP)]
    unnamed x47 -> x17, local copies, waits for them, and re-layouts: 9.1 us -> 1.03 us
    ppermute x0 -> x1, starting transfers between devices: none -> 6.13 us  [local(): lax.ppermute(placed, GRP, DIAGONAL)]
    ppermute x7 -> x8, starting transfers between devices: 4.85 us -> 9.73 us  [swap_chip(): return lax.ppermute(values, 'xl', SWAP)]
    ppermute x7, waiting for transfers between devices: 3.97 us -> 7.78 us  [from_ahead(): lax.ppermute(values, axis, [((i + step) % size, i) for i in range(size)])]
  transfers between devices with their start and end apart: 31 -> 30, of which waited for: 20 -> 22; matrix products, arithmetic and copies ran while one was open for 5% -> 3% of each run, Pallas kernels for 6% -> 4%
where the time goes in v5:
time: 204 us
  waiting for transfers between devices  69.4 us (34%)
  starting transfers between devices  51.2 us (25%)
  blocking collectives  40.9 us (20%)
  Pallas kernels  24.2 us (12%)
  other arithmetic  8.4 us (4%)
  matrix products  4.11 us (2%)
  local copies, waits for them, and re-layouts  3.76 us (2%)
    all_to_all x2, blocking collectives, exchange(): return lax.all_to_all(values, axes, split_axis=0, concat_axis=0, tiled=True)  40.9 us
    all_to_all x3, waiting for transfers between devices, exchange(): return lax.all_to_all(values, axes, split_axis=0, concat_axis=0, tiled=True)  33.9 us
    ppermute x8, waiting for transfers between devices, swap_chip(): return lax.ppermute(values, 'xl', SWAP)  18.9 us
    all_to_all x3, starting transfers between devices, exchange(): return lax.all_to_all(values, axes, split_axis=0, concat_axis=0, tiled=True)  15.4 us
    ppermute x9, starting transfers between devices, swap_core(): return lax.ppermute(values, 'co', SWAP)  10.3 us
    ppermute x8, starting transfers between devices, swap_chip(): return lax.ppermute(values, 'xl', SWAP)  9.73 us
    ppermute x7, waiting for transfers between devices, from_ahead(): lax.ppermute(values, axis, [((i + step) % size, i) for i in range(size)])  7.78 us
    pallas_call x1, Pallas kernels, local(): pl.pallas_call(lambda *refs: scatter_kernel(hard_count, tok_rows, *refs),...  7.21 us
  transfers between devices with their start and end apart: 30, of which 22 were waited for; matrix products, arithmetic and copies ran while one was open for 3% of the time, Pallas kernels for 4%

profile of v5, /device:TPU:1, one launch (start us, length us, event | category | flops | bytes accessed | tf_op | source)
XLA Modules:
  0.0 203.6 jit_solution(18335911697548056857)
XLA Ops:
  0.6 2.1 %collective-permute-start.1 = (bf16[48,4096]{1,0:T(8,128)(2,1)}, bf16[48,4096]{1,0:T(8,128)(2,1)S(1)}, u32[]{:S(2)}, u32[]{:S(2)}) collective-permute-start(bf16[48,4096]{1,0:T(8,128)(2,1)} %bitcast.74), channel_id=1, source_target_pairs={{0,64},{64,0},{1,65},{65,1},{2,66},{66,2},{3,67},{67,3},{4,68},{68... | collective-permute-start | bytes 1179656 | tf_op jit(solution)/shard_map/ppermute | solution.py:26
  4.4 6.9 %collective-permute-done.1.x2 = bf16[48,4096]{1,0:T(8,128)(2,1)S(1)} collective-permute-done((bf16[48,4096]{1,0:T(8,128)(2,1)}, bf16[48,4096]{1,0:T(8,128)(2,1)S(1)}, u32[]{:S(2)}, u32[]{:S(2)}) %collective-permute-start.1) | collective-permute-done | bytes 393248 | tf_op jit(solution)/shard_map/ppermute | solution.py:26
  11.3 1.7 collective-permute-start.2
  15.8 3.9 %shard_map.128 = (bf16[48,1024]{1,0:T(8,128)(2,1)S(1)}, bf16[48,1024]{1,0:T(8,128)(2,1)S(1)}, bf16[48,1024]{1,0:T(8,128)(2,1)S(1)}, bf16[48,1024]{1,0:T(8,128)(2,1)S(1)}) custom-call(bf16[48,4096]{1,0:T(8,128)(2,1)S(1)} %bitcast.76, bf16[48,4096]{1,0:T(8,128)(2,1)S(1)} %collective-permute-done.x1, bf16[48,4096]{1,0:T(8,128)(2,1)S(1)} %collective-permute-done.1.x2, ...), custom_call_target="tpu_custom_call" | custom-call | tf_op jit(solution)/shard_map/pallas_call | solution.py:259
  22.0 1.8 collective-permute-done.4.x2
  23.8 2.9 %collective-permute-done.5.x3 = bf16[48,1024]{1,0:T(8,128)(2,1)S(1)} collective-permute-done((bf16[48,1024]{1,0:T(8,128)(2,1)S(1)}, bf16[48,1024]{1,0:T(8,128)(2,1)S(1)}, u32[]{:S(2)}, u32[]{:S(2)}) %collective-permute-start.5) | collective-permute-done | bytes 98336 | tf_op jit(solution)/shard_map/ppermute | solution.py:271
  27.2 21.6 %all_to_all.25 = bf16[32,56,128]{2,1,0:T(8,128)(2,1)S(1)} all-to-all(bf16[32,56,128]{2,1,0:T(8,128)(2,1)S(1)} %get-tuple-element.33.spread), channel_id=1, replica_groups=mesh['xl'=2,'co'=2,'xh'=2,'y'=4,'z'=4] {'xh','y','z'}, dimensions={0} | all-to-all | bytes 917504 | tf_op jit(solution)/shard_map/all_to_all | solution.py:48
  49.9 1.6 collective-permute-start.6
  51.8 1.7 collective-permute-done.7
  53.5 3.2 %collective-permute-start.8 = (bf16[768,128]{1,0:T(8,128)(2,1)S(1)}, bf16[768,128]{1,0:T(8,128)(2,1)S(1)}, u32[]{:S(2)}, u32[]{:S(2)}) collective-permute-start(bf16[768,128]{1,0:T(8,128)(2,1)S(1)} %collective-permute-done.7), channel_id=1, source_target_pairs={{0,32},{32,0},{1,33},{33,1},{2,34},{34,2},{3,35},{35,3},{4,36},{36... | collective-permute-start | bytes 589832 | tf_op jit(solution)/shard_map/ppermute | solution.py:22
  57.8 6.2 %shard_map.130 = (bf16[7,768,128]{2,1,0:T(8,128)(2,1)S(1)}, f32[768,128]{1,0:T(8,128)S(1)}) custom-call(s32[5376]{0:T(1024)S(1)} %reshape.120.refs_0_, bf16[768,128]{1,0:T(8,128)(2,1)S(1)} %bitcast.71, bf16[3072,128]{1,0:T(8,128)(2,1)S(1)} %pad_maximum_fusion.1.refs_2_), custom_call_target="tpu_custom_call" | custom-call | tf_op jit(solution)/shard_map/pallas_call | solution.py:321
  65.5 4.7 %all-to-all-start.1 = ((f16[32,24,896]{2,1,0:T(8,128)(2,1)}), f16[32,24,896]{2,1,0:T(8,128)(2,1)}, u32[]{:S(2)}, u32[]{:S(2)}) async-start(f16[32,24,896]{2,1,0:T(8,128)(2,1)} %pad_maximum_fusion), calls=%async_computation.1 | async-start | bytes 2752512 | tf_op jit(solution)/shard_map/all_to_all | solution.py:48
  70.3 20.1 %all-to-all-done.1 = f16[32,24,896]{2,1,0:T(8,128)(2,1)} async-done(((f16[32,24,896]{2,1,0:T(8,128)(2,1)}), f16[32,24,896]{2,1,0:T(8,128)(2,1)}, u32[]{:S(2)}, u32[]{:S(2)}) %all-to-all-start.1) | async-done | bytes 1376288 | tf_op jit(solution)/shard_map/all_to_all | solution.py:48
  93.6 6.0 %all-to-all-start.3 = ((bf16[32,24,128]{2,1,0:T(8,128)(2,1)}), bf16[32,24,128]{2,1,0:T(8,128)(2,1)S(1)}, u32[]{:S(2)}, u32[]{:S(2)}) async-start(bf16[32,24,128]{2,1,0:T(8,128)(2,1)} %broadcast_in_dim.42), calls=%async_computation.3 | async-start | bytes 393216 | tf_op jit(solution)/shard_map/all_to_all | solution.py:48
  99.7 9.1 %all-to-all-done.3 = bf16[32,24,128]{2,1,0:T(8,128)(2,1)S(1)} async-done(((bf16[32,24,128]{2,1,0:T(8,128)(2,1)}), bf16[32,24,128]{2,1,0:T(8,128)(2,1)S(1)}, u32[]{:S(2)}, u32[]{:S(2)}) %all-to-all-start.3) | async-done | bytes 196640 | tf_op jit(solution)/shard_map/all_to_all | solution.py:48
  109.9 4.7 %all-to-all-start.2 = ((bf16[32,24,768]{2,1,0:T(8,128)(2,1)}), bf16[32,24,768]{2,1,0:T(8,128)(2,1)}, u32[]{:S(2)}, u32[]{:S(2)}) async-start(bf16[32,24,768]{2,1,0:T(8,128)(2,1)} %broadcast_in_dim.41), calls=%async_computation.2 | async-start | bytes 2359296 | tf_op jit(solution)/shard_map/all_to_all | solution.py:48
  114.5 7.2 %shard_map.131 = (bf16[3072,128]{1,0:T(8,128)(2,1)S(1)}, f32[768,128]{1,0:T(8,128)S(1)}) custom-call(s32[5376]{0:T(1024)S(1)} %reshape.120.refs_0_, bf16[768,128]{1,0:T(8,128)(2,1)S(1)} %bitcast.73, bf16[768,128]{1,0:T(8,128)(2,1)S(1)} %bitcast.72, bf16[7,768,128]{2,1,0:T(8,128)(2,1)S(1)} %get-tuple-element.35.refs_3_), custom_call_target="tpu_custom_call" | custom-call | tf_op jit(solution)/shard_map/pallas_call | solution.py:359
  121.8 2.2 %collective-permute-start.9 = (bf16[2,768,128]{2,1,0:T(8,128)(2,1)S(1)}, bf16[2,768,128]{2,1,0:T(8,128)(2,1)S(1)}, u32[]{:S(2)}, u32[]{:S(2)}) collective-permute-start(bf16[2,768,128]{2,1,0:T(8,128)(2,1)S(1)} %pad_maximum_fusion.2), channel_id=1, source_target_pairs={{0,32},{32,0},{1,33},{33,1},{2,34},{34,2},{3,35},{35,3},{4,36},{36... | collective-permute-start | bytes 1179656 | tf_op jit(solution)/shard_map/ppermute | solution.py:22
  126.3 4.7 %all-to-all-done.2 = bf16[32,24,768]{2,1,0:T(8,128)(2,1)} async-done(((bf16[32,24,768]{2,1,0:T(8,128)(2,1)}), bf16[32,24,768]{2,1,0:T(8,128)(2,1)}, u32[]{:S(2)}, u32[]{:S(2)}) %all-to-all-start.2) | async-done | bytes 1179680 | tf_op jit(solution)/shard_map/all_to_all | solution.py:48
  131.0 1.7 fusion.2
  132.8 1.9 fusion.1
  134.7 19.2 %all_to_all.26.sums = bf16[32,2,24,128]{3,2,1,0:T(8,128)(2,1)S(1)} all-to-all(bf16[32,2,24,128]{3,2,1,0:T(8,128)(2,1)S(1)} %pad_maximum_fusion.3), channel_id=1, replica_groups=mesh['xl'=2,'co'=2,'xh'=2,'y'=4,'z'=4] {'xh','y','z'}, dimensions={0} | all-to-all | bytes 786432 | tf_op jit(solution)/shard_map/all_to_all | solution.py:48
  154.9 2.4 %collective-permute-start.13 = (bf16[56,1024]{1,0:T(8,128)(2,1)S(1)}, bf16[56,1024]{1,0:T(8,128)(2,1)S(1)}, u32[]{:S(2)}, u32[]{:S(2)}) collective-permute-start(bf16[56,1024]{1,0:T(8,128)(2,1)S(1)} %get-tuple-element.44), channel_id=1, source_target_pairs={{0,96},{32,64},{64,32},{96,0},{1,97},{33,65},{65,33},{97,1},{2,98}... | collective-permute-start | bytes 344072 | tf_op jit(solution)/shard_map/ppermute | solution.py:401
  157.3 1.8 collective-permute-start.12
  159.8 4.0 %collective-permute-done.12.x2 = bf16[56,1024]{1,0:T(8,128)(2,1)S(1)} collective-permute-done((bf16[56,1024]{1,0:T(8,128)(2,1)S(1)}, bf16[56,1024]{1,0:T(8,128)(2,1)S(1)}, u32[]{:S(2)}, u32[]{:S(2)}) %collective-permute-start.12) | collective-permute-done | bytes 114720 | tf_op jit(solution)/shard_map/ppermute | solution.py:26
  163.8 5.3 %shard_map.133 = (bf16[2,48,4096]{2,1,0:T(8,128)(2,1)S(1)}, bf16[2,48,4096]{2,1,0:T(8,128)(2,1)S(1)}) custom-call(bf16[56,1024]{1,0:T(8,128)(2,1)S(1)} %get-tuple-element.41.x0, bf16[56,1024]{1,0:T(8,128)(2,1)S(1)} %collective-permute-done.11.x1, bf16[56,1024]{1,0:T(8,128)(2,1)S(1)} %collective-permute-done.12.x2, ...), custom_call_target="tpu_custom_call" | custom-call | tf_op jit(solution)/shard_map/pallas_call | solution.py:408
  169.4 2.1 %collective-permute-done.14 = bf16[2,48,4096]{2,1,0:T(8,128)(2,1)S(1)} collective-permute-done((bf16[2,48,4096]{2,1,0:T(8,128)(2,1)S(1)}, bf16[2,48,4096]{2,1,0:T(8,128)(2,1)S(1)}, u32[]{:S(2)}, u32[]{:S(2)}) %collective-permute-start.14) | collective-permute-done | bytes 786464 | tf_op jit(solution)/shard_map/ppermute | solution.py:22
  176.0 2.1 %collective-permute-done.17 = f32[48,128]{1,0:T(8,128)S(1)} collective-permute-done((f32[48,128]{1,0:T(8,128)S(1)}, f32[48,128]{1,0:T(8,128)S(1)}, u32[]{:S(2)}, u32[]{:S(2)}) %collective-permute-start.17) | collective-permute-done | bytes 24608 | tf_op jit(solution)/shard_map/ppermute | solution.py:31
  178.1 1.9 collective-permute-done.18
  184.2 2.2 %collective-permute-done.21 = f32[48,128]{1,0:T(8,128)S(1)} collective-permute-done((f32[48,128]{1,0:T(8,128)S(1)}, f32[48,128]{1,0:T(8,128)S(1)}, u32[]{:S(2)}, u32[]{:S(2)}) %collective-permute-start.21) | collective-permute-done | bytes 24608 | tf_op jit(solution)/shard_map/ppermute | solution.py:31
  188.7 3.1 %collective-permute-done.23 = f32[48,128]{1,0:T(8,128)S(1)} collective-permute-done((f32[48,128]{1,0:T(8,128)S(1)}, f32[48,128]{1,0:T(8,128)S(1)}, u32[]{:S(2)}, u32[]{:S(2)}) %collective-permute-start.23) | collective-permute-done | bytes 24608 | tf_op jit(solution)/shard_map/ppermute | solution.py:31
  192.0 6.1 %collective-permute-start.24 = (f32[10,1024]{1,0:T(8,128)S(1)}, f32[10,1024]{1,0:T(8,128)S(1)}, u32[]{:S(2)}, u32[]{:S(2)}) collective-permute-start(f32[10,1024]{1,0:T(8,128)S(1)} %pad_maximum_fusion.6), channel_id=1, source_target_pairs={{0,96},{32,64},{64,32},{96,0},{1,97},{33,65},{65,33},{97,1},{2,98}... | collective-permute-start | bytes 122888 | tf_op jit(solution)/shard_map/ppermute | solution.py:436
  (112 shorter events, 35.5 us)
Async XLA Ops:
  0.6 10.7 %collective-permute-start.1 = (bf16[48,4096]{1,0:T(8,128)(2,1)}, bf16[48,4096]{1,0:T(8,128)(2,1)S(1)}, u32[]{:S(2)}, u32[]{:S(2)}) collective-permute-start(bf16[48,4096]{1,0:T(8,128)(2,1)} %bitcast.74), channel_id=1, source_target_pairs={{0,64},{64,0},{1,65},{65,1},{2,66},{66,2},{3,67},{67,3},{4,68},{68... | collective-permute-start | bytes 1179656 | tf_op jit(solution)/shard_map/ppermute | solution.py:26
  2.8 12.0 %collective-permute-start = (bf16[48,4096]{1,0:T(8,128)(2,1)}, bf16[48,4096]{1,0:T(8,128)(2,1)S(1)}, u32[]{:S(2)}, u32[]{:S(2)}) collective-permute-start(bf16[48,4096]{1,0:T(8,128)(2,1)} %bitcast.75), channel_id=1, source_target_pairs={{0,32},{32,0},{1,33},{33,1},{2,34},{34,2},{3,35},{35,3},{4,36},{36... | collective-permute-start | bytes 1179656 | tf_op jit(solution)/shard_map/ppermute | solution.py:22
  11.3 3.5 %collective-permute-start.2 = (bf16[48,4096]{1,0:T(8,128)(2,1)S(1)}, bf16[48,4096]{1,0:T(8,128)(2,1)S(1)}, u32[]{:S(2)}, u32[]{:S(2)}) collective-permute-start(bf16[48,4096]{1,0:T(8,128)(2,1)S(1)} %collective-permute-done.1.x2), channel_id=1, source_target_pairs={{0,32},{32,0},{1,33},{33,1},{2,34},{34,2},{3,35},{35,3},{4,36},{36... | collective-permute-start | bytes 1179656 | tf_op jit(solution)/shard_map/ppermute | solution.py:22
  15.8 11.0 %copy-start.3 = (f32[4096]{0:T(1024)S(1)}, f32[4096]{0:T(1024)}, u32[]{:S(2)}) copy-start(f32[4096]{0:T(1024)} %param.13) | copy-start | bytes 49156
  15.8 11.0 %copy-start.4 = (f32[4096]{0:T(1024)S(1)}, f32[4096]{0:T(1024)}, u32[]{:S(2)}) copy-start(f32[4096]{0:T(1024)} %param.12) | copy-start | bytes 49156
  19.7 2.3 %collective-permute-start.3 = (bf16[48,1024]{1,0:T(8,128)(2,1)S(1)}, bf16[48,1024]{1,0:T(8,128)(2,1)S(1)}, u32[]{:S(2)}, u32[]{:S(2)}) collective-permute-start(bf16[48,1024]{1,0:T(8,128)(2,1)S(1)} %get-tuple-element.30), channel_id=1, source_target_pairs={{0,32},{32,0},{1,33},{33,1},{2,34},{34,2},{3,35},{35,3},{4,36},{36... | collective-permute-start | bytes 294920 | tf_op jit(solution)/shard_map/ppermute | solution.py:22
  19.8 4.0 %collective-permute-start.4 = (bf16[48,1024]{1,0:T(8,128)(2,1)S(1)}, bf16[48,1024]{1,0:T(8,128)(2,1)S(1)}, u32[]{:S(2)}, u32[]{:S(2)}) collective-permute-start(bf16[48,1024]{1,0:T(8,128)(2,1)S(1)} %get-tuple-element.31), channel_id=1, source_target_pairs={{0,64},{64,0},{1,65},{65,1},{2,66},{66,2},{3,67},{67,3},{4,68},{68... | collective-permute-start | bytes 294920 | tf_op jit(solution)/shard_map/ppermute | solution.py:26
  21.3 5.4 %collective-permute-start.5 = (bf16[48,1024]{1,0:T(8,128)(2,1)S(1)}, bf16[48,1024]{1,0:T(8,128)(2,1)S(1)}, u32[]{:S(2)}, u32[]{:S(2)}) collective-permute-start(bf16[48,1024]{1,0:T(8,128)(2,1)S(1)} %get-tuple-element.32), channel_id=1, source_target_pairs={{0,96},{32,64},{64,32},{96,0},{1,97},{33,65},{65,33},{97,1},{2,98}... | collective-permute-start | bytes 294920 | tf_op jit(solution)/shard_map/ppermute | solution.py:271
  48.9 4.6 %collective-permute-start.7 = (bf16[768,128]{1,0:T(8,128)(2,1)S(1)}, bf16[768,128]{1,0:T(8,128)(2,1)S(1)}, u32[]{:S(2)}, u32[]{:S(2)}) collective-permute-start(bf16[768,128]{1,0:T(8,128)(2,1)S(1)} %bitcast.84), channel_id=1, source_target_pairs={{0,64},{64,0},{1,65},{65,1},{2,66},{66,2},{3,67},{67,3},{4,68},{68... | collective-permute-start | bytes 589832 | tf_op jit(solution)/shard_map/ppermute | solution.py:26
  49.9 7.3 %collective-permute-start.6 = (bf16[768,128]{1,0:T(8,128)(2,1)S(1)}, bf16[768,128]{1,0:T(8,128)(2,1)S(1)}, u32[]{:S(2)}, u32[]{:S(2)}) collective-permute-start(bf16[768,128]{1,0:T(8,128)(2,1)S(1)} %bitcast.85), channel_id=1, source_target_pairs={{0,32},{32,0},{1,33},{33,1},{2,34},{34,2},{3,35},{35,3},{4,36},{36... | collective-permute-start | bytes 589832 | tf_op jit(solution)/shard_map/ppermute | solution.py:22
  53.5 4.3 %collective-permute-start.8 = (bf16[768,128]{1,0:T(8,128)(2,1)S(1)}, bf16[768,128]{1,0:T(8,128)(2,1)S(1)}, u32[]{:S(2)}, u32[]{:S(2)}) collective-permute-start(bf16[768,128]{1,0:T(8,128)(2,1)S(1)} %collective-permute-done.7), channel_id=1, source_target_pairs={{0,32},{32,0},{1,33},{33,1},{2,34},{34,2},{3,35},{35,3},{4,36},{36... | collective-permute-start | bytes 589832 | tf_op jit(solution)/shard_map/ppermute | solution.py:22
  65.5 24.9 %all-to-all-start.1 = ((f16[32,24,896]{2,1,0:T(8,128)(2,1)}), f16[32,24,896]{2,1,0:T(8,128)(2,1)}, u32[]{:S(2)}, u32[]{:S(2)}) async-start(f16[32,24,896]{2,1,0:T(8,128)(2,1)} %pad_maximum_fusion), calls=%async_computation.1 | async-start | bytes 2752512 | tf_op jit(solution)/shard_map/all_to_all | solution.py:48
  93.6 15.2 %all-to-all-start.3 = ((bf16[32,24,128]{2,1,0:T(8,128)(2,1)}), bf16[32,24,128]{2,1,0:T(8,128)(2,1)S(1)}, u32[]{:S(2)}, u32[]{:S(2)}) async-start(bf16[32,24,128]{2,1,0:T(8,128)(2,1)} %broadcast_in_dim.42), calls=%async_computation.3 | async-start | bytes 393216 | tf_op jit(solution)/shard_map/all_to_all | solution.py:48
  109.9 21.2 %all-to-all-start.2 = ((bf16[32,24,768]{2,1,0:T(8,128)(2,1)}), bf16[32,24,768]{2,1,0:T(8,128)(2,1)}, u32[]{:S(2)}, u32[]{:S(2)}) async-start(bf16[32,24,768]{2,1,0:T(8,128)(2,1)} %broadcast_in_dim.41), calls=%async_computation.2 | async-start | bytes 2359296 | tf_op jit(solution)/shard_map/all_to_all | solution.py:48
  121.8 3.6 %collective-permute-start.9 = (bf16[2,768,128]{2,1,0:T(8,128)(2,1)S(1)}, bf16[2,768,128]{2,1,0:T(8,128)(2,1)S(1)}, u32[]{:S(2)}, u32[]{:S(2)}) collective-permute-start(bf16[2,768,128]{2,1,0:T(8,128)(2,1)S(1)} %pad_maximum_fusion.2), channel_id=1, source_target_pairs={{0,32},{32,0},{1,33},{33,1},{2,34},{34,2},{3,35},{35,3},{4,36},{36... | collective-permute-start | bytes 1179656 | tf_op jit(solution)/shard_map/ppermute | solution.py:22
  125.5 7.2 %collective-permute-start.10 = (bf16[768,128]{1,0:T(8,128)(2,1)S(1)}, bf16[768,128]{1,0:T(8,128)(2,1)S(1)}, u32[]{:S(2)}, u32[]{:S(2)}) collective-permute-start(bf16[768,128]{1,0:T(8,128)(2,1)S(1)} %fusion.5), channel_id=1, source_target_pairs={{0,64},{64,0},{1,65},{65,1},{2,66},{66,2},{3,67},{67,3},{4,68},{68... | collective-permute-start | bytes 589832 | tf_op jit(solution)/shard_map/ppermute | solution.py:26
  154.9 4.9 %collective-permute-start.13 = (bf16[56,1024]{1,0:T(8,128)(2,1)S(1)}, bf16[56,1024]{1,0:T(8,128)(2,1)S(1)}, u32[]{:S(2)}, u32[]{:S(2)}) collective-permute-start(bf16[56,1024]{1,0:T(8,128)(2,1)S(1)} %get-tuple-element.44), channel_id=1, source_target_pairs={{0,96},{32,64},{64,32},{96,0},{1,97},{33,65},{65,33},{97,1},{2,98}... | collective-permute-start | bytes 344072 | tf_op jit(solution)/shard_map/ppermute | solution.py:401
  157.3 6.4 %collective-permute-start.12 = (bf16[56,1024]{1,0:T(8,128)(2,1)S(1)}, bf16[56,1024]{1,0:T(8,128)(2,1)S(1)}, u32[]{:S(2)}, u32[]{:S(2)}) collective-permute-start(bf16[56,1024]{1,0:T(8,128)(2,1)S(1)} %get-tuple-element.43), channel_id=1, source_target_pairs={{0,64},{64,0},{1,65},{65,1},{2,66},{66,2},{3,67},{67,3},{4,68},{68... | collective-permute-start | bytes 344072 | tf_op jit(solution)/shard_map/ppermute | solution.py:26
  159.1 4.6 %collective-permute-start.11 = (bf16[56,1024]{1,0:T(8,128)(2,1)S(1)}, bf16[56,1024]{1,0:T(8,128)(2,1)S(1)}, u32[]{:S(2)}, u32[]{:S(2)}) collective-permute-start(bf16[56,1024]{1,0:T(8,128)(2,1)S(1)} %get-tuple-element.42), channel_id=1, source_target_pairs={{0,32},{32,0},{1,33},{33,1},{2,34},{34,2},{3,35},{35,3},{4,36},{36... | collective-permute-start | bytes 344072 | tf_op jit(solution)/shard_map/ppermute | solution.py:22
  169.1 2.4 %collective-permute-start.14 = (bf16[2,48,4096]{2,1,0:T(8,128)(2,1)S(1)}, bf16[2,48,4096]{2,1,0:T(8,128)(2,1)S(1)}, u32[]{:S(2)}, u32[]{:S(2)}) collective-permute-start(bf16[2,48,4096]{2,1,0:T(8,128)(2,1)S(1)} %get-tuple-element.46), channel_id=1, source_target_pairs={{0,32},{32,0},{1,33},{33,1},{2,34},{34,2},{3,35},{35,3},{4,36},{36... | collective-permute-start | bytes 2359304 | tf_op jit(solution)/shard_map/ppermute | solution.py:22
  171.7 4.3 %collective-permute-start.15 = (f32[48,128]{1,0:T(8,128)S(1)}, f32[48,128]{1,0:T(8,128)S(1)}, u32[]{:S(2)}, u32[]{:S(2)}) collective-permute-start(f32[48,128]{1,0:T(8,128)S(1)} %reshape.124), channel_id=1, source_target_pairs={{2,0},{3,1},{0,2},{1,3},{6,4},{7,5},{4,6},{5,7},{10,8},{11,9},{8,1... | collective-permute-start | bytes 73736 | tf_op jit(solution)/shard_map/ppermute | solution.py:31
  173.1 3.0 %collective-permute-start.16 = (f32[48,128]{1,0:T(8,128)S(1)}, f32[48,128]{1,0:T(8,128)S(1)}, u32[]{:S(2)}, u32[]{:S(2)}) collective-permute-start(f32[48,128]{1,0:T(8,128)S(1)} %reshape.124), channel_id=1, source_target_pairs={{1,0},{2,1},{3,2},{0,3},{5,4},{6,5},{7,6},{4,7},{9,8},{10,9},{11,1... | collective-permute-start | bytes 73736 | tf_op jit(solution)/shard_map/ppermute | solution.py:31
  174.2 3.9 %collective-permute-start.17 = (f32[48,128]{1,0:T(8,128)S(1)}, f32[48,128]{1,0:T(8,128)S(1)}, u32[]{:S(2)}, u32[]{:S(2)}) collective-permute-start(f32[48,128]{1,0:T(8,128)S(1)} %reshape.124), channel_id=1, source_target_pairs={{3,0},{0,1},{1,2},{2,3},{7,4},{4,5},{5,6},{6,7},{11,8},{8,9},{9,10... | collective-permute-start | bytes 73736 | tf_op jit(solution)/shard_map/ppermute | solution.py:31
  174.5 5.5 %collective-permute-start.18 = (bf16[48,2048]{1,0:T(8,128)(2,1)S(1)}, bf16[48,2048]{1,0:T(8,128)(2,1)S(1)}, u32[]{:S(2)}, u32[]{:S(2)}) collective-permute-start(bf16[48,2048]{1,0:T(8,128)(2,1)S(1)} %get-tuple-element.64), channel_id=1, source_target_pairs={{0,64},{64,0},{1,65},{65,1},{2,66},{66,2},{3,67},{67,3},{4,68},{68... | collective-permute-start | bytes 589832 | tf_op jit(solution)/shard_map/ppermute | solution.py:26
  180.0 4.2 %collective-permute-start.19 = (f32[48,128]{1,0:T(8,128)S(1)}, f32[48,128]{1,0:T(8,128)S(1)}, u32[]{:S(2)}, u32[]{:S(2)}) collective-permute-start(f32[48,128]{1,0:T(8,128)S(1)} %add_add_fusion.1), channel_id=1, source_target_pairs={{8,0},{12,4},{0,8},{4,12},{9,1},{13,5},{1,9},{5,13},{10,2},{14,6},... | collective-permute-start | bytes 73736 | tf_op jit(solution)/shard_map/ppermute | solution.py:31
  181.3 2.9 %collective-permute-start.20 = (f32[48,128]{1,0:T(8,128)S(1)}, f32[48,128]{1,0:T(8,128)S(1)}, u32[]{:S(2)}, u32[]{:S(2)}) collective-permute-start(f32[48,128]{1,0:T(8,128)S(1)} %add_add_fusion.1), channel_id=1, source_target_pairs={{4,0},{8,4},{12,8},{0,12},{5,1},{9,5},{13,9},{1,13},{6,2},{10,6},{... | collective-permute-start | bytes 73736 | tf_op jit(solution)/shard_map/ppermute | solution.py:31
  182.3 4.2 %collective-permute-start.21 = (f32[48,128]{1,0:T(8,128)S(1)}, f32[48,128]{1,0:T(8,128)S(1)}, u32[]{:S(2)}, u32[]{:S(2)}) collective-permute-start(f32[48,128]{1,0:T(8,128)S(1)} %add_add_fusion.1), channel_id=1, source_target_pairs={{12,0},{0,4},{4,8},{8,12},{13,1},{1,5},{5,9},{9,13},{14,2},{2,6},{... | collective-permute-start | bytes 73736 | tf_op jit(solution)/shard_map/ppermute | solution.py:31
  183.0 4.6 %collective-permute-start.22 = (bf16[48,2048]{1,0:T(8,128)(2,1)S(1)}, bf16[48,2048]{1,0:T(8,128)(2,1)S(1)}, u32[]{:S(2)}, u32[]{:S(2)}) collective-permute-start(bf16[48,2048]{1,0:T(8,128)(2,1)S(1)} %get-tuple-element.63), channel_id=1, source_target_pairs={{0,64},{64,0},{1,65},{65,1},{2,66},{66,2},{3,67},{67,3},{4,68},{68... | collective-permute-start | bytes 589832 | tf_op jit(solution)/shard_map/ppermute | solution.py:26
  187.6 4.2 %collective-permute-start.23 = (f32[48,128]{1,0:T(8,128)S(1)}, f32[48,128]{1,0:T(8,128)S(1)}, u32[]{:S(2)}, u32[]{:S(2)}) collective-permute-start(f32[48,128]{1,0:T(8,128)S(1)} %add_add_fusion), channel_id=1, source_target_pairs={{16,0},{0,16},{17,1},{1,17},{18,2},{2,18},{19,3},{3,19},{20,4},{4,... | collective-permute-start | bytes 73736 | tf_op jit(solution)/shard_map/ppermute | solution.py:31
  192.0 8.8 %collective-permute-start.24 = (f32[10,1024]{1,0:T(8,128)S(1)}, f32[10,1024]{1,0:T(8,128)S(1)}, u32[]{:S(2)}, u32[]{:S(2)}) collective-permute-start(f32[10,1024]{1,0:T(8,128)S(1)} %pad_maximum_fusion.6), channel_id=1, source_target_pairs={{0,96},{32,64},{64,32},{96,0},{1,97},{33,65},{65,33},{97,1},{2,98}... | collective-permute-start | bytes 122888 | tf_op jit(solution)/shard_map/ppermute | solution.py:436
  198.1 4.1 %collective-permute-start.25 = (f32[10,1024]{1,0:T(8,128)S(1)}, f32[10,1024]{1,0:T(8,128)S(1)}, u32[]{:S(2)}, u32[]{:S(2)}) collective-permute-start(f32[10,1024]{1,0:T(8,128)S(1)} %pad_maximum_fusion.6), channel_id=1, source_target_pairs={{0,64},{64,0},{1,65},{65,1},{2,66},{66,2},{3,67},{67,3},{4,68},{68... | collective-permute-start | bytes 122888 | tf_op jit(solution)/shard_map/ppermute | solution.py:26
  198.3 3.9 %collective-permute-start.26 = (f32[10,1024]{1,0:T(8,128)S(1)}, f32[10,1024]{1,0:T(8,128)S(1)}, u32[]{:S(2)}, u32[]{:S(2)}) collective-permute-start(f32[10,1024]{1,0:T(8,128)S(1)} %pad_maximum_fusion.6), channel_id=1, source_target_pairs={{0,32},{32,0},{1,33},{33,1},{2,34},{34,2},{3,35},{35,3},{4,36},{36... | collective-permute-start | bytes 122888 | tf_op jit(solution)/shard_map/ppermute | solution.py:22
  (6 other events, 42.2 us)

commit v6 on v5

--- a/solution.py
+++ b/solution.py
@@ -36,12 +36,6 @@
         return values + from_ahead(values, axis, 1)
     one, two, three = [from_ahead(values, axis, step) for step in (1, 2, 3)]
     return (values + two) + (one + three)
-
-
-def gather_ahead(values, axis):
-    return jnp.stack(
-        [values] + [from_ahead(values, axis, step) for step in range(1, lax.axis_size(axis))]
-    )
 
 
 def exchange(values, axes):
@@ -86,11 +80,12 @@
 
 def pullback_kernel(
     me, task, sums, spread, pooled, inv_rms, inv_norm, gain, bias_row,
-    y0, y1, y2, y3, grad, vectors, held,
+    y0, y1, y2, y3, vectors, grad, held,
 ):
     rows, width = pooled.shape
     half = rows // 2
     quarter = width // 4
+    lines = width // LANES
     rms, norm = inv_rms[...], inv_norm[...]
 
     def across(values):
@@ -115,30 +110,19 @@
         here = slice(b * LANES, (b + 1) * LANES)
         normed, unit = embedded(b)
         d_mixture = norm * (grad[:, here] - unit * along)
-        vectors[0:1, here] = jnp.sum(d_mixture * normed, axis=0, keepdims=True)
-        vectors[2:3, here] = jnp.sum(d_mixture, axis=0, keepdims=True)
+        vectors[b : b + 1, :] = jnp.sum(d_mixture * normed, axis=0, keepdims=True)
+        vectors[2 * lines + b : 2 * lines + b + 1, :] = jnp.sum(d_mixture, axis=0, keepdims=True)
         d_normed = d_mixture * gain[:, here]
         grad[:, here] = d_normed
         inner = inner + d_normed * normed
     inner = across(inner) / width
-    line = lax.broadcasted_iota(jnp.int32, (8, LANES), 0)
-    for b in range(width // LANES):
+    for b in range(lines):
         here = slice(b * LANES, (b + 1) * LANES)
         d_pooled = rms * (grad[:, here] - pooled[:, here] * rms * inner)
-        three = [
-            vectors[0:1, here],
-            jnp.sum(d_pooled, axis=0, keepdims=True),
-            vectors[2:3, here],
-        ]
-        extra = jnp.full((8, LANES), task[0].astype(F32))
-        for i, value in enumerate(three):
-            high = value.astype(BF16).astype(F32)
-            extra = jnp.where(line == i, high, extra)
-            extra = jnp.where(line == i + 3, value - high, extra)
+        vectors[lines + b : lines + b + 1, :] = jnp.sum(d_pooled, axis=0, keepdims=True)
         start = b * LANES % quarter
-        held[b * LANES // quarter, :, start : start + LANES] = jnp.concatenate(
-            [LOSS_SCALE * d_pooled, extra]
-        ).astype(BF16)
+        held[b * LANES // quarter, :, start : start + LANES] = (LOSS_SCALE * d_pooled).astype(BF16)
+    vectors[3 * lines :, :] = jnp.full((8, LANES), task[0].astype(F32))
     for i, y_ref in enumerate((y0, y1, y2, y3)):
         y_ref[...] = held[me[0] ^ i]
 
@@ -219,7 +203,7 @@
     depth = held.shape[1]
     rows = keep_ref.shape[1]
     copies = stream_chunks(w_ref, held, sems)
-    x = jnp.concatenate([x_ref[:rows, :] for x_ref in (x0, x1, x2, x3)])
+    x = jnp.concatenate([x_ref[...] for x_ref in (x0, x1, x2, x3)])
     for c, copy in enumerate(copies):
         copy.wait()
         term = lax.dot_general(x, held[c], (((1,), (1,)), ((), ())), preferred_element_type=F32)
@@ -227,6 +211,26 @@
         for i in range(4):
             out_ref = send_ref if i % 2 else keep_ref
             out_ref[i // 2, :, here] = term[i * rows : (i + 1) * rows].astype(BF16)
+
+
+def finish_kernel(blocks, v0, v1, v2, v3, gain_ref, bias_ref, task_ref):
+    lines = gain_ref.shape[0]
+    four = (v0, v1, v2, v3)
+
+    def total(start):
+        parts = [v[start : start + lines, :] for v in four]
+        return (parts[0] + parts[1]) + (parts[2] + parts[3])
+
+    gain_ref[...] = total(0)
+    bias_ref[...] = total(lines)
+    row = lax.broadcasted_iota(jnp.int32, (8, LANES), 0).astype(F32)
+    chosen = [
+        jnp.where(jnp.abs(v[3 * lines :, :] / blocks - row) < 0.5, 1.0, 0.0) for v in four
+    ]
+    for b in range(lines):
+        here = slice(2 * lines + b, 2 * lines + b + 1)
+        parts = [mask * v[here, :] for mask, v in zip(chosen, four)]
+        task_ref[:, b * LANES : (b + 1) * LANES] = (parts[0] + parts[1]) + (parts[2] + parts[3])
 
 
 def local(resid, attn, out_proj, out_bias, gain, task_bias, task_ids, neg_owner, neg_row):
@@ -237,8 +241,6 @@
     blocks = lax.axis_size(BLK)
     pairs = blocks * tok_rows
     me = lax.axis_index(GRP)
-    core = lax.axis_index("co")
-    chip = lax.axis_index("xl")
     vmem = pl.BlockSpec(memory_space=pltpu.VMEM)
     smem = pl.BlockSpec(memory_space=pltpu.SMEM)
     params = pltpu.CompilerParams(vmem_limit_bytes=24 * 1024 * 1024)
@@ -270,10 +272,6 @@
         swap_chip(columns[2]),
         lax.ppermute(columns[3], GRP, DIAGONAL),
     ]
-
-    def by_group(items):
-        items = [jnp.where(core == 1, items[i ^ 1], items[i]) for i in range(4)]
-        return [jnp.where(chip == 1, items[i ^ 2], items[i]) for i in range(4)]
 
     half = LANES // 2
     fill = ((0, 1), (0, half - tok_rows))
@@ -381,16 +379,16 @@
     ).astype(BF16)
     sums = exchange(sums, BLK)
 
-    part_shape = jax.ShapeDtypeStruct((row_count + 8, width // 4), BF16)
-    cols = pl.pallas_call(
+    lines = width // LANES
+    *cols, vectors = pl.pallas_call(
         pullback_kernel,
-        out_shape=[part_shape] * 4,
+        out_shape=[jax.ShapeDtypeStruct((row_count, width // 4), BF16)] * 4
+        + [jax.ShapeDtypeStruct((3 * lines + 8, LANES), F32)],
         in_specs=[smem] * 2 + [vmem] * 7,
-        out_specs=[vmem] * 4,
+        out_specs=[vmem] * 5,
         scratch_shapes=[
             pltpu.VMEM((row_count, width), F32),
-            pltpu.VMEM((8, width), F32),
-            pltpu.VMEM((4, row_count + 8, width // 4), BF16),
+            pltpu.VMEM((4, row_count, width // 4), BF16),
         ],
         compiler_params=params,
     )(place, task_ids, sums, own_spread, pooled, inv_rms, inv_norm, gain[None], bias_row)
@@ -400,11 +398,7 @@
         swap_chip(cols[2]),
         lax.ppermute(cols[3], GRP, DIAGONAL),
     ]
-    extra = jnp.stack([part[row_count:] for part in cols])
-    vectors = extra[:, :3].astype(F32) + extra[:, 3:6].astype(F32)
-    tasks = extra[:, 6, :1].astype(jnp.int32)
-    both = (vectors[0, :2] + vectors[1, :2]) + (vectors[2, :2] + vectors[3, :2])
-    vectors = jnp.concatenate([both, vectors[:, 2]]).reshape(-1, LANES)
+    vectors, *cols = lax.optimization_barrier((sum_over(vectors, "z"), *cols))
     keep, send = pl.pallas_call(
         backward_kernel,
         out_shape=[jax.ShapeDtypeStruct((2, row_count, width), BF16)] * 2,
@@ -413,35 +407,36 @@
         scratch_shapes=held,
         compiler_params=stream,
     )(*cols, out_proj)
+    vectors, keep, send = lax.optimization_barrier((vectors, keep, send))
+    vectors = sum_over(sum_over(vectors, "y"), "xh")
     crossed = swap_core(send)
     far_sum = (keep[1].astype(F32) + crossed[1].astype(F32)).astype(BF16)
-    far_sum, vectors = lax.optimization_barrier((far_sum, vectors))
     first = swap_chip(far_sum[:, : width // 2])
-    vectors, first = lax.optimization_barrier((sum_over(vectors, "z"), first))
     second = swap_chip(far_sum[:, width // 2 :])
-    vectors, second = lax.optimization_barrier((sum_over(vectors, "y"), second))
+    vectors, first = lax.optimization_barrier((vectors, first))
     far_sum = jnp.concatenate([first, second], axis=1).astype(F32)
     grad_attn = keep[0].astype(F32) + crossed[0].astype(F32) + far_sum
 
-    vectors = sum_over(vectors, "xh")
-    vectors = vectors.reshape(6, -1)
-    onehot = (tasks == jnp.arange(task_bias.shape[0])[None, :]).astype(F32)
-    placed = onehot[:, :, None] * vectors[2:, None, :]
-    placed = (placed[0] + placed[1]) + (placed[2] + placed[3])
-    placed = jnp.concatenate([vectors[:2], placed])
-    whole = [
-        placed,
-        swap_core(placed),
-        swap_chip(placed),
-        lax.ppermute(placed, GRP, DIAGONAL),
-    ]
-    whole = jnp.concatenate(by_group(whole), axis=1)
+    four = [
+        vectors,
+        swap_core(vectors),
+        swap_chip(vectors),
+        lax.ppermute(vectors, GRP, DIAGONAL),
+    ]
+    grad_gain, grad_out_bias, grad_task_bias = pl.pallas_call(
+        lambda *refs: finish_kernel(blocks, *refs),
+        out_shape=[jax.ShapeDtypeStruct((lines, LANES), F32)] * 2
+        + [jax.ShapeDtypeStruct(task_bias.shape, F32)],
+        in_specs=[vmem] * 4,
+        out_specs=[vmem] * 3,
+        compiler_params=params,
+    )(*four)
     return (
         losses,
         grad_attn.reshape(2, tok_rows, width),
-        whole[0],
-        whole[2:],
-        whole[1],
+        grad_gain.reshape(width),
+        grad_task_bias,
+        grad_out_bias.reshape(width),
     )
 
 

time: 204 us -> 195 us (0.956)
  waiting for transfers between devices: 69.4 us -> 64.6 us
  starting transfers between devices: 51.2 us -> 48.3 us
    ppermute x9, starting transfers between devices: 10.3 us -> 15.5 us  [swap_core(): return lax.ppermute(values, 'co', SWAP)]
    ppermute x8, waiting for transfers between devices: 18.9 us -> 14 us  [swap_chip(): return lax.ppermute(values, 'xl', SWAP)]
    ppermute x1, starting transfers between devices: 6.13 us -> 1.43 us  [local(): lax.ppermute(vectors, GRP, DIAGONAL)]
    ppermute x8, starting transfers between devices: 9.73 us -> 7.26 us  [swap_chip(): return lax.ppermute(values, 'xl', SWAP)]
    ppermute x9, waiting for transfers between devices: 3.96 us -> 1.9 us  [swap_core(): return lax.ppermute(values, 'co', SWAP)]
  transfers between devices with their start and end apart: 30 -> 30, of which waited for: 22 -> 16; matrix products, arithmetic and copies ran while one was open for 3% -> 3% of each run, Pallas kernels for 4% -> 4%
where the time goes in v6:
time: 195 us
  waiting for transfers between devices  64.6 us (33%)
  starting transfers between devices  48.3 us (25%)
  blocking collectives  40.9 us (21%)
  Pallas kernels  24.8 us (13%)
  other arithmetic  7.36 us (4%)
  matrix products  4.11 us (2%)
  local copies, waits for them, and re-layouts  3.03 us (2%)
    all_to_all x2, blocking collectives, exchange(): return lax.all_to_all(values, axes, split_axis=0, concat_axis=0, tiled=True)  40.9 us
    all_to_all x3, waiting for transfers between devices, exchange(): return lax.all_to_all(values, axes, split_axis=0, concat_axis=0, tiled=True)  33.9 us
    ppermute x9, starting transfers between devices, swap_core(): return lax.ppermute(values, 'co', SWAP)  15.5 us
    all_to_all x3, starting transfers between devices, exchange(): return lax.all_to_all(values, axes, split_axis=0, concat_axis=0, tiled=True)  15.4 us
    ppermute x8, waiting for transfers between devices, swap_chip(): return lax.ppermute(values, 'xl', SWAP)  14 us
    ppermute x7, waiting for transfers between devices, from_ahead(): lax.ppermute(values, axis, [((i + step) % size, i) for i in range(size)])  8.27 us
    ppermute x8, starting transfers between devices, swap_chip(): return lax.ppermute(values, 'xl', SWAP)  7.26 us
    pallas_call x1, Pallas kernels, local(): pl.pallas_call(lambda *refs: scatter_kernel(hard_count, tok_rows, *refs),...  7.21 us
  transfers between devices with their start and end apart: 30, of which 16 were waited for; matrix products, arithmetic and copies ran while one was open for 3% of the time, Pallas kernels for 4%

profile of v6, /device:TPU:1, one launch (start us, length us, event | category | flops | bytes accessed | tf_op | source)
XLA Modules:
  0.0 194.7 jit_solution(10432652850469742069)
XLA Ops:
  0.6 2.1 %collective-permute-start.1 = (bf16[48,4096]{1,0:T(8,128)(2,1)}, bf16[48,4096]{1,0:T(8,128)(2,1)S(1)}, u32[]{:S(2)}, u32[]{:S(2)}) collective-permute-start(bf16[48,4096]{1,0:T(8,128)(2,1)} %bitcast.59), channel_id=1, source_target_pairs={{0,64},{64,0},{1,65},{65,1},{2,66},{66,2},{3,67},{67,3},{4,68},{68... | collective-permute-start | bytes 1179656 | tf_op jit(solution)/shard_map/ppermute | solution.py:26
  4.4 6.9 %collective-permute-done.1.x2 = bf16[48,4096]{1,0:T(8,128)(2,1)S(1)} collective-permute-done((bf16[48,4096]{1,0:T(8,128)(2,1)}, bf16[48,4096]{1,0:T(8,128)(2,1)S(1)}, u32[]{:S(2)}, u32[]{:S(2)}) %collective-permute-start.1) | collective-permute-done | bytes 393248 | tf_op jit(solution)/shard_map/ppermute | solution.py:26
  11.3 1.7 collective-permute-start.2
  15.8 3.9 %shard_map.128 = (bf16[48,1024]{1,0:T(8,128)(2,1)S(1)}, bf16[48,1024]{1,0:T(8,128)(2,1)S(1)}, bf16[48,1024]{1,0:T(8,128)(2,1)S(1)}, bf16[48,1024]{1,0:T(8,128)(2,1)S(1)}) custom-call(bf16[48,4096]{1,0:T(8,128)(2,1)S(1)} %bitcast.61, bf16[48,4096]{1,0:T(8,128)(2,1)S(1)} %collective-permute-done.x1, bf16[48,4096]{1,0:T(8,128)(2,1)S(1)} %collective-permute-done.1.x2, ...), custom_call_target="tpu_custom_call" | custom-call | tf_op jit(solution)/shard_map/pallas_call | solution.py:261
  22.0 1.8 collective-permute-done.4.x2
  23.8 2.9 %collective-permute-done.5.x3 = bf16[48,1024]{1,0:T(8,128)(2,1)S(1)} collective-permute-done((bf16[48,1024]{1,0:T(8,128)(2,1)S(1)}, bf16[48,1024]{1,0:T(8,128)(2,1)S(1)}, u32[]{:S(2)}, u32[]{:S(2)}) %collective-permute-start.5) | collective-permute-done | bytes 98336 | tf_op jit(solution)/shard_map/ppermute | solution.py:273
  27.2 21.6 %all_to_all.25 = bf16[32,56,128]{2,1,0:T(8,128)(2,1)S(1)} all-to-all(bf16[32,56,128]{2,1,0:T(8,128)(2,1)S(1)} %get-tuple-element.41.spread), channel_id=1, replica_groups=mesh['xl'=2,'co'=2,'xh'=2,'y'=4,'z'=4] {'xh','y','z'}, dimensions={0} | all-to-all | bytes 917504 | tf_op jit(solution)/shard_map/all_to_all | solution.py:42
  49.9 1.6 collective-permute-start.6
  51.8 1.7 collective-permute-done.7
  53.5 3.2 %collective-permute-start.8 = (bf16[768,128]{1,0:T(8,128)(2,1)S(1)}, bf16[768,128]{1,0:T(8,128)(2,1)S(1)}, u32[]{:S(2)}, u32[]{:S(2)}) collective-permute-start(bf16[768,128]{1,0:T(8,128)(2,1)S(1)} %collective-permute-done.7), channel_id=1, source_target_pairs={{0,32},{32,0},{1,33},{33,1},{2,34},{34,2},{3,35},{35,3},{4,36},{36... | collective-permute-start | bytes 589832 | tf_op jit(solution)/shard_map/ppermute | solution.py:22
  57.8 6.2 %shard_map.130 = (bf16[7,768,128]{2,1,0:T(8,128)(2,1)S(1)}, f32[768,128]{1,0:T(8,128)S(1)}) custom-call(s32[5376]{0:T(1024)S(1)} %reshape.82.refs_0_, bf16[768,128]{1,0:T(8,128)(2,1)S(1)} %bitcast.56, bf16[3072,128]{1,0:T(8,128)(2,1)S(1)} %pad_maximum_fusion.1.refs_2_), custom_call_target="tpu_custom_call" | custom-call | tf_op jit(solution)/shard_map/pallas_call | solution.py:319
  65.5 4.7 %all-to-all-start.1 = ((f16[32,24,896]{2,1,0:T(8,128)(2,1)}), f16[32,24,896]{2,1,0:T(8,128)(2,1)}, u32[]{:S(2)}, u32[]{:S(2)}) async-start(f16[32,24,896]{2,1,0:T(8,128)(2,1)} %pad_maximum_fusion), calls=%async_computation.1 | async-start | bytes 2752512 | tf_op jit(solution)/shard_map/all_to_all | solution.py:42
  70.3 20.1 %all-to-all-done.1 = f16[32,24,896]{2,1,0:T(8,128)(2,1)} async-done(((f16[32,24,896]{2,1,0:T(8,128)(2,1)}), f16[32,24,896]{2,1,0:T(8,128)(2,1)}, u32[]{:S(2)}, u32[]{:S(2)}) %all-to-all-start.1) | async-done | bytes 1376288 | tf_op jit(solution)/shard_map/all_to_all | solution.py:42
  90.4 1.5 convert_reduce_fusion
  93.6 6.0 %all-to-all-start.3 = ((bf16[32,24,128]{2,1,0:T(8,128)(2,1)}), bf16[32,24,128]{2,1,0:T(8,128)(2,1)S(1)}, u32[]{:S(2)}, u32[]{:S(2)}) async-start(bf16[32,24,128]{2,1,0:T(8,128)(2,1)} %broadcast_in_dim.39), calls=%async_computation.3 | async-start | bytes 393216 | tf_op jit(solution)/shard_map/all_to_all | solution.py:42
  99.7 9.1 %all-to-all-done.3 = bf16[32,24,128]{2,1,0:T(8,128)(2,1)S(1)} async-done(((bf16[32,24,128]{2,1,0:T(8,128)(2,1)}), bf16[32,24,128]{2,1,0:T(8,128)(2,1)S(1)}, u32[]{:S(2)}, u32[]{:S(2)}) %all-to-all-start.3) | async-done | bytes 196640 | tf_op jit(solution)/shard_map/all_to_all | solution.py:42
  109.9 4.7 %all-to-all-start.2 = ((bf16[32,24,768]{2,1,0:T(8,128)(2,1)}), bf16[32,24,768]{2,1,0:T(8,128)(2,1)}, u32[]{:S(2)}, u32[]{:S(2)}) async-start(bf16[32,24,768]{2,1,0:T(8,128)(2,1)} %broadcast_in_dim.38), calls=%async_computation.2 | async-start | bytes 2359296 | tf_op jit(solution)/shard_map/all_to_all | solution.py:42
  114.5 7.2 %shard_map.131 = (bf16[3072,128]{1,0:T(8,128)(2,1)S(1)}, f32[768,128]{1,0:T(8,128)S(1)}) custom-call(s32[5376]{0:T(1024)S(1)} %reshape.82.refs_0_, bf16[768,128]{1,0:T(8,128)(2,1)S(1)} %bitcast.58, bf16[768,128]{1,0:T(8,128)(2,1)S(1)} %bitcast.57, bf16[7,768,128]{2,1,0:T(8,128)(2,1)S(1)} %get-tuple-element.43.refs_3_), custom_call_target="tpu_custom_call" | custom-call | tf_op jit(solution)/shard_map/pallas_call | solution.py:357
  121.9 2.2 %collective-permute-start.9 = (bf16[2,768,128]{2,1,0:T(8,128)(2,1)S(1)}, bf16[2,768,128]{2,1,0:T(8,128)(2,1)S(1)}, u32[]{:S(2)}, u32[]{:S(2)}) collective-permute-start(bf16[2,768,128]{2,1,0:T(8,128)(2,1)S(1)} %pad_maximum_fusion.2), channel_id=1, source_target_pairs={{0,32},{32,0},{1,33},{33,1},{2,34},{34,2},{3,35},{35,3},{4,36},{36... | collective-permute-start | bytes 1179656 | tf_op jit(solution)/shard_map/ppermute | solution.py:22
  126.3 4.7 %all-to-all-done.2 = bf16[32,24,768]{2,1,0:T(8,128)(2,1)} async-done(((bf16[32,24,768]{2,1,0:T(8,128)(2,1)}), bf16[32,24,768]{2,1,0:T(8,128)(2,1)}, u32[]{:S(2)}, u32[]{:S(2)}) %all-to-all-start.2) | async-done | bytes 1179680 | tf_op jit(solution)/shard_map/all_to_all | solution.py:42
  131.0 1.7 fusion.2
  132.8 1.9 fusion.1
  134.7 19.2 %all_to_all.26.sums = bf16[32,2,24,128]{3,2,1,0:T(8,128)(2,1)S(1)} all-to-all(bf16[32,2,24,128]{3,2,1,0:T(8,128)(2,1)S(1)} %pad_maximum_fusion.3), channel_id=1, replica_groups=mesh['xl'=2,'co'=2,'xh'=2,'y'=4,'z'=4] {'xh','y','z'}, dimensions={0} | all-to-all | bytes 786432 | tf_op jit(solution)/shard_map/all_to_all | solution.py:42
  154.9 1.8 collective-permute-start.11
  158.2 3.2 %collective-permute-start.14 = (bf16[48,1024]{1,0:T(8,128)(2,1)S(1)}, bf16[48,1024]{1,0:T(8,128)(2,1)S(1)}, u32[]{:S(2)}, u32[]{:S(2)}) collective-permute-start(bf16[48,1024]{1,0:T(8,128)(2,1)S(1)} %get-tuple-element.51), channel_id=1, source_target_pairs={{0,32},{32,0},{1,33},{33,1},{2,34},{34,2},{3,35},{35,3},{4,36},{36... | collective-permute-start | bytes 294920 | tf_op jit(solution)/shard_map/ppermute | solution.py:22
  161.4 1.6 collective-permute-start.16
  163.1 2.8 %collective-permute-done.15.x2 = bf16[48,1024]{1,0:T(8,128)(2,1)S(1)} collective-permute-done((bf16[48,1024]{1,0:T(8,128)(2,1)S(1)}, bf16[48,1024]{1,0:T(8,128)(2,1)S(1)}, u32[]{:S(2)}, u32[]{:S(2)}) %collective-permute-start.15) | collective-permute-done | bytes 98336 | tf_op jit(solution)/shard_map/ppermute | solution.py:26
  165.8 2.3 %collective-permute-done.16.x3 = bf16[48,1024]{1,0:T(8,128)(2,1)S(1)} collective-permute-done((bf16[48,1024]{1,0:T(8,128)(2,1)S(1)}, bf16[48,1024]{1,0:T(8,128)(2,1)S(1)}, u32[]{:S(2)}, u32[]{:S(2)}) %collective-permute-start.16) | collective-permute-done | bytes 98336 | tf_op jit(solution)/shard_map/ppermute | solution.py:399
  168.2 5.3 %shard_map.133 = (bf16[2,48,4096]{2,1,0:T(8,128)(2,1)S(1)}, bf16[2,48,4096]{2,1,0:T(8,128)(2,1)S(1)}) custom-call(bf16[48,1024]{1,0:T(8,128)(2,1)S(1)} %get-tuple-element.55.x0, bf16[48,1024]{1,0:T(8,128)(2,1)S(1)} %collective-permute-done.14.x1, bf16[48,1024]{1,0:T(8,128)(2,1)S(1)} %collective-permute-done.15.x2, ...), custom_call_target="tpu_custom_call" | custom-call | tf_op jit(solution)/shard_map/pallas_call | solution.py:402
  178.9 1.7 collective-permute-done.20
  181.3 5.8 %collective-permute-done.21 = f32[104,128]{1,0:T(8,128)S(1)} collective-permute-done((f32[104,128]{1,0:T(8,128)S(1)}, f32[104,128]{1,0:T(8,128)S(1)}, u32[]{:S(2)}, u32[]{:S(2)}) %collective-permute-start.21) | collective-permute-done | bytes 53280 | tf_op jit(solution)/shard_map/ppermute | solution.py:31
  187.2 2.0 %collective-permute-start.24 = (f32[104,128]{1,0:T(8,128)S(1)}, f32[104,128]{1,0:T(8,128)S(1)}, u32[]{:S(2)}, u32[]{:S(2)}) collective-permute-start(f32[104,128]{1,0:T(8,128)S(1)} %add.115.refs_0_), channel_id=1, source_target_pairs={{0,32},{32,0},{1,33},{33,1},{2,34},{34,2},{3,35},{35,3},{4,36},{36... | collective-permute-start | bytes 159752 | tf_op jit(solution)/shard_map/ppermute | solution.py:22
  (89 shorter events, 29.5 us)
Async XLA Ops:
  0.6 10.7 %collective-permute-start.1 = (bf16[48,4096]{1,0:T(8,128)(2,1)}, bf16[48,4096]{1,0:T(8,128)(2,1)S(1)}, u32[]{:S(2)}, u32[]{:S(2)}) collective-permute-start(bf16[48,4096]{1,0:T(8,128)(2,1)} %bitcast.59), channel_id=1, source_target_pairs={{0,64},{64,0},{1,65},{65,1},{2,66},{66,2},{3,67},{67,3},{4,68},{68... | collective-permute-start | bytes 1179656 | tf_op jit(solution)/shard_map/ppermute | solution.py:26
  2.8 12.0 %collective-permute-start = (bf16[48,4096]{1,0:T(8,128)(2,1)}, bf16[48,4096]{1,0:T(8,128)(2,1)S(1)}, u32[]{:S(2)}, u32[]{:S(2)}) collective-permute-start(bf16[48,4096]{1,0:T(8,128)(2,1)} %bitcast.60), channel_id=1, source_target_pairs={{0,32},{32,0},{1,33},{33,1},{2,34},{34,2},{3,35},{35,3},{4,36},{36... | collective-permute-start | bytes 1179656 | tf_op jit(solution)/shard_map/ppermute | solution.py:22
  11.3 3.5 %collective-permute-start.2 = (bf16[48,4096]{1,0:T(8,128)(2,1)S(1)}, bf16[48,4096]{1,0:T(8,128)(2,1)S(1)}, u32[]{:S(2)}, u32[]{:S(2)}) collective-permute-start(bf16[48,4096]{1,0:T(8,128)(2,1)S(1)} %collective-permute-done.1.x2), channel_id=1, source_target_pairs={{0,32},{32,0},{1,33},{33,1},{2,34},{34,2},{3,35},{35,3},{4,36},{36... | collective-permute-start | bytes 1179656 | tf_op jit(solution)/shard_map/ppermute | solution.py:22
  15.8 11.0 %copy-start.3 = (f32[4096]{0:T(1024)S(1)}, f32[4096]{0:T(1024)}, u32[]{:S(2)}) copy-start(f32[4096]{0:T(1024)} %param.13) | copy-start | bytes 49156
  15.8 11.0 %copy-start.4 = (f32[4096]{0:T(1024)S(1)}, f32[4096]{0:T(1024)}, u32[]{:S(2)}) copy-start(f32[4096]{0:T(1024)} %param.12) | copy-start | bytes 49156
  19.7 2.3 %collective-permute-start.3 = (bf16[48,1024]{1,0:T(8,128)(2,1)S(1)}, bf16[48,1024]{1,0:T(8,128)(2,1)S(1)}, u32[]{:S(2)}, u32[]{:S(2)}) collective-permute-start(bf16[48,1024]{1,0:T(8,128)(2,1)S(1)} %get-tuple-element.38), channel_id=1, source_target_pairs={{0,32},{32,0},{1,33},{33,1},{2,34},{34,2},{3,35},{35,3},{4,36},{36... | collective-permute-start | bytes 294920 | tf_op jit(solution)/shard_map/ppermute | solution.py:22
  19.8 4.0 %collective-permute-start.4 = (bf16[48,1024]{1,0:T(8,128)(2,1)S(1)}, bf16[48,1024]{1,0:T(8,128)(2,1)S(1)}, u32[]{:S(2)}, u32[]{:S(2)}) collective-permute-start(bf16[48,1024]{1,0:T(8,128)(2,1)S(1)} %get-tuple-element.39), channel_id=1, source_target_pairs={{0,64},{64,0},{1,65},{65,1},{2,66},{66,2},{3,67},{67,3},{4,68},{68... | collective-permute-start | bytes 294920 | tf_op jit(solution)/shard_map/ppermute | solution.py:26
  21.3 5.4 %collective-permute-start.5 = (bf16[48,1024]{1,0:T(8,128)(2,1)S(1)}, bf16[48,1024]{1,0:T(8,128)(2,1)S(1)}, u32[]{:S(2)}, u32[]{:S(2)}) collective-permute-start(bf16[48,1024]{1,0:T(8,128)(2,1)S(1)} %get-tuple-element.40), channel_id=1, source_target_pairs={{0,96},{32,64},{64,32},{96,0},{1,97},{33,65},{65,33},{97,1},{2,98}... | collective-permute-start | bytes 294920 | tf_op jit(solution)/shard_map/ppermute | solution.py:273
  48.9 4.6 %collective-permute-start.7 = (bf16[768,128]{1,0:T(8,128)(2,1)S(1)}, bf16[768,128]{1,0:T(8,128)(2,1)S(1)}, u32[]{:S(2)}, u32[]{:S(2)}) collective-permute-start(bf16[768,128]{1,0:T(8,128)(2,1)S(1)} %bitcast.69), channel_id=1, source_target_pairs={{0,64},{64,0},{1,65},{65,1},{2,66},{66,2},{3,67},{67,3},{4,68},{68... | collective-permute-start | bytes 589832 | tf_op jit(solution)/shard_map/ppermute | solution.py:26
  49.9 7.3 %collective-permute-start.6 = (bf16[768,128]{1,0:T(8,128)(2,1)S(1)}, bf16[768,128]{1,0:T(8,128)(2,1)S(1)}, u32[]{:S(2)}, u32[]{:S(2)}) collective-permute-start(bf16[768,128]{1,0:T(8,128)(2,1)S(1)} %bitcast.70), channel_id=1, source_target_pairs={{0,32},{32,0},{1,33},{33,1},{2,34},{34,2},{3,35},{35,3},{4,36},{36... | collective-permute-start | bytes 589832 | tf_op jit(solution)/shard_map/ppermute | solution.py:22
  53.5 4.3 %collective-permute-start.8 = (bf16[768,128]{1,0:T(8,128)(2,1)S(1)}, bf16[768,128]{1,0:T(8,128)(2,1)S(1)}, u32[]{:S(2)}, u32[]{:S(2)}) collective-permute-start(bf16[768,128]{1,0:T(8,128)(2,1)S(1)} %collective-permute-done.7), channel_id=1, source_target_pairs={{0,32},{32,0},{1,33},{33,1},{2,34},{34,2},{3,35},{35,3},{4,36},{36... | collective-permute-start | bytes 589832 | tf_op jit(solution)/shard_map/ppermute | solution.py:22
  65.5 24.9 %all-to-all-start.1 = ((f16[32,24,896]{2,1,0:T(8,128)(2,1)}), f16[32,24,896]{2,1,0:T(8,128)(2,1)}, u32[]{:S(2)}, u32[]{:S(2)}) async-start(f16[32,24,896]{2,1,0:T(8,128)(2,1)} %pad_maximum_fusion), calls=%async_computation.1 | async-start | bytes 2752512 | tf_op jit(solution)/shard_map/all_to_all | solution.py:42
  93.6 15.2 %all-to-all-start.3 = ((bf16[32,24,128]{2,1,0:T(8,128)(2,1)}), bf16[32,24,128]{2,1,0:T(8,128)(2,1)S(1)}, u32[]{:S(2)}, u32[]{:S(2)}) async-start(bf16[32,24,128]{2,1,0:T(8,128)(2,1)} %broadcast_in_dim.39), calls=%async_computation.3 | async-start | bytes 393216 | tf_op jit(solution)/shard_map/all_to_all | solution.py:42
  109.9 21.2 %all-to-all-start.2 = ((bf16[32,24,768]{2,1,0:T(8,128)(2,1)}), bf16[32,24,768]{2,1,0:T(8,128)(2,1)}, u32[]{:S(2)}, u32[]{:S(2)}) async-start(bf16[32,24,768]{2,1,0:T(8,128)(2,1)} %broadcast_in_dim.38), calls=%async_computation.2 | async-start | bytes 2359296 | tf_op jit(solution)/shard_map/all_to_all | solution.py:42
  121.9 3.6 %collective-permute-start.9 = (bf16[2,768,128]{2,1,0:T(8,128)(2,1)S(1)}, bf16[2,768,128]{2,1,0:T(8,128)(2,1)S(1)}, u32[]{:S(2)}, u32[]{:S(2)}) collective-permute-start(bf16[2,768,128]{2,1,0:T(8,128)(2,1)S(1)} %pad_maximum_fusion.2), channel_id=1, source_target_pairs={{0,32},{32,0},{1,33},{33,1},{2,34},{34,2},{3,35},{35,3},{4,36},{36... | collective-permute-start | bytes 1179656 | tf_op jit(solution)/shard_map/ppermute | solution.py:22
  125.6 7.2 %collective-permute-start.10 = (bf16[768,128]{1,0:T(8,128)(2,1)S(1)}, bf16[768,128]{1,0:T(8,128)(2,1)S(1)}, u32[]{:S(2)}, u32[]{:S(2)}) collective-permute-start(bf16[768,128]{1,0:T(8,128)(2,1)S(1)} %fusion.5), channel_id=1, source_target_pairs={{0,64},{64,0},{1,65},{65,1},{2,66},{66,2},{3,67},{67,3},{4,68},{68... | collective-permute-start | bytes 589832 | tf_op jit(solution)/shard_map/ppermute | solution.py:26
  154.9 6.5 %collective-permute-start.11 = (f32[104,128]{1,0:T(8,128)S(1)}, f32[104,128]{1,0:T(8,128)S(1)}, u32[]{:S(2)}, u32[]{:S(2)}) collective-permute-start(f32[104,128]{1,0:T(8,128)S(1)} %get-tuple-element.49), channel_id=1, source_target_pairs={{2,0},{3,1},{0,2},{1,3},{6,4},{7,5},{4,6},{5,7},{10,8},{11,9},{8,1... | collective-permute-start | bytes 159752 | tf_op jit(solution)/shard_map/ppermute | solution.py:31
  156.7 6.3 %collective-permute-start.12 = (f32[104,128]{1,0:T(8,128)S(1)}, f32[104,128]{1,0:T(8,128)S(1)}, u32[]{:S(2)}, u32[]{:S(2)}) collective-permute-start(f32[104,128]{1,0:T(8,128)S(1)} %get-tuple-element.49), channel_id=1, source_target_pairs={{1,0},{2,1},{3,2},{0,3},{5,4},{6,5},{7,6},{4,7},{9,8},{10,9},{11,1... | collective-permute-start | bytes 159752 | tf_op jit(solution)/shard_map/ppermute | solution.py:31
  157.8 5.3 %collective-permute-start.13 = (f32[104,128]{1,0:T(8,128)S(1)}, f32[104,128]{1,0:T(8,128)S(1)}, u32[]{:S(2)}, u32[]{:S(2)}) collective-permute-start(f32[104,128]{1,0:T(8,128)S(1)} %get-tuple-element.49), channel_id=1, source_target_pairs={{3,0},{0,1},{1,2},{2,3},{7,4},{4,5},{5,6},{6,7},{11,8},{8,9},{9,10... | collective-permute-start | bytes 159752 | tf_op jit(solution)/shard_map/ppermute | solution.py:31
  158.2 4.8 %collective-permute-start.14 = (bf16[48,1024]{1,0:T(8,128)(2,1)S(1)}, bf16[48,1024]{1,0:T(8,128)(2,1)S(1)}, u32[]{:S(2)}, u32[]{:S(2)}) collective-permute-start(bf16[48,1024]{1,0:T(8,128)(2,1)S(1)} %get-tuple-element.51), channel_id=1, source_target_pairs={{0,32},{32,0},{1,33},{33,1},{2,34},{34,2},{3,35},{35,3},{4,36},{36... | collective-permute-start | bytes 294920 | tf_op jit(solution)/shard_map/ppermute | solution.py:22
  161.4 4.4 %collective-permute-start.15 = (bf16[48,1024]{1,0:T(8,128)(2,1)S(1)}, bf16[48,1024]{1,0:T(8,128)(2,1)S(1)}, u32[]{:S(2)}, u32[]{:S(2)}) collective-permute-start(bf16[48,1024]{1,0:T(8,128)(2,1)S(1)} %get-tuple-element.52), channel_id=1, source_target_pairs={{0,64},{64,0},{1,65},{65,1},{2,66},{66,2},{3,67},{67,3},{4,68},{68... | collective-permute-start | bytes 294920 | tf_op jit(solution)/shard_map/ppermute | solution.py:26
  161.4 6.8 %collective-permute-start.16 = (bf16[48,1024]{1,0:T(8,128)(2,1)S(1)}, bf16[48,1024]{1,0:T(8,128)(2,1)S(1)}, u32[]{:S(2)}, u32[]{:S(2)}) collective-permute-start(bf16[48,1024]{1,0:T(8,128)(2,1)S(1)} %get-tuple-element.53), channel_id=1, source_target_pairs={{0,96},{32,64},{64,32},{96,0},{1,97},{33,65},{65,33},{97,1},{2,98}... | collective-permute-start | bytes 294920 | tf_op jit(solution)/shard_map/ppermute | solution.py:399
  173.5 2.9 %collective-permute-start.17 = (bf16[2,48,4096]{2,1,0:T(8,128)(2,1)S(1)}, bf16[2,48,4096]{2,1,0:T(8,128)(2,1)S(1)}, u32[]{:S(2)}, u32[]{:S(2)}) collective-permute-start(bf16[2,48,4096]{2,1,0:T(8,128)(2,1)S(1)} %get-tuple-element.62), channel_id=1, source_target_pairs={{0,32},{32,0},{1,33},{33,1},{2,34},{34,2},{3,35},{35,3},{4,36},{36... | collective-permute-start | bytes 2359304 | tf_op jit(solution)/shard_map/ppermute | solution.py:22
  174.0 4.9 %collective-permute-start.18 = (f32[104,128]{1,0:T(8,128)S(1)}, f32[104,128]{1,0:T(8,128)S(1)}, u32[]{:S(2)}, u32[]{:S(2)}) collective-permute-start(f32[104,128]{1,0:T(8,128)S(1)} %add_add_fusion.1), channel_id=1, source_target_pairs={{8,0},{12,4},{0,8},{4,12},{9,1},{13,5},{1,9},{5,13},{10,2},{14,6},... | collective-permute-start | bytes 159752 | tf_op jit(solution)/shard_map/ppermute | solution.py:31
  174.8 4.1 %collective-permute-start.19 = (f32[104,128]{1,0:T(8,128)S(1)}, f32[104,128]{1,0:T(8,128)S(1)}, u32[]{:S(2)}, u32[]{:S(2)}) collective-permute-start(f32[104,128]{1,0:T(8,128)S(1)} %add_add_fusion.1), channel_id=1, source_target_pairs={{4,0},{8,4},{12,8},{0,12},{5,1},{9,5},{13,9},{1,13},{6,2},{10,6},{... | collective-permute-start | bytes 159752 | tf_op jit(solution)/shard_map/ppermute | solution.py:31
  176.4 4.2 %collective-permute-start.20 = (f32[104,128]{1,0:T(8,128)S(1)}, f32[104,128]{1,0:T(8,128)S(1)}, u32[]{:S(2)}, u32[]{:S(2)}) collective-permute-start(f32[104,128]{1,0:T(8,128)S(1)} %add_add_fusion.1), channel_id=1, source_target_pairs={{12,0},{0,4},{4,8},{8,12},{13,1},{1,5},{5,9},{9,13},{14,2},{2,6},{... | collective-permute-start | bytes 159752 | tf_op jit(solution)/shard_map/ppermute | solution.py:31
  176.6 10.6 %collective-permute-start.22 = (bf16[48,2048]{1,0:T(8,128)(2,1)S(1)}, bf16[48,2048]{1,0:T(8,128)(2,1)S(1)}, u32[]{:S(2)}, u32[]{:S(2)}) collective-permute-start(bf16[48,2048]{1,0:T(8,128)(2,1)S(1)} %get-tuple-element.79), channel_id=1, source_target_pairs={{0,64},{64,0},{1,65},{65,1},{2,66},{66,2},{3,67},{67,3},{4,68},{68... | collective-permute-start | bytes 589832 | tf_op jit(solution)/shard_map/ppermute | solution.py:26
  176.7 14.3 %collective-permute-start.23 = (bf16[48,2048]{1,0:T(8,128)(2,1)S(1)}, bf16[48,2048]{1,0:T(8,128)(2,1)S(1)}, u32[]{:S(2)}, u32[]{:S(2)}) collective-permute-start(bf16[48,2048]{1,0:T(8,128)(2,1)S(1)} %get-tuple-element.80), channel_id=1, source_target_pairs={{0,64},{64,0},{1,65},{65,1},{2,66},{66,2},{3,67},{67,3},{4,68},{68... | collective-permute-start | bytes 589832 | tf_op jit(solution)/shard_map/ppermute | solution.py:26
  180.6 6.6 %collective-permute-start.21 = (f32[104,128]{1,0:T(8,128)S(1)}, f32[104,128]{1,0:T(8,128)S(1)}, u32[]{:S(2)}, u32[]{:S(2)}) collective-permute-start(f32[104,128]{1,0:T(8,128)S(1)} %add_add_fusion), channel_id=1, source_target_pairs={{16,0},{0,16},{17,1},{1,17},{18,2},{2,18},{19,3},{3,19},{20,4},{4,... | collective-permute-start | bytes 159752 | tf_op jit(solution)/shard_map/ppermute | solution.py:31
  187.2 4.7 %collective-permute-start.24 = (f32[104,128]{1,0:T(8,128)S(1)}, f32[104,128]{1,0:T(8,128)S(1)}, u32[]{:S(2)}, u32[]{:S(2)}) collective-permute-start(f32[104,128]{1,0:T(8,128)S(1)} %add.115.refs_0_), channel_id=1, source_target_pairs={{0,32},{32,0},{1,33},{33,1},{2,34},{34,2},{3,35},{35,3},{4,36},{36... | collective-permute-start | bytes 159752 | tf_op jit(solution)/shard_map/ppermute | solution.py:22
  189.2 3.4 %collective-permute-start.25 = (f32[104,128]{1,0:T(8,128)S(1)}, f32[104,128]{1,0:T(8,128)S(1)}, u32[]{:S(2)}, u32[]{:S(2)}) collective-permute-start(f32[104,128]{1,0:T(8,128)S(1)} %add.115.refs_0_), channel_id=1, source_target_pairs={{0,64},{64,0},{1,65},{65,1},{2,66},{66,2},{3,67},{67,3},{4,68},{68... | collective-permute-start | bytes 159752 | tf_op jit(solution)/shard_map/ppermute | solution.py:26
  189.5 4.4 %collective-permute-start.26 = (f32[104,128]{1,0:T(8,128)S(1)}, f32[104,128]{1,0:T(8,128)S(1)}, u32[]{:S(2)}, u32[]{:S(2)}) collective-permute-start(f32[104,128]{1,0:T(8,128)S(1)} %add.115.refs_0_), channel_id=1, source_target_pairs={{0,96},{32,64},{64,32},{96,0},{1,97},{33,65},{65,33},{97,1},{2,98}... | collective-permute-start | bytes 159752 | tf_op jit(solution)/shard_map/ppermute | solution.py:424
  (6 other events, 42.2 us)

commit v7 on v6

--- a/solution.py
+++ b/solution.py
@@ -213,6 +213,39 @@
             out_ref[i // 2, :, here] = term[i * rows : (i + 1) * rows].astype(BF16)
 
 
+def softmax_kernel(hard_count, at, score_ref, losses_ref, hard_ref, group_ref):
+    rows, width = score_ref.shape
+    pairs = width - LANES
+    scores = score_ref[:, :pairs] / TAU
+    weights = jnp.exp(scores)
+    slot = lax.broadcasted_iota(jnp.int32, (rows, LANES), 1)
+    hard_weights = jnp.where(slot < hard_count, jnp.exp(score_ref[:, pairs:] / TAU), 0.0)
+    totals = jnp.sum(weights, axis=1, keepdims=True) + jnp.sum(hard_weights, axis=1, keepdims=True)
+    column = lax.broadcasted_iota(jnp.int32, (rows, pairs), 1)
+    row = lax.broadcasted_iota(jnp.int32, (rows, pairs), 0)
+    own = jnp.sum(jnp.where(column == row + at[0], scores, 0.0), axis=1, keepdims=True)
+    losses_ref[...] = jnp.broadcast_to(jnp.log(totals) - own, (rows, LANES))
+    hard_probs = (hard_weights / totals).astype(BF16)
+    probs = (weights / totals).astype(BF16)
+    for b in range(hard_ref.shape[0]):
+        hard_ref[b] = hard_probs
+        group_ref[b] = probs
+
+
+def sums_kernel(probs_ref, q_ref, p_ref, hard_ref, add_ref, near_ref, far_ref, out_ref):
+    tok_rows = out_ref.shape[2]
+    probs = probs_ref[...]
+    sum_q = jnp.dot(probs, p_ref[...], preferred_element_type=F32) + hard_ref[...]
+    sum_p = lax.dot_general(
+        probs, q_ref[...], (((0,), (0,)), ((), ())), preferred_element_type=F32
+    )
+    sum_p = sum_p + add_ref[...].astype(F32) + near_ref[...].astype(F32) + far_ref[...].astype(F32)
+    for b in range(out_ref.shape[0]):
+        here = slice(b * tok_rows, (b + 1) * tok_rows)
+        out_ref[b, 0] = sum_q[here].astype(BF16)
+        out_ref[b, 1] = sum_p[here].astype(BF16)
+
+
 def finish_kernel(blocks, v0, v1, v2, v3, gain_ref, bias_ref, task_ref):
     lines = gain_ref.shape[0]
     four = (v0, v1, v2, v3)
@@ -332,27 +365,21 @@
     )(ids, q_all, p_all)
     part = jnp.concatenate([score_part, hard_part], axis=1).astype(SEND)
     part = exchange(part.reshape(blocks, tok_rows, pairs + LANES), BLK)
-    part = jnp.sum(part.astype(F32), axis=0) / TAU
-    scores = part[:, :pairs]
-    hard = part[:, pairs:]
-
-    column = lax.broadcasted_iota(jnp.int32, scores.shape, 1)
-    row = lax.broadcasted_iota(jnp.int32, scores.shape, 0)
-    weights = jnp.exp(scores)
-    slot = lax.broadcasted_iota(jnp.int32, hard.shape, 1)
-    hard_weights = jnp.where(slot < hard_count, jnp.exp(hard), 0.0)
-    totals = jnp.sum(weights, axis=1, keepdims=True) + jnp.sum(hard_weights, axis=1, keepdims=True)
-    own_column = lax.axis_index(BLK) * tok_rows + row
-    own_score = jnp.sum(jnp.where(column == own_column, scores, 0.0), axis=1)
-    losses = jnp.log(totals[:, 0]) - own_score
-
-    def spread_rows(values):
-        values = values.astype(BF16)
-        values = exchange(jnp.broadcast_to(values[None], (blocks,) + values.shape), BLK)
-        return values.reshape((pairs,) + values.shape[2:])
-
-    hard_probs = spread_rows(hard_weights / totals)
-    group_probs = spread_rows(weights / totals)
+    part = jnp.sum(part.astype(F32), axis=0)
+    losses, hard_probs, group_probs = pl.pallas_call(
+        lambda *refs: softmax_kernel(hard_count, *refs),
+        out_shape=(
+            jax.ShapeDtypeStruct((tok_rows, LANES), F32),
+            jax.ShapeDtypeStruct((blocks, tok_rows, LANES), BF16),
+            jax.ShapeDtypeStruct((blocks, tok_rows, pairs), BF16),
+        ),
+        in_specs=[smem, vmem],
+        out_specs=(vmem,) * 3,
+        compiler_params=params,
+    )((lax.axis_index(BLK) * tok_rows).astype(jnp.int32).reshape(1), part)
+    losses = losses[:, 0]
+    hard_probs = exchange(hard_probs, BLK).reshape(pairs, LANES)
+    group_probs = exchange(group_probs, BLK).reshape(pairs, pairs)
 
     hard_add, hard_sum = pl.pallas_call(
         lambda *refs: scatter_kernel(hard_count, tok_rows, *refs),
@@ -367,16 +394,15 @@
         compiler_params=params,
     )(ids, hard_probs, q_all, negatives)
     hard_add = hard_add.reshape(4, pairs, LANES)
-    crossed = swap_core(jnp.stack([hard_add[1], hard_add[3]])).astype(F32)
-    over_chip = swap_chip((hard_add[2].astype(F32) + crossed[1]).astype(BF16)).astype(F32)
-    sum_q = jnp.dot(group_probs, p_own, preferred_element_type=F32) + hard_sum
-    sum_p = lax.dot_general(
-        group_probs, q_all, (((0,), (0,)), ((), ())), preferred_element_type=F32
-    )
-    sum_p = sum_p + (hard_add[0].astype(F32) + crossed[0] + over_chip)
-    sums = jnp.stack(
-        [sum_q.reshape(blocks, tok_rows, LANES), sum_p.reshape(blocks, tok_rows, LANES)], axis=1
-    ).astype(BF16)
+    crossed = swap_core(jnp.stack([hard_add[1], hard_add[3]]))
+    over_chip = swap_chip((hard_add[2].astype(F32) + crossed[1].astype(F32)).astype(BF16))
+    sums = pl.pallas_call(
+        sums_kernel,
+        out_shape=jax.ShapeDtypeStruct((blocks, 2, tok_rows, LANES), BF16),
+        in_specs=[vmem] * 7,
+        out_specs=vmem,
+        compiler_params=params,
+    )(group_probs, q_all, p_own, hard_sum, hard_add[0], crossed[0], over_chip)
     sums = exchange(sums, BLK)
 
     lines = width // LANES
@@ -398,7 +424,7 @@
         swap_chip(cols[2]),
         lax.ppermute(cols[3], GRP, DIAGONAL),
     ]
-    vectors, *cols = lax.optimization_barrier((sum_over(vectors, "z"), *cols))
+    vectors, *cols = lax.optimization_barrier((sum_over(vectors, "xh"), *cols))
     keep, send = pl.pallas_call(
         backward_kernel,
         out_shape=[jax.ShapeDtypeStruct((2, row_count, width), BF16)] * 2,
@@ -408,9 +434,11 @@
         compiler_params=stream,
     )(*cols, out_proj)
     vectors, keep, send = lax.optimization_barrier((vectors, keep, send))
-    vectors = sum_over(sum_over(vectors, "y"), "xh")
+    vectors = sum_over(vectors, "y")
     crossed = swap_core(send)
     far_sum = (keep[1].astype(F32) + crossed[1].astype(F32)).astype(BF16)
+    far_sum, vectors = lax.optimization_barrier((far_sum, vectors))
+    vectors = sum_over(vectors, "z")
     first = swap_chip(far_sum[:, : width // 2])
     second = swap_chip(far_sum[:, width // 2 :])
     vectors, first = lax.optimization_barrier((vectors, first))

time: 195 us -> 195 us (level)
  blocking collectives: 40.9 us -> 56 us
  waiting for transfers between devices: 64.6 us -> 55.4 us
  starting transfers between devices: 48.3 us -> 43.9 us
  matrix products: 4.11 us -> 0.52 us
    all_to_all x2 -> x3, blocking collectives: 40.9 us -> 56 us  [exchange(): return lax.all_to_all(values, axes, split_axis=0, concat_axis=0, tiled=True)]
    all_to_all x3 -> x2, waiting for transfers between devices: 33.9 us -> 20.2 us  [exchange(): return lax.all_to_all(values, axes, split_axis=0, concat_axis=0, tiled=True)]
    all_to_all x3 -> x2, starting transfers between devices: 15.4 us -> 8.62 us  [exchange(): return lax.all_to_all(values, axes, split_axis=0, concat_axis=0, tiled=True)]
    ppermute x8, waiting for transfers between devices: 14 us -> 18.2 us  [swap_chip(): return lax.ppermute(values, 'xl', SWAP)]
    ppermute x7, waiting for transfers between devices: 8.27 us -> 12.3 us  [from_ahead(): lax.ppermute(values, axis, [((i + step) % size, i) for i in range(size)])]
    dot_general x2 -> x0, matrix products: 3.6 us -> none  [the longest x1 1.85 us: local(): lax.dot_general(group_probs, q_all, (((0,), (0,)), ((), ())), preferred_e...]
    ppermute x1, starting transfers between devices: 1.43 us -> 4.79 us  [local(): lax.ppermute(vectors, GRP, DIAGONAL)]
    unnamed x16 -> x20, local copies, waits for them, and re-layouts: 1.02 us -> 3.96 us
  transfers between devices with their start and end apart: 30 -> 29, of which waited for: 16 -> 14; matrix products, arithmetic and copies ran while one was open for 3% -> 2% of each run, Pallas kernels for 4% -> 4%
where the time goes in v7:
time: 195 us; the launch traced here: 194 us
  blocking collectives  56 us (29%)
  waiting for transfers between devices  55.4 us (28%)
  starting transfers between devices  43.9 us (23%)
  Pallas kernels  25.9 us (13%)
  other arithmetic  6.26 us (3%)
  local copies, waits for them, and re-layouts  4.81 us (2%)
    all_to_all x3, blocking collectives, exchange(): return lax.all_to_all(values, axes, split_axis=0, concat_axis=0, tiled=True)  56 us
    all_to_all x2, waiting for transfers between devices, exchange(): return lax.all_to_all(values, axes, split_axis=0, concat_axis=0, tiled=True)  20.2 us
    ppermute x8, waiting for transfers between devices, swap_chip(): return lax.ppermute(values, 'xl', SWAP)  18.2 us
    ppermute x9, starting transfers between devices, swap_core(): return lax.ppermute(values, 'co', SWAP)  13.6 us
    ppermute x7, waiting for transfers between devices, from_ahead(): lax.ppermute(values, axis, [((i + step) % size, i) for i in range(size)])  12.3 us
    ppermute x8, starting transfers between devices, swap_chip(): return lax.ppermute(values, 'xl', SWAP)  8.96 us
    all_to_all x2, starting transfers between devices, exchange(): return lax.all_to_all(values, axes, split_axis=0, concat_axis=0, tiled=True)  8.62 us
    pallas_call x1, Pallas kernels, local(): pl.pallas_call(lambda *refs: scatter_kernel(hard_count, tok_rows, *refs),...  7.2 us
  transfers between devices with their start and end apart: 29, of which 14 were waited for; matrix products, arithmetic and copies ran while one was open for 2% of the time, Pallas kernels for 4%

profile of v7, /device:TPU:1, one launch (start us, length us, event | category | flops | bytes accessed | tf_op | source)
XLA Modules:
  0.0 194.4 jit_solution(4102212254822875556)
XLA Ops:
  0.6 2.1 %collective-permute-start.1 = (bf16[48,4096]{1,0:T(8,128)(2,1)}, bf16[48,4096]{1,0:T(8,128)(2,1)S(1)}, u32[]{:S(2)}, u32[]{:S(2)}) collective-permute-start(bf16[48,4096]{1,0:T(8,128)(2,1)} %bitcast.49), channel_id=1, source_target_pairs={{0,64},{64,0},{1,65},{65,1},{2,66},{66,2},{3,67},{67,3},{4,68},{68... | collective-permute-start | bytes 1179656 | tf_op jit(solution)/shard_map/ppermute | solution.py:26
  4.4 6.9 %collective-permute-done.1.x2 = bf16[48,4096]{1,0:T(8,128)(2,1)S(1)} collective-permute-done((bf16[48,4096]{1,0:T(8,128)(2,1)}, bf16[48,4096]{1,0:T(8,128)(2,1)S(1)}, u32[]{:S(2)}, u32[]{:S(2)}) %collective-permute-start.1) | collective-permute-done | bytes 393248 | tf_op jit(solution)/shard_map/ppermute | solution.py:26
  11.3 1.7 collective-permute-start.2
  15.8 3.9 %shard_map.128 = (bf16[48,1024]{1,0:T(8,128)(2,1)S(1)}, bf16[48,1024]{1,0:T(8,128)(2,1)S(1)}, bf16[48,1024]{1,0:T(8,128)(2,1)S(1)}, bf16[48,1024]{1,0:T(8,128)(2,1)S(1)}) custom-call(bf16[48,4096]{1,0:T(8,128)(2,1)S(1)} %bitcast.51, bf16[48,4096]{1,0:T(8,128)(2,1)S(1)} %collective-permute-done.x1, bf16[48,4096]{1,0:T(8,128)(2,1)S(1)} %collective-permute-done.1.x2, ...), custom_call_target="tpu_custom_call" | custom-call | tf_op jit(solution)/shard_map/pallas_call | solution.py:294
  19.8 1.5 collective-permute-start.4
  22.0 1.8 collective-permute-done.4.x2
  23.8 2.9 %collective-permute-done.5.x3 = bf16[48,1024]{1,0:T(8,128)(2,1)S(1)} collective-permute-done((bf16[48,1024]{1,0:T(8,128)(2,1)S(1)}, bf16[48,1024]{1,0:T(8,128)(2,1)S(1)}, u32[]{:S(2)}, u32[]{:S(2)}) %collective-permute-start.5) | collective-permute-done | bytes 98336 | tf_op jit(solution)/shard_map/ppermute | solution.py:306
  27.3 21.6 %all_to_all.25 = bf16[32,56,128]{2,1,0:T(8,128)(2,1)S(1)} all-to-all(bf16[32,56,128]{2,1,0:T(8,128)(2,1)S(1)} %get-tuple-element.46.spread), channel_id=1, replica_groups=mesh['xl'=2,'co'=2,'xh'=2,'y'=4,'z'=4] {'xh','y','z'}, dimensions={0} | all-to-all | bytes 917504 | tf_op jit(solution)/shard_map/all_to_all | solution.py:42
  49.9 1.6 collective-permute-start.6
  51.8 1.7 collective-permute-done.7
  53.5 3.2 %collective-permute-start.8 = (bf16[768,128]{1,0:T(8,128)(2,1)S(1)}, bf16[768,128]{1,0:T(8,128)(2,1)S(1)}, u32[]{:S(2)}, u32[]{:S(2)}) collective-permute-start(bf16[768,128]{1,0:T(8,128)(2,1)S(1)} %collective-permute-done.7), channel_id=1, source_target_pairs={{0,32},{32,0},{1,33},{33,1},{2,34},{34,2},{3,35},{35,3},{4,36},{36... | collective-permute-start | bytes 589832 | tf_op jit(solution)/shard_map/ppermute | solution.py:22
  57.8 6.2 %shard_map.130 = (bf16[7,768,128]{2,1,0:T(8,128)(2,1)S(1)}, f32[768,128]{1,0:T(8,128)S(1)}) custom-call(s32[5376]{0:T(1024)S(1)} %reshape.80.refs_0_, bf16[768,128]{1,0:T(8,128)(2,1)S(1)} %bitcast.45, bf16[3072,128]{1,0:T(8,128)(2,1)S(1)} %pad_maximum_fusion.1.refs_2_), custom_call_target="tpu_custom_call" | custom-call | tf_op jit(solution)/shard_map/pallas_call | solution.py:352
  65.5 4.7 %all-to-all-start.1 = ((f16[32,24,896]{2,1,0:T(8,128)(2,1)}), f16[32,24,896]{2,1,0:T(8,128)(2,1)}, u32[]{:S(2)}, u32[]{:S(2)}) async-start(f16[32,24,896]{2,1,0:T(8,128)(2,1)} %pad_maximum_fusion), calls=%async_computation.1 | async-start | bytes 2752512 | tf_op jit(solution)/shard_map/all_to_all | solution.py:42
  70.2 20.2 %all-to-all-done.1 = f16[32,24,896]{2,1,0:T(8,128)(2,1)} async-done(((f16[32,24,896]{2,1,0:T(8,128)(2,1)}), f16[32,24,896]{2,1,0:T(8,128)(2,1)}, u32[]{:S(2)}, u32[]{:S(2)}) %all-to-all-start.1) | async-done | bytes 1376288 | tf_op jit(solution)/shard_map/all_to_all | solution.py:42
  90.4 1.5 convert_reduce_fusion.refs_1_
  93.2 15.1 %all_to_all.26 = bf16[32,24,128]{2,1,0:T(8,128)(2,1)} all-to-all(bf16[32,24,128]{2,1,0:T(8,128)(2,1)S(1)} %get-tuple-element.50), channel_id=1, replica_groups=mesh['xl'=2,'co'=2,'xh'=2,'y'=4,'z'=4] {'xh','y','z'}, dimensions={0} | all-to-all | bytes 393216 | tf_op jit(solution)/shard_map/all_to_all | solution.py:42
  108.3 3.9 %all-to-all-start.2 = ((bf16[32,24,768]{2,1,0:T(8,128)(2,1)}), bf16[32,24,768]{2,1,0:T(8,128)(2,1)S(1)}, u32[]{:S(2)}, u32[]{:S(2)}) async-start(bf16[32,24,768]{2,1,0:T(8,128)(2,1)} %copy-done), calls=%async_computation.2 | async-start | bytes 2359296 | tf_op jit(solution)/shard_map/all_to_all | solution.py:42
  113.1 7.2 %shard_map.132 = (bf16[3072,128]{1,0:T(8,128)(2,1)S(1)}, f32[768,128]{1,0:T(8,128)S(1)}) custom-call(s32[5376]{0:T(1024)S(1)} %reshape.80.refs_0_, bf16[768,128]{1,0:T(8,128)(2,1)S(1)} %bitcast.48, bf16[768,128]{1,0:T(8,128)(2,1)S(1)} %bitcast.46, bf16[7,768,128]{2,1,0:T(8,128)(2,1)S(1)} %get-tuple-element.51.refs_3_), custom_call_target="tpu_custom_call" | custom-call | tf_op jit(solution)/shard_map/pallas_call | solution.py:384
  120.4 2.2 %collective-permute-start.9 = (bf16[2,768,128]{2,1,0:T(8,128)(2,1)S(1)}, bf16[2,768,128]{2,1,0:T(8,128)(2,1)S(1)}, u32[]{:S(2)}, u32[]{:S(2)}) collective-permute-start(bf16[2,768,128]{2,1,0:T(8,128)(2,1)S(1)} %pad_maximum_fusion.2), channel_id=1, source_target_pairs={{0,32},{32,0},{1,33},{33,1},{2,34},{34,2},{3,35},{35,3},{4,36},{36... | collective-permute-start | bytes 1179656 | tf_op jit(solution)/shard_map/ppermute | solution.py:22
  124.9 5.6 %collective-permute-done.10.far_ref = bf16[768,128]{1,0:T(8,128)(2,1)S(1)} collective-permute-done((bf16[768,128]{1,0:T(8,128)(2,1)S(1)}, bf16[768,128]{1,0:T(8,128)(2,1)S(1)}, u32[]{:S(2)}, u32[]{:S(2)}) %collective-permute-start.10) | collective-permute-done | bytes 196640 | tf_op jit(solution)/shard_map/ppermute | solution.py:26
  132.3 19.3 %all_to_all.27.sums = bf16[32,2,24,128]{3,2,1,0:T(8,128)(2,1)S(1)} all-to-all(bf16[32,2,24,128]{3,2,1,0:T(8,128)(2,1)S(1)} %shard_map.133), channel_id=1, replica_groups=mesh['xl'=2,'co'=2,'xh'=2,'y'=4,'z'=4] {'xh','y','z'}, dimensions={0} | all-to-all | bytes 786432 | tf_op jit(solution)/shard_map/all_to_all | solution.py:42
  152.6 2.8 %collective-permute-start.12 = (bf16[48,1024]{1,0:T(8,128)(2,1)S(1)}, bf16[48,1024]{1,0:T(8,128)(2,1)S(1)}, u32[]{:S(2)}, u32[]{:S(2)}) collective-permute-start(bf16[48,1024]{1,0:T(8,128)(2,1)S(1)} %get-tuple-element.59), channel_id=1, source_target_pairs={{0,32},{32,0},{1,33},{33,1},{2,34},{34,2},{3,35},{35,3},{4,36},{36... | collective-permute-start | bytes 294920 | tf_op jit(solution)/shard_map/ppermute | solution.py:22
  157.8 5.5 %collective-permute-done.11 = f32[104,128]{1,0:T(8,128)S(1)} collective-permute-done((f32[104,128]{1,0:T(8,128)S(1)}, f32[104,128]{1,0:T(8,128)S(1)}, u32[]{:S(2)}, u32[]{:S(2)}) %collective-permute-start.11) | collective-permute-done | bytes 53280 | tf_op jit(solution)/shard_map/ppermute | solution.py:31
  163.4 5.3 %shard_map.135 = (bf16[2,48,4096]{2,1,0:T(8,128)(2,1)S(1)}, bf16[2,48,4096]{2,1,0:T(8,128)(2,1)S(1)}) custom-call(bf16[48,1024]{1,0:T(8,128)(2,1)S(1)} %get-tuple-element.63.x0, bf16[48,1024]{1,0:T(8,128)(2,1)S(1)} %collective-permute-done.12.x1, bf16[48,1024]{1,0:T(8,128)(2,1)S(1)} %collective-permute-done.13.x2, ...), custom_call_target="tpu_custom_call" | custom-call | tf_op jit(solution)/shard_map/pallas_call | solution.py:428
  170.1 2.3 %collective-permute-start.17 = (f32[104,128]{1,0:T(8,128)S(1)}, f32[104,128]{1,0:T(8,128)S(1)}, u32[]{:S(2)}, u32[]{:S(2)}) collective-permute-start(f32[104,128]{1,0:T(8,128)S(1)} %add.72), channel_id=1, source_target_pairs={{4,0},{8,4},{12,8},{0,12},{5,1},{9,5},{13,9},{1,13},{6,2},{10,6},{... | collective-permute-start | bytes 159752 | tf_op jit(solution)/shard_map/ppermute | solution.py:31
  174.3 2.6 %collective-permute-done.16 = f32[104,128]{1,0:T(8,128)S(1)} collective-permute-done((f32[104,128]{1,0:T(8,128)S(1)}, f32[104,128]{1,0:T(8,128)S(1)}, u32[]{:S(2)}, u32[]{:S(2)}) %collective-permute-start.16) | collective-permute-done | bytes 53280 | tf_op jit(solution)/shard_map/ppermute | solution.py:31
  177.2 2.7 %collective-permute-start.20 = (f32[104,128]{1,0:T(8,128)S(1)}, f32[104,128]{1,0:T(8,128)S(1)}, u32[]{:S(2)}, u32[]{:S(2)}) collective-permute-start(f32[104,128]{1,0:T(8,128)S(1)} %add_add_fusion.1), channel_id=1, source_target_pairs={{1,0},{2,1},{3,2},{0,3},{5,4},{6,5},{7,6},{4,7},{9,8},{10,9},{11,1... | collective-permute-start | bytes 159752 | tf_op jit(solution)/shard_map/ppermute | solution.py:31
  180.0 1.5 collective-permute-start.23
  181.4 2.9 %collective-permute-done.19 = f32[104,128]{1,0:T(8,128)S(1)} collective-permute-done((f32[104,128]{1,0:T(8,128)S(1)}, f32[104,128]{1,0:T(8,128)S(1)}, u32[]{:S(2)}, u32[]{:S(2)}) %collective-permute-start.19) | collective-permute-done | bytes 53280 | tf_op jit(solution)/shard_map/ppermute | solution.py:31
  184.5 4.8 %collective-permute-start.26 = (f32[104,128]{1,0:T(8,128)S(1)}, f32[104,128]{1,0:T(8,128)S(1)}, u32[]{:S(2)}, u32[]{:S(2)}) collective-permute-start(f32[104,128]{1,0:T(8,128)S(1)} %add_add_fusion.refs_0_), channel_id=1, source_target_pairs={{0,96},{32,64},{64,32},{96,0},{1,97},{33,65},{65,33},{97,1},{2,98}... | collective-permute-start | bytes 159752 | tf_op jit(solution)/shard_map/ppermute | solution.py:452
  189.3 1.5 collective-permute-start.25
  191.7 2.0 %collective-permute-done.25.refs_2_ = f32[104,128]{1,0:T(8,128)S(1)} collective-permute-done((f32[104,128]{1,0:T(8,128)S(1)}, f32[104,128]{1,0:T(8,128)S(1)}, u32[]{:S(2)}, u32[]{:S(2)}) %collective-permute-start.25) | collective-permute-done | bytes 53280 | tf_op jit(solution)/shard_map/ppermute | solution.py:26
  (82 shorter events, 23.9 us)
Async XLA Ops:
  0.6 10.7 %collective-permute-start.1 = (bf16[48,4096]{1,0:T(8,128)(2,1)}, bf16[48,4096]{1,0:T(8,128)(2,1)S(1)}, u32[]{:S(2)}, u32[]{:S(2)}) collective-permute-start(bf16[48,4096]{1,0:T(8,128)(2,1)} %bitcast.49), channel_id=1, source_target_pairs={{0,64},{64,0},{1,65},{65,1},{2,66},{66,2},{3,67},{67,3},{4,68},{68... | collective-permute-start | bytes 1179656 | tf_op jit(solution)/shard_map/ppermute | solution.py:26
  2.8 12.0 %collective-permute-start = (bf16[48,4096]{1,0:T(8,128)(2,1)}, bf16[48,4096]{1,0:T(8,128)(2,1)S(1)}, u32[]{:S(2)}, u32[]{:S(2)}) collective-permute-start(bf16[48,4096]{1,0:T(8,128)(2,1)} %bitcast.50), channel_id=1, source_target_pairs={{0,32},{32,0},{1,33},{33,1},{2,34},{34,2},{3,35},{35,3},{4,36},{36... | collective-permute-start | bytes 1179656 | tf_op jit(solution)/shard_map/ppermute | solution.py:22
  11.3 3.5 %collective-permute-start.2 = (bf16[48,4096]{1,0:T(8,128)(2,1)S(1)}, bf16[48,4096]{1,0:T(8,128)(2,1)S(1)}, u32[]{:S(2)}, u32[]{:S(2)}) collective-permute-start(bf16[48,4096]{1,0:T(8,128)(2,1)S(1)} %collective-permute-done.1.x2), channel_id=1, source_target_pairs={{0,32},{32,0},{1,33},{33,1},{2,34},{34,2},{3,35},{35,3},{4,36},{36... | collective-permute-start | bytes 1179656 | tf_op jit(solution)/shard_map/ppermute | solution.py:22
  15.8 11.0 %copy-start.9 = (f32[4096]{0:T(1024)S(1)}, f32[4096]{0:T(1024)}, u32[]{:S(2)}) copy-start(f32[4096]{0:T(1024)} %param.12) | copy-start | bytes 49156
  19.7 2.3 %collective-permute-start.3 = (bf16[48,1024]{1,0:T(8,128)(2,1)S(1)}, bf16[48,1024]{1,0:T(8,128)(2,1)S(1)}, u32[]{:S(2)}, u32[]{:S(2)}) collective-permute-start(bf16[48,1024]{1,0:T(8,128)(2,1)S(1)} %get-tuple-element.43), channel_id=1, source_target_pairs={{0,32},{32,0},{1,33},{33,1},{2,34},{34,2},{3,35},{35,3},{4,36},{36... | collective-permute-start | bytes 294920 | tf_op jit(solution)/shard_map/ppermute | solution.py:22
  19.8 4.0 %collective-permute-start.4 = (bf16[48,1024]{1,0:T(8,128)(2,1)S(1)}, bf16[48,1024]{1,0:T(8,128)(2,1)S(1)}, u32[]{:S(2)}, u32[]{:S(2)}) collective-permute-start(bf16[48,1024]{1,0:T(8,128)(2,1)S(1)} %get-tuple-element.44), channel_id=1, source_target_pairs={{0,64},{64,0},{1,65},{65,1},{2,66},{66,2},{3,67},{67,3},{4,68},{68... | collective-permute-start | bytes 294920 | tf_op jit(solution)/shard_map/ppermute | solution.py:26
  21.3 5.4 %collective-permute-start.5 = (bf16[48,1024]{1,0:T(8,128)(2,1)S(1)}, bf16[48,1024]{1,0:T(8,128)(2,1)S(1)}, u32[]{:S(2)}, u32[]{:S(2)}) collective-permute-start(bf16[48,1024]{1,0:T(8,128)(2,1)S(1)} %get-tuple-element.45), channel_id=1, source_target_pairs={{0,96},{32,64},{64,32},{96,0},{1,97},{33,65},{65,33},{97,1},{2,98}... | collective-permute-start | bytes 294920 | tf_op jit(solution)/shard_map/ppermute | solution.py:306
  27.2 21.7 %copy-start.2 = (f32[48,4096]{1,0:T(8,128)}, f32[48,4096]{1,0:T(8,128)S(1)}, u32[]{:S(2)}) copy-start(f32[48,4096]{1,0:T(8,128)S(1)} %get-tuple-element.54.pooled) | copy-start | bytes 2359300
  48.9 4.6 %collective-permute-start.7 = (bf16[768,128]{1,0:T(8,128)(2,1)S(1)}, bf16[768,128]{1,0:T(8,128)(2,1)S(1)}, u32[]{:S(2)}, u32[]{:S(2)}) collective-permute-start(bf16[768,128]{1,0:T(8,128)(2,1)S(1)} %bitcast.40), channel_id=1, source_target_pairs={{0,64},{64,0},{1,65},{65,1},{2,66},{66,2},{3,67},{67,3},{4,68},{68... | collective-permute-start | bytes 589832 | tf_op jit(solution)/shard_map/ppermute | solution.py:26
  49.9 7.3 %collective-permute-start.6 = (bf16[768,128]{1,0:T(8,128)(2,1)S(1)}, bf16[768,128]{1,0:T(8,128)(2,1)S(1)}, u32[]{:S(2)}, u32[]{:S(2)}) collective-permute-start(bf16[768,128]{1,0:T(8,128)(2,1)S(1)} %bitcast.41), channel_id=1, source_target_pairs={{0,32},{32,0},{1,33},{33,1},{2,34},{34,2},{3,35},{35,3},{4,36},{36... | collective-permute-start | bytes 589832 | tf_op jit(solution)/shard_map/ppermute | solution.py:22
  53.5 4.3 %collective-permute-start.8 = (bf16[768,128]{1,0:T(8,128)(2,1)S(1)}, bf16[768,128]{1,0:T(8,128)(2,1)S(1)}, u32[]{:S(2)}, u32[]{:S(2)}) collective-permute-start(bf16[768,128]{1,0:T(8,128)(2,1)S(1)} %collective-permute-done.7), channel_id=1, source_target_pairs={{0,32},{32,0},{1,33},{33,1},{2,34},{34,2},{3,35},{35,3},{4,36},{36... | collective-permute-start | bytes 589832 | tf_op jit(solution)/shard_map/ppermute | solution.py:22
  65.5 24.9 %all-to-all-start.1 = ((f16[32,24,896]{2,1,0:T(8,128)(2,1)}), f16[32,24,896]{2,1,0:T(8,128)(2,1)}, u32[]{:S(2)}, u32[]{:S(2)}) async-start(f16[32,24,896]{2,1,0:T(8,128)(2,1)} %pad_maximum_fusion), calls=%async_computation.1 | async-start | bytes 2752512 | tf_op jit(solution)/shard_map/all_to_all | solution.py:42
  108.3 22.2 %all-to-all-start.2 = ((bf16[32,24,768]{2,1,0:T(8,128)(2,1)}), bf16[32,24,768]{2,1,0:T(8,128)(2,1)S(1)}, u32[]{:S(2)}, u32[]{:S(2)}) async-start(bf16[32,24,768]{2,1,0:T(8,128)(2,1)} %copy-done), calls=%async_computation.2 | async-start | bytes 2359296 | tf_op jit(solution)/shard_map/all_to_all | solution.py:42
  120.4 3.6 %collective-permute-start.9 = (bf16[2,768,128]{2,1,0:T(8,128)(2,1)S(1)}, bf16[2,768,128]{2,1,0:T(8,128)(2,1)S(1)}, u32[]{:S(2)}, u32[]{:S(2)}) collective-permute-start(bf16[2,768,128]{2,1,0:T(8,128)(2,1)S(1)} %pad_maximum_fusion.2), channel_id=1, source_target_pairs={{0,32},{32,0},{1,33},{33,1},{2,34},{34,2},{3,35},{35,3},{4,36},{36... | collective-permute-start | bytes 1179656 | tf_op jit(solution)/shard_map/ppermute | solution.py:22
  124.1 6.4 %collective-permute-start.10 = (bf16[768,128]{1,0:T(8,128)(2,1)S(1)}, bf16[768,128]{1,0:T(8,128)(2,1)S(1)}, u32[]{:S(2)}, u32[]{:S(2)}) collective-permute-start(bf16[768,128]{1,0:T(8,128)(2,1)S(1)} %fusion.1), channel_id=1, source_target_pairs={{0,64},{64,0},{1,65},{65,1},{2,66},{66,2},{3,67},{67,3},{4,68},{68... | collective-permute-start | bytes 589832 | tf_op jit(solution)/shard_map/ppermute | solution.py:26
  131.5 20.1 %copy-start.3 = (f32[48,4096]{1,0:T(8,128)S(1)}, f32[48,4096]{1,0:T(8,128)}, u32[]{:S(2)}) copy-start(f32[48,4096]{1,0:T(8,128)} %copy-done.2) | copy-start | bytes 2359300
  152.6 10.8 %collective-permute-start.12 = (bf16[48,1024]{1,0:T(8,128)(2,1)S(1)}, bf16[48,1024]{1,0:T(8,128)(2,1)S(1)}, u32[]{:S(2)}, u32[]{:S(2)}) collective-permute-start(bf16[48,1024]{1,0:T(8,128)(2,1)S(1)} %get-tuple-element.59), channel_id=1, source_target_pairs={{0,32},{32,0},{1,33},{33,1},{2,34},{34,2},{3,35},{35,3},{4,36},{36... | collective-permute-start | bytes 294920 | tf_op jit(solution)/shard_map/ppermute | solution.py:22
  155.4 8.0 %collective-permute-start.13 = (bf16[48,1024]{1,0:T(8,128)(2,1)S(1)}, bf16[48,1024]{1,0:T(8,128)(2,1)S(1)}, u32[]{:S(2)}, u32[]{:S(2)}) collective-permute-start(bf16[48,1024]{1,0:T(8,128)(2,1)S(1)} %get-tuple-element.60), channel_id=1, source_target_pairs={{0,64},{64,0},{1,65},{65,1},{2,66},{66,2},{3,67},{67,3},{4,68},{68... | collective-permute-start | bytes 294920 | tf_op jit(solution)/shard_map/ppermute | solution.py:26
  156.0 7.4 %collective-permute-start.14 = (bf16[48,1024]{1,0:T(8,128)(2,1)S(1)}, bf16[48,1024]{1,0:T(8,128)(2,1)S(1)}, u32[]{:S(2)}, u32[]{:S(2)}) collective-permute-start(bf16[48,1024]{1,0:T(8,128)(2,1)S(1)} %get-tuple-element.61), channel_id=1, source_target_pairs={{0,96},{32,64},{64,32},{96,0},{1,97},{33,65},{65,33},{97,1},{2,98}... | collective-permute-start | bytes 294920 | tf_op jit(solution)/shard_map/ppermute | solution.py:425
  157.2 6.2 %collective-permute-start.11 = (f32[104,128]{1,0:T(8,128)S(1)}, f32[104,128]{1,0:T(8,128)S(1)}, u32[]{:S(2)}, u32[]{:S(2)}) collective-permute-start(f32[104,128]{1,0:T(8,128)S(1)} %get-tuple-element.57), channel_id=1, source_target_pairs={{16,0},{0,16},{17,1},{1,17},{18,2},{2,18},{19,3},{3,19},{20,4},{4,... | collective-permute-start | bytes 159752 | tf_op jit(solution)/shard_map/ppermute | solution.py:31
  168.8 8.2 %collective-permute-start.15 = (bf16[2,48,4096]{2,1,0:T(8,128)(2,1)S(1)}, bf16[2,48,4096]{2,1,0:T(8,128)(2,1)S(1)}, u32[]{:S(2)}, u32[]{:S(2)}) collective-permute-start(bf16[2,48,4096]{2,1,0:T(8,128)(2,1)S(1)} %get-tuple-element.70), channel_id=1, source_target_pairs={{0,32},{32,0},{1,33},{33,1},{2,34},{34,2},{3,35},{35,3},{4,36},{36... | collective-permute-start | bytes 2359304 | tf_op jit(solution)/shard_map/ppermute | solution.py:22
  169.7 4.6 %collective-permute-start.18 = (f32[104,128]{1,0:T(8,128)S(1)}, f32[104,128]{1,0:T(8,128)S(1)}, u32[]{:S(2)}, u32[]{:S(2)}) collective-permute-start(f32[104,128]{1,0:T(8,128)S(1)} %add.72), channel_id=1, source_target_pairs={{12,0},{0,4},{4,8},{8,12},{13,1},{1,5},{5,9},{9,13},{14,2},{2,6},{... | collective-permute-start | bytes 159752 | tf_op jit(solution)/shard_map/ppermute | solution.py:31
  170.1 4.2 %collective-permute-start.17 = (f32[104,128]{1,0:T(8,128)S(1)}, f32[104,128]{1,0:T(8,128)S(1)}, u32[]{:S(2)}, u32[]{:S(2)}) collective-permute-start(f32[104,128]{1,0:T(8,128)S(1)} %add.72), channel_id=1, source_target_pairs={{4,0},{8,4},{12,8},{0,12},{5,1},{9,5},{13,9},{1,13},{6,2},{10,6},{... | collective-permute-start | bytes 159752 | tf_op jit(solution)/shard_map/ppermute | solution.py:31
  172.4 4.5 %collective-permute-start.16 = (f32[104,128]{1,0:T(8,128)S(1)}, f32[104,128]{1,0:T(8,128)S(1)}, u32[]{:S(2)}, u32[]{:S(2)}) collective-permute-start(f32[104,128]{1,0:T(8,128)S(1)} %add.72), channel_id=1, source_target_pairs={{8,0},{12,4},{0,8},{4,12},{9,1},{13,5},{1,9},{5,13},{10,2},{14,6},... | collective-permute-start | bytes 159752 | tf_op jit(solution)/shard_map/ppermute | solution.py:31
  177.1 4.3 %collective-permute-start.21 = (f32[104,128]{1,0:T(8,128)S(1)}, f32[104,128]{1,0:T(8,128)S(1)}, u32[]{:S(2)}, u32[]{:S(2)}) collective-permute-start(f32[104,128]{1,0:T(8,128)S(1)} %add_add_fusion.1), channel_id=1, source_target_pairs={{3,0},{0,1},{1,2},{2,3},{7,4},{4,5},{5,6},{6,7},{11,8},{8,9},{9,10... | collective-permute-start | bytes 159752 | tf_op jit(solution)/shard_map/ppermute | solution.py:31
  177.2 4.3 %collective-permute-start.20 = (f32[104,128]{1,0:T(8,128)S(1)}, f32[104,128]{1,0:T(8,128)S(1)}, u32[]{:S(2)}, u32[]{:S(2)}) collective-permute-start(f32[104,128]{1,0:T(8,128)S(1)} %add_add_fusion.1), channel_id=1, source_target_pairs={{1,0},{2,1},{3,2},{0,3},{5,4},{6,5},{7,6},{4,7},{9,8},{10,9},{11,1... | collective-permute-start | bytes 159752 | tf_op jit(solution)/shard_map/ppermute | solution.py:31
  179.8 4.5 %collective-permute-start.19 = (f32[104,128]{1,0:T(8,128)S(1)}, f32[104,128]{1,0:T(8,128)S(1)}, u32[]{:S(2)}, u32[]{:S(2)}) collective-permute-start(f32[104,128]{1,0:T(8,128)S(1)} %add_add_fusion.1), channel_id=1, source_target_pairs={{2,0},{3,1},{0,2},{1,3},{6,4},{7,5},{4,6},{5,7},{10,8},{11,9},{8,1... | collective-permute-start | bytes 159752 | tf_op jit(solution)/shard_map/ppermute | solution.py:31
  179.9 4.6 %collective-permute-start.22 = (bf16[48,2048]{1,0:T(8,128)(2,1)S(1)}, bf16[48,2048]{1,0:T(8,128)(2,1)S(1)}, u32[]{:S(2)}, u32[]{:S(2)}) collective-permute-start(bf16[48,2048]{1,0:T(8,128)(2,1)S(1)} %get-tuple-element.86), channel_id=1, source_target_pairs={{0,64},{64,0},{1,65},{65,1},{2,66},{66,2},{3,67},{67,3},{4,68},{68... | collective-permute-start | bytes 589832 | tf_op jit(solution)/shard_map/ppermute | solution.py:26
  180.0 10.8 %collective-permute-start.23 = (bf16[48,2048]{1,0:T(8,128)(2,1)S(1)}, bf16[48,2048]{1,0:T(8,128)(2,1)S(1)}, u32[]{:S(2)}, u32[]{:S(2)}) collective-permute-start(bf16[48,2048]{1,0:T(8,128)(2,1)S(1)} %get-tuple-element.87), channel_id=1, source_target_pairs={{0,64},{64,0},{1,65},{65,1},{2,66},{66,2},{3,67},{67,3},{4,68},{68... | collective-permute-start | bytes 589832 | tf_op jit(solution)/shard_map/ppermute | solution.py:26
  184.5 7.2 %collective-permute-start.26 = (f32[104,128]{1,0:T(8,128)S(1)}, f32[104,128]{1,0:T(8,128)S(1)}, u32[]{:S(2)}, u32[]{:S(2)}) collective-permute-start(f32[104,128]{1,0:T(8,128)S(1)} %add_add_fusion.refs_0_), channel_id=1, source_target_pairs={{0,96},{32,64},{64,32},{96,0},{1,97},{33,65},{65,33},{97,1},{2,98}... | collective-permute-start | bytes 159752 | tf_op jit(solution)/shard_map/ppermute | solution.py:452
  189.3 4.4 %collective-permute-start.25 = (f32[104,128]{1,0:T(8,128)S(1)}, f32[104,128]{1,0:T(8,128)S(1)}, u32[]{:S(2)}, u32[]{:S(2)}) collective-permute-start(f32[104,128]{1,0:T(8,128)S(1)} %add_add_fusion.refs_0_), channel_id=1, source_target_pairs={{0,64},{64,0},{1,65},{65,1},{2,66},{66,2},{3,67},{67,3},{4,68},{68... | collective-permute-start | bytes 159752 | tf_op jit(solution)/shard_map/ppermute | solution.py:26
  190.7 2.9 %collective-permute-start.24 = (f32[104,128]{1,0:T(8,128)S(1)}, f32[104,128]{1,0:T(8,128)S(1)}, u32[]{:S(2)}, u32[]{:S(2)}) collective-permute-start(f32[104,128]{1,0:T(8,128)S(1)} %add_add_fusion.refs_0_), channel_id=1, source_target_pairs={{0,32},{32,0},{1,33},{33,1},{2,34},{34,2},{3,35},{35,3},{4,36},{36... | collective-permute-start | bytes 159752 | tf_op jit(solution)/shard_map/ppermute | solution.py:22
  (7 other events, 30.4 us)

commit v8 on v7

--- a/solution.py
+++ b/solution.py
@@ -283,6 +283,16 @@
     attn_rows = attn.reshape(row_count, width)
     far_rows = swap_chip(attn_rows)
     near_rows = swap_core(attn_rows)
+    half = LANES // 2
+    fill = ((0, 1), (0, half - tok_rows))
+    requests = jnp.concatenate(
+        [jnp.pad(neg_owner.T, fill), jnp.pad(neg_row.T, fill)], axis=1
+    ).astype(BF16)
+    task_onehot = (jnp.arange(task_bias.shape[0]) == task_ids[0]).astype(F32)
+    bias_row = jnp.sum(task_onehot[:, None] * task_bias, axis=0, keepdims=True)
+    far_rows, near_rows, requests, bias_row = lax.optimization_barrier(
+        (far_rows, near_rows, requests, bias_row)
+    )
 
 
     chunks = 8
@@ -306,13 +316,6 @@
         lax.ppermute(columns[3], GRP, DIAGONAL),
     ]
 
-    half = LANES // 2
-    fill = ((0, 1), (0, half - tok_rows))
-    requests = jnp.concatenate(
-        [jnp.pad(neg_owner.T, fill), jnp.pad(neg_row.T, fill)], axis=1
-    ).astype(BF16)
-    task_onehot = (jnp.arange(task_bias.shape[0]) == task_ids[0]).astype(F32)
-    bias_row = jnp.sum(task_onehot[:, None] * task_bias, axis=0, keepdims=True)
     place = me.astype(jnp.int32).reshape(1)
     rows_f32 = jax.ShapeDtypeStruct((row_count, LANES), F32)
     own_spread, pooled, inv_rms, inv_norm = pl.pallas_call(
@@ -437,11 +440,10 @@
     vectors = sum_over(vectors, "y")
     crossed = swap_core(send)
     far_sum = (keep[1].astype(F32) + crossed[1].astype(F32)).astype(BF16)
-    far_sum, vectors = lax.optimization_barrier((far_sum, vectors))
-    vectors = sum_over(vectors, "z")
     first = swap_chip(far_sum[:, : width // 2])
     second = swap_chip(far_sum[:, width // 2 :])
     vectors, first = lax.optimization_barrier((vectors, first))
+    vectors = sum_over(vectors, "z")
     far_sum = jnp.concatenate([first, second], axis=1).astype(F32)
     grad_attn = keep[0].astype(F32) + crossed[0].astype(F32) + far_sum
 

time: 195 us -> 195 us (level)
  waiting for transfers between devices: 55.4 us -> 59.1 us
  starting transfers between devices: 43.9 us -> 40.2 us
    ppermute x8, starting transfers between devices: 8.96 us -> 5.52 us  [swap_chip(): return lax.ppermute(values, 'xl', SWAP)]
  transfers between devices with their start and end apart: 29 -> 29, of which waited for: 14 -> 16; matrix products, arithmetic and copies ran while one was open for 2% -> 2% of each run, Pallas kernels for 4% -> 4%
where the time goes in v8:
time: 195 us; the launch traced here: 194 us
  waiting for transfers between devices  59.1 us (30%)
  blocking collectives  56 us (29%)
  starting transfers between devices  40.2 us (21%)
  Pallas kernels  25.9 us (13%)
  other arithmetic  6.27 us (3%)
  local copies, waits for them, and re-layouts  4.82 us (2%)
    all_to_all x3, blocking collectives, exchange(): return lax.all_to_all(values, axes, split_axis=0, concat_axis=0, tiled=True)  56 us
    all_to_all x2, waiting for transfers between devices, exchange(): return lax.all_to_all(values, axes, split_axis=0, concat_axis=0, tiled=True)  20.2 us
    ppermute x8, waiting for transfers between devices, swap_chip(): return lax.ppermute(values, 'xl', SWAP)  20.1 us
    ppermute x9, starting transfers between devices, swap_core(): return lax.ppermute(values, 'co', SWAP)  14.6 us
    ppermute x7, waiting for transfers between devices, from_ahead(): lax.ppermute(values, axis, [((i + step) % size, i) for i in range(size)])  13.2 us
    all_to_all x2, starting transfers between devices, exchange(): return lax.all_to_all(values, axes, split_axis=0, concat_axis=0, tiled=True)  8.63 us
    pallas_call x1, Pallas kernels, local(): pl.pallas_call(lambda *refs: scatter_kernel(hard_count, tok_rows, *refs),...  7.19 us
    pallas_call x1, Pallas kernels, local(): pl.pallas_call(lambda *refs: gather_kernel(hard_count, tok_rows, *refs),...  6.24 us
  transfers between devices with their start and end apart: 29, of which 16 were waited for; matrix products, arithmetic and copies ran while one was open for 2% of the time, Pallas kernels for 4%

profile of v8, /device:TPU:1, one launch (start us, length us, event | category | flops | bytes accessed | tf_op | source)
XLA Modules:
  0.0 194.4 jit_solution(17909421269840267456)
XLA Ops:
  0.6 1.5 collective-permute-start.1
  5.9 7.1 %collective-permute-done.x2 = bf16[48,4096]{1,0:T(8,128)(2,1)S(1)} collective-permute-done((bf16[48,4096]{1,0:T(8,128)(2,1)}, bf16[48,4096]{1,0:T(8,128)(2,1)S(1)}, u32[]{:S(2)}, u32[]{:S(2)}) %collective-permute-start) | collective-permute-done | bytes 393248 | tf_op jit(solution)/shard_map/ppermute | solution.py:26
  16.2 3.9 %shard_map.128 = (bf16[48,1024]{1,0:T(8,128)(2,1)S(1)}, bf16[48,1024]{1,0:T(8,128)(2,1)S(1)}, bf16[48,1024]{1,0:T(8,128)(2,1)S(1)}, bf16[48,1024]{1,0:T(8,128)(2,1)S(1)}) custom-call(bf16[48,4096]{1,0:T(8,128)(2,1)S(1)} %bitcast.51, bf16[48,4096]{1,0:T(8,128)(2,1)S(1)} %collective-permute-done.1.x1, bf16[48,4096]{1,0:T(8,128)(2,1)S(1)} %collective-permute-done.x2, ...), custom_call_target="tpu_custom_call" | custom-call | tf_op jit(solution)/shard_map/pallas_call | solution.py:304
  22.4 2.5 %collective-permute-done.4.x2 = bf16[48,1024]{1,0:T(8,128)(2,1)S(1)} collective-permute-done((bf16[48,1024]{1,0:T(8,128)(2,1)S(1)}, bf16[48,1024]{1,0:T(8,128)(2,1)S(1)}, u32[]{:S(2)}, u32[]{:S(2)}) %collective-permute-start.4) | collective-permute-done | bytes 98336 | tf_op jit(solution)/shard_map/ppermute | solution.py:26
  24.9 2.4 %collective-permute-done.5.x3 = bf16[48,1024]{1,0:T(8,128)(2,1)S(1)} collective-permute-done((bf16[48,1024]{1,0:T(8,128)(2,1)S(1)}, bf16[48,1024]{1,0:T(8,128)(2,1)S(1)}, u32[]{:S(2)}, u32[]{:S(2)}) %collective-permute-start.5) | collective-permute-done | bytes 98336 | tf_op jit(solution)/shard_map/ppermute | solution.py:316
  27.7 21.6 %all_to_all.25 = bf16[32,56,128]{2,1,0:T(8,128)(2,1)S(1)} all-to-all(bf16[32,56,128]{2,1,0:T(8,128)(2,1)S(1)} %get-tuple-element.52.spread), channel_id=1, replica_groups=mesh['xl'=2,'co'=2,'xh'=2,'y'=4,'z'=4] {'xh','y','z'}, dimensions={0} | all-to-all | bytes 917504 | tf_op jit(solution)/shard_map/all_to_all | solution.py:42
  49.8 2.5 %collective-permute-start.6 = (bf16[768,128]{1,0:T(8,128)(2,1)S(1)}, bf16[768,128]{1,0:T(8,128)(2,1)S(1)}, u32[]{:S(2)}, u32[]{:S(2)}) collective-permute-start(bf16[768,128]{1,0:T(8,128)(2,1)S(1)} %bitcast.41), channel_id=1, source_target_pairs={{0,32},{32,0},{1,33},{33,1},{2,34},{34,2},{3,35},{35,3},{4,36},{36... | collective-permute-start | bytes 589832 | tf_op jit(solution)/shard_map/ppermute | solution.py:22
  52.5 1.5 collective-permute-done.7
  54.0 3.3 %collective-permute-start.8 = (bf16[768,128]{1,0:T(8,128)(2,1)S(1)}, bf16[768,128]{1,0:T(8,128)(2,1)S(1)}, u32[]{:S(2)}, u32[]{:S(2)}) collective-permute-start(bf16[768,128]{1,0:T(8,128)(2,1)S(1)} %collective-permute-done.7), channel_id=1, source_target_pairs={{0,32},{32,0},{1,33},{33,1},{2,34},{34,2},{3,35},{35,3},{4,36},{36... | collective-permute-start | bytes 589832 | tf_op jit(solution)/shard_map/ppermute | solution.py:22
  58.4 6.2 %shard_map.130 = (bf16[7,768,128]{2,1,0:T(8,128)(2,1)S(1)}, f32[768,128]{1,0:T(8,128)S(1)}) custom-call(s32[5376]{0:T(1024)S(1)} %reshape.80.refs_0_, bf16[768,128]{1,0:T(8,128)(2,1)S(1)} %bitcast.45, bf16[3072,128]{1,0:T(8,128)(2,1)S(1)} %pad_maximum_fusion.1.refs_2_), custom_call_target="tpu_custom_call" | custom-call | tf_op jit(solution)/shard_map/pallas_call | solution.py:355
  64.7 1.4 pad_maximum_fusion
  66.1 4.7 %all-to-all-start.1 = ((f16[32,24,896]{2,1,0:T(8,128)(2,1)}), f16[32,24,896]{2,1,0:T(8,128)(2,1)}, u32[]{:S(2)}, u32[]{:S(2)}) async-start(f16[32,24,896]{2,1,0:T(8,128)(2,1)} %pad_maximum_fusion), calls=%async_computation.1 | async-start | bytes 2752512 | tf_op jit(solution)/shard_map/all_to_all | solution.py:42
  70.8 20.2 %all-to-all-done.1 = f16[32,24,896]{2,1,0:T(8,128)(2,1)} async-done(((f16[32,24,896]{2,1,0:T(8,128)(2,1)}), f16[32,24,896]{2,1,0:T(8,128)(2,1)}, u32[]{:S(2)}, u32[]{:S(2)}) %all-to-all-start.1) | async-done | bytes 1376288 | tf_op jit(solution)/shard_map/all_to_all | solution.py:42
  91.0 1.5 convert_reduce_fusion.refs_1_
  93.8 15.1 %all_to_all.26 = bf16[32,24,128]{2,1,0:T(8,128)(2,1)} all-to-all(bf16[32,24,128]{2,1,0:T(8,128)(2,1)S(1)} %get-tuple-element.56), channel_id=1, replica_groups=mesh['xl'=2,'co'=2,'xh'=2,'y'=4,'z'=4] {'xh','y','z'}, dimensions={0} | all-to-all | bytes 393216 | tf_op jit(solution)/shard_map/all_to_all | solution.py:42
  108.9 3.9 %all-to-all-start.2 = ((bf16[32,24,768]{2,1,0:T(8,128)(2,1)}), bf16[32,24,768]{2,1,0:T(8,128)(2,1)S(1)}, u32[]{:S(2)}, u32[]{:S(2)}) async-start(bf16[32,24,768]{2,1,0:T(8,128)(2,1)} %copy-done), calls=%async_computation.2 | async-start | bytes 2359296 | tf_op jit(solution)/shard_map/all_to_all | solution.py:42
  113.7 7.2 %shard_map.132 = (bf16[3072,128]{1,0:T(8,128)(2,1)S(1)}, f32[768,128]{1,0:T(8,128)S(1)}) custom-call(s32[5376]{0:T(1024)S(1)} %reshape.80.refs_0_, bf16[768,128]{1,0:T(8,128)(2,1)S(1)} %bitcast.48, bf16[768,128]{1,0:T(8,128)(2,1)S(1)} %bitcast.46, bf16[7,768,128]{2,1,0:T(8,128)(2,1)S(1)} %get-tuple-element.57.refs_3_), custom_call_target="tpu_custom_call" | custom-call | tf_op jit(solution)/shard_map/pallas_call | solution.py:387
  121.1 2.2 %collective-permute-start.9 = (bf16[2,768,128]{2,1,0:T(8,128)(2,1)S(1)}, bf16[2,768,128]{2,1,0:T(8,128)(2,1)S(1)}, u32[]{:S(2)}, u32[]{:S(2)}) collective-permute-start(bf16[2,768,128]{2,1,0:T(8,128)(2,1)S(1)} %pad_maximum_fusion.2), channel_id=1, source_target_pairs={{0,32},{32,0},{1,33},{33,1},{2,34},{34,2},{3,35},{35,3},{4,36},{36... | collective-permute-start | bytes 1179656 | tf_op jit(solution)/shard_map/ppermute | solution.py:22
  125.3 5.8 %collective-permute-done.10.far_ref = bf16[768,128]{1,0:T(8,128)(2,1)S(1)} collective-permute-done((bf16[768,128]{1,0:T(8,128)(2,1)S(1)}, bf16[768,128]{1,0:T(8,128)(2,1)S(1)}, u32[]{:S(2)}, u32[]{:S(2)}) %collective-permute-start.10) | collective-permute-done | bytes 196640 | tf_op jit(solution)/shard_map/ppermute | solution.py:26
  132.9 19.3 %all_to_all.27.sums = bf16[32,2,24,128]{3,2,1,0:T(8,128)(2,1)S(1)} all-to-all(bf16[32,2,24,128]{3,2,1,0:T(8,128)(2,1)S(1)} %shard_map.133), channel_id=1, replica_groups=mesh['xl'=2,'co'=2,'xh'=2,'y'=4,'z'=4] {'xh','y','z'}, dimensions={0} | all-to-all | bytes 786432 | tf_op jit(solution)/shard_map/all_to_all | solution.py:42
  153.2 2.8 %collective-permute-start.12 = (bf16[48,1024]{1,0:T(8,128)(2,1)S(1)}, bf16[48,1024]{1,0:T(8,128)(2,1)S(1)}, u32[]{:S(2)}, u32[]{:S(2)}) collective-permute-start(bf16[48,1024]{1,0:T(8,128)(2,1)S(1)} %get-tuple-element.65), channel_id=1, source_target_pairs={{0,32},{32,0},{1,33},{33,1},{2,34},{34,2},{3,35},{35,3},{4,36},{36... | collective-permute-start | bytes 294920 | tf_op jit(solution)/shard_map/ppermute | solution.py:22
  156.3 1.4 collective-permute-start.14
  158.4 5.3 %collective-permute-done.11 = f32[104,128]{1,0:T(8,128)S(1)} collective-permute-done((f32[104,128]{1,0:T(8,128)S(1)}, f32[104,128]{1,0:T(8,128)S(1)}, u32[]{:S(2)}, u32[]{:S(2)}) %collective-permute-start.11) | collective-permute-done | bytes 53280 | tf_op jit(solution)/shard_map/ppermute | solution.py:31
  163.8 5.3 %shard_map.135 = (bf16[2,48,4096]{2,1,0:T(8,128)(2,1)S(1)}, bf16[2,48,4096]{2,1,0:T(8,128)(2,1)S(1)}) custom-call(bf16[48,1024]{1,0:T(8,128)(2,1)S(1)} %get-tuple-element.69.x0, bf16[48,1024]{1,0:T(8,128)(2,1)S(1)} %collective-permute-done.12.x1, bf16[48,1024]{1,0:T(8,128)(2,1)S(1)} %collective-permute-done.13.x2, ...), custom_call_target="tpu_custom_call" | custom-call | tf_op jit(solution)/shard_map/pallas_call | solution.py:431
  170.5 2.3 %collective-permute-start.17 = (f32[104,128]{1,0:T(8,128)S(1)}, f32[104,128]{1,0:T(8,128)S(1)}, u32[]{:S(2)}, u32[]{:S(2)}) collective-permute-start(f32[104,128]{1,0:T(8,128)S(1)} %add.72), channel_id=1, source_target_pairs={{4,0},{8,4},{12,8},{0,12},{5,1},{9,5},{13,9},{1,13},{6,2},{10,6},{... | collective-permute-start | bytes 159752 | tf_op jit(solution)/shard_map/ppermute | solution.py:31
  173.1 1.6 collective-permute-done.18
  174.7 2.6 %collective-permute-done.16 = f32[104,128]{1,0:T(8,128)S(1)} collective-permute-done((f32[104,128]{1,0:T(8,128)S(1)}, f32[104,128]{1,0:T(8,128)S(1)}, u32[]{:S(2)}, u32[]{:S(2)}) %collective-permute-start.16) | collective-permute-done | bytes 53280 | tf_op jit(solution)/shard_map/ppermute | solution.py:31
  178.8 2.5 %collective-permute-start.22 = (f32[104,128]{1,0:T(8,128)S(1)}, f32[104,128]{1,0:T(8,128)S(1)}, u32[]{:S(2)}, u32[]{:S(2)}) collective-permute-start(f32[104,128]{1,0:T(8,128)S(1)} %add_add_fusion.1), channel_id=1, source_target_pairs={{1,0},{2,1},{3,2},{0,3},{5,4},{6,5},{7,6},{4,7},{9,8},{10,9},{11,1... | collective-permute-start | bytes 159752 | tf_op jit(solution)/shard_map/ppermute | solution.py:31
  182.8 3.0 %collective-permute-done.21 = f32[104,128]{1,0:T(8,128)S(1)} collective-permute-done((f32[104,128]{1,0:T(8,128)S(1)}, f32[104,128]{1,0:T(8,128)S(1)}, u32[]{:S(2)}, u32[]{:S(2)}) %collective-permute-start.21) | collective-permute-done | bytes 53280 | tf_op jit(solution)/shard_map/ppermute | solution.py:31
  185.8 3.5 %collective-permute-start.26 = (f32[104,128]{1,0:T(8,128)S(1)}, f32[104,128]{1,0:T(8,128)S(1)}, u32[]{:S(2)}, u32[]{:S(2)}) collective-permute-start(f32[104,128]{1,0:T(8,128)S(1)} %add_add_fusion.refs_0_), channel_id=1, source_target_pairs={{0,96},{32,64},{64,32},{96,0},{1,97},{33,65},{65,33},{97,1},{2,98}... | collective-permute-start | bytes 159752 | tf_op jit(solution)/shard_map/ppermute | solution.py:454
  189.3 1.5 collective-permute-start.25
  191.8 1.9 collective-permute-done.25.refs_2_
  (82 shorter events, 25.3 us)
Async XLA Ops:
  0.6 5.3 %collective-permute-start.1 = (bf16[48,4096]{1,0:T(8,128)(2,1)}, bf16[48,4096]{1,0:T(8,128)(2,1)S(1)}, u32[]{:S(2)}, u32[]{:S(2)}) collective-permute-start(bf16[48,4096]{1,0:T(8,128)(2,1)} %bitcast.49), channel_id=1, source_target_pairs={{0,32},{32,0},{1,33},{33,1},{2,34},{34,2},{3,35},{35,3},{4,36},{36... | collective-permute-start | bytes 1179656 | tf_op jit(solution)/shard_map/ppermute | solution.py:22
  2.1 10.9 %collective-permute-start = (bf16[48,4096]{1,0:T(8,128)(2,1)}, bf16[48,4096]{1,0:T(8,128)(2,1)S(1)}, u32[]{:S(2)}, u32[]{:S(2)}) collective-permute-start(bf16[48,4096]{1,0:T(8,128)(2,1)} %bitcast.50), channel_id=1, source_target_pairs={{0,64},{64,0},{1,65},{65,1},{2,66},{66,2},{3,67},{67,3},{4,68},{68... | collective-permute-start | bytes 1179656 | tf_op jit(solution)/shard_map/ppermute | solution.py:26
  13.0 2.2 %collective-permute-start.2 = (bf16[48,4096]{1,0:T(8,128)(2,1)S(1)}, bf16[48,4096]{1,0:T(8,128)(2,1)S(1)}, u32[]{:S(2)}, u32[]{:S(2)}) collective-permute-start(bf16[48,4096]{1,0:T(8,128)(2,1)S(1)} %collective-permute-done.x2), channel_id=1, source_target_pairs={{0,32},{32,0},{1,33},{33,1},{2,34},{34,2},{3,35},{35,3},{4,36},{36... | collective-permute-start | bytes 1179656 | tf_op jit(solution)/shard_map/ppermute | solution.py:22
  16.2 11.0 %copy-start.9 = (f32[4096]{0:T(1024)S(1)}, f32[4096]{0:T(1024)}, u32[]{:S(2)}) copy-start(f32[4096]{0:T(1024)} %param.12) | copy-start | bytes 49156
  20.2 2.2 %collective-permute-start.3 = (bf16[48,1024]{1,0:T(8,128)(2,1)S(1)}, bf16[48,1024]{1,0:T(8,128)(2,1)S(1)}, u32[]{:S(2)}, u32[]{:S(2)}) collective-permute-start(bf16[48,1024]{1,0:T(8,128)(2,1)S(1)} %get-tuple-element.47), channel_id=1, source_target_pairs={{0,32},{32,0},{1,33},{33,1},{2,34},{34,2},{3,35},{35,3},{4,36},{36... | collective-permute-start | bytes 294920 | tf_op jit(solution)/shard_map/ppermute | solution.py:22
  20.6 4.3 %collective-permute-start.4 = (bf16[48,1024]{1,0:T(8,128)(2,1)S(1)}, bf16[48,1024]{1,0:T(8,128)(2,1)S(1)}, u32[]{:S(2)}, u32[]{:S(2)}) collective-permute-start(bf16[48,1024]{1,0:T(8,128)(2,1)S(1)} %get-tuple-element.48), channel_id=1, source_target_pairs={{0,64},{64,0},{1,65},{65,1},{2,66},{66,2},{3,67},{67,3},{4,68},{68... | collective-permute-start | bytes 294920 | tf_op jit(solution)/shard_map/ppermute | solution.py:26
  21.9 5.3 %collective-permute-start.5 = (bf16[48,1024]{1,0:T(8,128)(2,1)S(1)}, bf16[48,1024]{1,0:T(8,128)(2,1)S(1)}, u32[]{:S(2)}, u32[]{:S(2)}) collective-permute-start(bf16[48,1024]{1,0:T(8,128)(2,1)S(1)} %get-tuple-element.49), channel_id=1, source_target_pairs={{0,96},{32,64},{64,32},{96,0},{1,97},{33,65},{65,33},{97,1},{2,98}... | collective-permute-start | bytes 294920 | tf_op jit(solution)/shard_map/ppermute | solution.py:316
  27.7 21.6 %copy-start.2 = (f32[48,4096]{1,0:T(8,128)}, f32[48,4096]{1,0:T(8,128)S(1)}, u32[]{:S(2)}) copy-start(f32[48,4096]{1,0:T(8,128)S(1)} %get-tuple-element.60.pooled) | copy-start | bytes 2359300
  49.4 4.6 %collective-permute-start.7 = (bf16[768,128]{1,0:T(8,128)(2,1)S(1)}, bf16[768,128]{1,0:T(8,128)(2,1)S(1)}, u32[]{:S(2)}, u32[]{:S(2)}) collective-permute-start(bf16[768,128]{1,0:T(8,128)(2,1)S(1)} %bitcast.40), channel_id=1, source_target_pairs={{0,64},{64,0},{1,65},{65,1},{2,66},{66,2},{3,67},{67,3},{4,68},{68... | collective-permute-start | bytes 589832 | tf_op jit(solution)/shard_map/ppermute | solution.py:26
  49.8 8.1 %collective-permute-start.6 = (bf16[768,128]{1,0:T(8,128)(2,1)S(1)}, bf16[768,128]{1,0:T(8,128)(2,1)S(1)}, u32[]{:S(2)}, u32[]{:S(2)}) collective-permute-start(bf16[768,128]{1,0:T(8,128)(2,1)S(1)} %bitcast.41), channel_id=1, source_target_pairs={{0,32},{32,0},{1,33},{33,1},{2,34},{34,2},{3,35},{35,3},{4,36},{36... | collective-permute-start | bytes 589832 | tf_op jit(solution)/shard_map/ppermute | solution.py:22
  54.0 4.4 %collective-permute-start.8 = (bf16[768,128]{1,0:T(8,128)(2,1)S(1)}, bf16[768,128]{1,0:T(8,128)(2,1)S(1)}, u32[]{:S(2)}, u32[]{:S(2)}) collective-permute-start(bf16[768,128]{1,0:T(8,128)(2,1)S(1)} %collective-permute-done.7), channel_id=1, source_target_pairs={{0,32},{32,0},{1,33},{33,1},{2,34},{34,2},{3,35},{35,3},{4,36},{36... | collective-permute-start | bytes 589832 | tf_op jit(solution)/shard_map/ppermute | solution.py:22
  66.1 24.9 %all-to-all-start.1 = ((f16[32,24,896]{2,1,0:T(8,128)(2,1)}), f16[32,24,896]{2,1,0:T(8,128)(2,1)}, u32[]{:S(2)}, u32[]{:S(2)}) async-start(f16[32,24,896]{2,1,0:T(8,128)(2,1)} %pad_maximum_fusion), calls=%async_computation.1 | async-start | bytes 2752512 | tf_op jit(solution)/shard_map/all_to_all | solution.py:42
  108.9 22.2 %all-to-all-start.2 = ((bf16[32,24,768]{2,1,0:T(8,128)(2,1)}), bf16[32,24,768]{2,1,0:T(8,128)(2,1)S(1)}, u32[]{:S(2)}, u32[]{:S(2)}) async-start(bf16[32,24,768]{2,1,0:T(8,128)(2,1)} %copy-done), calls=%async_computation.2 | async-start | bytes 2359296 | tf_op jit(solution)/shard_map/all_to_all | solution.py:42
  121.1 3.6 %collective-permute-start.9 = (bf16[2,768,128]{2,1,0:T(8,128)(2,1)S(1)}, bf16[2,768,128]{2,1,0:T(8,128)(2,1)S(1)}, u32[]{:S(2)}, u32[]{:S(2)}) collective-permute-start(bf16[2,768,128]{2,1,0:T(8,128)(2,1)S(1)} %pad_maximum_fusion.2), channel_id=1, source_target_pairs={{0,32},{32,0},{1,33},{33,1},{2,34},{34,2},{3,35},{35,3},{4,36},{36... | collective-permute-start | bytes 1179656 | tf_op jit(solution)/shard_map/ppermute | solution.py:22
  124.7 6.4 %collective-permute-start.10 = (bf16[768,128]{1,0:T(8,128)(2,1)S(1)}, bf16[768,128]{1,0:T(8,128)(2,1)S(1)}, u32[]{:S(2)}, u32[]{:S(2)}) collective-permute-start(bf16[768,128]{1,0:T(8,128)(2,1)S(1)} %fusion.1), channel_id=1, source_target_pairs={{0,64},{64,0},{1,65},{65,1},{2,66},{66,2},{3,67},{67,3},{4,68},{68... | collective-permute-start | bytes 589832 | tf_op jit(solution)/shard_map/ppermute | solution.py:26
  132.0 20.2 %copy-start.3 = (f32[48,4096]{1,0:T(8,128)S(1)}, f32[48,4096]{1,0:T(8,128)}, u32[]{:S(2)}) copy-start(f32[48,4096]{1,0:T(8,128)} %copy-done.2) | copy-start | bytes 2359300
  153.2 10.6 %collective-permute-start.12 = (bf16[48,1024]{1,0:T(8,128)(2,1)S(1)}, bf16[48,1024]{1,0:T(8,128)(2,1)S(1)}, u32[]{:S(2)}, u32[]{:S(2)}) collective-permute-start(bf16[48,1024]{1,0:T(8,128)(2,1)S(1)} %get-tuple-element.65), channel_id=1, source_target_pairs={{0,32},{32,0},{1,33},{33,1},{2,34},{34,2},{3,35},{35,3},{4,36},{36... | collective-permute-start | bytes 294920 | tf_op jit(solution)/shard_map/ppermute | solution.py:22
  156.0 7.8 %collective-permute-start.13 = (bf16[48,1024]{1,0:T(8,128)(2,1)S(1)}, bf16[48,1024]{1,0:T(8,128)(2,1)S(1)}, u32[]{:S(2)}, u32[]{:S(2)}) collective-permute-start(bf16[48,1024]{1,0:T(8,128)(2,1)S(1)} %get-tuple-element.66), channel_id=1, source_target_pairs={{0,64},{64,0},{1,65},{65,1},{2,66},{66,2},{3,67},{67,3},{4,68},{68... | collective-permute-start | bytes 294920 | tf_op jit(solution)/shard_map/ppermute | solution.py:26
  156.3 7.4 %collective-permute-start.14 = (bf16[48,1024]{1,0:T(8,128)(2,1)S(1)}, bf16[48,1024]{1,0:T(8,128)(2,1)S(1)}, u32[]{:S(2)}, u32[]{:S(2)}) collective-permute-start(bf16[48,1024]{1,0:T(8,128)(2,1)S(1)} %get-tuple-element.67), channel_id=1, source_target_pairs={{0,96},{32,64},{64,32},{96,0},{1,97},{33,65},{65,33},{97,1},{2,98}... | collective-permute-start | bytes 294920 | tf_op jit(solution)/shard_map/ppermute | solution.py:428
  157.7 6.0 %collective-permute-start.11 = (f32[104,128]{1,0:T(8,128)S(1)}, f32[104,128]{1,0:T(8,128)S(1)}, u32[]{:S(2)}, u32[]{:S(2)}) collective-permute-start(f32[104,128]{1,0:T(8,128)S(1)} %get-tuple-element.63), channel_id=1, source_target_pairs={{16,0},{0,16},{17,1},{1,17},{18,2},{2,18},{19,3},{3,19},{20,4},{4,... | collective-permute-start | bytes 159752 | tf_op jit(solution)/shard_map/ppermute | solution.py:31
  169.1 3.7 %collective-permute-start.15 = (bf16[2,48,4096]{2,1,0:T(8,128)(2,1)S(1)}, bf16[2,48,4096]{2,1,0:T(8,128)(2,1)S(1)}, u32[]{:S(2)}, u32[]{:S(2)}) collective-permute-start(bf16[2,48,4096]{2,1,0:T(8,128)(2,1)S(1)} %get-tuple-element.76), channel_id=1, source_target_pairs={{0,32},{32,0},{1,33},{33,1},{2,34},{34,2},{3,35},{35,3},{4,36},{36... | collective-permute-start | bytes 2359304 | tf_op jit(solution)/shard_map/ppermute | solution.py:22
  170.1 4.6 %collective-permute-start.18 = (f32[104,128]{1,0:T(8,128)S(1)}, f32[104,128]{1,0:T(8,128)S(1)}, u32[]{:S(2)}, u32[]{:S(2)}) collective-permute-start(f32[104,128]{1,0:T(8,128)S(1)} %add.72), channel_id=1, source_target_pairs={{12,0},{0,4},{4,8},{8,12},{13,1},{1,5},{5,9},{9,13},{14,2},{2,6},{... | collective-permute-start | bytes 159752 | tf_op jit(solution)/shard_map/ppermute | solution.py:31
  170.5 4.2 %collective-permute-start.17 = (f32[104,128]{1,0:T(8,128)S(1)}, f32[104,128]{1,0:T(8,128)S(1)}, u32[]{:S(2)}, u32[]{:S(2)}) collective-permute-start(f32[104,128]{1,0:T(8,128)S(1)} %add.72), channel_id=1, source_target_pairs={{4,0},{8,4},{12,8},{0,12},{5,1},{9,5},{13,9},{1,13},{6,2},{10,6},{... | collective-permute-start | bytes 159752 | tf_op jit(solution)/shard_map/ppermute | solution.py:31
  172.8 4.5 %collective-permute-start.16 = (f32[104,128]{1,0:T(8,128)S(1)}, f32[104,128]{1,0:T(8,128)S(1)}, u32[]{:S(2)}, u32[]{:S(2)}) collective-permute-start(f32[104,128]{1,0:T(8,128)S(1)} %add.72), channel_id=1, source_target_pairs={{8,0},{12,4},{0,8},{4,12},{9,1},{13,5},{1,9},{5,13},{10,2},{14,6},... | collective-permute-start | bytes 159752 | tf_op jit(solution)/shard_map/ppermute | solution.py:31
  173.0 5.6 %collective-permute-start.19 = (bf16[48,2048]{1,0:T(8,128)(2,1)S(1)}, bf16[48,2048]{1,0:T(8,128)(2,1)S(1)}, u32[]{:S(2)}, u32[]{:S(2)}) collective-permute-start(bf16[48,2048]{1,0:T(8,128)(2,1)S(1)} %get-tuple-element.90), channel_id=1, source_target_pairs={{0,64},{64,0},{1,65},{65,1},{2,66},{66,2},{3,67},{67,3},{4,68},{68... | collective-permute-start | bytes 589832 | tf_op jit(solution)/shard_map/ppermute | solution.py:26
  178.6 4.2 %collective-permute-start.23 = (f32[104,128]{1,0:T(8,128)S(1)}, f32[104,128]{1,0:T(8,128)S(1)}, u32[]{:S(2)}, u32[]{:S(2)}) collective-permute-start(f32[104,128]{1,0:T(8,128)S(1)} %add_add_fusion.1), channel_id=1, source_target_pairs={{3,0},{0,1},{1,2},{2,3},{7,4},{4,5},{5,6},{6,7},{11,8},{8,9},{9,10... | collective-permute-start | bytes 159752 | tf_op jit(solution)/shard_map/ppermute | solution.py:31
  178.8 4.0 %collective-permute-start.22 = (f32[104,128]{1,0:T(8,128)S(1)}, f32[104,128]{1,0:T(8,128)S(1)}, u32[]{:S(2)}, u32[]{:S(2)}) collective-permute-start(f32[104,128]{1,0:T(8,128)S(1)} %add_add_fusion.1), channel_id=1, source_target_pairs={{1,0},{2,1},{3,2},{0,3},{5,4},{6,5},{7,6},{4,7},{9,8},{10,9},{11,1... | collective-permute-start | bytes 159752 | tf_op jit(solution)/shard_map/ppermute | solution.py:31
  181.3 4.5 %collective-permute-start.21 = (f32[104,128]{1,0:T(8,128)S(1)}, f32[104,128]{1,0:T(8,128)S(1)}, u32[]{:S(2)}, u32[]{:S(2)}) collective-permute-start(f32[104,128]{1,0:T(8,128)S(1)} %add_add_fusion.1), channel_id=1, source_target_pairs={{2,0},{3,1},{0,2},{1,3},{6,4},{7,5},{4,6},{5,7},{10,8},{11,9},{8,1... | collective-permute-start | bytes 159752 | tf_op jit(solution)/shard_map/ppermute | solution.py:31
  181.9 8.8 %collective-permute-start.20 = (bf16[48,2048]{1,0:T(8,128)(2,1)S(1)}, bf16[48,2048]{1,0:T(8,128)(2,1)S(1)}, u32[]{:S(2)}, u32[]{:S(2)}) collective-permute-start(bf16[48,2048]{1,0:T(8,128)(2,1)S(1)} %get-tuple-element.91), channel_id=1, source_target_pairs={{0,64},{64,0},{1,65},{65,1},{2,66},{66,2},{3,67},{67,3},{4,68},{68... | collective-permute-start | bytes 589832 | tf_op jit(solution)/shard_map/ppermute | solution.py:26
  185.8 5.9 %collective-permute-start.26 = (f32[104,128]{1,0:T(8,128)S(1)}, f32[104,128]{1,0:T(8,128)S(1)}, u32[]{:S(2)}, u32[]{:S(2)}) collective-permute-start(f32[104,128]{1,0:T(8,128)S(1)} %add_add_fusion.refs_0_), channel_id=1, source_target_pairs={{0,96},{32,64},{64,32},{96,0},{1,97},{33,65},{65,33},{97,1},{2,98}... | collective-permute-start | bytes 159752 | tf_op jit(solution)/shard_map/ppermute | solution.py:454
  189.3 4.4 %collective-permute-start.25 = (f32[104,128]{1,0:T(8,128)S(1)}, f32[104,128]{1,0:T(8,128)S(1)}, u32[]{:S(2)}, u32[]{:S(2)}) collective-permute-start(f32[104,128]{1,0:T(8,128)S(1)} %add_add_fusion.refs_0_), channel_id=1, source_target_pairs={{0,64},{64,0},{1,65},{65,1},{2,66},{66,2},{3,67},{67,3},{4,68},{68... | collective-permute-start | bytes 159752 | tf_op jit(solution)/shard_map/ppermute | solution.py:26
  190.8 2.9 %collective-permute-start.24 = (f32[104,128]{1,0:T(8,128)S(1)}, f32[104,128]{1,0:T(8,128)S(1)}, u32[]{:S(2)}, u32[]{:S(2)}) collective-permute-start(f32[104,128]{1,0:T(8,128)S(1)} %add_add_fusion.refs_0_), channel_id=1, source_target_pairs={{0,32},{32,0},{1,33},{33,1},{2,34},{34,2},{3,35},{35,3},{4,36},{36... | collective-permute-start | bytes 159752 | tf_op jit(solution)/shard_map/ppermute | solution.py:22
  (7 other events, 30.3 us)

commit v9 on v8

--- a/solution.py
+++ b/solution.py
@@ -149,7 +149,7 @@
     hard_ref[...] = hard
 
 
-def scatter_kernel(hard_count, tok_rows, ids, w_ref, q_ref, neg_ref, add_ref, sum_ref, slot, *parts):
+def scatter_kernel(hard_count, tok_rows, ids, w_ref, q_ref, neg_ref, add_ref, slot, *parts):
     rows = q_ref.shape[0]
     for part in parts:
         part[...] = jnp.zeros_like(part)
@@ -159,7 +159,7 @@
         weight = w_ref[:, k : k + 1].astype(F32)
         slot[k] = weight * q
         total = total + weight * neg_ref[k].astype(F32)
-    sum_ref[...] = total
+    add_ref[4 * rows :, :] = total.astype(BF16)
 
     def place(block, carry):
         for i in range(tok_rows):
@@ -172,7 +172,7 @@
     added = parts[0][...]
     for k in range(1, hard_count):
         added = added + parts[k][...]
-    add_ref[...] = added.astype(BF16)
+    add_ref[: 4 * rows, :] = added.astype(BF16)
 
 
 def stream_chunks(w_ref, held, sems):
@@ -213,7 +213,7 @@
             out_ref[i // 2, :, here] = term[i * rows : (i + 1) * rows].astype(BF16)
 
 
-def softmax_kernel(hard_count, at, score_ref, losses_ref, hard_ref, group_ref):
+def softmax_kernel(hard_count, at, score_ref, losses_ref, hard_ref, group_ref, held, sem):
     rows, width = score_ref.shape
     pairs = width - LANES
     scores = score_ref[:, :pairs] / TAU
@@ -226,16 +226,23 @@
     own = jnp.sum(jnp.where(column == row + at[0], scores, 0.0), axis=1, keepdims=True)
     losses_ref[...] = jnp.broadcast_to(jnp.log(totals) - own, (rows, LANES))
     hard_probs = (hard_weights / totals).astype(BF16)
-    probs = (weights / totals).astype(BF16)
+    held[...] = (weights / totals).astype(BF16)
+    copies = [
+        pltpu.make_async_copy(held, group_ref.at[b], sem.at[b]) for b in range(group_ref.shape[0])
+    ]
+    for copy in copies:
+        copy.start()
     for b in range(hard_ref.shape[0]):
         hard_ref[b] = hard_probs
-        group_ref[b] = probs
+    for copy in copies:
+        copy.wait()
 
 
 def sums_kernel(probs_ref, q_ref, p_ref, hard_ref, add_ref, near_ref, far_ref, out_ref):
     tok_rows = out_ref.shape[2]
     probs = probs_ref[...]
-    sum_q = jnp.dot(probs, p_ref[...], preferred_element_type=F32) + hard_ref[...]
+    sum_q = jnp.dot(probs, p_ref[...], preferred_element_type=F32)
+    sum_q = sum_q + hard_ref[...].astype(F32)
     sum_p = lax.dot_general(
         probs, q_ref[...], (((0,), (0,)), ((), ())), preferred_element_type=F32
     )
@@ -377,26 +384,27 @@
             jax.ShapeDtypeStruct((blocks, tok_rows, pairs), BF16),
         ),
         in_specs=[smem, vmem],
-        out_specs=(vmem,) * 3,
-        compiler_params=params,
+        out_specs=(vmem, vmem, hbm),
+        scratch_shapes=[
+            pltpu.VMEM((tok_rows, pairs), BF16),
+            pltpu.SemaphoreType.DMA((blocks,)),
+        ],
+        compiler_params=pltpu.CompilerParams(vmem_limit_bytes=58 * 1024 * 1024),
     )((lax.axis_index(BLK) * tok_rows).astype(jnp.int32).reshape(1), part)
     losses = losses[:, 0]
     hard_probs = exchange(hard_probs, BLK).reshape(pairs, LANES)
     group_probs = exchange(group_probs, BLK).reshape(pairs, pairs)
 
-    hard_add, hard_sum = pl.pallas_call(
+    hard_add = pl.pallas_call(
         lambda *refs: scatter_kernel(hard_count, tok_rows, *refs),
-        out_shape=(
-            jax.ShapeDtypeStruct((4 * pairs, LANES), BF16),
-            jax.ShapeDtypeStruct((pairs, LANES), F32),
-        ),
+        out_shape=jax.ShapeDtypeStruct((5 * pairs, LANES), BF16),
         in_specs=[smem, vmem, vmem, vmem],
-        out_specs=(vmem, vmem),
+        out_specs=vmem,
         scratch_shapes=[pltpu.VMEM((hard_count, pairs, LANES), F32)]
         + [pltpu.VMEM((4 * pairs, LANES), F32)] * hard_count,
         compiler_params=params,
     )(ids, hard_probs, q_all, negatives)
-    hard_add = hard_add.reshape(4, pairs, LANES)
+    hard_add = hard_add.reshape(5, pairs, LANES)
     crossed = swap_core(jnp.stack([hard_add[1], hard_add[3]]))
     over_chip = swap_chip((hard_add[2].astype(F32) + crossed[1].astype(F32)).astype(BF16))
     sums = pl.pallas_call(
@@ -405,7 +413,7 @@
         in_specs=[vmem] * 7,
         out_specs=vmem,
         compiler_params=params,
-    )(group_probs, q_all, p_own, hard_sum, hard_add[0], crossed[0], over_chip)
+    )(group_probs, q_all, p_own, hard_add[4], hard_add[0], crossed[0], over_chip)
     sums = exchange(sums, BLK)
 
     lines = width // LANES

time: 195 us -> 197 us (1.010)
  Pallas kernels: 25.9 us -> 28.7 us
  local copies, waits for them, and re-layouts: 4.82 us -> 2.81 us
    pallas_call x1, Pallas kernels: 0.19 us -> 3.03 us  [local(): pl.pallas_call(lambda *refs: softmax_kernel(hard_count, *refs), out_shape...]
    unnamed x20 -> x16, local copies, waits for them, and re-layouts: 3.97 us -> 1.94 us
where the time goes in v9:
time: 197 us; the launch traced here: 196 us
  waiting for transfers between devices  59.1 us (30%)
  blocking collectives  56.2 us (29%)
  starting transfers between devices  40.2 us (20%)
  Pallas kernels  28.7 us (15%)
  other arithmetic  6.9 us (4%)
  local copies, waits for them, and re-layouts  2.81 us (1%)
    all_to_all x3, blocking collectives, exchange(): return lax.all_to_all(values, axes, split_axis=0, concat_axis=0, tiled=True)  56.2 us
    all_to_all x2, waiting for transfers between devices, exchange(): return lax.all_to_all(values, axes, split_axis=0, concat_axis=0, tiled=True)  20.2 us
    ppermute x8, waiting for transfers between devices, swap_chip(): return lax.ppermute(values, 'xl', SWAP)  20.1 us
    ppermute x9, starting transfers between devices, swap_core(): return lax.ppermute(values, 'co', SWAP)  14.6 us
    ppermute x7, waiting for transfers between devices, from_ahead(): lax.ppermute(values, axis, [((i + step) % size, i) for i in range(size)])  13.2 us
    all_to_all x2, starting transfers between devices, exchange(): return lax.all_to_all(values, axes, split_axis=0, concat_axis=0, tiled=True)  8.64 us
    pallas_call x1, Pallas kernels, local(): pl.pallas_call(lambda *refs: scatter_kernel(hard_count, tok_rows, *refs),...  7.2 us
    pallas_call x1, Pallas kernels, local(): pl.pallas_call(lambda *refs: gather_kernel(hard_count, tok_rows, *refs),...  6.24 us
  transfers between devices with their start and end apart: 29, of which 16 were waited for; matrix products, arithmetic and copies ran while one was open for 2% of the time, Pallas kernels for 4%

profile of v9, /device:TPU:1, one launch (start us, length us, event | category | flops | bytes accessed | tf_op | source)
XLA Modules:
  0.0 196.1 jit_solution(17443833263061572923)
XLA Ops:
  0.6 1.5 collective-permute-start.1
  5.9 7.1 %collective-permute-done.x2 = bf16[48,4096]{1,0:T(8,128)(2,1)S(1)} collective-permute-done((bf16[48,4096]{1,0:T(8,128)(2,1)}, bf16[48,4096]{1,0:T(8,128)(2,1)S(1)}, u32[]{:S(2)}, u32[]{:S(2)}) %collective-permute-start) | collective-permute-done | bytes 393248 | tf_op jit(solution)/shard_map/ppermute | solution.py:26
  16.2 3.9 %shard_map.128 = (bf16[48,1024]{1,0:T(8,128)(2,1)S(1)}, bf16[48,1024]{1,0:T(8,128)(2,1)S(1)}, bf16[48,1024]{1,0:T(8,128)(2,1)S(1)}, bf16[48,1024]{1,0:T(8,128)(2,1)S(1)}) custom-call(bf16[48,4096]{1,0:T(8,128)(2,1)S(1)} %bitcast.51, bf16[48,4096]{1,0:T(8,128)(2,1)S(1)} %collective-permute-done.1.x1, bf16[48,4096]{1,0:T(8,128)(2,1)S(1)} %collective-permute-done.x2, ...), custom_call_target="tpu_custom_call" | custom-call | tf_op jit(solution)/shard_map/pallas_call | solution.py:311
  22.4 2.5 %collective-permute-done.4.x2 = bf16[48,1024]{1,0:T(8,128)(2,1)S(1)} collective-permute-done((bf16[48,1024]{1,0:T(8,128)(2,1)S(1)}, bf16[48,1024]{1,0:T(8,128)(2,1)S(1)}, u32[]{:S(2)}, u32[]{:S(2)}) %collective-permute-start.4) | collective-permute-done | bytes 98336 | tf_op jit(solution)/shard_map/ppermute | solution.py:26
  24.9 2.4 %collective-permute-done.5.x3 = bf16[48,1024]{1,0:T(8,128)(2,1)S(1)} collective-permute-done((bf16[48,1024]{1,0:T(8,128)(2,1)S(1)}, bf16[48,1024]{1,0:T(8,128)(2,1)S(1)}, u32[]{:S(2)}, u32[]{:S(2)}) %collective-permute-start.5) | collective-permute-done | bytes 98336 | tf_op jit(solution)/shard_map/ppermute | solution.py:323
  27.7 21.6 %all_to_all.25 = bf16[32,56,128]{2,1,0:T(8,128)(2,1)S(1)} all-to-all(bf16[32,56,128]{2,1,0:T(8,128)(2,1)S(1)} %get-tuple-element.50.spread), channel_id=1, replica_groups=mesh['xl'=2,'co'=2,'xh'=2,'y'=4,'z'=4] {'xh','y','z'}, dimensions={0} | all-to-all | bytes 917504 | tf_op jit(solution)/shard_map/all_to_all | solution.py:42
  49.8 2.5 %collective-permute-start.6 = (bf16[768,128]{1,0:T(8,128)(2,1)S(1)}, bf16[768,128]{1,0:T(8,128)(2,1)S(1)}, u32[]{:S(2)}, u32[]{:S(2)}) collective-permute-start(bf16[768,128]{1,0:T(8,128)(2,1)S(1)} %bitcast.41), channel_id=1, source_target_pairs={{0,32},{32,0},{1,33},{33,1},{2,34},{34,2},{3,35},{35,3},{4,36},{36... | collective-permute-start | bytes 589832 | tf_op jit(solution)/shard_map/ppermute | solution.py:22
  52.5 1.5 collective-permute-done.7
  54.0 3.3 %collective-permute-start.8 = (bf16[768,128]{1,0:T(8,128)(2,1)S(1)}, bf16[768,128]{1,0:T(8,128)(2,1)S(1)}, u32[]{:S(2)}, u32[]{:S(2)}) collective-permute-start(bf16[768,128]{1,0:T(8,128)(2,1)S(1)} %collective-permute-done.7), channel_id=1, source_target_pairs={{0,32},{32,0},{1,33},{33,1},{2,34},{34,2},{3,35},{35,3},{4,36},{36... | collective-permute-start | bytes 589832 | tf_op jit(solution)/shard_map/ppermute | solution.py:22
  58.4 6.2 %shard_map.130 = (bf16[7,768,128]{2,1,0:T(8,128)(2,1)S(1)}, f32[768,128]{1,0:T(8,128)S(1)}) custom-call(s32[5376]{0:T(1024)S(1)} %reshape.82.refs_0_, bf16[768,128]{1,0:T(8,128)(2,1)S(1)} %bitcast.45, bf16[3072,128]{1,0:T(8,128)(2,1)S(1)} %pad_maximum_fusion.1.refs_2_), custom_call_target="tpu_custom_call" | custom-call | tf_op jit(solution)/shard_map/pallas_call | solution.py:362
  64.7 1.4 pad_maximum_fusion
  66.1 4.7 %all-to-all-start.1 = ((f16[32,24,896]{2,1,0:T(8,128)(2,1)}), f16[32,24,896]{2,1,0:T(8,128)(2,1)}, u32[]{:S(2)}, u32[]{:S(2)}) async-start(f16[32,24,896]{2,1,0:T(8,128)(2,1)} %pad_maximum_fusion), calls=%async_computation.1 | async-start | bytes 2752512 | tf_op jit(solution)/shard_map/all_to_all | solution.py:42
  70.8 20.2 %all-to-all-done.1 = f16[32,24,896]{2,1,0:T(8,128)(2,1)} async-done(((f16[32,24,896]{2,1,0:T(8,128)(2,1)}), f16[32,24,896]{2,1,0:T(8,128)(2,1)}, u32[]{:S(2)}, u32[]{:S(2)}) %all-to-all-start.1) | async-done | bytes 1376288 | tf_op jit(solution)/shard_map/all_to_all | solution.py:42
  91.0 2.2 %convert_reduce_fusion.refs_1_ = f32[24,896]{1,0:T(8,128)} fusion(f16[32,24,896]{2,1,0:T(8,128)(2,1)} %all-to-all-done.1), kind=kLoop, calls=%fused_computation | loop fusion | flops 1354752 | bytes 1462272 | tf_op jit(solution)/shard_map/reduce_sum | solution.py:378
  93.2 3.0 %shard_map.131 = (f32[24,128]{1,0:T(8,128)}, bf16[32,24,128]{2,1,0:T(8,128)(2,1)}, bf16[32,24,768]{2,1,0:T(8,128)(2,1)}) custom-call(s32[1]{0:T(128)} %bitcast.refs_0_, f32[24,896]{1,0:T(8,128)} %convert_reduce_fusion.refs_1_), custom_call_target="tpu_custom_call" | custom-call | tf_op jit(solution)/shard_map/pallas_call | solution.py:379
  96.2 15.3 %all_to_all.26 = bf16[32,24,128]{2,1,0:T(8,128)(2,1)} all-to-all(bf16[32,24,128]{2,1,0:T(8,128)(2,1)} %get-tuple-element.54), channel_id=1, replica_groups=mesh['xl'=2,'co'=2,'xh'=2,'y'=4,'z'=4] {'xh','y','z'}, dimensions={0} | all-to-all | bytes 393216 | tf_op jit(solution)/shard_map/all_to_all | solution.py:42
  111.5 3.9 %all-to-all-start.2 = ((bf16[32,24,768]{2,1,0:T(8,128)(2,1)}), bf16[32,24,768]{2,1,0:T(8,128)(2,1)S(1)}, u32[]{:S(2)}, u32[]{:S(2)}) async-start(bf16[32,24,768]{2,1,0:T(8,128)(2,1)} %get-tuple-element.53), calls=%async_computation.2 | async-start | bytes 2359296 | tf_op jit(solution)/shard_map/all_to_all | solution.py:42
  116.4 7.2 %shard_map.132 = bf16[3840,128]{1,0:T(8,128)(2,1)S(1)} custom-call(s32[5376]{0:T(1024)S(1)} %reshape.82.refs_0_, bf16[768,128]{1,0:T(8,128)(2,1)S(1)} %bitcast.48, bf16[768,128]{1,0:T(8,128)(2,1)S(1)} %bitcast.46, bf16[7,768,128]{2,1,0:T(8,128)(2,1)S(1)} %get-tuple-element.55.refs_3_), custom_call_target="tpu_custom_call" | custom-call | tf_op jit(solution)/shard_map/pallas_call | solution.py:398
  123.7 2.2 %collective-permute-start.9 = (bf16[2,768,128]{2,1,0:T(8,128)(2,1)S(1)}, bf16[2,768,128]{2,1,0:T(8,128)(2,1)S(1)}, u32[]{:S(2)}, u32[]{:S(2)}) collective-permute-start(bf16[2,768,128]{2,1,0:T(8,128)(2,1)S(1)} %pad_maximum_fusion.2), channel_id=1, source_target_pairs={{0,32},{32,0},{1,33},{33,1},{2,34},{34,2},{3,35},{35,3},{4,36},{36... | collective-permute-start | bytes 1179656 | tf_op jit(solution)/shard_map/ppermute | solution.py:22
  127.9 5.8 %collective-permute-done.10.far_ref = bf16[768,128]{1,0:T(8,128)(2,1)S(1)} collective-permute-done((bf16[768,128]{1,0:T(8,128)(2,1)S(1)}, bf16[768,128]{1,0:T(8,128)(2,1)S(1)}, u32[]{:S(2)}, u32[]{:S(2)}) %collective-permute-start.10) | collective-permute-done | bytes 196640 | tf_op jit(solution)/shard_map/ppermute | solution.py:26
  134.5 19.3 %all_to_all.27.sums = bf16[32,2,24,128]{3,2,1,0:T(8,128)(2,1)S(1)} all-to-all(bf16[32,2,24,128]{3,2,1,0:T(8,128)(2,1)S(1)} %shard_map.133), channel_id=1, replica_groups=mesh['xl'=2,'co'=2,'xh'=2,'y'=4,'z'=4] {'xh','y','z'}, dimensions={0} | all-to-all | bytes 786432 | tf_op jit(solution)/shard_map/all_to_all | solution.py:42
  154.9 2.8 %collective-permute-start.12 = (bf16[48,1024]{1,0:T(8,128)(2,1)S(1)}, bf16[48,1024]{1,0:T(8,128)(2,1)S(1)}, u32[]{:S(2)}, u32[]{:S(2)}) collective-permute-start(bf16[48,1024]{1,0:T(8,128)(2,1)S(1)} %get-tuple-element.61), channel_id=1, source_target_pairs={{0,32},{32,0},{1,33},{33,1},{2,34},{34,2},{3,35},{35,3},{4,36},{36... | collective-permute-start | bytes 294920 | tf_op jit(solution)/shard_map/ppermute | solution.py:22
  160.1 5.3 %collective-permute-done.11 = f32[104,128]{1,0:T(8,128)S(1)} collective-permute-done((f32[104,128]{1,0:T(8,128)S(1)}, f32[104,128]{1,0:T(8,128)S(1)}, u32[]{:S(2)}, u32[]{:S(2)}) %collective-permute-start.11) | collective-permute-done | bytes 53280 | tf_op jit(solution)/shard_map/ppermute | solution.py:31
  165.5 5.3 %shard_map.135 = (bf16[2,48,4096]{2,1,0:T(8,128)(2,1)S(1)}, bf16[2,48,4096]{2,1,0:T(8,128)(2,1)S(1)}) custom-call(bf16[48,1024]{1,0:T(8,128)(2,1)S(1)} %get-tuple-element.65.x0, bf16[48,1024]{1,0:T(8,128)(2,1)S(1)} %collective-permute-done.12.x1, bf16[48,1024]{1,0:T(8,128)(2,1)S(1)} %collective-permute-done.13.x2, ...), custom_call_target="tpu_custom_call" | custom-call | tf_op jit(solution)/shard_map/pallas_call | solution.py:439
  172.1 2.3 %collective-permute-start.17 = (f32[104,128]{1,0:T(8,128)S(1)}, f32[104,128]{1,0:T(8,128)S(1)}, u32[]{:S(2)}, u32[]{:S(2)}) collective-permute-start(f32[104,128]{1,0:T(8,128)S(1)} %add.72), channel_id=1, source_target_pairs={{4,0},{8,4},{12,8},{0,12},{5,1},{9,5},{13,9},{1,13},{6,2},{10,6},{... | collective-permute-start | bytes 159752 | tf_op jit(solution)/shard_map/ppermute | solution.py:31
  174.8 1.6 collective-permute-done.18
  176.4 2.6 %collective-permute-done.16 = f32[104,128]{1,0:T(8,128)S(1)} collective-permute-done((f32[104,128]{1,0:T(8,128)S(1)}, f32[104,128]{1,0:T(8,128)S(1)}, u32[]{:S(2)}, u32[]{:S(2)}) %collective-permute-start.16) | collective-permute-done | bytes 53280 | tf_op jit(solution)/shard_map/ppermute | solution.py:31
  180.5 2.5 %collective-permute-start.22 = (f32[104,128]{1,0:T(8,128)S(1)}, f32[104,128]{1,0:T(8,128)S(1)}, u32[]{:S(2)}, u32[]{:S(2)}) collective-permute-start(f32[104,128]{1,0:T(8,128)S(1)} %add_add_fusion.1), channel_id=1, source_target_pairs={{1,0},{2,1},{3,2},{0,3},{5,4},{6,5},{7,6},{4,7},{9,8},{10,9},{11,1... | collective-permute-start | bytes 159752 | tf_op jit(solution)/shard_map/ppermute | solution.py:31
  184.5 3.0 %collective-permute-done.21 = f32[104,128]{1,0:T(8,128)S(1)} collective-permute-done((f32[104,128]{1,0:T(8,128)S(1)}, f32[104,128]{1,0:T(8,128)S(1)}, u32[]{:S(2)}, u32[]{:S(2)}) %collective-permute-start.21) | collective-permute-done | bytes 53280 | tf_op jit(solution)/shard_map/ppermute | solution.py:31
  187.5 3.5 %collective-permute-start.26 = (f32[104,128]{1,0:T(8,128)S(1)}, f32[104,128]{1,0:T(8,128)S(1)}, u32[]{:S(2)}, u32[]{:S(2)}) collective-permute-start(f32[104,128]{1,0:T(8,128)S(1)} %add_add_fusion.refs_0_), channel_id=1, source_target_pairs={{0,96},{32,64},{64,32},{96,0},{1,97},{33,65},{65,33},{97,1},{2,98}... | collective-permute-start | bytes 159752 | tf_op jit(solution)/shard_map/ppermute | solution.py:462
  191.0 1.5 collective-permute-start.25
  193.4 1.9 collective-permute-done.25.refs_2_
  (78 shorter events, 24.5 us)
Async XLA Ops:
  0.6 5.3 %collective-permute-start.1 = (bf16[48,4096]{1,0:T(8,128)(2,1)}, bf16[48,4096]{1,0:T(8,128)(2,1)S(1)}, u32[]{:S(2)}, u32[]{:S(2)}) collective-permute-start(bf16[48,4096]{1,0:T(8,128)(2,1)} %bitcast.49), channel_id=1, source_target_pairs={{0,32},{32,0},{1,33},{33,1},{2,34},{34,2},{3,35},{35,3},{4,36},{36... | collective-permute-start | bytes 1179656 | tf_op jit(solution)/shard_map/ppermute | solution.py:22
  2.1 10.9 %collective-permute-start = (bf16[48,4096]{1,0:T(8,128)(2,1)}, bf16[48,4096]{1,0:T(8,128)(2,1)S(1)}, u32[]{:S(2)}, u32[]{:S(2)}) collective-permute-start(bf16[48,4096]{1,0:T(8,128)(2,1)} %bitcast.50), channel_id=1, source_target_pairs={{0,64},{64,0},{1,65},{65,1},{2,66},{66,2},{3,67},{67,3},{4,68},{68... | collective-permute-start | bytes 1179656 | tf_op jit(solution)/shard_map/ppermute | solution.py:26
  13.0 2.2 %collective-permute-start.2 = (bf16[48,4096]{1,0:T(8,128)(2,1)S(1)}, bf16[48,4096]{1,0:T(8,128)(2,1)S(1)}, u32[]{:S(2)}, u32[]{:S(2)}) collective-permute-start(bf16[48,4096]{1,0:T(8,128)(2,1)S(1)} %collective-permute-done.x2), channel_id=1, source_target_pairs={{0,32},{32,0},{1,33},{33,1},{2,34},{34,2},{3,35},{35,3},{4,36},{36... | collective-permute-start | bytes 1179656 | tf_op jit(solution)/shard_map/ppermute | solution.py:22
  20.2 2.2 %collective-permute-start.3 = (bf16[48,1024]{1,0:T(8,128)(2,1)S(1)}, bf16[48,1024]{1,0:T(8,128)(2,1)S(1)}, u32[]{:S(2)}, u32[]{:S(2)}) collective-permute-start(bf16[48,1024]{1,0:T(8,128)(2,1)S(1)} %get-tuple-element.45), channel_id=1, source_target_pairs={{0,32},{32,0},{1,33},{33,1},{2,34},{34,2},{3,35},{35,3},{4,36},{36... | collective-permute-start | bytes 294920 | tf_op jit(solution)/shard_map/ppermute | solution.py:22
  20.6 4.3 %collective-permute-start.4 = (bf16[48,1024]{1,0:T(8,128)(2,1)S(1)}, bf16[48,1024]{1,0:T(8,128)(2,1)S(1)}, u32[]{:S(2)}, u32[]{:S(2)}) collective-permute-start(bf16[48,1024]{1,0:T(8,128)(2,1)S(1)} %get-tuple-element.46), channel_id=1, source_target_pairs={{0,64},{64,0},{1,65},{65,1},{2,66},{66,2},{3,67},{67,3},{4,68},{68... | collective-permute-start | bytes 294920 | tf_op jit(solution)/shard_map/ppermute | solution.py:26
  21.9 5.3 %collective-permute-start.5 = (bf16[48,1024]{1,0:T(8,128)(2,1)S(1)}, bf16[48,1024]{1,0:T(8,128)(2,1)S(1)}, u32[]{:S(2)}, u32[]{:S(2)}) collective-permute-start(bf16[48,1024]{1,0:T(8,128)(2,1)S(1)} %get-tuple-element.47), channel_id=1, source_target_pairs={{0,96},{32,64},{64,32},{96,0},{1,97},{33,65},{65,33},{97,1},{2,98}... | collective-permute-start | bytes 294920 | tf_op jit(solution)/shard_map/ppermute | solution.py:323
  27.7 21.6 %copy-start = (f32[48,4096]{1,0:T(8,128)}, f32[48,4096]{1,0:T(8,128)S(1)}, u32[]{:S(2)}) copy-start(f32[48,4096]{1,0:T(8,128)S(1)} %get-tuple-element.56.pooled) | copy-start | bytes 2359300
  49.4 4.6 %collective-permute-start.7 = (bf16[768,128]{1,0:T(8,128)(2,1)S(1)}, bf16[768,128]{1,0:T(8,128)(2,1)S(1)}, u32[]{:S(2)}, u32[]{:S(2)}) collective-permute-start(bf16[768,128]{1,0:T(8,128)(2,1)S(1)} %bitcast.40), channel_id=1, source_target_pairs={{0,64},{64,0},{1,65},{65,1},{2,66},{66,2},{3,67},{67,3},{4,68},{68... | collective-permute-start | bytes 589832 | tf_op jit(solution)/shard_map/ppermute | solution.py:26
  49.8 8.1 %collective-permute-start.6 = (bf16[768,128]{1,0:T(8,128)(2,1)S(1)}, bf16[768,128]{1,0:T(8,128)(2,1)S(1)}, u32[]{:S(2)}, u32[]{:S(2)}) collective-permute-start(bf16[768,128]{1,0:T(8,128)(2,1)S(1)} %bitcast.41), channel_id=1, source_target_pairs={{0,32},{32,0},{1,33},{33,1},{2,34},{34,2},{3,35},{35,3},{4,36},{36... | collective-permute-start | bytes 589832 | tf_op jit(solution)/shard_map/ppermute | solution.py:22
  54.0 4.4 %collective-permute-start.8 = (bf16[768,128]{1,0:T(8,128)(2,1)S(1)}, bf16[768,128]{1,0:T(8,128)(2,1)S(1)}, u32[]{:S(2)}, u32[]{:S(2)}) collective-permute-start(bf16[768,128]{1,0:T(8,128)(2,1)S(1)} %collective-permute-done.7), channel_id=1, source_target_pairs={{0,32},{32,0},{1,33},{33,1},{2,34},{34,2},{3,35},{35,3},{4,36},{36... | collective-permute-start | bytes 589832 | tf_op jit(solution)/shard_map/ppermute | solution.py:22
  66.1 24.9 %all-to-all-start.1 = ((f16[32,24,896]{2,1,0:T(8,128)(2,1)}), f16[32,24,896]{2,1,0:T(8,128)(2,1)}, u32[]{:S(2)}, u32[]{:S(2)}) async-start(f16[32,24,896]{2,1,0:T(8,128)(2,1)} %pad_maximum_fusion), calls=%async_computation.1 | async-start | bytes 2752512 | tf_op jit(solution)/shard_map/all_to_all | solution.py:42
  111.5 22.2 %all-to-all-start.2 = ((bf16[32,24,768]{2,1,0:T(8,128)(2,1)}), bf16[32,24,768]{2,1,0:T(8,128)(2,1)S(1)}, u32[]{:S(2)}, u32[]{:S(2)}) async-start(bf16[32,24,768]{2,1,0:T(8,128)(2,1)} %get-tuple-element.53), calls=%async_computation.2 | async-start | bytes 2359296 | tf_op jit(solution)/shard_map/all_to_all | solution.py:42
  123.7 3.6 %collective-permute-start.9 = (bf16[2,768,128]{2,1,0:T(8,128)(2,1)S(1)}, bf16[2,768,128]{2,1,0:T(8,128)(2,1)S(1)}, u32[]{:S(2)}, u32[]{:S(2)}) collective-permute-start(bf16[2,768,128]{2,1,0:T(8,128)(2,1)S(1)} %pad_maximum_fusion.2), channel_id=1, source_target_pairs={{0,32},{32,0},{1,33},{33,1},{2,34},{34,2},{3,35},{35,3},{4,36},{36... | collective-permute-start | bytes 1179656 | tf_op jit(solution)/shard_map/ppermute | solution.py:22
  127.3 6.4 %collective-permute-start.10 = (bf16[768,128]{1,0:T(8,128)(2,1)S(1)}, bf16[768,128]{1,0:T(8,128)(2,1)S(1)}, u32[]{:S(2)}, u32[]{:S(2)}) collective-permute-start(bf16[768,128]{1,0:T(8,128)(2,1)S(1)} %fusion.1), channel_id=1, source_target_pairs={{0,64},{64,0},{1,65},{65,1},{2,66},{66,2},{3,67},{67,3},{4,68},{68... | collective-permute-start | bytes 589832 | tf_op jit(solution)/shard_map/ppermute | solution.py:26
  133.7 20.1 %copy-start.1 = (f32[48,4096]{1,0:T(8,128)S(1)}, f32[48,4096]{1,0:T(8,128)}, u32[]{:S(2)}) copy-start(f32[48,4096]{1,0:T(8,128)} %copy-done) | copy-start | bytes 2359300
  154.9 10.6 %collective-permute-start.12 = (bf16[48,1024]{1,0:T(8,128)(2,1)S(1)}, bf16[48,1024]{1,0:T(8,128)(2,1)S(1)}, u32[]{:S(2)}, u32[]{:S(2)}) collective-permute-start(bf16[48,1024]{1,0:T(8,128)(2,1)S(1)} %get-tuple-element.61), channel_id=1, source_target_pairs={{0,32},{32,0},{1,33},{33,1},{2,34},{34,2},{3,35},{35,3},{4,36},{36... | collective-permute-start | bytes 294920 | tf_op jit(solution)/shard_map/ppermute | solution.py:22
  157.7 7.8 %collective-permute-start.13 = (bf16[48,1024]{1,0:T(8,128)(2,1)S(1)}, bf16[48,1024]{1,0:T(8,128)(2,1)S(1)}, u32[]{:S(2)}, u32[]{:S(2)}) collective-permute-start(bf16[48,1024]{1,0:T(8,128)(2,1)S(1)} %get-tuple-element.62), channel_id=1, source_target_pairs={{0,64},{64,0},{1,65},{65,1},{2,66},{66,2},{3,67},{67,3},{4,68},{68... | collective-permute-start | bytes 294920 | tf_op jit(solution)/shard_map/ppermute | solution.py:26
  158.0 7.4 %collective-permute-start.14 = (bf16[48,1024]{1,0:T(8,128)(2,1)S(1)}, bf16[48,1024]{1,0:T(8,128)(2,1)S(1)}, u32[]{:S(2)}, u32[]{:S(2)}) collective-permute-start(bf16[48,1024]{1,0:T(8,128)(2,1)S(1)} %get-tuple-element.63), channel_id=1, source_target_pairs={{0,96},{32,64},{64,32},{96,0},{1,97},{33,65},{65,33},{97,1},{2,98}... | collective-permute-start | bytes 294920 | tf_op jit(solution)/shard_map/ppermute | solution.py:436
  159.4 6.0 %collective-permute-start.11 = (f32[104,128]{1,0:T(8,128)S(1)}, f32[104,128]{1,0:T(8,128)S(1)}, u32[]{:S(2)}, u32[]{:S(2)}) collective-permute-start(f32[104,128]{1,0:T(8,128)S(1)} %get-tuple-element.59), channel_id=1, source_target_pairs={{16,0},{0,16},{17,1},{1,17},{18,2},{2,18},{19,3},{3,19},{20,4},{4,... | collective-permute-start | bytes 159752 | tf_op jit(solution)/shard_map/ppermute | solution.py:31
  170.8 12.2 %copy-start.7 = (f32[24,128]{1,0:T(8,128)S(1)}, f32[24,128]{1,0:T(8,128)}, u32[]{:S(2)}) copy-start(f32[24,128]{1,0:T(8,128)} %get-tuple-element.52) | copy-start | bytes 36868
  170.8 3.7 %collective-permute-start.15 = (bf16[2,48,4096]{2,1,0:T(8,128)(2,1)S(1)}, bf16[2,48,4096]{2,1,0:T(8,128)(2,1)S(1)}, u32[]{:S(2)}, u32[]{:S(2)}) collective-permute-start(bf16[2,48,4096]{2,1,0:T(8,128)(2,1)S(1)} %get-tuple-element.72), channel_id=1, source_target_pairs={{0,32},{32,0},{1,33},{33,1},{2,34},{34,2},{3,35},{35,3},{4,36},{36... | collective-permute-start | bytes 2359304 | tf_op jit(solution)/shard_map/ppermute | solution.py:22
  171.8 4.6 %collective-permute-start.18 = (f32[104,128]{1,0:T(8,128)S(1)}, f32[104,128]{1,0:T(8,128)S(1)}, u32[]{:S(2)}, u32[]{:S(2)}) collective-permute-start(f32[104,128]{1,0:T(8,128)S(1)} %add.72), channel_id=1, source_target_pairs={{12,0},{0,4},{4,8},{8,12},{13,1},{1,5},{5,9},{9,13},{14,2},{2,6},{... | collective-permute-start | bytes 159752 | tf_op jit(solution)/shard_map/ppermute | solution.py:31
  172.1 4.2 %collective-permute-start.17 = (f32[104,128]{1,0:T(8,128)S(1)}, f32[104,128]{1,0:T(8,128)S(1)}, u32[]{:S(2)}, u32[]{:S(2)}) collective-permute-start(f32[104,128]{1,0:T(8,128)S(1)} %add.72), channel_id=1, source_target_pairs={{4,0},{8,4},{12,8},{0,12},{5,1},{9,5},{13,9},{1,13},{6,2},{10,6},{... | collective-permute-start | bytes 159752 | tf_op jit(solution)/shard_map/ppermute | solution.py:31
  174.5 4.5 %collective-permute-start.16 = (f32[104,128]{1,0:T(8,128)S(1)}, f32[104,128]{1,0:T(8,128)S(1)}, u32[]{:S(2)}, u32[]{:S(2)}) collective-permute-start(f32[104,128]{1,0:T(8,128)S(1)} %add.72), channel_id=1, source_target_pairs={{8,0},{12,4},{0,8},{4,12},{9,1},{13,5},{1,9},{5,13},{10,2},{14,6},... | collective-permute-start | bytes 159752 | tf_op jit(solution)/shard_map/ppermute | solution.py:31
  174.7 5.6 %collective-permute-start.19 = (bf16[48,2048]{1,0:T(8,128)(2,1)S(1)}, bf16[48,2048]{1,0:T(8,128)(2,1)S(1)}, u32[]{:S(2)}, u32[]{:S(2)}) collective-permute-start(bf16[48,2048]{1,0:T(8,128)(2,1)S(1)} %get-tuple-element.87), channel_id=1, source_target_pairs={{0,64},{64,0},{1,65},{65,1},{2,66},{66,2},{3,67},{67,3},{4,68},{68... | collective-permute-start | bytes 589832 | tf_op jit(solution)/shard_map/ppermute | solution.py:26
  180.3 4.2 %collective-permute-start.23 = (f32[104,128]{1,0:T(8,128)S(1)}, f32[104,128]{1,0:T(8,128)S(1)}, u32[]{:S(2)}, u32[]{:S(2)}) collective-permute-start(f32[104,128]{1,0:T(8,128)S(1)} %add_add_fusion.1), channel_id=1, source_target_pairs={{3,0},{0,1},{1,2},{2,3},{7,4},{4,5},{5,6},{6,7},{11,8},{8,9},{9,10... | collective-permute-start | bytes 159752 | tf_op jit(solution)/shard_map/ppermute | solution.py:31
  180.5 4.0 %collective-permute-start.22 = (f32[104,128]{1,0:T(8,128)S(1)}, f32[104,128]{1,0:T(8,128)S(1)}, u32[]{:S(2)}, u32[]{:S(2)}) collective-permute-start(f32[104,128]{1,0:T(8,128)S(1)} %add_add_fusion.1), channel_id=1, source_target_pairs={{1,0},{2,1},{3,2},{0,3},{5,4},{6,5},{7,6},{4,7},{9,8},{10,9},{11,1... | collective-permute-start | bytes 159752 | tf_op jit(solution)/shard_map/ppermute | solution.py:31
  183.0 4.5 %collective-permute-start.21 = (f32[104,128]{1,0:T(8,128)S(1)}, f32[104,128]{1,0:T(8,128)S(1)}, u32[]{:S(2)}, u32[]{:S(2)}) collective-permute-start(f32[104,128]{1,0:T(8,128)S(1)} %add_add_fusion.1), channel_id=1, source_target_pairs={{2,0},{3,1},{0,2},{1,3},{6,4},{7,5},{4,6},{5,7},{10,8},{11,9},{8,1... | collective-permute-start | bytes 159752 | tf_op jit(solution)/shard_map/ppermute | solution.py:31
  183.6 8.8 %collective-permute-start.20 = (bf16[48,2048]{1,0:T(8,128)(2,1)S(1)}, bf16[48,2048]{1,0:T(8,128)(2,1)S(1)}, u32[]{:S(2)}, u32[]{:S(2)}) collective-permute-start(bf16[48,2048]{1,0:T(8,128)(2,1)S(1)} %get-tuple-element.88), channel_id=1, source_target_pairs={{0,64},{64,0},{1,65},{65,1},{2,66},{66,2},{3,67},{67,3},{4,68},{68... | collective-permute-start | bytes 589832 | tf_op jit(solution)/shard_map/ppermute | solution.py:26
  187.5 5.9 %collective-permute-start.26 = (f32[104,128]{1,0:T(8,128)S(1)}, f32[104,128]{1,0:T(8,128)S(1)}, u32[]{:S(2)}, u32[]{:S(2)}) collective-permute-start(f32[104,128]{1,0:T(8,128)S(1)} %add_add_fusion.refs_0_), channel_id=1, source_target_pairs={{0,96},{32,64},{64,32},{96,0},{1,97},{33,65},{65,33},{97,1},{2,98}... | collective-permute-start | bytes 159752 | tf_op jit(solution)/shard_map/ppermute | solution.py:462
  191.0 4.4 %collective-permute-start.25 = (f32[104,128]{1,0:T(8,128)S(1)}, f32[104,128]{1,0:T(8,128)S(1)}, u32[]{:S(2)}, u32[]{:S(2)}) collective-permute-start(f32[104,128]{1,0:T(8,128)S(1)} %add_add_fusion.refs_0_), channel_id=1, source_target_pairs={{0,64},{64,0},{1,65},{65,1},{2,66},{66,2},{3,67},{67,3},{4,68},{68... | collective-permute-start | bytes 159752 | tf_op jit(solution)/shard_map/ppermute | solution.py:26
  192.5 2.9 %collective-permute-start.24 = (f32[104,128]{1,0:T(8,128)S(1)}, f32[104,128]{1,0:T(8,128)S(1)}, u32[]{:S(2)}, u32[]{:S(2)}) collective-permute-start(f32[104,128]{1,0:T(8,128)S(1)} %add_add_fusion.refs_0_), channel_id=1, source_target_pairs={{0,32},{32,0},{1,33},{33,1},{2,34},{34,2},{3,35},{35,3},{4,36},{36... | collective-permute-start | bytes 159752 | tf_op jit(solution)/shard_map/ppermute | solution.py:22
  (5 other events, 34.9 us)

commit v10 on v9

--- a/solution.py
+++ b/solution.py
@@ -29,6 +29,15 @@
 def from_ahead(values, axis, step):
     size = lax.axis_size(axis)
     return lax.ppermute(values, axis, [((i + step) % size, i) for i in range(size)])
+
+
+def double_over(values, axis):
+    size = lax.axis_size(axis)
+    step = 1
+    while step < size:
+        values = values + lax.ppermute(values, axis, [(i, i ^ step) for i in range(size)])
+        step *= 2
+    return values
 
 
 def sum_over(values, axis):
@@ -213,7 +222,7 @@
             out_ref[i // 2, :, here] = term[i * rows : (i + 1) * rows].astype(BF16)
 
 
-def softmax_kernel(hard_count, at, score_ref, losses_ref, hard_ref, group_ref, held, sem):
+def softmax_kernel(hard_count, at, score_ref, losses_ref, hard_ref, group_ref):
     rows, width = score_ref.shape
     pairs = width - LANES
     scores = score_ref[:, :pairs] / TAU
@@ -226,16 +235,10 @@
     own = jnp.sum(jnp.where(column == row + at[0], scores, 0.0), axis=1, keepdims=True)
     losses_ref[...] = jnp.broadcast_to(jnp.log(totals) - own, (rows, LANES))
     hard_probs = (hard_weights / totals).astype(BF16)
-    held[...] = (weights / totals).astype(BF16)
-    copies = [
-        pltpu.make_async_copy(held, group_ref.at[b], sem.at[b]) for b in range(group_ref.shape[0])
-    ]
-    for copy in copies:
-        copy.start()
+    probs = (weights / totals).astype(BF16)
     for b in range(hard_ref.shape[0]):
         hard_ref[b] = hard_probs
-    for copy in copies:
-        copy.wait()
+        group_ref[b] = probs
 
 
 def sums_kernel(probs_ref, q_ref, p_ref, hard_ref, add_ref, near_ref, far_ref, out_ref):
@@ -384,12 +387,8 @@
             jax.ShapeDtypeStruct((blocks, tok_rows, pairs), BF16),
         ),
         in_specs=[smem, vmem],
-        out_specs=(vmem, vmem, hbm),
-        scratch_shapes=[
-            pltpu.VMEM((tok_rows, pairs), BF16),
-            pltpu.SemaphoreType.DMA((blocks,)),
-        ],
-        compiler_params=pltpu.CompilerParams(vmem_limit_bytes=58 * 1024 * 1024),
+        out_specs=(vmem,) * 3,
+        compiler_params=params,
     )((lax.axis_index(BLK) * tok_rows).astype(jnp.int32).reshape(1), part)
     losses = losses[:, 0]
     hard_probs = exchange(hard_probs, BLK).reshape(pairs, LANES)
@@ -450,8 +449,8 @@
     far_sum = (keep[1].astype(F32) + crossed[1].astype(F32)).astype(BF16)
     first = swap_chip(far_sum[:, : width // 2])
     second = swap_chip(far_sum[:, width // 2 :])
+    vectors = double_over(vectors, "z")
     vectors, first = lax.optimization_barrier((vectors, first))
-    vectors = sum_over(vectors, "z")
     far_sum = jnp.concatenate([first, second], axis=1).astype(F32)
     grad_attn = keep[0].astype(F32) + crossed[0].astype(F32) + far_sum
 

time: 197 us -> 194 us (0.985)
  Pallas kernels: 28.7 us -> 25.9 us
    ppermute x0 -> x2, waiting for transfers between devices: none -> 6.22 us  [double_over(): lax.ppermute(values, axis, [(i, i ^ step) for i in range(size)])]
    ppermute x7 -> x4, waiting for transfers between devices: 13.2 us -> 8.01 us  [from_ahead(): lax.ppermute(values, axis, [((i + step) % size, i) for i in range(size)])]
    pallas_call x1, Pallas kernels: 3.03 us -> 0.19 us  [local(): pl.pallas_call(lambda *refs: softmax_kernel(hard_count, *refs), out_shape...]
    ppermute x7 -> x4, starting transfers between devices: 6.1 us -> 3.41 us  [from_ahead(): lax.ppermute(values, axis, [((i + step) % size, i) for i in range(size)])]
  transfers between devices with their start and end apart: 29 -> 28, of which waited for: 16 -> 15; matrix products, arithmetic and copies ran while one was open for 2% -> 2% of each run, Pallas kernels for 4% -> 4%
where the time goes in v10:
time: 194 us; the launch traced here: 193 us
  waiting for transfers between devices  58.8 us (30%)
  blocking collectives  56 us (29%)
  starting transfers between devices  40.2 us (21%)
  Pallas kernels  25.9 us (13%)
  other arithmetic  6.28 us (3%)
  local copies, waits for them, and re-layouts  3.83 us (2%)
    all_to_all x3, blocking collectives, exchange(): return lax.all_to_all(values, axes, split_axis=0, concat_axis=0, tiled=True)  56 us
    all_to_all x2, waiting for transfers between devices, exchange(): return lax.all_to_all(values, axes, split_axis=0, concat_axis=0, tiled=True)  20.2 us
    ppermute x8, waiting for transfers between devices, swap_chip(): return lax.ppermute(values, 'xl', SWAP)  18.8 us
    ppermute x9, starting transfers between devices, swap_core(): return lax.ppermute(values, 'co', SWAP)  14.6 us
    all_to_all x2, starting transfers between devices, exchange(): return lax.all_to_all(values, axes, split_axis=0, concat_axis=0, tiled=True)  8.63 us
    ppermute x4, waiting for transfers between devices, from_ahead(): lax.ppermute(values, axis, [((i + step) % size, i) for i in range(size)])  8.01 us
    pallas_call x1, Pallas kernels, local(): pl.pallas_call(lambda *refs: scatter_kernel(hard_count, tok_rows, *refs),...  7.2 us
    ppermute x8, starting transfers between devices, swap_chip(): return lax.ppermute(values, 'xl', SWAP)  6.96 us
  transfers between devices with their start and end apart: 28, of which 15 were waited for; matrix products, arithmetic and copies ran while one was open for 2% of the time, Pallas kernels for 4%

profile of v10, /device:TPU:1, one launch (start us, length us, event | category | flops | bytes accessed | tf_op | source)
XLA Modules:
  0.0 193.1 jit_solution(8104884115197237609)
XLA Ops:
  0.6 1.5 collective-permute-start.1
  5.9 7.1 %collective-permute-done.x2 = bf16[48,4096]{1,0:T(8,128)(2,1)S(1)} collective-permute-done((bf16[48,4096]{1,0:T(8,128)(2,1)}, bf16[48,4096]{1,0:T(8,128)(2,1)S(1)}, u32[]{:S(2)}, u32[]{:S(2)}) %collective-permute-start) | collective-permute-done | bytes 393248 | tf_op jit(solution)/shard_map/ppermute | solution.py:26
  16.2 3.9 %shard_map.128 = (bf16[48,1024]{1,0:T(8,128)(2,1)S(1)}, bf16[48,1024]{1,0:T(8,128)(2,1)S(1)}, bf16[48,1024]{1,0:T(8,128)(2,1)S(1)}, bf16[48,1024]{1,0:T(8,128)(2,1)S(1)}) custom-call(bf16[48,4096]{1,0:T(8,128)(2,1)S(1)} %bitcast.51, bf16[48,4096]{1,0:T(8,128)(2,1)S(1)} %collective-permute-done.1.x1, bf16[48,4096]{1,0:T(8,128)(2,1)S(1)} %collective-permute-done.x2, ...), custom_call_target="tpu_custom_call" | custom-call | tf_op jit(solution)/shard_map/pallas_call | solution.py:314
  22.4 2.5 %collective-permute-done.4.x2 = bf16[48,1024]{1,0:T(8,128)(2,1)S(1)} collective-permute-done((bf16[48,1024]{1,0:T(8,128)(2,1)S(1)}, bf16[48,1024]{1,0:T(8,128)(2,1)S(1)}, u32[]{:S(2)}, u32[]{:S(2)}) %collective-permute-start.4) | collective-permute-done | bytes 98336 | tf_op jit(solution)/shard_map/ppermute | solution.py:26
  24.9 2.4 %collective-permute-done.5.x3 = bf16[48,1024]{1,0:T(8,128)(2,1)S(1)} collective-permute-done((bf16[48,1024]{1,0:T(8,128)(2,1)S(1)}, bf16[48,1024]{1,0:T(8,128)(2,1)S(1)}, u32[]{:S(2)}, u32[]{:S(2)}) %collective-permute-start.5) | collective-permute-done | bytes 98336 | tf_op jit(solution)/shard_map/ppermute | solution.py:326
  27.7 21.6 %all_to_all.25 = bf16[32,56,128]{2,1,0:T(8,128)(2,1)S(1)} all-to-all(bf16[32,56,128]{2,1,0:T(8,128)(2,1)S(1)} %get-tuple-element.50.spread), channel_id=1, replica_groups=mesh['xl'=2,'co'=2,'xh'=2,'y'=4,'z'=4] {'xh','y','z'}, dimensions={0} | all-to-all | bytes 917504 | tf_op jit(solution)/shard_map/all_to_all | solution.py:51
  49.8 2.5 %collective-permute-start.6 = (bf16[768,128]{1,0:T(8,128)(2,1)S(1)}, bf16[768,128]{1,0:T(8,128)(2,1)S(1)}, u32[]{:S(2)}, u32[]{:S(2)}) collective-permute-start(bf16[768,128]{1,0:T(8,128)(2,1)S(1)} %bitcast.41), channel_id=1, source_target_pairs={{0,32},{32,0},{1,33},{33,1},{2,34},{34,2},{3,35},{35,3},{4,36},{36... | collective-permute-start | bytes 589832 | tf_op jit(solution)/shard_map/ppermute | solution.py:22
  52.5 1.5 collective-permute-done.7
  54.0 3.3 %collective-permute-start.8 = (bf16[768,128]{1,0:T(8,128)(2,1)S(1)}, bf16[768,128]{1,0:T(8,128)(2,1)S(1)}, u32[]{:S(2)}, u32[]{:S(2)}) collective-permute-start(bf16[768,128]{1,0:T(8,128)(2,1)S(1)} %collective-permute-done.7), channel_id=1, source_target_pairs={{0,32},{32,0},{1,33},{33,1},{2,34},{34,2},{3,35},{35,3},{4,36},{36... | collective-permute-start | bytes 589832 | tf_op jit(solution)/shard_map/ppermute | solution.py:22
  58.4 6.2 %shard_map.130 = (bf16[7,768,128]{2,1,0:T(8,128)(2,1)S(1)}, f32[768,128]{1,0:T(8,128)S(1)}) custom-call(s32[5376]{0:T(1024)S(1)} %reshape.82.refs_0_, bf16[768,128]{1,0:T(8,128)(2,1)S(1)} %bitcast.45, bf16[3072,128]{1,0:T(8,128)(2,1)S(1)} %pad_maximum_fusion.1.refs_2_), custom_call_target="tpu_custom_call" | custom-call | tf_op jit(solution)/shard_map/pallas_call | solution.py:365
  64.7 1.4 pad_maximum_fusion
  66.1 4.7 %all-to-all-start.1 = ((f16[32,24,896]{2,1,0:T(8,128)(2,1)}), f16[32,24,896]{2,1,0:T(8,128)(2,1)}, u32[]{:S(2)}, u32[]{:S(2)}) async-start(f16[32,24,896]{2,1,0:T(8,128)(2,1)} %pad_maximum_fusion), calls=%async_computation.1 | async-start | bytes 2752512 | tf_op jit(solution)/shard_map/all_to_all | solution.py:51
  70.8 20.2 %all-to-all-done.1 = f16[32,24,896]{2,1,0:T(8,128)(2,1)} async-done(((f16[32,24,896]{2,1,0:T(8,128)(2,1)}), f16[32,24,896]{2,1,0:T(8,128)(2,1)}, u32[]{:S(2)}, u32[]{:S(2)}) %all-to-all-start.1) | async-done | bytes 1376288 | tf_op jit(solution)/shard_map/all_to_all | solution.py:51
  91.0 1.5 convert_reduce_fusion.refs_1_
  93.8 15.1 %all_to_all.26 = bf16[32,24,128]{2,1,0:T(8,128)(2,1)} all-to-all(bf16[32,24,128]{2,1,0:T(8,128)(2,1)S(1)} %get-tuple-element.54), channel_id=1, replica_groups=mesh['xl'=2,'co'=2,'xh'=2,'y'=4,'z'=4] {'xh','y','z'}, dimensions={0} | all-to-all | bytes 393216 | tf_op jit(solution)/shard_map/all_to_all | solution.py:51
  108.9 3.9 %all-to-all-start.2 = ((bf16[32,24,768]{2,1,0:T(8,128)(2,1)}), bf16[32,24,768]{2,1,0:T(8,128)(2,1)S(1)}, u32[]{:S(2)}, u32[]{:S(2)}) async-start(bf16[32,24,768]{2,1,0:T(8,128)(2,1)} %copy-done), calls=%async_computation.2 | async-start | bytes 2359296 | tf_op jit(solution)/shard_map/all_to_all | solution.py:51
  113.8 7.2 %shard_map.132 = bf16[3840,128]{1,0:T(8,128)(2,1)S(1)} custom-call(s32[5376]{0:T(1024)S(1)} %reshape.82.refs_0_, bf16[768,128]{1,0:T(8,128)(2,1)S(1)} %bitcast.48, bf16[768,128]{1,0:T(8,128)(2,1)S(1)} %bitcast.46, bf16[7,768,128]{2,1,0:T(8,128)(2,1)S(1)} %get-tuple-element.55.refs_3_), custom_call_target="tpu_custom_call" | custom-call | tf_op jit(solution)/shard_map/pallas_call | solution.py:397
  121.1 2.2 %collective-permute-start.9 = (bf16[2,768,128]{2,1,0:T(8,128)(2,1)S(1)}, bf16[2,768,128]{2,1,0:T(8,128)(2,1)S(1)}, u32[]{:S(2)}, u32[]{:S(2)}) collective-permute-start(bf16[2,768,128]{2,1,0:T(8,128)(2,1)S(1)} %pad_maximum_fusion.2), channel_id=1, source_target_pairs={{0,32},{32,0},{1,33},{33,1},{2,34},{34,2},{3,35},{35,3},{4,36},{36... | collective-permute-start | bytes 1179656 | tf_op jit(solution)/shard_map/ppermute | solution.py:22
  125.3 5.8 %collective-permute-done.10.far_ref = bf16[768,128]{1,0:T(8,128)(2,1)S(1)} collective-permute-done((bf16[768,128]{1,0:T(8,128)(2,1)S(1)}, bf16[768,128]{1,0:T(8,128)(2,1)S(1)}, u32[]{:S(2)}, u32[]{:S(2)}) %collective-permute-start.10) | collective-permute-done | bytes 196640 | tf_op jit(solution)/shard_map/ppermute | solution.py:26
  131.9 19.3 %all_to_all.27.sums = bf16[32,2,24,128]{3,2,1,0:T(8,128)(2,1)S(1)} all-to-all(bf16[32,2,24,128]{3,2,1,0:T(8,128)(2,1)S(1)} %shard_map.133), channel_id=1, replica_groups=mesh['xl'=2,'co'=2,'xh'=2,'y'=4,'z'=4] {'xh','y','z'}, dimensions={0} | all-to-all | bytes 786432 | tf_op jit(solution)/shard_map/all_to_all | solution.py:51
  152.2 2.8 %collective-permute-start.12 = (bf16[48,1024]{1,0:T(8,128)(2,1)S(1)}, bf16[48,1024]{1,0:T(8,128)(2,1)S(1)}, u32[]{:S(2)}, u32[]{:S(2)}) collective-permute-start(bf16[48,1024]{1,0:T(8,128)(2,1)S(1)} %get-tuple-element.61), channel_id=1, source_target_pairs={{0,32},{32,0},{1,33},{33,1},{2,34},{34,2},{3,35},{35,3},{4,36},{36... | collective-permute-start | bytes 294920 | tf_op jit(solution)/shard_map/ppermute | solution.py:22
  155.4 1.4 collective-permute-start.14
  157.4 5.3 %collective-permute-done.11 = f32[104,128]{1,0:T(8,128)S(1)} collective-permute-done((f32[104,128]{1,0:T(8,128)S(1)}, f32[104,128]{1,0:T(8,128)S(1)}, u32[]{:S(2)}, u32[]{:S(2)}) %collective-permute-start.11) | collective-permute-done | bytes 53280 | tf_op jit(solution)/shard_map/ppermute | solution.py:31
  162.8 5.3 %shard_map.135 = (bf16[2,48,4096]{2,1,0:T(8,128)(2,1)S(1)}, bf16[2,48,4096]{2,1,0:T(8,128)(2,1)S(1)}) custom-call(bf16[48,1024]{1,0:T(8,128)(2,1)S(1)} %get-tuple-element.65.x0, bf16[48,1024]{1,0:T(8,128)(2,1)S(1)} %collective-permute-done.12.x1, bf16[48,1024]{1,0:T(8,128)(2,1)S(1)} %collective-permute-done.13.x2, ...), custom_call_target="tpu_custom_call" | custom-call | tf_op jit(solution)/shard_map/pallas_call | solution.py:438
  169.5 2.3 %collective-permute-start.17 = (f32[104,128]{1,0:T(8,128)S(1)}, f32[104,128]{1,0:T(8,128)S(1)}, u32[]{:S(2)}, u32[]{:S(2)}) collective-permute-start(f32[104,128]{1,0:T(8,128)S(1)} %add.69), channel_id=1, source_target_pairs={{4,0},{8,4},{12,8},{0,12},{5,1},{9,5},{13,9},{1,13},{6,2},{10,6},{... | collective-permute-start | bytes 159752 | tf_op jit(solution)/shard_map/ppermute | solution.py:31
  172.2 1.5 collective-permute-start.22
  173.7 2.6 %collective-permute-done.16 = f32[104,128]{1,0:T(8,128)S(1)} collective-permute-done((f32[104,128]{1,0:T(8,128)S(1)}, f32[104,128]{1,0:T(8,128)S(1)}, u32[]{:S(2)}, u32[]{:S(2)}) %collective-permute-start.16) | collective-permute-done | bytes 53280 | tf_op jit(solution)/shard_map/ppermute | solution.py:31
  176.4 3.3 %collective-permute-done.19 = f32[104,128]{1,0:T(8,128)S(1)} collective-permute-done((f32[104,128]{1,0:T(8,128)S(1)}, f32[104,128]{1,0:T(8,128)S(1)}, u32[]{:S(2)}, u32[]{:S(2)}) %collective-permute-start.19) | collective-permute-done | bytes 53280 | tf_op jit(solution)/shard_map/ppermute | solution.py:38
  181.3 3.0 %collective-permute-done.20 = f32[104,128]{1,0:T(8,128)S(1)} collective-permute-done((f32[104,128]{1,0:T(8,128)S(1)}, f32[104,128]{1,0:T(8,128)S(1)}, u32[]{:S(2)}, u32[]{:S(2)}) %collective-permute-start.20) | collective-permute-done | bytes 53280 | tf_op jit(solution)/shard_map/ppermute | solution.py:38
  184.3 3.7 %collective-permute-start.25 = (f32[104,128]{1,0:T(8,128)S(1)}, f32[104,128]{1,0:T(8,128)S(1)}, u32[]{:S(2)}, u32[]{:S(2)}) collective-permute-start(f32[104,128]{1,0:T(8,128)S(1)} %add.76.refs_0_), channel_id=1, source_target_pairs={{0,96},{32,64},{64,32},{96,0},{1,97},{33,65},{65,33},{97,1},{2,98}... | collective-permute-start | bytes 159752 | tf_op jit(solution)/shard_map/ppermute | solution.py:461
  188.0 1.5 collective-permute-start.24
  190.5 1.9 %collective-permute-done.24.refs_2_ = f32[104,128]{1,0:T(8,128)S(1)} collective-permute-done((f32[104,128]{1,0:T(8,128)S(1)}, f32[104,128]{1,0:T(8,128)S(1)}, u32[]{:S(2)}, u32[]{:S(2)}) %collective-permute-start.24) | collective-permute-done | bytes 53280 | tf_op jit(solution)/shard_map/ppermute | solution.py:26
  (77 shorter events, 23.1 us)
Async XLA Ops:
  0.6 5.3 %collective-permute-start.1 = (bf16[48,4096]{1,0:T(8,128)(2,1)}, bf16[48,4096]{1,0:T(8,128)(2,1)S(1)}, u32[]{:S(2)}, u32[]{:S(2)}) collective-permute-start(bf16[48,4096]{1,0:T(8,128)(2,1)} %bitcast.49), channel_id=1, source_target_pairs={{0,32},{32,0},{1,33},{33,1},{2,34},{34,2},{3,35},{35,3},{4,36},{36... | collective-permute-start | bytes 1179656 | tf_op jit(solution)/shard_map/ppermute | solution.py:22
  2.1 10.9 %collective-permute-start = (bf16[48,4096]{1,0:T(8,128)(2,1)}, bf16[48,4096]{1,0:T(8,128)(2,1)S(1)}, u32[]{:S(2)}, u32[]{:S(2)}) collective-permute-start(bf16[48,4096]{1,0:T(8,128)(2,1)} %bitcast.50), channel_id=1, source_target_pairs={{0,64},{64,0},{1,65},{65,1},{2,66},{66,2},{3,67},{67,3},{4,68},{68... | collective-permute-start | bytes 1179656 | tf_op jit(solution)/shard_map/ppermute | solution.py:26
  13.0 2.2 %collective-permute-start.2 = (bf16[48,4096]{1,0:T(8,128)(2,1)S(1)}, bf16[48,4096]{1,0:T(8,128)(2,1)S(1)}, u32[]{:S(2)}, u32[]{:S(2)}) collective-permute-start(bf16[48,4096]{1,0:T(8,128)(2,1)S(1)} %collective-permute-done.x2), channel_id=1, source_target_pairs={{0,32},{32,0},{1,33},{33,1},{2,34},{34,2},{3,35},{35,3},{4,36},{36... | collective-permute-start | bytes 1179656 | tf_op jit(solution)/shard_map/ppermute | solution.py:22
  16.2 11.0 %copy-start.6 = (f32[4096]{0:T(1024)S(1)}, f32[4096]{0:T(1024)}, u32[]{:S(2)}) copy-start(f32[4096]{0:T(1024)} %param.13) | copy-start | bytes 49156
  16.2 11.0 %copy-start.7 = (f32[4096]{0:T(1024)S(1)}, f32[4096]{0:T(1024)}, u32[]{:S(2)}) copy-start(f32[4096]{0:T(1024)} %param.12) | copy-start | bytes 49156
  20.2 2.2 %collective-permute-start.3 = (bf16[48,1024]{1,0:T(8,128)(2,1)S(1)}, bf16[48,1024]{1,0:T(8,128)(2,1)S(1)}, u32[]{:S(2)}, u32[]{:S(2)}) collective-permute-start(bf16[48,1024]{1,0:T(8,128)(2,1)S(1)} %get-tuple-element.45), channel_id=1, source_target_pairs={{0,32},{32,0},{1,33},{33,1},{2,34},{34,2},{3,35},{35,3},{4,36},{36... | collective-permute-start | bytes 294920 | tf_op jit(solution)/shard_map/ppermute | solution.py:22
  20.6 4.3 %collective-permute-start.4 = (bf16[48,1024]{1,0:T(8,128)(2,1)S(1)}, bf16[48,1024]{1,0:T(8,128)(2,1)S(1)}, u32[]{:S(2)}, u32[]{:S(2)}) collective-permute-start(bf16[48,1024]{1,0:T(8,128)(2,1)S(1)} %get-tuple-element.46), channel_id=1, source_target_pairs={{0,64},{64,0},{1,65},{65,1},{2,66},{66,2},{3,67},{67,3},{4,68},{68... | collective-permute-start | bytes 294920 | tf_op jit(solution)/shard_map/ppermute | solution.py:26
  21.9 5.3 %collective-permute-start.5 = (bf16[48,1024]{1,0:T(8,128)(2,1)S(1)}, bf16[48,1024]{1,0:T(8,128)(2,1)S(1)}, u32[]{:S(2)}, u32[]{:S(2)}) collective-permute-start(bf16[48,1024]{1,0:T(8,128)(2,1)S(1)} %get-tuple-element.47), channel_id=1, source_target_pairs={{0,96},{32,64},{64,32},{96,0},{1,97},{33,65},{65,33},{97,1},{2,98}... | collective-permute-start | bytes 294920 | tf_op jit(solution)/shard_map/ppermute | solution.py:326
  27.7 21.6 %copy-start.1 = (f32[48,4096]{1,0:T(8,128)}, f32[48,4096]{1,0:T(8,128)S(1)}, u32[]{:S(2)}) copy-start(f32[48,4096]{1,0:T(8,128)S(1)} %get-tuple-element.56.pooled) | copy-start | bytes 2359300
  49.4 4.6 %collective-permute-start.7 = (bf16[768,128]{1,0:T(8,128)(2,1)S(1)}, bf16[768,128]{1,0:T(8,128)(2,1)S(1)}, u32[]{:S(2)}, u32[]{:S(2)}) collective-permute-start(bf16[768,128]{1,0:T(8,128)(2,1)S(1)} %bitcast.40), channel_id=1, source_target_pairs={{0,64},{64,0},{1,65},{65,1},{2,66},{66,2},{3,67},{67,3},{4,68},{68... | collective-permute-start | bytes 589832 | tf_op jit(solution)/shard_map/ppermute | solution.py:26
  49.8 8.1 %collective-permute-start.6 = (bf16[768,128]{1,0:T(8,128)(2,1)S(1)}, bf16[768,128]{1,0:T(8,128)(2,1)S(1)}, u32[]{:S(2)}, u32[]{:S(2)}) collective-permute-start(bf16[768,128]{1,0:T(8,128)(2,1)S(1)} %bitcast.41), channel_id=1, source_target_pairs={{0,32},{32,0},{1,33},{33,1},{2,34},{34,2},{3,35},{35,3},{4,36},{36... | collective-permute-start | bytes 589832 | tf_op jit(solution)/shard_map/ppermute | solution.py:22
  54.0 4.4 %collective-permute-start.8 = (bf16[768,128]{1,0:T(8,128)(2,1)S(1)}, bf16[768,128]{1,0:T(8,128)(2,1)S(1)}, u32[]{:S(2)}, u32[]{:S(2)}) collective-permute-start(bf16[768,128]{1,0:T(8,128)(2,1)S(1)} %collective-permute-done.7), channel_id=1, source_target_pairs={{0,32},{32,0},{1,33},{33,1},{2,34},{34,2},{3,35},{35,3},{4,36},{36... | collective-permute-start | bytes 589832 | tf_op jit(solution)/shard_map/ppermute | solution.py:22
  66.1 24.9 %all-to-all-start.1 = ((f16[32,24,896]{2,1,0:T(8,128)(2,1)}), f16[32,24,896]{2,1,0:T(8,128)(2,1)}, u32[]{:S(2)}, u32[]{:S(2)}) async-start(f16[32,24,896]{2,1,0:T(8,128)(2,1)} %pad_maximum_fusion), calls=%async_computation.1 | async-start | bytes 2752512 | tf_op jit(solution)/shard_map/all_to_all | solution.py:51
  108.9 22.2 %all-to-all-start.2 = ((bf16[32,24,768]{2,1,0:T(8,128)(2,1)}), bf16[32,24,768]{2,1,0:T(8,128)(2,1)S(1)}, u32[]{:S(2)}, u32[]{:S(2)}) async-start(bf16[32,24,768]{2,1,0:T(8,128)(2,1)} %copy-done), calls=%async_computation.2 | async-start | bytes 2359296 | tf_op jit(solution)/shard_map/all_to_all | solution.py:51
  121.1 3.6 %collective-permute-start.9 = (bf16[2,768,128]{2,1,0:T(8,128)(2,1)S(1)}, bf16[2,768,128]{2,1,0:T(8,128)(2,1)S(1)}, u32[]{:S(2)}, u32[]{:S(2)}) collective-permute-start(bf16[2,768,128]{2,1,0:T(8,128)(2,1)S(1)} %pad_maximum_fusion.2), channel_id=1, source_target_pairs={{0,32},{32,0},{1,33},{33,1},{2,34},{34,2},{3,35},{35,3},{4,36},{36... | collective-permute-start | bytes 1179656 | tf_op jit(solution)/shard_map/ppermute | solution.py:22
  124.7 6.4 %collective-permute-start.10 = (bf16[768,128]{1,0:T(8,128)(2,1)S(1)}, bf16[768,128]{1,0:T(8,128)(2,1)S(1)}, u32[]{:S(2)}, u32[]{:S(2)}) collective-permute-start(bf16[768,128]{1,0:T(8,128)(2,1)S(1)} %fusion.1), channel_id=1, source_target_pairs={{0,64},{64,0},{1,65},{65,1},{2,66},{66,2},{3,67},{67,3},{4,68},{68... | collective-permute-start | bytes 589832 | tf_op jit(solution)/shard_map/ppermute | solution.py:26
  131.1 20.1 %copy-start.2 = (f32[48,4096]{1,0:T(8,128)S(1)}, f32[48,4096]{1,0:T(8,128)}, u32[]{:S(2)}) copy-start(f32[48,4096]{1,0:T(8,128)} %copy-done.1) | copy-start | bytes 2359300
  152.2 10.6 %collective-permute-start.12 = (bf16[48,1024]{1,0:T(8,128)(2,1)S(1)}, bf16[48,1024]{1,0:T(8,128)(2,1)S(1)}, u32[]{:S(2)}, u32[]{:S(2)}) collective-permute-start(bf16[48,1024]{1,0:T(8,128)(2,1)S(1)} %get-tuple-element.61), channel_id=1, source_target_pairs={{0,32},{32,0},{1,33},{33,1},{2,34},{34,2},{3,35},{35,3},{4,36},{36... | collective-permute-start | bytes 294920 | tf_op jit(solution)/shard_map/ppermute | solution.py:22
  155.0 7.8 %collective-permute-start.13 = (bf16[48,1024]{1,0:T(8,128)(2,1)S(1)}, bf16[48,1024]{1,0:T(8,128)(2,1)S(1)}, u32[]{:S(2)}, u32[]{:S(2)}) collective-permute-start(bf16[48,1024]{1,0:T(8,128)(2,1)S(1)} %get-tuple-element.62), channel_id=1, source_target_pairs={{0,64},{64,0},{1,65},{65,1},{2,66},{66,2},{3,67},{67,3},{4,68},{68... | collective-permute-start | bytes 294920 | tf_op jit(solution)/shard_map/ppermute | solution.py:26
  155.4 7.4 %collective-permute-start.14 = (bf16[48,1024]{1,0:T(8,128)(2,1)S(1)}, bf16[48,1024]{1,0:T(8,128)(2,1)S(1)}, u32[]{:S(2)}, u32[]{:S(2)}) collective-permute-start(bf16[48,1024]{1,0:T(8,128)(2,1)S(1)} %get-tuple-element.63), channel_id=1, source_target_pairs={{0,96},{32,64},{64,32},{96,0},{1,97},{33,65},{65,33},{97,1},{2,98}... | collective-permute-start | bytes 294920 | tf_op jit(solution)/shard_map/ppermute | solution.py:435
  156.8 6.0 %collective-permute-start.11 = (f32[104,128]{1,0:T(8,128)S(1)}, f32[104,128]{1,0:T(8,128)S(1)}, u32[]{:S(2)}, u32[]{:S(2)}) collective-permute-start(f32[104,128]{1,0:T(8,128)S(1)} %get-tuple-element.59), channel_id=1, source_target_pairs={{16,0},{0,16},{17,1},{1,17},{18,2},{2,18},{19,3},{3,19},{20,4},{4,... | collective-permute-start | bytes 159752 | tf_op jit(solution)/shard_map/ppermute | solution.py:31
  168.2 3.7 %collective-permute-start.15 = (bf16[2,48,4096]{2,1,0:T(8,128)(2,1)S(1)}, bf16[2,48,4096]{2,1,0:T(8,128)(2,1)S(1)}, u32[]{:S(2)}, u32[]{:S(2)}) collective-permute-start(bf16[2,48,4096]{2,1,0:T(8,128)(2,1)S(1)} %get-tuple-element.72), channel_id=1, source_target_pairs={{0,32},{32,0},{1,33},{33,1},{2,34},{34,2},{3,35},{35,3},{4,36},{36... | collective-permute-start | bytes 2359304 | tf_op jit(solution)/shard_map/ppermute | solution.py:22
  169.1 4.6 %collective-permute-start.18 = (f32[104,128]{1,0:T(8,128)S(1)}, f32[104,128]{1,0:T(8,128)S(1)}, u32[]{:S(2)}, u32[]{:S(2)}) collective-permute-start(f32[104,128]{1,0:T(8,128)S(1)} %add.69), channel_id=1, source_target_pairs={{12,0},{0,4},{4,8},{8,12},{13,1},{1,5},{5,9},{9,13},{14,2},{2,6},{... | collective-permute-start | bytes 159752 | tf_op jit(solution)/shard_map/ppermute | solution.py:31
  169.5 4.2 %collective-permute-start.17 = (f32[104,128]{1,0:T(8,128)S(1)}, f32[104,128]{1,0:T(8,128)S(1)}, u32[]{:S(2)}, u32[]{:S(2)}) collective-permute-start(f32[104,128]{1,0:T(8,128)S(1)} %add.69), channel_id=1, source_target_pairs={{4,0},{8,4},{12,8},{0,12},{5,1},{9,5},{13,9},{1,13},{6,2},{10,6},{... | collective-permute-start | bytes 159752 | tf_op jit(solution)/shard_map/ppermute | solution.py:31
  171.8 4.5 %collective-permute-start.16 = (f32[104,128]{1,0:T(8,128)S(1)}, f32[104,128]{1,0:T(8,128)S(1)}, u32[]{:S(2)}, u32[]{:S(2)}) collective-permute-start(f32[104,128]{1,0:T(8,128)S(1)} %add.69), channel_id=1, source_target_pairs={{8,0},{12,4},{0,8},{4,12},{9,1},{13,5},{1,9},{5,13},{10,2},{14,6},... | collective-permute-start | bytes 159752 | tf_op jit(solution)/shard_map/ppermute | solution.py:31
  172.1 12.2 %collective-permute-start.21 = (bf16[48,2048]{1,0:T(8,128)(2,1)S(1)}, bf16[48,2048]{1,0:T(8,128)(2,1)S(1)}, u32[]{:S(2)}, u32[]{:S(2)}) collective-permute-start(bf16[48,2048]{1,0:T(8,128)(2,1)S(1)} %get-tuple-element.87), channel_id=1, source_target_pairs={{0,64},{64,0},{1,65},{65,1},{2,66},{66,2},{3,67},{67,3},{4,68},{68... | collective-permute-start | bytes 589832 | tf_op jit(solution)/shard_map/ppermute | solution.py:26
  172.2 17.3 %collective-permute-start.22 = (bf16[48,2048]{1,0:T(8,128)(2,1)S(1)}, bf16[48,2048]{1,0:T(8,128)(2,1)S(1)}, u32[]{:S(2)}, u32[]{:S(2)}) collective-permute-start(bf16[48,2048]{1,0:T(8,128)(2,1)S(1)} %get-tuple-element.88), channel_id=1, source_target_pairs={{0,64},{64,0},{1,65},{65,1},{2,66},{66,2},{3,67},{67,3},{4,68},{68... | collective-permute-start | bytes 589832 | tf_op jit(solution)/shard_map/ppermute | solution.py:26
  176.3 3.4 %collective-permute-start.19 = (f32[104,128]{1,0:T(8,128)S(1)}, f32[104,128]{1,0:T(8,128)S(1)}, u32[]{:S(2)}, u32[]{:S(2)}) collective-permute-start(f32[104,128]{1,0:T(8,128)S(1)} %add_add_fusion), channel_id=1, source_target_pairs={{0,1},{1,0},{2,3},{3,2},{4,5},{5,4},{6,7},{7,6},{8,9},{9,8},{10,11... | collective-permute-start | bytes 159752 | tf_op jit(solution)/shard_map/ppermute | solution.py:38
  179.7 4.6 %collective-permute-start.20 = (f32[104,128]{1,0:T(8,128)S(1)}, f32[104,128]{1,0:T(8,128)S(1)}, u32[]{:S(2)}, u32[]{:S(2)}) collective-permute-start(f32[104,128]{1,0:T(8,128)S(1)} %add.75), channel_id=1, source_target_pairs={{0,2},{1,3},{2,0},{3,1},{4,6},{5,7},{6,4},{7,5},{8,10},{9,11},{10,... | collective-permute-start | bytes 159752 | tf_op jit(solution)/shard_map/ppermute | solution.py:38
  184.3 6.2 %collective-permute-start.25 = (f32[104,128]{1,0:T(8,128)S(1)}, f32[104,128]{1,0:T(8,128)S(1)}, u32[]{:S(2)}, u32[]{:S(2)}) collective-permute-start(f32[104,128]{1,0:T(8,128)S(1)} %add.76.refs_0_), channel_id=1, source_target_pairs={{0,96},{32,64},{64,32},{96,0},{1,97},{33,65},{65,33},{97,1},{2,98}... | collective-permute-start | bytes 159752 | tf_op jit(solution)/shard_map/ppermute | solution.py:461
  188.0 4.4 %collective-permute-start.24 = (f32[104,128]{1,0:T(8,128)S(1)}, f32[104,128]{1,0:T(8,128)S(1)}, u32[]{:S(2)}, u32[]{:S(2)}) collective-permute-start(f32[104,128]{1,0:T(8,128)S(1)} %add.76.refs_0_), channel_id=1, source_target_pairs={{0,64},{64,0},{1,65},{65,1},{2,66},{66,2},{3,67},{67,3},{4,68},{68... | collective-permute-start | bytes 159752 | tf_op jit(solution)/shard_map/ppermute | solution.py:26
  189.5 2.9 %collective-permute-start.23 = (f32[104,128]{1,0:T(8,128)S(1)}, f32[104,128]{1,0:T(8,128)S(1)}, u32[]{:S(2)}, u32[]{:S(2)}) collective-permute-start(f32[104,128]{1,0:T(8,128)S(1)} %add.76.refs_0_), channel_id=1, source_target_pairs={{0,32},{32,0},{1,33},{33,1},{2,34},{34,2},{3,35},{35,3},{4,36},{36... | collective-permute-start | bytes 159752 | tf_op jit(solution)/shard_map/ppermute | solution.py:22
  (4 other events, 14.0 us)

commit v11 on v10

--- a/solution.py
+++ b/solution.py
@@ -447,11 +447,10 @@
     vectors = sum_over(vectors, "y")
     crossed = swap_core(send)
     far_sum = (keep[1].astype(F32) + crossed[1].astype(F32)).astype(BF16)
-    first = swap_chip(far_sum[:, : width // 2])
-    second = swap_chip(far_sum[:, width // 2 :])
+    far_sum = swap_chip(far_sum)
     vectors = double_over(vectors, "z")
-    vectors, first = lax.optimization_barrier((vectors, first))
-    far_sum = jnp.concatenate([first, second], axis=1).astype(F32)
+    vectors, far_sum = lax.optimization_barrier((vectors, far_sum))
+    far_sum = far_sum.astype(F32)
     grad_attn = keep[0].astype(F32) + crossed[0].astype(F32) + far_sum
 
     four = [

time: 194 us -> 194 us (level)
    ppermute x8 -> x7, starting transfers between devices: 6.96 us -> 5.5 us  [swap_chip(): return lax.ppermute(values, 'xl', SWAP)]
    ppermute x8 -> x7, waiting for transfers between devices: 18.8 us -> 18.7 us  [swap_chip(): return lax.ppermute(values, 'xl', SWAP)]
  transfers between devices with their start and end apart: 28 -> 27, of which waited for: 15 -> 15; matrix products, arithmetic and copies ran while one was open for 2% -> 2% of each run, Pallas kernels for 4% -> 4%
where the time goes in v11:
time: 194 us; the launch traced here: 193 us
  waiting for transfers between devices  60.3 us (31%)
  blocking collectives  56 us (29%)
  starting transfers between devices  38.8 us (20%)
  Pallas kernels  25.9 us (13%)
  other arithmetic  6.25 us (3%)
  local copies, waits for them, and re-layouts  3.82 us (2%)
    all_to_all x3, blocking collectives, exchange(): return lax.all_to_all(values, axes, split_axis=0, concat_axis=0, tiled=True)  56 us
    all_to_all x2, waiting for transfers between devices, exchange(): return lax.all_to_all(values, axes, split_axis=0, concat_axis=0, tiled=True)  20.2 us
    ppermute x7, waiting for transfers between devices, swap_chip(): return lax.ppermute(values, 'xl', SWAP)  18.7 us
    ppermute x9, starting transfers between devices, swap_core(): return lax.ppermute(values, 'co', SWAP)  14.6 us
    ppermute x4, waiting for transfers between devices, from_ahead(): lax.ppermute(values, axis, [((i + step) % size, i) for i in range(size)])  9.57 us
    all_to_all x2, starting transfers between devices, exchange(): return lax.all_to_all(values, axes, split_axis=0, concat_axis=0, tiled=True)  8.63 us
    pallas_call x1, Pallas kernels, local(): pl.pallas_call(lambda *refs: scatter_kernel(hard_count, tok_rows, *refs),...  7.2 us
    pallas_call x1, Pallas kernels, local(): pl.pallas_call(lambda *refs: gather_kernel(hard_count, tok_rows, *refs),...  6.24 us
  transfers between devices with their start and end apart: 27, of which 15 were waited for; matrix products, arithmetic and copies ran while one was open for 2% of the time, Pallas kernels for 4%

profile of v11, /device:TPU:1, one launch (start us, length us, event | category | flops | bytes accessed | tf_op | source)
XLA Modules:
  0.0 193.1 jit_solution(7552535739123496159)
XLA Ops:
  0.6 1.5 collective-permute-start.1
  5.9 7.1 %collective-permute-done.x2 = bf16[48,4096]{1,0:T(8,128)(2,1)S(1)} collective-permute-done((bf16[48,4096]{1,0:T(8,128)(2,1)}, bf16[48,4096]{1,0:T(8,128)(2,1)S(1)}, u32[]{:S(2)}, u32[]{:S(2)}) %collective-permute-start) | collective-permute-done | bytes 393248 | tf_op jit(solution)/shard_map/ppermute | solution.py:26
  16.2 3.9 %shard_map.128 = (bf16[48,1024]{1,0:T(8,128)(2,1)S(1)}, bf16[48,1024]{1,0:T(8,128)(2,1)S(1)}, bf16[48,1024]{1,0:T(8,128)(2,1)S(1)}, bf16[48,1024]{1,0:T(8,128)(2,1)S(1)}) custom-call(bf16[48,4096]{1,0:T(8,128)(2,1)S(1)} %bitcast.51, bf16[48,4096]{1,0:T(8,128)(2,1)S(1)} %collective-permute-done.1.x1, bf16[48,4096]{1,0:T(8,128)(2,1)S(1)} %collective-permute-done.x2, ...), custom_call_target="tpu_custom_call" | custom-call | tf_op jit(solution)/shard_map/pallas_call | solution.py:314
  22.4 2.5 %collective-permute-done.4.x2 = bf16[48,1024]{1,0:T(8,128)(2,1)S(1)} collective-permute-done((bf16[48,1024]{1,0:T(8,128)(2,1)S(1)}, bf16[48,1024]{1,0:T(8,128)(2,1)S(1)}, u32[]{:S(2)}, u32[]{:S(2)}) %collective-permute-start.4) | collective-permute-done | bytes 98336 | tf_op jit(solution)/shard_map/ppermute | solution.py:26
  24.9 2.4 %collective-permute-done.5.x3 = bf16[48,1024]{1,0:T(8,128)(2,1)S(1)} collective-permute-done((bf16[48,1024]{1,0:T(8,128)(2,1)S(1)}, bf16[48,1024]{1,0:T(8,128)(2,1)S(1)}, u32[]{:S(2)}, u32[]{:S(2)}) %collective-permute-start.5) | collective-permute-done | bytes 98336 | tf_op jit(solution)/shard_map/ppermute | solution.py:326
  27.7 21.6 %all_to_all.25 = bf16[32,56,128]{2,1,0:T(8,128)(2,1)S(1)} all-to-all(bf16[32,56,128]{2,1,0:T(8,128)(2,1)S(1)} %get-tuple-element.50.spread), channel_id=1, replica_groups=mesh['xl'=2,'co'=2,'xh'=2,'y'=4,'z'=4] {'xh','y','z'}, dimensions={0} | all-to-all | bytes 917504 | tf_op jit(solution)/shard_map/all_to_all | solution.py:51
  49.8 2.5 %collective-permute-start.6 = (bf16[768,128]{1,0:T(8,128)(2,1)S(1)}, bf16[768,128]{1,0:T(8,128)(2,1)S(1)}, u32[]{:S(2)}, u32[]{:S(2)}) collective-permute-start(bf16[768,128]{1,0:T(8,128)(2,1)S(1)} %bitcast.41), channel_id=1, source_target_pairs={{0,32},{32,0},{1,33},{33,1},{2,34},{34,2},{3,35},{35,3},{4,36},{36... | collective-permute-start | bytes 589832 | tf_op jit(solution)/shard_map/ppermute | solution.py:22
  52.5 1.5 collective-permute-done.7
  54.0 3.3 %collective-permute-start.8 = (bf16[768,128]{1,0:T(8,128)(2,1)S(1)}, bf16[768,128]{1,0:T(8,128)(2,1)S(1)}, u32[]{:S(2)}, u32[]{:S(2)}) collective-permute-start(bf16[768,128]{1,0:T(8,128)(2,1)S(1)} %collective-permute-done.7), channel_id=1, source_target_pairs={{0,32},{32,0},{1,33},{33,1},{2,34},{34,2},{3,35},{35,3},{4,36},{36... | collective-permute-start | bytes 589832 | tf_op jit(solution)/shard_map/ppermute | solution.py:22
  58.4 6.2 %shard_map.130 = (bf16[7,768,128]{2,1,0:T(8,128)(2,1)S(1)}, f32[768,128]{1,0:T(8,128)S(1)}) custom-call(s32[5376]{0:T(1024)S(1)} %reshape.80.refs_0_, bf16[768,128]{1,0:T(8,128)(2,1)S(1)} %bitcast.45, bf16[3072,128]{1,0:T(8,128)(2,1)S(1)} %pad_maximum_fusion.1.refs_2_), custom_call_target="tpu_custom_call" | custom-call | tf_op jit(solution)/shard_map/pallas_call | solution.py:365
  64.7 1.4 pad_maximum_fusion
  66.1 4.7 %all-to-all-start.1 = ((f16[32,24,896]{2,1,0:T(8,128)(2,1)}), f16[32,24,896]{2,1,0:T(8,128)(2,1)}, u32[]{:S(2)}, u32[]{:S(2)}) async-start(f16[32,24,896]{2,1,0:T(8,128)(2,1)} %pad_maximum_fusion), calls=%async_computation.1 | async-start | bytes 2752512 | tf_op jit(solution)/shard_map/all_to_all | solution.py:51
  70.8 20.2 %all-to-all-done.1 = f16[32,24,896]{2,1,0:T(8,128)(2,1)} async-done(((f16[32,24,896]{2,1,0:T(8,128)(2,1)}), f16[32,24,896]{2,1,0:T(8,128)(2,1)}, u32[]{:S(2)}, u32[]{:S(2)}) %all-to-all-start.1) | async-done | bytes 1376288 | tf_op jit(solution)/shard_map/all_to_all | solution.py:51
  91.0 1.5 convert_reduce_fusion.refs_1_
  93.8 15.1 %all_to_all.26 = bf16[32,24,128]{2,1,0:T(8,128)(2,1)} all-to-all(bf16[32,24,128]{2,1,0:T(8,128)(2,1)S(1)} %get-tuple-element.54), channel_id=1, replica_groups=mesh['xl'=2,'co'=2,'xh'=2,'y'=4,'z'=4] {'xh','y','z'}, dimensions={0} | all-to-all | bytes 393216 | tf_op jit(solution)/shard_map/all_to_all | solution.py:51
  108.9 3.9 %all-to-all-start.2 = ((bf16[32,24,768]{2,1,0:T(8,128)(2,1)}), bf16[32,24,768]{2,1,0:T(8,128)(2,1)S(1)}, u32[]{:S(2)}, u32[]{:S(2)}) async-start(bf16[32,24,768]{2,1,0:T(8,128)(2,1)} %copy-done), calls=%async_computation.2 | async-start | bytes 2359296 | tf_op jit(solution)/shard_map/all_to_all | solution.py:51
  113.8 7.2 %shard_map.132 = bf16[3840,128]{1,0:T(8,128)(2,1)S(1)} custom-call(s32[5376]{0:T(1024)S(1)} %reshape.80.refs_0_, bf16[768,128]{1,0:T(8,128)(2,1)S(1)} %bitcast.48, bf16[768,128]{1,0:T(8,128)(2,1)S(1)} %bitcast.46, bf16[7,768,128]{2,1,0:T(8,128)(2,1)S(1)} %get-tuple-element.55.refs_3_), custom_call_target="tpu_custom_call" | custom-call | tf_op jit(solution)/shard_map/pallas_call | solution.py:397
  121.1 2.2 %collective-permute-start.9 = (bf16[2,768,128]{2,1,0:T(8,128)(2,1)S(1)}, bf16[2,768,128]{2,1,0:T(8,128)(2,1)S(1)}, u32[]{:S(2)}, u32[]{:S(2)}) collective-permute-start(bf16[2,768,128]{2,1,0:T(8,128)(2,1)S(1)} %pad_maximum_fusion.2), channel_id=1, source_target_pairs={{0,32},{32,0},{1,33},{33,1},{2,34},{34,2},{3,35},{35,3},{4,36},{36... | collective-permute-start | bytes 1179656 | tf_op jit(solution)/shard_map/ppermute | solution.py:22
  125.3 5.8 %collective-permute-done.10.far_ref = bf16[768,128]{1,0:T(8,128)(2,1)S(1)} collective-permute-done((bf16[768,128]{1,0:T(8,128)(2,1)S(1)}, bf16[768,128]{1,0:T(8,128)(2,1)S(1)}, u32[]{:S(2)}, u32[]{:S(2)}) %collective-permute-start.10) | collective-permute-done | bytes 196640 | tf_op jit(solution)/shard_map/ppermute | solution.py:26
  131.9 19.3 %all_to_all.27.sums = bf16[32,2,24,128]{3,2,1,0:T(8,128)(2,1)S(1)} all-to-all(bf16[32,2,24,128]{3,2,1,0:T(8,128)(2,1)S(1)} %shard_map.133), channel_id=1, replica_groups=mesh['xl'=2,'co'=2,'xh'=2,'y'=4,'z'=4] {'xh','y','z'}, dimensions={0} | all-to-all | bytes 786432 | tf_op jit(solution)/shard_map/all_to_all | solution.py:51
  152.2 2.8 %collective-permute-start.12 = (bf16[48,1024]{1,0:T(8,128)(2,1)S(1)}, bf16[48,1024]{1,0:T(8,128)(2,1)S(1)}, u32[]{:S(2)}, u32[]{:S(2)}) collective-permute-start(bf16[48,1024]{1,0:T(8,128)(2,1)S(1)} %get-tuple-element.61), channel_id=1, source_target_pairs={{0,32},{32,0},{1,33},{33,1},{2,34},{34,2},{3,35},{35,3},{4,36},{36... | collective-permute-start | bytes 294920 | tf_op jit(solution)/shard_map/ppermute | solution.py:22
  155.4 1.4 collective-permute-start.14
  157.5 5.3 %collective-permute-done.11 = f32[104,128]{1,0:T(8,128)S(1)} collective-permute-done((f32[104,128]{1,0:T(8,128)S(1)}, f32[104,128]{1,0:T(8,128)S(1)}, u32[]{:S(2)}, u32[]{:S(2)}) %collective-permute-start.11) | collective-permute-done | bytes 53280 | tf_op jit(solution)/shard_map/ppermute | solution.py:31
  162.8 5.3 %shard_map.135 = (bf16[2,48,4096]{2,1,0:T(8,128)(2,1)S(1)}, bf16[2,48,4096]{2,1,0:T(8,128)(2,1)S(1)}) custom-call(bf16[48,1024]{1,0:T(8,128)(2,1)S(1)} %get-tuple-element.65.x0, bf16[48,1024]{1,0:T(8,128)(2,1)S(1)} %collective-permute-done.12.x1, bf16[48,1024]{1,0:T(8,128)(2,1)S(1)} %collective-permute-done.13.x2, ...), custom_call_target="tpu_custom_call" | custom-call | tf_op jit(solution)/shard_map/pallas_call | solution.py:438
  169.5 2.3 %collective-permute-start.17 = (f32[104,128]{1,0:T(8,128)S(1)}, f32[104,128]{1,0:T(8,128)S(1)}, u32[]{:S(2)}, u32[]{:S(2)}) collective-permute-start(f32[104,128]{1,0:T(8,128)S(1)} %add.67), channel_id=1, source_target_pairs={{4,0},{8,4},{12,8},{0,12},{5,1},{9,5},{13,9},{1,13},{6,2},{10,6},{... | collective-permute-start | bytes 159752 | tf_op jit(solution)/shard_map/ppermute | solution.py:31
  172.1 1.7 collective-permute-done.18
  173.7 2.6 %collective-permute-done.16 = f32[104,128]{1,0:T(8,128)S(1)} collective-permute-done((f32[104,128]{1,0:T(8,128)S(1)}, f32[104,128]{1,0:T(8,128)S(1)}, u32[]{:S(2)}, u32[]{:S(2)}) %collective-permute-start.16) | collective-permute-done | bytes 53280 | tf_op jit(solution)/shard_map/ppermute | solution.py:31
  176.4 3.3 %collective-permute-done.19 = f32[104,128]{1,0:T(8,128)S(1)} collective-permute-done((f32[104,128]{1,0:T(8,128)S(1)}, f32[104,128]{1,0:T(8,128)S(1)}, u32[]{:S(2)}, u32[]{:S(2)}) %collective-permute-start.19) | collective-permute-done | bytes 53280 | tf_op jit(solution)/shard_map/ppermute | solution.py:38
  181.3 2.9 %collective-permute-done.20 = f32[104,128]{1,0:T(8,128)S(1)} collective-permute-done((f32[104,128]{1,0:T(8,128)S(1)}, f32[104,128]{1,0:T(8,128)S(1)}, u32[]{:S(2)}, u32[]{:S(2)}) %collective-permute-start.20) | collective-permute-done | bytes 53280 | tf_op jit(solution)/shard_map/ppermute | solution.py:38
  184.3 3.7 %collective-permute-start.24 = (f32[104,128]{1,0:T(8,128)S(1)}, f32[104,128]{1,0:T(8,128)S(1)}, u32[]{:S(2)}, u32[]{:S(2)}) collective-permute-start(f32[104,128]{1,0:T(8,128)S(1)} %add.74.refs_0_), channel_id=1, source_target_pairs={{0,96},{32,64},{64,32},{96,0},{1,97},{33,65},{65,33},{97,1},{2,98}... | collective-permute-start | bytes 159752 | tf_op jit(solution)/shard_map/ppermute | solution.py:460
  188.0 1.5 collective-permute-start.23
  190.5 1.9 collective-permute-done.23.refs_2_
  (74 shorter events, 23.0 us)
Async XLA Ops:
  0.6 5.3 %collective-permute-start.1 = (bf16[48,4096]{1,0:T(8,128)(2,1)}, bf16[48,4096]{1,0:T(8,128)(2,1)S(1)}, u32[]{:S(2)}, u32[]{:S(2)}) collective-permute-start(bf16[48,4096]{1,0:T(8,128)(2,1)} %bitcast.49), channel_id=1, source_target_pairs={{0,32},{32,0},{1,33},{33,1},{2,34},{34,2},{3,35},{35,3},{4,36},{36... | collective-permute-start | bytes 1179656 | tf_op jit(solution)/shard_map/ppermute | solution.py:22
  2.1 10.9 %collective-permute-start = (bf16[48,4096]{1,0:T(8,128)(2,1)}, bf16[48,4096]{1,0:T(8,128)(2,1)S(1)}, u32[]{:S(2)}, u32[]{:S(2)}) collective-permute-start(bf16[48,4096]{1,0:T(8,128)(2,1)} %bitcast.50), channel_id=1, source_target_pairs={{0,64},{64,0},{1,65},{65,1},{2,66},{66,2},{3,67},{67,3},{4,68},{68... | collective-permute-start | bytes 1179656 | tf_op jit(solution)/shard_map/ppermute | solution.py:26
  13.0 2.2 %collective-permute-start.2 = (bf16[48,4096]{1,0:T(8,128)(2,1)S(1)}, bf16[48,4096]{1,0:T(8,128)(2,1)S(1)}, u32[]{:S(2)}, u32[]{:S(2)}) collective-permute-start(bf16[48,4096]{1,0:T(8,128)(2,1)S(1)} %collective-permute-done.x2), channel_id=1, source_target_pairs={{0,32},{32,0},{1,33},{33,1},{2,34},{34,2},{3,35},{35,3},{4,36},{36... | collective-permute-start | bytes 1179656 | tf_op jit(solution)/shard_map/ppermute | solution.py:22
  16.2 11.0 %copy-start.5 = (bf16[2,24,4096]{2,1,0:T(8,128)(2,1)S(1)}, bf16[2,24,4096]{2,1,0:T(8,128)(2,1)}, u32[]{:S(2)}) copy-start(bf16[2,24,4096]{2,1,0:T(8,128)(2,1)} %param.9) | copy-start | bytes 1179652
  16.2 11.0 %copy-start.6 = (f32[4096]{0:T(1024)S(1)}, f32[4096]{0:T(1024)}, u32[]{:S(2)}) copy-start(f32[4096]{0:T(1024)} %param.13) | copy-start | bytes 49156
  16.2 11.0 %copy-start.7 = (f32[4096]{0:T(1024)S(1)}, f32[4096]{0:T(1024)}, u32[]{:S(2)}) copy-start(f32[4096]{0:T(1024)} %param.12) | copy-start | bytes 49156
  20.2 2.2 %collective-permute-start.3 = (bf16[48,1024]{1,0:T(8,128)(2,1)S(1)}, bf16[48,1024]{1,0:T(8,128)(2,1)S(1)}, u32[]{:S(2)}, u32[]{:S(2)}) collective-permute-start(bf16[48,1024]{1,0:T(8,128)(2,1)S(1)} %get-tuple-element.45), channel_id=1, source_target_pairs={{0,32},{32,0},{1,33},{33,1},{2,34},{34,2},{3,35},{35,3},{4,36},{36... | collective-permute-start | bytes 294920 | tf_op jit(solution)/shard_map/ppermute | solution.py:22
  20.6 4.3 %collective-permute-start.4 = (bf16[48,1024]{1,0:T(8,128)(2,1)S(1)}, bf16[48,1024]{1,0:T(8,128)(2,1)S(1)}, u32[]{:S(2)}, u32[]{:S(2)}) collective-permute-start(bf16[48,1024]{1,0:T(8,128)(2,1)S(1)} %get-tuple-element.46), channel_id=1, source_target_pairs={{0,64},{64,0},{1,65},{65,1},{2,66},{66,2},{3,67},{67,3},{4,68},{68... | collective-permute-start | bytes 294920 | tf_op jit(solution)/shard_map/ppermute | solution.py:26
  21.9 5.3 %collective-permute-start.5 = (bf16[48,1024]{1,0:T(8,128)(2,1)S(1)}, bf16[48,1024]{1,0:T(8,128)(2,1)S(1)}, u32[]{:S(2)}, u32[]{:S(2)}) collective-permute-start(bf16[48,1024]{1,0:T(8,128)(2,1)S(1)} %get-tuple-element.47), channel_id=1, source_target_pairs={{0,96},{32,64},{64,32},{96,0},{1,97},{33,65},{65,33},{97,1},{2,98}... | collective-permute-start | bytes 294920 | tf_op jit(solution)/shard_map/ppermute | solution.py:326
  27.7 21.6 %copy-start.1 = (f32[48,4096]{1,0:T(8,128)}, f32[48,4096]{1,0:T(8,128)S(1)}, u32[]{:S(2)}) copy-start(f32[48,4096]{1,0:T(8,128)S(1)} %get-tuple-element.56.pooled) | copy-start | bytes 2359300
  49.4 4.6 %collective-permute-start.7 = (bf16[768,128]{1,0:T(8,128)(2,1)S(1)}, bf16[768,128]{1,0:T(8,128)(2,1)S(1)}, u32[]{:S(2)}, u32[]{:S(2)}) collective-permute-start(bf16[768,128]{1,0:T(8,128)(2,1)S(1)} %bitcast.40), channel_id=1, source_target_pairs={{0,64},{64,0},{1,65},{65,1},{2,66},{66,2},{3,67},{67,3},{4,68},{68... | collective-permute-start | bytes 589832 | tf_op jit(solution)/shard_map/ppermute | solution.py:26
  49.8 8.1 %collective-permute-start.6 = (bf16[768,128]{1,0:T(8,128)(2,1)S(1)}, bf16[768,128]{1,0:T(8,128)(2,1)S(1)}, u32[]{:S(2)}, u32[]{:S(2)}) collective-permute-start(bf16[768,128]{1,0:T(8,128)(2,1)S(1)} %bitcast.41), channel_id=1, source_target_pairs={{0,32},{32,0},{1,33},{33,1},{2,34},{34,2},{3,35},{35,3},{4,36},{36... | collective-permute-start | bytes 589832 | tf_op jit(solution)/shard_map/ppermute | solution.py:22
  54.0 4.4 %collective-permute-start.8 = (bf16[768,128]{1,0:T(8,128)(2,1)S(1)}, bf16[768,128]{1,0:T(8,128)(2,1)S(1)}, u32[]{:S(2)}, u32[]{:S(2)}) collective-permute-start(bf16[768,128]{1,0:T(8,128)(2,1)S(1)} %collective-permute-done.7), channel_id=1, source_target_pairs={{0,32},{32,0},{1,33},{33,1},{2,34},{34,2},{3,35},{35,3},{4,36},{36... | collective-permute-start | bytes 589832 | tf_op jit(solution)/shard_map/ppermute | solution.py:22
  66.1 24.9 %all-to-all-start.1 = ((f16[32,24,896]{2,1,0:T(8,128)(2,1)}), f16[32,24,896]{2,1,0:T(8,128)(2,1)}, u32[]{:S(2)}, u32[]{:S(2)}) async-start(f16[32,24,896]{2,1,0:T(8,128)(2,1)} %pad_maximum_fusion), calls=%async_computation.1 | async-start | bytes 2752512 | tf_op jit(solution)/shard_map/all_to_all | solution.py:51
  108.9 22.2 %all-to-all-start.2 = ((bf16[32,24,768]{2,1,0:T(8,128)(2,1)}), bf16[32,24,768]{2,1,0:T(8,128)(2,1)S(1)}, u32[]{:S(2)}, u32[]{:S(2)}) async-start(bf16[32,24,768]{2,1,0:T(8,128)(2,1)} %copy-done), calls=%async_computation.2 | async-start | bytes 2359296 | tf_op jit(solution)/shard_map/all_to_all | solution.py:51
  121.1 3.6 %collective-permute-start.9 = (bf16[2,768,128]{2,1,0:T(8,128)(2,1)S(1)}, bf16[2,768,128]{2,1,0:T(8,128)(2,1)S(1)}, u32[]{:S(2)}, u32[]{:S(2)}) collective-permute-start(bf16[2,768,128]{2,1,0:T(8,128)(2,1)S(1)} %pad_maximum_fusion.2), channel_id=1, source_target_pairs={{0,32},{32,0},{1,33},{33,1},{2,34},{34,2},{3,35},{35,3},{4,36},{36... | collective-permute-start | bytes 1179656 | tf_op jit(solution)/shard_map/ppermute | solution.py:22
  124.7 6.4 %collective-permute-start.10 = (bf16[768,128]{1,0:T(8,128)(2,1)S(1)}, bf16[768,128]{1,0:T(8,128)(2,1)S(1)}, u32[]{:S(2)}, u32[]{:S(2)}) collective-permute-start(bf16[768,128]{1,0:T(8,128)(2,1)S(1)} %fusion.1), channel_id=1, source_target_pairs={{0,64},{64,0},{1,65},{65,1},{2,66},{66,2},{3,67},{67,3},{4,68},{68... | collective-permute-start | bytes 589832 | tf_op jit(solution)/shard_map/ppermute | solution.py:26
  131.1 20.1 %copy-start.2 = (f32[48,4096]{1,0:T(8,128)S(1)}, f32[48,4096]{1,0:T(8,128)}, u32[]{:S(2)}) copy-start(f32[48,4096]{1,0:T(8,128)} %copy-done.1) | copy-start | bytes 2359300
  152.2 10.6 %collective-permute-start.12 = (bf16[48,1024]{1,0:T(8,128)(2,1)S(1)}, bf16[48,1024]{1,0:T(8,128)(2,1)S(1)}, u32[]{:S(2)}, u32[]{:S(2)}) collective-permute-start(bf16[48,1024]{1,0:T(8,128)(2,1)S(1)} %get-tuple-element.61), channel_id=1, source_target_pairs={{0,32},{32,0},{1,33},{33,1},{2,34},{34,2},{3,35},{35,3},{4,36},{36... | collective-permute-start | bytes 294920 | tf_op jit(solution)/shard_map/ppermute | solution.py:22
  155.0 7.8 %collective-permute-start.13 = (bf16[48,1024]{1,0:T(8,128)(2,1)S(1)}, bf16[48,1024]{1,0:T(8,128)(2,1)S(1)}, u32[]{:S(2)}, u32[]{:S(2)}) collective-permute-start(bf16[48,1024]{1,0:T(8,128)(2,1)S(1)} %get-tuple-element.62), channel_id=1, source_target_pairs={{0,64},{64,0},{1,65},{65,1},{2,66},{66,2},{3,67},{67,3},{4,68},{68... | collective-permute-start | bytes 294920 | tf_op jit(solution)/shard_map/ppermute | solution.py:26
  155.4 7.4 %collective-permute-start.14 = (bf16[48,1024]{1,0:T(8,128)(2,1)S(1)}, bf16[48,1024]{1,0:T(8,128)(2,1)S(1)}, u32[]{:S(2)}, u32[]{:S(2)}) collective-permute-start(bf16[48,1024]{1,0:T(8,128)(2,1)S(1)} %get-tuple-element.63), channel_id=1, source_target_pairs={{0,96},{32,64},{64,32},{96,0},{1,97},{33,65},{65,33},{97,1},{2,98}... | collective-permute-start | bytes 294920 | tf_op jit(solution)/shard_map/ppermute | solution.py:435
  156.8 6.0 %collective-permute-start.11 = (f32[104,128]{1,0:T(8,128)S(1)}, f32[104,128]{1,0:T(8,128)S(1)}, u32[]{:S(2)}, u32[]{:S(2)}) collective-permute-start(f32[104,128]{1,0:T(8,128)S(1)} %get-tuple-element.59), channel_id=1, source_target_pairs={{16,0},{0,16},{17,1},{1,17},{18,2},{2,18},{19,3},{3,19},{20,4},{4,... | collective-permute-start | bytes 159752 | tf_op jit(solution)/shard_map/ppermute | solution.py:31
  168.2 3.7 %collective-permute-start.15 = (bf16[2,48,4096]{2,1,0:T(8,128)(2,1)S(1)}, bf16[2,48,4096]{2,1,0:T(8,128)(2,1)S(1)}, u32[]{:S(2)}, u32[]{:S(2)}) collective-permute-start(bf16[2,48,4096]{2,1,0:T(8,128)(2,1)S(1)} %get-tuple-element.72), channel_id=1, source_target_pairs={{0,32},{32,0},{1,33},{33,1},{2,34},{34,2},{3,35},{35,3},{4,36},{36... | collective-permute-start | bytes 2359304 | tf_op jit(solution)/shard_map/ppermute | solution.py:22
  169.1 4.6 %collective-permute-start.18 = (f32[104,128]{1,0:T(8,128)S(1)}, f32[104,128]{1,0:T(8,128)S(1)}, u32[]{:S(2)}, u32[]{:S(2)}) collective-permute-start(f32[104,128]{1,0:T(8,128)S(1)} %add.67), channel_id=1, source_target_pairs={{12,0},{0,4},{4,8},{8,12},{13,1},{1,5},{5,9},{9,13},{14,2},{2,6},{... | collective-permute-start | bytes 159752 | tf_op jit(solution)/shard_map/ppermute | solution.py:31
  169.5 4.2 %collective-permute-start.17 = (f32[104,128]{1,0:T(8,128)S(1)}, f32[104,128]{1,0:T(8,128)S(1)}, u32[]{:S(2)}, u32[]{:S(2)}) collective-permute-start(f32[104,128]{1,0:T(8,128)S(1)} %add.67), channel_id=1, source_target_pairs={{4,0},{8,4},{12,8},{0,12},{5,1},{9,5},{13,9},{1,13},{6,2},{10,6},{... | collective-permute-start | bytes 159752 | tf_op jit(solution)/shard_map/ppermute | solution.py:31
  171.8 4.5 %collective-permute-start.16 = (f32[104,128]{1,0:T(8,128)S(1)}, f32[104,128]{1,0:T(8,128)S(1)}, u32[]{:S(2)}, u32[]{:S(2)}) collective-permute-start(f32[104,128]{1,0:T(8,128)S(1)} %add.67), channel_id=1, source_target_pairs={{8,0},{12,4},{0,8},{4,12},{9,1},{13,5},{1,9},{5,13},{10,2},{14,6},... | collective-permute-start | bytes 159752 | tf_op jit(solution)/shard_map/ppermute | solution.py:31
  172.0 12.3 %collective-permute-start.21 = (bf16[48,4096]{1,0:T(8,128)(2,1)S(1)}, bf16[48,4096]{1,0:T(8,128)(2,1)S(1)}, u32[]{:S(2)}, u32[]{:S(2)}) collective-permute-start(bf16[48,4096]{1,0:T(8,128)(2,1)S(1)} %fusion), channel_id=1, source_target_pairs={{0,64},{64,0},{1,65},{65,1},{2,66},{66,2},{3,67},{67,3},{4,68},{68... | collective-permute-start | bytes 1179656 | tf_op jit(solution)/shard_map/ppermute | solution.py:26
  176.3 3.4 %collective-permute-start.19 = (f32[104,128]{1,0:T(8,128)S(1)}, f32[104,128]{1,0:T(8,128)S(1)}, u32[]{:S(2)}, u32[]{:S(2)}) collective-permute-start(f32[104,128]{1,0:T(8,128)S(1)} %add_add_fusion), channel_id=1, source_target_pairs={{0,1},{1,0},{2,3},{3,2},{4,5},{5,4},{6,7},{7,6},{8,9},{9,8},{10,11... | collective-permute-start | bytes 159752 | tf_op jit(solution)/shard_map/ppermute | solution.py:38
  179.7 4.6 %collective-permute-start.20 = (f32[104,128]{1,0:T(8,128)S(1)}, f32[104,128]{1,0:T(8,128)S(1)}, u32[]{:S(2)}, u32[]{:S(2)}) collective-permute-start(f32[104,128]{1,0:T(8,128)S(1)} %add.73), channel_id=1, source_target_pairs={{0,2},{1,3},{2,0},{3,1},{4,6},{5,7},{6,4},{7,5},{8,10},{9,11},{10,... | collective-permute-start | bytes 159752 | tf_op jit(solution)/shard_map/ppermute | solution.py:38
  184.3 6.2 %collective-permute-start.24 = (f32[104,128]{1,0:T(8,128)S(1)}, f32[104,128]{1,0:T(8,128)S(1)}, u32[]{:S(2)}, u32[]{:S(2)}) collective-permute-start(f32[104,128]{1,0:T(8,128)S(1)} %add.74.refs_0_), channel_id=1, source_target_pairs={{0,96},{32,64},{64,32},{96,0},{1,97},{33,65},{65,33},{97,1},{2,98}... | collective-permute-start | bytes 159752 | tf_op jit(solution)/shard_map/ppermute | solution.py:460
  188.0 4.4 %collective-permute-start.23 = (f32[104,128]{1,0:T(8,128)S(1)}, f32[104,128]{1,0:T(8,128)S(1)}, u32[]{:S(2)}, u32[]{:S(2)}) collective-permute-start(f32[104,128]{1,0:T(8,128)S(1)} %add.74.refs_0_), channel_id=1, source_target_pairs={{0,64},{64,0},{1,65},{65,1},{2,66},{66,2},{3,67},{67,3},{4,68},{68... | collective-permute-start | bytes 159752 | tf_op jit(solution)/shard_map/ppermute | solution.py:26
  189.5 2.9 %collective-permute-start.22 = (f32[104,128]{1,0:T(8,128)S(1)}, f32[104,128]{1,0:T(8,128)S(1)}, u32[]{:S(2)}, u32[]{:S(2)}) collective-permute-start(f32[104,128]{1,0:T(8,128)S(1)} %add.74.refs_0_), channel_id=1, source_target_pairs={{0,32},{32,0},{1,33},{33,1},{2,34},{34,2},{3,35},{35,3},{4,36},{36... | collective-permute-start | bytes 159752 | tf_op jit(solution)/shard_map/ppermute | solution.py:22
  (3 other events, 3.0 us)

commit v12 on v11

--- a/solution.py
+++ b/solution.py
@@ -444,7 +444,7 @@
         compiler_params=stream,
     )(*cols, out_proj)
     vectors, keep, send = lax.optimization_barrier((vectors, keep, send))
-    vectors = sum_over(vectors, "y")
+    vectors = double_over(vectors, "y")
     crossed = swap_core(send)
     far_sum = (keep[1].astype(F32) + crossed[1].astype(F32)).astype(BF16)
     far_sum = swap_chip(far_sum)

time: 194 us -> 198 us (1.021)
  waiting for transfers between devices: 60.3 us -> 63.5 us
    ppermute x2 -> x4, waiting for transfers between devices: 6.21 us -> 12.1 us  [double_over(): lax.ppermute(values, axis, [(i, i ^ step) for i in range(size)])]
    ppermute x4 -> x1, waiting for transfers between devices: 9.57 us -> 5.32 us  [from_ahead(): lax.ppermute(values, axis, [((i + step) % size, i) for i in range(size)])]
    ppermute x1, starting transfers between devices: 3.69 us -> 6.62 us  [local(): lax.ppermute(vectors, GRP, DIAGONAL)]
    ppermute x4 -> x1, starting transfers between devices: 3.42 us -> 0.68 us  [from_ahead(): lax.ppermute(values, axis, [((i + step) % size, i) for i in range(size)])]
  transfers between devices with their start and end apart: 27 -> 26, of which waited for: 15 -> 17; matrix products, arithmetic and copies ran while one was open for 2% -> 2% of each run, Pallas kernels for 4% -> 4%
where the time goes in v12:
time: 198 us; the launch traced here: 197 us
  waiting for transfers between devices  63.5 us (32%)
  blocking collectives  56 us (28%)
  starting transfers between devices  39.7 us (20%)
  Pallas kernels  25.9 us (13%)
  other arithmetic  6.26 us (3%)
  local copies, waits for them, and re-layouts  3.8 us (2%)
    all_to_all x3, blocking collectives, exchange(): return lax.all_to_all(values, axes, split_axis=0, concat_axis=0, tiled=True)  56 us
    all_to_all x2, waiting for transfers between devices, exchange(): return lax.all_to_all(values, axes, split_axis=0, concat_axis=0, tiled=True)  20.2 us
    ppermute x7, waiting for transfers between devices, swap_chip(): return lax.ppermute(values, 'xl', SWAP)  18 us
    ppermute x9, starting transfers between devices, swap_core(): return lax.ppermute(values, 'co', SWAP)  15.1 us
    ppermute x4, waiting for transfers between devices, double_over(): lax.ppermute(values, axis, [(i, i ^ step) for i in range(size)])  12.1 us
    all_to_all x2, starting transfers between devices, exchange(): return lax.all_to_all(values, axes, split_axis=0, concat_axis=0, tiled=True)  8.63 us
    pallas_call x1, Pallas kernels, local(): pl.pallas_call(lambda *refs: scatter_kernel(hard_count, tok_rows, *refs),...  7.2 us
    ppermute x1, starting transfers between devices, local(): lax.ppermute(vectors, GRP, DIAGONAL)  6.62 us
  transfers between devices with their start and end apart: 26, of which 17 were waited for; matrix products, arithmetic and copies ran while one was open for 2% of the time, Pallas kernels for 4%

profile of v12, /device:TPU:1, one launch (start us, length us, event | category | flops | bytes accessed | tf_op | source)
XLA Modules:
  0.0 197.3 jit_solution(9362569310502540792)
XLA Ops:
  0.6 1.5 collective-permute-start.1
  5.9 7.1 %collective-permute-done.x2 = bf16[48,4096]{1,0:T(8,128)(2,1)S(1)} collective-permute-done((bf16[48,4096]{1,0:T(8,128)(2,1)}, bf16[48,4096]{1,0:T(8,128)(2,1)S(1)}, u32[]{:S(2)}, u32[]{:S(2)}) %collective-permute-start) | collective-permute-done | bytes 393248 | tf_op jit(solution)/shard_map/ppermute | solution.py:26
  13.9 1.3 collective-permute-done.2.x3
  16.2 3.9 %shard_map.128 = (bf16[48,1024]{1,0:T(8,128)(2,1)S(1)}, bf16[48,1024]{1,0:T(8,128)(2,1)S(1)}, bf16[48,1024]{1,0:T(8,128)(2,1)S(1)}, bf16[48,1024]{1,0:T(8,128)(2,1)S(1)}) custom-call(bf16[48,4096]{1,0:T(8,128)(2,1)S(1)} %bitcast.51, bf16[48,4096]{1,0:T(8,128)(2,1)S(1)} %collective-permute-done.1.x1, bf16[48,4096]{1,0:T(8,128)(2,1)S(1)} %collective-permute-done.x2, ...), custom_call_target="tpu_custom_call" | custom-call | tf_op jit(solution)/shard_map/pallas_call | solution.py:314
  22.4 2.5 %collective-permute-done.4.x2 = bf16[48,1024]{1,0:T(8,128)(2,1)S(1)} collective-permute-done((bf16[48,1024]{1,0:T(8,128)(2,1)S(1)}, bf16[48,1024]{1,0:T(8,128)(2,1)S(1)}, u32[]{:S(2)}, u32[]{:S(2)}) %collective-permute-start.4) | collective-permute-done | bytes 98336 | tf_op jit(solution)/shard_map/ppermute | solution.py:26
  24.9 2.4 %collective-permute-done.5.x3 = bf16[48,1024]{1,0:T(8,128)(2,1)S(1)} collective-permute-done((bf16[48,1024]{1,0:T(8,128)(2,1)S(1)}, bf16[48,1024]{1,0:T(8,128)(2,1)S(1)}, u32[]{:S(2)}, u32[]{:S(2)}) %collective-permute-start.5) | collective-permute-done | bytes 98336 | tf_op jit(solution)/shard_map/ppermute | solution.py:326
  27.7 21.6 %all_to_all.25 = bf16[32,56,128]{2,1,0:T(8,128)(2,1)S(1)} all-to-all(bf16[32,56,128]{2,1,0:T(8,128)(2,1)S(1)} %get-tuple-element.50.spread), channel_id=1, replica_groups=mesh['xl'=2,'co'=2,'xh'=2,'y'=4,'z'=4] {'xh','y','z'}, dimensions={0} | all-to-all | bytes 917504 | tf_op jit(solution)/shard_map/all_to_all | solution.py:51
  49.8 2.5 %collective-permute-start.6 = (bf16[768,128]{1,0:T(8,128)(2,1)S(1)}, bf16[768,128]{1,0:T(8,128)(2,1)S(1)}, u32[]{:S(2)}, u32[]{:S(2)}) collective-permute-start(bf16[768,128]{1,0:T(8,128)(2,1)S(1)} %bitcast.41), channel_id=1, source_target_pairs={{0,32},{32,0},{1,33},{33,1},{2,34},{34,2},{3,35},{35,3},{4,36},{36... | collective-permute-start | bytes 589832 | tf_op jit(solution)/shard_map/ppermute | solution.py:22
  52.5 1.5 collective-permute-done.7
  54.0 3.3 %collective-permute-start.8 = (bf16[768,128]{1,0:T(8,128)(2,1)S(1)}, bf16[768,128]{1,0:T(8,128)(2,1)S(1)}, u32[]{:S(2)}, u32[]{:S(2)}) collective-permute-start(bf16[768,128]{1,0:T(8,128)(2,1)S(1)} %collective-permute-done.7), channel_id=1, source_target_pairs={{0,32},{32,0},{1,33},{33,1},{2,34},{34,2},{3,35},{35,3},{4,36},{36... | collective-permute-start | bytes 589832 | tf_op jit(solution)/shard_map/ppermute | solution.py:22
  58.4 6.2 %shard_map.130 = (bf16[7,768,128]{2,1,0:T(8,128)(2,1)S(1)}, f32[768,128]{1,0:T(8,128)S(1)}) custom-call(s32[5376]{0:T(1024)S(1)} %reshape.80.refs_0_, bf16[768,128]{1,0:T(8,128)(2,1)S(1)} %bitcast.45, bf16[3072,128]{1,0:T(8,128)(2,1)S(1)} %pad_maximum_fusion.1.refs_2_), custom_call_target="tpu_custom_call" | custom-call | tf_op jit(solution)/shard_map/pallas_call | solution.py:365
  64.7 1.4 pad_maximum_fusion
  66.1 4.7 %all-to-all-start.1 = ((f16[32,24,896]{2,1,0:T(8,128)(2,1)}), f16[32,24,896]{2,1,0:T(8,128)(2,1)}, u32[]{:S(2)}, u32[]{:S(2)}) async-start(f16[32,24,896]{2,1,0:T(8,128)(2,1)} %pad_maximum_fusion), calls=%async_computation.1 | async-start | bytes 2752512 | tf_op jit(solution)/shard_map/all_to_all | solution.py:51
  70.8 20.2 %all-to-all-done.1 = f16[32,24,896]{2,1,0:T(8,128)(2,1)} async-done(((f16[32,24,896]{2,1,0:T(8,128)(2,1)}), f16[32,24,896]{2,1,0:T(8,128)(2,1)}, u32[]{:S(2)}, u32[]{:S(2)}) %all-to-all-start.1) | async-done | bytes 1376288 | tf_op jit(solution)/shard_map/all_to_all | solution.py:51
  91.0 1.5 convert_reduce_fusion.refs_1_
  93.8 15.1 %all_to_all.26 = bf16[32,24,128]{2,1,0:T(8,128)(2,1)} all-to-all(bf16[32,24,128]{2,1,0:T(8,128)(2,1)S(1)} %get-tuple-element.54), channel_id=1, replica_groups=mesh['xl'=2,'co'=2,'xh'=2,'y'=4,'z'=4] {'xh','y','z'}, dimensions={0} | all-to-all | bytes 393216 | tf_op jit(solution)/shard_map/all_to_all | solution.py:51
  108.9 3.9 %all-to-all-start.2 = ((bf16[32,24,768]{2,1,0:T(8,128)(2,1)}), bf16[32,24,768]{2,1,0:T(8,128)(2,1)S(1)}, u32[]{:S(2)}, u32[]{:S(2)}) async-start(bf16[32,24,768]{2,1,0:T(8,128)(2,1)} %copy-done), calls=%async_computation.2 | async-start | bytes 2359296 | tf_op jit(solution)/shard_map/all_to_all | solution.py:51
  113.8 7.2 %shard_map.132 = bf16[3840,128]{1,0:T(8,128)(2,1)S(1)} custom-call(s32[5376]{0:T(1024)S(1)} %reshape.80.refs_0_, bf16[768,128]{1,0:T(8,128)(2,1)S(1)} %bitcast.48, bf16[768,128]{1,0:T(8,128)(2,1)S(1)} %bitcast.46, bf16[7,768,128]{2,1,0:T(8,128)(2,1)S(1)} %get-tuple-element.55.refs_3_), custom_call_target="tpu_custom_call" | custom-call | tf_op jit(solution)/shard_map/pallas_call | solution.py:397
  121.1 2.2 %collective-permute-start.9 = (bf16[2,768,128]{2,1,0:T(8,128)(2,1)S(1)}, bf16[2,768,128]{2,1,0:T(8,128)(2,1)S(1)}, u32[]{:S(2)}, u32[]{:S(2)}) collective-permute-start(bf16[2,768,128]{2,1,0:T(8,128)(2,1)S(1)} %pad_maximum_fusion.2), channel_id=1, source_target_pairs={{0,32},{32,0},{1,33},{33,1},{2,34},{34,2},{3,35},{35,3},{4,36},{36... | collective-permute-start | bytes 1179656 | tf_op jit(solution)/shard_map/ppermute | solution.py:22
  123.3 1.3 collective-permute-done.9
  125.3 5.8 %collective-permute-done.10.far_ref = bf16[768,128]{1,0:T(8,128)(2,1)S(1)} collective-permute-done((bf16[768,128]{1,0:T(8,128)(2,1)S(1)}, bf16[768,128]{1,0:T(8,128)(2,1)S(1)}, u32[]{:S(2)}, u32[]{:S(2)}) %collective-permute-start.10) | collective-permute-done | bytes 196640 | tf_op jit(solution)/shard_map/ppermute | solution.py:26
  131.9 19.3 %all_to_all.27.sums = bf16[32,2,24,128]{3,2,1,0:T(8,128)(2,1)S(1)} all-to-all(bf16[32,2,24,128]{3,2,1,0:T(8,128)(2,1)S(1)} %shard_map.133), channel_id=1, replica_groups=mesh['xl'=2,'co'=2,'xh'=2,'y'=4,'z'=4] {'xh','y','z'}, dimensions={0} | all-to-all | bytes 786432 | tf_op jit(solution)/shard_map/all_to_all | solution.py:51
  152.2 2.8 %collective-permute-start.12 = (bf16[48,1024]{1,0:T(8,128)(2,1)S(1)}, bf16[48,1024]{1,0:T(8,128)(2,1)S(1)}, u32[]{:S(2)}, u32[]{:S(2)}) collective-permute-start(bf16[48,1024]{1,0:T(8,128)(2,1)S(1)} %get-tuple-element.61), channel_id=1, source_target_pairs={{0,32},{32,0},{1,33},{33,1},{2,34},{34,2},{3,35},{35,3},{4,36},{36... | collective-permute-start | bytes 294920 | tf_op jit(solution)/shard_map/ppermute | solution.py:22
  155.4 1.4 collective-permute-start.14
  157.4 5.3 %collective-permute-done.11 = f32[104,128]{1,0:T(8,128)S(1)} collective-permute-done((f32[104,128]{1,0:T(8,128)S(1)}, f32[104,128]{1,0:T(8,128)S(1)}, u32[]{:S(2)}, u32[]{:S(2)}) %collective-permute-start.11) | collective-permute-done | bytes 53280 | tf_op jit(solution)/shard_map/ppermute | solution.py:31
  162.8 5.3 %shard_map.135 = (bf16[2,48,4096]{2,1,0:T(8,128)(2,1)S(1)}, bf16[2,48,4096]{2,1,0:T(8,128)(2,1)S(1)}) custom-call(bf16[48,1024]{1,0:T(8,128)(2,1)S(1)} %get-tuple-element.65.x0, bf16[48,1024]{1,0:T(8,128)(2,1)S(1)} %collective-permute-done.12.x1, bf16[48,1024]{1,0:T(8,128)(2,1)S(1)} %collective-permute-done.13.x2, ...), custom_call_target="tpu_custom_call" | custom-call | tf_op jit(solution)/shard_map/pallas_call | solution.py:438
  169.1 1.9 collective-permute-done.15
  171.6 2.6 %collective-permute-done.16 = f32[104,128]{1,0:T(8,128)S(1)} collective-permute-done((f32[104,128]{1,0:T(8,128)S(1)}, f32[104,128]{1,0:T(8,128)S(1)}, u32[]{:S(2)}, u32[]{:S(2)}) %collective-permute-start.16) | collective-permute-done | bytes 53280 | tf_op jit(solution)/shard_map/ppermute | solution.py:38
  175.6 3.2 %collective-permute-done.17 = f32[104,128]{1,0:T(8,128)S(1)} collective-permute-done((f32[104,128]{1,0:T(8,128)S(1)}, f32[104,128]{1,0:T(8,128)S(1)}, u32[]{:S(2)}, u32[]{:S(2)}) %collective-permute-start.17) | collective-permute-done | bytes 53280 | tf_op jit(solution)/shard_map/ppermute | solution.py:38
  179.0 3.3 %collective-permute-done.18 = f32[104,128]{1,0:T(8,128)S(1)} collective-permute-done((f32[104,128]{1,0:T(8,128)S(1)}, f32[104,128]{1,0:T(8,128)S(1)}, u32[]{:S(2)}, u32[]{:S(2)}) %collective-permute-start.18) | collective-permute-done | bytes 53280 | tf_op jit(solution)/shard_map/ppermute | solution.py:38
  183.9 2.9 %collective-permute-done.19 = f32[104,128]{1,0:T(8,128)S(1)} collective-permute-done((f32[104,128]{1,0:T(8,128)S(1)}, f32[104,128]{1,0:T(8,128)S(1)}, u32[]{:S(2)}, u32[]{:S(2)}) %collective-permute-start.19) | collective-permute-done | bytes 53280 | tf_op jit(solution)/shard_map/ppermute | solution.py:38
  186.8 6.6 %collective-permute-start.23 = (f32[104,128]{1,0:T(8,128)S(1)}, f32[104,128]{1,0:T(8,128)S(1)}, u32[]{:S(2)}, u32[]{:S(2)}) collective-permute-start(f32[104,128]{1,0:T(8,128)S(1)} %add.70.refs_0_), channel_id=1, source_target_pairs={{0,96},{32,64},{64,32},{96,0},{1,97},{33,65},{65,33},{97,1},{2,98}... | collective-permute-start | bytes 159752 | tf_op jit(solution)/shard_map/ppermute | solution.py:460
  (73 shorter events, 23.7 us)
Async XLA Ops:
  0.6 5.3 %collective-permute-start.1 = (bf16[48,4096]{1,0:T(8,128)(2,1)}, bf16[48,4096]{1,0:T(8,128)(2,1)S(1)}, u32[]{:S(2)}, u32[]{:S(2)}) collective-permute-start(bf16[48,4096]{1,0:T(8,128)(2,1)} %bitcast.49), channel_id=1, source_target_pairs={{0,32},{32,0},{1,33},{33,1},{2,34},{34,2},{3,35},{35,3},{4,36},{36... | collective-permute-start | bytes 1179656 | tf_op jit(solution)/shard_map/ppermute | solution.py:22
  2.1 10.9 %collective-permute-start = (bf16[48,4096]{1,0:T(8,128)(2,1)}, bf16[48,4096]{1,0:T(8,128)(2,1)S(1)}, u32[]{:S(2)}, u32[]{:S(2)}) collective-permute-start(bf16[48,4096]{1,0:T(8,128)(2,1)} %bitcast.50), channel_id=1, source_target_pairs={{0,64},{64,0},{1,65},{65,1},{2,66},{66,2},{3,67},{67,3},{4,68},{68... | collective-permute-start | bytes 1179656 | tf_op jit(solution)/shard_map/ppermute | solution.py:26
  13.0 2.2 %collective-permute-start.2 = (bf16[48,4096]{1,0:T(8,128)(2,1)S(1)}, bf16[48,4096]{1,0:T(8,128)(2,1)S(1)}, u32[]{:S(2)}, u32[]{:S(2)}) collective-permute-start(bf16[48,4096]{1,0:T(8,128)(2,1)S(1)} %collective-permute-done.x2), channel_id=1, source_target_pairs={{0,32},{32,0},{1,33},{33,1},{2,34},{34,2},{3,35},{35,3},{4,36},{36... | collective-permute-start | bytes 1179656 | tf_op jit(solution)/shard_map/ppermute | solution.py:22
  16.2 11.0 %copy-start.5 = (bf16[2,24,4096]{2,1,0:T(8,128)(2,1)S(1)}, bf16[2,24,4096]{2,1,0:T(8,128)(2,1)}, u32[]{:S(2)}) copy-start(bf16[2,24,4096]{2,1,0:T(8,128)(2,1)} %param.9) | copy-start | bytes 1179652
  16.2 11.0 %copy-start.6 = (f32[4096]{0:T(1024)S(1)}, f32[4096]{0:T(1024)}, u32[]{:S(2)}) copy-start(f32[4096]{0:T(1024)} %param.13) | copy-start | bytes 49156
  16.2 11.0 %copy-start.7 = (f32[4096]{0:T(1024)S(1)}, f32[4096]{0:T(1024)}, u32[]{:S(2)}) copy-start(f32[4096]{0:T(1024)} %param.12) | copy-start | bytes 49156
  20.2 2.2 %collective-permute-start.3 = (bf16[48,1024]{1,0:T(8,128)(2,1)S(1)}, bf16[48,1024]{1,0:T(8,128)(2,1)S(1)}, u32[]{:S(2)}, u32[]{:S(2)}) collective-permute-start(bf16[48,1024]{1,0:T(8,128)(2,1)S(1)} %get-tuple-element.45), channel_id=1, source_target_pairs={{0,32},{32,0},{1,33},{33,1},{2,34},{34,2},{3,35},{35,3},{4,36},{36... | collective-permute-start | bytes 294920 | tf_op jit(solution)/shard_map/ppermute | solution.py:22
  20.6 4.3 %collective-permute-start.4 = (bf16[48,1024]{1,0:T(8,128)(2,1)S(1)}, bf16[48,1024]{1,0:T(8,128)(2,1)S(1)}, u32[]{:S(2)}, u32[]{:S(2)}) collective-permute-start(bf16[48,1024]{1,0:T(8,128)(2,1)S(1)} %get-tuple-element.46), channel_id=1, source_target_pairs={{0,64},{64,0},{1,65},{65,1},{2,66},{66,2},{3,67},{67,3},{4,68},{68... | collective-permute-start | bytes 294920 | tf_op jit(solution)/shard_map/ppermute | solution.py:26
  21.9 5.3 %collective-permute-start.5 = (bf16[48,1024]{1,0:T(8,128)(2,1)S(1)}, bf16[48,1024]{1,0:T(8,128)(2,1)S(1)}, u32[]{:S(2)}, u32[]{:S(2)}) collective-permute-start(bf16[48,1024]{1,0:T(8,128)(2,1)S(1)} %get-tuple-element.47), channel_id=1, source_target_pairs={{0,96},{32,64},{64,32},{96,0},{1,97},{33,65},{65,33},{97,1},{2,98}... | collective-permute-start | bytes 294920 | tf_op jit(solution)/shard_map/ppermute | solution.py:326
  27.7 21.6 %copy-start.1 = (f32[48,4096]{1,0:T(8,128)}, f32[48,4096]{1,0:T(8,128)S(1)}, u32[]{:S(2)}) copy-start(f32[48,4096]{1,0:T(8,128)S(1)} %get-tuple-element.56.pooled) | copy-start | bytes 2359300
  49.4 4.6 %collective-permute-start.7 = (bf16[768,128]{1,0:T(8,128)(2,1)S(1)}, bf16[768,128]{1,0:T(8,128)(2,1)S(1)}, u32[]{:S(2)}, u32[]{:S(2)}) collective-permute-start(bf16[768,128]{1,0:T(8,128)(2,1)S(1)} %bitcast.40), channel_id=1, source_target_pairs={{0,64},{64,0},{1,65},{65,1},{2,66},{66,2},{3,67},{67,3},{4,68},{68... | collective-permute-start | bytes 589832 | tf_op jit(solution)/shard_map/ppermute | solution.py:26
  49.8 8.1 %collective-permute-start.6 = (bf16[768,128]{1,0:T(8,128)(2,1)S(1)}, bf16[768,128]{1,0:T(8,128)(2,1)S(1)}, u32[]{:S(2)}, u32[]{:S(2)}) collective-permute-start(bf16[768,128]{1,0:T(8,128)(2,1)S(1)} %bitcast.41), channel_id=1, source_target_pairs={{0,32},{32,0},{1,33},{33,1},{2,34},{34,2},{3,35},{35,3},{4,36},{36... | collective-permute-start | bytes 589832 | tf_op jit(solution)/shard_map/ppermute | solution.py:22
  54.0 4.4 %collective-permute-start.8 = (bf16[768,128]{1,0:T(8,128)(2,1)S(1)}, bf16[768,128]{1,0:T(8,128)(2,1)S(1)}, u32[]{:S(2)}, u32[]{:S(2)}) collective-permute-start(bf16[768,128]{1,0:T(8,128)(2,1)S(1)} %collective-permute-done.7), channel_id=1, source_target_pairs={{0,32},{32,0},{1,33},{33,1},{2,34},{34,2},{3,35},{35,3},{4,36},{36... | collective-permute-start | bytes 589832 | tf_op jit(solution)/shard_map/ppermute | solution.py:22
  66.1 24.9 %all-to-all-start.1 = ((f16[32,24,896]{2,1,0:T(8,128)(2,1)}), f16[32,24,896]{2,1,0:T(8,128)(2,1)}, u32[]{:S(2)}, u32[]{:S(2)}) async-start(f16[32,24,896]{2,1,0:T(8,128)(2,1)} %pad_maximum_fusion), calls=%async_computation.1 | async-start | bytes 2752512 | tf_op jit(solution)/shard_map/all_to_all | solution.py:51
  92.7 1.0 copy-start
  108.9 22.2 %all-to-all-start.2 = ((bf16[32,24,768]{2,1,0:T(8,128)(2,1)}), bf16[32,24,768]{2,1,0:T(8,128)(2,1)S(1)}, u32[]{:S(2)}, u32[]{:S(2)}) async-start(bf16[32,24,768]{2,1,0:T(8,128)(2,1)} %copy-done), calls=%async_computation.2 | async-start | bytes 2359296 | tf_op jit(solution)/shard_map/all_to_all | solution.py:51
  121.1 3.6 %collective-permute-start.9 = (bf16[2,768,128]{2,1,0:T(8,128)(2,1)S(1)}, bf16[2,768,128]{2,1,0:T(8,128)(2,1)S(1)}, u32[]{:S(2)}, u32[]{:S(2)}) collective-permute-start(bf16[2,768,128]{2,1,0:T(8,128)(2,1)S(1)} %pad_maximum_fusion.2), channel_id=1, source_target_pairs={{0,32},{32,0},{1,33},{33,1},{2,34},{34,2},{3,35},{35,3},{4,36},{36... | collective-permute-start | bytes 1179656 | tf_op jit(solution)/shard_map/ppermute | solution.py:22
  124.7 6.4 %collective-permute-start.10 = (bf16[768,128]{1,0:T(8,128)(2,1)S(1)}, bf16[768,128]{1,0:T(8,128)(2,1)S(1)}, u32[]{:S(2)}, u32[]{:S(2)}) collective-permute-start(bf16[768,128]{1,0:T(8,128)(2,1)S(1)} %fusion.1), channel_id=1, source_target_pairs={{0,64},{64,0},{1,65},{65,1},{2,66},{66,2},{3,67},{67,3},{4,68},{68... | collective-permute-start | bytes 589832 | tf_op jit(solution)/shard_map/ppermute | solution.py:26
  131.1 20.1 %copy-start.2 = (f32[48,4096]{1,0:T(8,128)S(1)}, f32[48,4096]{1,0:T(8,128)}, u32[]{:S(2)}) copy-start(f32[48,4096]{1,0:T(8,128)} %copy-done.1) | copy-start | bytes 2359300
  152.2 10.6 %collective-permute-start.12 = (bf16[48,1024]{1,0:T(8,128)(2,1)S(1)}, bf16[48,1024]{1,0:T(8,128)(2,1)S(1)}, u32[]{:S(2)}, u32[]{:S(2)}) collective-permute-start(bf16[48,1024]{1,0:T(8,128)(2,1)S(1)} %get-tuple-element.61), channel_id=1, source_target_pairs={{0,32},{32,0},{1,33},{33,1},{2,34},{34,2},{3,35},{35,3},{4,36},{36... | collective-permute-start | bytes 294920 | tf_op jit(solution)/shard_map/ppermute | solution.py:22
  155.0 7.8 %collective-permute-start.13 = (bf16[48,1024]{1,0:T(8,128)(2,1)S(1)}, bf16[48,1024]{1,0:T(8,128)(2,1)S(1)}, u32[]{:S(2)}, u32[]{:S(2)}) collective-permute-start(bf16[48,1024]{1,0:T(8,128)(2,1)S(1)} %get-tuple-element.62), channel_id=1, source_target_pairs={{0,64},{64,0},{1,65},{65,1},{2,66},{66,2},{3,67},{67,3},{4,68},{68... | collective-permute-start | bytes 294920 | tf_op jit(solution)/shard_map/ppermute | solution.py:26
  155.4 7.4 %collective-permute-start.14 = (bf16[48,1024]{1,0:T(8,128)(2,1)S(1)}, bf16[48,1024]{1,0:T(8,128)(2,1)S(1)}, u32[]{:S(2)}, u32[]{:S(2)}) collective-permute-start(bf16[48,1024]{1,0:T(8,128)(2,1)S(1)} %get-tuple-element.63), channel_id=1, source_target_pairs={{0,96},{32,64},{64,32},{96,0},{1,97},{33,65},{65,33},{97,1},{2,98}... | collective-permute-start | bytes 294920 | tf_op jit(solution)/shard_map/ppermute | solution.py:435
  156.8 6.0 %collective-permute-start.11 = (f32[104,128]{1,0:T(8,128)S(1)}, f32[104,128]{1,0:T(8,128)S(1)}, u32[]{:S(2)}, u32[]{:S(2)}) collective-permute-start(f32[104,128]{1,0:T(8,128)S(1)} %get-tuple-element.59), channel_id=1, source_target_pairs={{16,0},{0,16},{17,1},{1,17},{18,2},{2,18},{19,3},{3,19},{20,4},{4,... | collective-permute-start | bytes 159752 | tf_op jit(solution)/shard_map/ppermute | solution.py:31
  168.2 2.9 %collective-permute-start.15 = (bf16[2,48,4096]{2,1,0:T(8,128)(2,1)S(1)}, bf16[2,48,4096]{2,1,0:T(8,128)(2,1)S(1)}, u32[]{:S(2)}, u32[]{:S(2)}) collective-permute-start(bf16[2,48,4096]{2,1,0:T(8,128)(2,1)S(1)} %get-tuple-element.72), channel_id=1, source_target_pairs={{0,32},{32,0},{1,33},{33,1},{2,34},{34,2},{3,35},{35,3},{4,36},{36... | collective-permute-start | bytes 2359304 | tf_op jit(solution)/shard_map/ppermute | solution.py:22
  171.1 15.7 %collective-permute-start.20 = (bf16[48,4096]{1,0:T(8,128)(2,1)S(1)}, bf16[48,4096]{1,0:T(8,128)(2,1)S(1)}, u32[]{:S(2)}, u32[]{:S(2)}) collective-permute-start(bf16[48,4096]{1,0:T(8,128)(2,1)S(1)} %fusion), channel_id=1, source_target_pairs={{0,64},{64,0},{1,65},{65,1},{2,66},{66,2},{3,67},{67,3},{4,68},{68... | collective-permute-start | bytes 1179656 | tf_op jit(solution)/shard_map/ppermute | solution.py:26
  171.2 3.1 %collective-permute-start.16 = (f32[104,128]{1,0:T(8,128)S(1)}, f32[104,128]{1,0:T(8,128)S(1)}, u32[]{:S(2)}, u32[]{:S(2)}) collective-permute-start(f32[104,128]{1,0:T(8,128)S(1)} %add.64), channel_id=1, source_target_pairs={{0,4},{4,0},{8,12},{12,8},{1,5},{5,1},{9,13},{13,9},{2,6},{6,2},{1... | collective-permute-start | bytes 159752 | tf_op jit(solution)/shard_map/ppermute | solution.py:38
  174.3 4.6 %collective-permute-start.17 = (f32[104,128]{1,0:T(8,128)S(1)}, f32[104,128]{1,0:T(8,128)S(1)}, u32[]{:S(2)}, u32[]{:S(2)}) collective-permute-start(f32[104,128]{1,0:T(8,128)S(1)} %add.67), channel_id=1, source_target_pairs={{0,8},{4,12},{8,0},{12,4},{1,9},{5,13},{9,1},{13,5},{2,10},{6,14},... | collective-permute-start | bytes 159752 | tf_op jit(solution)/shard_map/ppermute | solution.py:38
  178.9 3.4 %collective-permute-start.18 = (f32[104,128]{1,0:T(8,128)S(1)}, f32[104,128]{1,0:T(8,128)S(1)}, u32[]{:S(2)}, u32[]{:S(2)}) collective-permute-start(f32[104,128]{1,0:T(8,128)S(1)} %add.68), channel_id=1, source_target_pairs={{0,1},{1,0},{2,3},{3,2},{4,5},{5,4},{6,7},{7,6},{8,9},{9,8},{10,11... | collective-permute-start | bytes 159752 | tf_op jit(solution)/shard_map/ppermute | solution.py:38
  182.2 4.6 %collective-permute-start.19 = (f32[104,128]{1,0:T(8,128)S(1)}, f32[104,128]{1,0:T(8,128)S(1)}, u32[]{:S(2)}, u32[]{:S(2)}) collective-permute-start(f32[104,128]{1,0:T(8,128)S(1)} %add.69), channel_id=1, source_target_pairs={{0,2},{1,3},{2,0},{3,1},{4,6},{5,7},{6,4},{7,5},{8,10},{9,11},{10,... | collective-permute-start | bytes 159752 | tf_op jit(solution)/shard_map/ppermute | solution.py:38
  186.8 8.6 %collective-permute-start.23 = (f32[104,128]{1,0:T(8,128)S(1)}, f32[104,128]{1,0:T(8,128)S(1)}, u32[]{:S(2)}, u32[]{:S(2)}) collective-permute-start(f32[104,128]{1,0:T(8,128)S(1)} %add.70.refs_0_), channel_id=1, source_target_pairs={{0,96},{32,64},{64,32},{96,0},{1,97},{33,65},{65,33},{97,1},{2,98}... | collective-permute-start | bytes 159752 | tf_op jit(solution)/shard_map/ppermute | solution.py:460
  193.5 3.1 %collective-permute-start.22 = (f32[104,128]{1,0:T(8,128)S(1)}, f32[104,128]{1,0:T(8,128)S(1)}, u32[]{:S(2)}, u32[]{:S(2)}) collective-permute-start(f32[104,128]{1,0:T(8,128)S(1)} %add.70.refs_0_), channel_id=1, source_target_pairs={{0,64},{64,0},{1,65},{65,1},{2,66},{66,2},{3,67},{67,3},{4,68},{68... | collective-permute-start | bytes 159752 | tf_op jit(solution)/shard_map/ppermute | solution.py:26
  193.5 3.1 %collective-permute-start.21 = (f32[104,128]{1,0:T(8,128)S(1)}, f32[104,128]{1,0:T(8,128)S(1)}, u32[]{:S(2)}, u32[]{:S(2)}) collective-permute-start(f32[104,128]{1,0:T(8,128)S(1)} %add.70.refs_0_), channel_id=1, source_target_pairs={{0,32},{32,0},{1,33},{33,1},{2,34},{34,2},{3,35},{35,3},{4,36},{36... | collective-permute-start | bytes 159752 | tf_op jit(solution)/shard_map/ppermute | solution.py:22
  (2 other events, 1.9 us)

commit v13 on v12

--- a/solution.py
+++ b/solution.py
@@ -448,7 +448,7 @@
     crossed = swap_core(send)
     far_sum = (keep[1].astype(F32) + crossed[1].astype(F32)).astype(BF16)
     far_sum = swap_chip(far_sum)
-    vectors = double_over(vectors, "z")
+    vectors = sum_over(vectors, "z")
     vectors, far_sum = lax.optimization_barrier((vectors, far_sum))
     far_sum = far_sum.astype(F32)
     grad_attn = keep[0].astype(F32) + crossed[0].astype(F32) + far_sum

time: 198 us -> 194 us (0.980)
  waiting for transfers between devices: 63.5 us -> 59.8 us
    ppermute x4 -> x2, waiting for transfers between devices: 12.1 us -> 6.05 us  [double_over(): lax.ppermute(values, axis, [(i, i ^ step) for i in range(size)])]
    ppermute x1 -> x4, waiting for transfers between devices: 5.32 us -> 9.26 us  [from_ahead(): lax.ppermute(values, axis, [((i + step) % size, i) for i in range(size)])]
    ppermute x1, starting transfers between devices: 6.62 us -> 3.56 us  [local(): lax.ppermute(vectors, GRP, DIAGONAL)]
    ppermute x1 -> x4, starting transfers between devices: 0.68 us -> 3.42 us  [from_ahead(): lax.ppermute(values, axis, [((i + step) % size, i) for i in range(size)])]
  transfers between devices with their start and end apart: 26 -> 27, of which waited for: 17 -> 15; matrix products, arithmetic and copies ran while one was open for 2% -> 2% of each run, Pallas kernels for 4% -> 4%
where the time goes in v13:
time: 194 us; the launch traced here: 193 us
  waiting for transfers between devices  59.8 us (31%)
  blocking collectives  56 us (29%)
  starting transfers between devices  39.3 us (20%)
  Pallas kernels  25.9 us (13%)
  other arithmetic  6.25 us (3%)
  local copies, waits for them, and re-layouts  3.82 us (2%)
    all_to_all x3, blocking collectives, exchange(): return lax.all_to_all(values, axes, split_axis=0, concat_axis=0, tiled=True)  56 us
    all_to_all x2, waiting for transfers between devices, exchange(): return lax.all_to_all(values, axes, split_axis=0, concat_axis=0, tiled=True)  20.2 us
    ppermute x7, waiting for transfers between devices, swap_chip(): return lax.ppermute(values, 'xl', SWAP)  18.7 us
    ppermute x9, starting transfers between devices, swap_core(): return lax.ppermute(values, 'co', SWAP)  14.6 us
    ppermute x4, waiting for transfers between devices, from_ahead(): lax.ppermute(values, axis, [((i + step) % size, i) for i in range(size)])  9.26 us
    all_to_all x2, starting transfers between devices, exchange(): return lax.all_to_all(values, axes, split_axis=0, concat_axis=0, tiled=True)  8.63 us
    pallas_call x1, Pallas kernels, local(): pl.pallas_call(lambda *refs: scatter_kernel(hard_count, tok_rows, *refs),...  7.2 us
    pallas_call x1, Pallas kernels, local(): pl.pallas_call(lambda *refs: gather_kernel(hard_count, tok_rows, *refs),...  6.24 us
  transfers between devices with their start and end apart: 27, of which 15 were waited for; matrix products, arithmetic and copies ran while one was open for 2% of the time, Pallas kernels for 4%

profile of v13, /device:TPU:1, one launch (start us, length us, event | category | flops | bytes accessed | tf_op | source)
XLA Modules:
  0.0 193.1 jit_solution(16327932357457324825)
XLA Ops:
  0.6 1.5 collective-permute-start.1
  5.9 7.1 %collective-permute-done.x2 = bf16[48,4096]{1,0:T(8,128)(2,1)S(1)} collective-permute-done((bf16[48,4096]{1,0:T(8,128)(2,1)}, bf16[48,4096]{1,0:T(8,128)(2,1)S(1)}, u32[]{:S(2)}, u32[]{:S(2)}) %collective-permute-start) | collective-permute-done | bytes 393248 | tf_op jit(solution)/shard_map/ppermute | solution.py:26
  16.2 3.9 %shard_map.128 = (bf16[48,1024]{1,0:T(8,128)(2,1)S(1)}, bf16[48,1024]{1,0:T(8,128)(2,1)S(1)}, bf16[48,1024]{1,0:T(8,128)(2,1)S(1)}, bf16[48,1024]{1,0:T(8,128)(2,1)S(1)}) custom-call(bf16[48,4096]{1,0:T(8,128)(2,1)S(1)} %bitcast.51, bf16[48,4096]{1,0:T(8,128)(2,1)S(1)} %collective-permute-done.1.x1, bf16[48,4096]{1,0:T(8,128)(2,1)S(1)} %collective-permute-done.x2, ...), custom_call_target="tpu_custom_call" | custom-call | tf_op jit(solution)/shard_map/pallas_call | solution.py:314
  22.4 2.5 %collective-permute-done.4.x2 = bf16[48,1024]{1,0:T(8,128)(2,1)S(1)} collective-permute-done((bf16[48,1024]{1,0:T(8,128)(2,1)S(1)}, bf16[48,1024]{1,0:T(8,128)(2,1)S(1)}, u32[]{:S(2)}, u32[]{:S(2)}) %collective-permute-start.4) | collective-permute-done | bytes 98336 | tf_op jit(solution)/shard_map/ppermute | solution.py:26
  24.9 2.4 %collective-permute-done.5.x3 = bf16[48,1024]{1,0:T(8,128)(2,1)S(1)} collective-permute-done((bf16[48,1024]{1,0:T(8,128)(2,1)S(1)}, bf16[48,1024]{1,0:T(8,128)(2,1)S(1)}, u32[]{:S(2)}, u32[]{:S(2)}) %collective-permute-start.5) | collective-permute-done | bytes 98336 | tf_op jit(solution)/shard_map/ppermute | solution.py:326
  27.7 21.6 %all_to_all.25 = bf16[32,56,128]{2,1,0:T(8,128)(2,1)S(1)} all-to-all(bf16[32,56,128]{2,1,0:T(8,128)(2,1)S(1)} %get-tuple-element.50.spread), channel_id=1, replica_groups=mesh['xl'=2,'co'=2,'xh'=2,'y'=4,'z'=4] {'xh','y','z'}, dimensions={0} | all-to-all | bytes 917504 | tf_op jit(solution)/shard_map/all_to_all | solution.py:51
  49.8 2.5 %collective-permute-start.6 = (bf16[768,128]{1,0:T(8,128)(2,1)S(1)}, bf16[768,128]{1,0:T(8,128)(2,1)S(1)}, u32[]{:S(2)}, u32[]{:S(2)}) collective-permute-start(bf16[768,128]{1,0:T(8,128)(2,1)S(1)} %bitcast.41), channel_id=1, source_target_pairs={{0,32},{32,0},{1,33},{33,1},{2,34},{34,2},{3,35},{35,3},{4,36},{36... | collective-permute-start | bytes 589832 | tf_op jit(solution)/shard_map/ppermute | solution.py:22
  52.5 1.5 collective-permute-done.7
  54.0 3.3 %collective-permute-start.8 = (bf16[768,128]{1,0:T(8,128)(2,1)S(1)}, bf16[768,128]{1,0:T(8,128)(2,1)S(1)}, u32[]{:S(2)}, u32[]{:S(2)}) collective-permute-start(bf16[768,128]{1,0:T(8,128)(2,1)S(1)} %collective-permute-done.7), channel_id=1, source_target_pairs={{0,32},{32,0},{1,33},{33,1},{2,34},{34,2},{3,35},{35,3},{4,36},{36... | collective-permute-start | bytes 589832 | tf_op jit(solution)/shard_map/ppermute | solution.py:22
  58.4 6.2 %shard_map.130 = (bf16[7,768,128]{2,1,0:T(8,128)(2,1)S(1)}, f32[768,128]{1,0:T(8,128)S(1)}) custom-call(s32[5376]{0:T(1024)S(1)} %reshape.80.refs_0_, bf16[768,128]{1,0:T(8,128)(2,1)S(1)} %bitcast.45, bf16[3072,128]{1,0:T(8,128)(2,1)S(1)} %pad_maximum_fusion.1.refs_2_), custom_call_target="tpu_custom_call" | custom-call | tf_op jit(solution)/shard_map/pallas_call | solution.py:365
  64.7 1.4 pad_maximum_fusion
  66.1 4.7 %all-to-all-start.1 = ((f16[32,24,896]{2,1,0:T(8,128)(2,1)}), f16[32,24,896]{2,1,0:T(8,128)(2,1)}, u32[]{:S(2)}, u32[]{:S(2)}) async-start(f16[32,24,896]{2,1,0:T(8,128)(2,1)} %pad_maximum_fusion), calls=%async_computation.1 | async-start | bytes 2752512 | tf_op jit(solution)/shard_map/all_to_all | solution.py:51
  70.8 20.2 %all-to-all-done.1 = f16[32,24,896]{2,1,0:T(8,128)(2,1)} async-done(((f16[32,24,896]{2,1,0:T(8,128)(2,1)}), f16[32,24,896]{2,1,0:T(8,128)(2,1)}, u32[]{:S(2)}, u32[]{:S(2)}) %all-to-all-start.1) | async-done | bytes 1376288 | tf_op jit(solution)/shard_map/all_to_all | solution.py:51
  91.0 1.5 convert_reduce_fusion.refs_1_
  93.8 15.1 %all_to_all.26 = bf16[32,24,128]{2,1,0:T(8,128)(2,1)} all-to-all(bf16[32,24,128]{2,1,0:T(8,128)(2,1)S(1)} %get-tuple-element.54), channel_id=1, replica_groups=mesh['xl'=2,'co'=2,'xh'=2,'y'=4,'z'=4] {'xh','y','z'}, dimensions={0} | all-to-all | bytes 393216 | tf_op jit(solution)/shard_map/all_to_all | solution.py:51
  108.9 3.9 %all-to-all-start.2 = ((bf16[32,24,768]{2,1,0:T(8,128)(2,1)}), bf16[32,24,768]{2,1,0:T(8,128)(2,1)S(1)}, u32[]{:S(2)}, u32[]{:S(2)}) async-start(bf16[32,24,768]{2,1,0:T(8,128)(2,1)} %copy-done), calls=%async_computation.2 | async-start | bytes 2359296 | tf_op jit(solution)/shard_map/all_to_all | solution.py:51
  113.8 7.2 %shard_map.132 = bf16[3840,128]{1,0:T(8,128)(2,1)S(1)} custom-call(s32[5376]{0:T(1024)S(1)} %reshape.80.refs_0_, bf16[768,128]{1,0:T(8,128)(2,1)S(1)} %bitcast.48, bf16[768,128]{1,0:T(8,128)(2,1)S(1)} %bitcast.46, bf16[7,768,128]{2,1,0:T(8,128)(2,1)S(1)} %get-tuple-element.55.refs_3_), custom_call_target="tpu_custom_call" | custom-call | tf_op jit(solution)/shard_map/pallas_call | solution.py:397
  121.1 2.2 %collective-permute-start.9 = (bf16[2,768,128]{2,1,0:T(8,128)(2,1)S(1)}, bf16[2,768,128]{2,1,0:T(8,128)(2,1)S(1)}, u32[]{:S(2)}, u32[]{:S(2)}) collective-permute-start(bf16[2,768,128]{2,1,0:T(8,128)(2,1)S(1)} %pad_maximum_fusion.2), channel_id=1, source_target_pairs={{0,32},{32,0},{1,33},{33,1},{2,34},{34,2},{3,35},{35,3},{4,36},{36... | collective-permute-start | bytes 1179656 | tf_op jit(solution)/shard_map/ppermute | solution.py:22
  123.3 1.3 collective-permute-done.9
  125.3 5.8 %collective-permute-done.10.far_ref = bf16[768,128]{1,0:T(8,128)(2,1)S(1)} collective-permute-done((bf16[768,128]{1,0:T(8,128)(2,1)S(1)}, bf16[768,128]{1,0:T(8,128)(2,1)S(1)}, u32[]{:S(2)}, u32[]{:S(2)}) %collective-permute-start.10) | collective-permute-done | bytes 196640 | tf_op jit(solution)/shard_map/ppermute | solution.py:26
  131.9 19.3 %all_to_all.27.sums = bf16[32,2,24,128]{3,2,1,0:T(8,128)(2,1)S(1)} all-to-all(bf16[32,2,24,128]{3,2,1,0:T(8,128)(2,1)S(1)} %shard_map.133), channel_id=1, replica_groups=mesh['xl'=2,'co'=2,'xh'=2,'y'=4,'z'=4] {'xh','y','z'}, dimensions={0} | all-to-all | bytes 786432 | tf_op jit(solution)/shard_map/all_to_all | solution.py:51
  152.2 2.8 %collective-permute-start.12 = (bf16[48,1024]{1,0:T(8,128)(2,1)S(1)}, bf16[48,1024]{1,0:T(8,128)(2,1)S(1)}, u32[]{:S(2)}, u32[]{:S(2)}) collective-permute-start(bf16[48,1024]{1,0:T(8,128)(2,1)S(1)} %get-tuple-element.61), channel_id=1, source_target_pairs={{0,32},{32,0},{1,33},{33,1},{2,34},{34,2},{3,35},{35,3},{4,36},{36... | collective-permute-start | bytes 294920 | tf_op jit(solution)/shard_map/ppermute | solution.py:22
  155.4 1.4 collective-permute-start.14
  157.4 5.3 %collective-permute-done.11 = f32[104,128]{1,0:T(8,128)S(1)} collective-permute-done((f32[104,128]{1,0:T(8,128)S(1)}, f32[104,128]{1,0:T(8,128)S(1)}, u32[]{:S(2)}, u32[]{:S(2)}) %collective-permute-start.11) | collective-permute-done | bytes 53280 | tf_op jit(solution)/shard_map/ppermute | solution.py:31
  162.8 5.3 %shard_map.135 = (bf16[2,48,4096]{2,1,0:T(8,128)(2,1)S(1)}, bf16[2,48,4096]{2,1,0:T(8,128)(2,1)S(1)}) custom-call(bf16[48,1024]{1,0:T(8,128)(2,1)S(1)} %get-tuple-element.65.x0, bf16[48,1024]{1,0:T(8,128)(2,1)S(1)} %collective-permute-done.12.x1, bf16[48,1024]{1,0:T(8,128)(2,1)S(1)} %collective-permute-done.13.x2, ...), custom_call_target="tpu_custom_call" | custom-call | tf_op jit(solution)/shard_map/pallas_call | solution.py:438
  169.5 3.0 %collective-permute-done.16 = f32[104,128]{1,0:T(8,128)S(1)} collective-permute-done((f32[104,128]{1,0:T(8,128)S(1)}, f32[104,128]{1,0:T(8,128)S(1)}, u32[]{:S(2)}, u32[]{:S(2)}) %collective-permute-start.16) | collective-permute-done | bytes 53280 | tf_op jit(solution)/shard_map/ppermute | solution.py:38
  174.1 3.0 %collective-permute-done.17 = f32[104,128]{1,0:T(8,128)S(1)} collective-permute-done((f32[104,128]{1,0:T(8,128)S(1)}, f32[104,128]{1,0:T(8,128)S(1)}, u32[]{:S(2)}, u32[]{:S(2)}) %collective-permute-start.17) | collective-permute-done | bytes 53280 | tf_op jit(solution)/shard_map/ppermute | solution.py:38
  177.2 2.7 %collective-permute-start.19 = (f32[104,128]{1,0:T(8,128)S(1)}, f32[104,128]{1,0:T(8,128)S(1)}, u32[]{:S(2)}, u32[]{:S(2)}) collective-permute-start(f32[104,128]{1,0:T(8,128)S(1)} %add.71), channel_id=1, source_target_pairs={{1,0},{2,1},{3,2},{0,3},{5,4},{6,5},{7,6},{4,7},{9,8},{10,9},{11,1... | collective-permute-start | bytes 159752 | tf_op jit(solution)/shard_map/ppermute | solution.py:31
  181.4 3.0 %collective-permute-done.18 = f32[104,128]{1,0:T(8,128)S(1)} collective-permute-done((f32[104,128]{1,0:T(8,128)S(1)}, f32[104,128]{1,0:T(8,128)S(1)}, u32[]{:S(2)}, u32[]{:S(2)}) %collective-permute-start.18) | collective-permute-done | bytes 53280 | tf_op jit(solution)/shard_map/ppermute | solution.py:31
  184.4 3.6 %collective-permute-start.24 = (f32[104,128]{1,0:T(8,128)S(1)}, f32[104,128]{1,0:T(8,128)S(1)}, u32[]{:S(2)}, u32[]{:S(2)}) collective-permute-start(f32[104,128]{1,0:T(8,128)S(1)} %add_add_fusion.refs_0_), channel_id=1, source_target_pairs={{0,96},{32,64},{64,32},{96,0},{1,97},{33,65},{65,33},{97,1},{2,98}... | collective-permute-start | bytes 159752 | tf_op jit(solution)/shard_map/ppermute | solution.py:460
  188.0 1.5 collective-permute-start.23
  190.5 1.9 collective-permute-done.23.refs_2_
  (74 shorter events, 22.8 us)
Async XLA Ops:
  0.6 5.3 %collective-permute-start.1 = (bf16[48,4096]{1,0:T(8,128)(2,1)}, bf16[48,4096]{1,0:T(8,128)(2,1)S(1)}, u32[]{:S(2)}, u32[]{:S(2)}) collective-permute-start(bf16[48,4096]{1,0:T(8,128)(2,1)} %bitcast.49), channel_id=1, source_target_pairs={{0,32},{32,0},{1,33},{33,1},{2,34},{34,2},{3,35},{35,3},{4,36},{36... | collective-permute-start | bytes 1179656 | tf_op jit(solution)/shard_map/ppermute | solution.py:22
  2.1 10.9 %collective-permute-start = (bf16[48,4096]{1,0:T(8,128)(2,1)}, bf16[48,4096]{1,0:T(8,128)(2,1)S(1)}, u32[]{:S(2)}, u32[]{:S(2)}) collective-permute-start(bf16[48,4096]{1,0:T(8,128)(2,1)} %bitcast.50), channel_id=1, source_target_pairs={{0,64},{64,0},{1,65},{65,1},{2,66},{66,2},{3,67},{67,3},{4,68},{68... | collective-permute-start | bytes 1179656 | tf_op jit(solution)/shard_map/ppermute | solution.py:26
  13.0 2.2 %collective-permute-start.2 = (bf16[48,4096]{1,0:T(8,128)(2,1)S(1)}, bf16[48,4096]{1,0:T(8,128)(2,1)S(1)}, u32[]{:S(2)}, u32[]{:S(2)}) collective-permute-start(bf16[48,4096]{1,0:T(8,128)(2,1)S(1)} %collective-permute-done.x2), channel_id=1, source_target_pairs={{0,32},{32,0},{1,33},{33,1},{2,34},{34,2},{3,35},{35,3},{4,36},{36... | collective-permute-start | bytes 1179656 | tf_op jit(solution)/shard_map/ppermute | solution.py:22
  16.2 11.0 %copy-start.5 = (bf16[2,24,4096]{2,1,0:T(8,128)(2,1)S(1)}, bf16[2,24,4096]{2,1,0:T(8,128)(2,1)}, u32[]{:S(2)}) copy-start(bf16[2,24,4096]{2,1,0:T(8,128)(2,1)} %param.9) | copy-start | bytes 1179652
  16.2 11.0 %copy-start.6 = (f32[4096]{0:T(1024)S(1)}, f32[4096]{0:T(1024)}, u32[]{:S(2)}) copy-start(f32[4096]{0:T(1024)} %param.13) | copy-start | bytes 49156
  16.2 11.0 %copy-start.7 = (f32[4096]{0:T(1024)S(1)}, f32[4096]{0:T(1024)}, u32[]{:S(2)}) copy-start(f32[4096]{0:T(1024)} %param.12) | copy-start | bytes 49156
  20.2 2.2 %collective-permute-start.3 = (bf16[48,1024]{1,0:T(8,128)(2,1)S(1)}, bf16[48,1024]{1,0:T(8,128)(2,1)S(1)}, u32[]{:S(2)}, u32[]{:S(2)}) collective-permute-start(bf16[48,1024]{1,0:T(8,128)(2,1)S(1)} %get-tuple-element.45), channel_id=1, source_target_pairs={{0,32},{32,0},{1,33},{33,1},{2,34},{34,2},{3,35},{35,3},{4,36},{36... | collective-permute-start | bytes 294920 | tf_op jit(solution)/shard_map/ppermute | solution.py:22
  20.6 4.3 %collective-permute-start.4 = (bf16[48,1024]{1,0:T(8,128)(2,1)S(1)}, bf16[48,1024]{1,0:T(8,128)(2,1)S(1)}, u32[]{:S(2)}, u32[]{:S(2)}) collective-permute-start(bf16[48,1024]{1,0:T(8,128)(2,1)S(1)} %get-tuple-element.46), channel_id=1, source_target_pairs={{0,64},{64,0},{1,65},{65,1},{2,66},{66,2},{3,67},{67,3},{4,68},{68... | collective-permute-start | bytes 294920 | tf_op jit(solution)/shard_map/ppermute | solution.py:26
  21.9 5.3 %collective-permute-start.5 = (bf16[48,1024]{1,0:T(8,128)(2,1)S(1)}, bf16[48,1024]{1,0:T(8,128)(2,1)S(1)}, u32[]{:S(2)}, u32[]{:S(2)}) collective-permute-start(bf16[48,1024]{1,0:T(8,128)(2,1)S(1)} %get-tuple-element.47), channel_id=1, source_target_pairs={{0,96},{32,64},{64,32},{96,0},{1,97},{33,65},{65,33},{97,1},{2,98}... | collective-permute-start | bytes 294920 | tf_op jit(solution)/shard_map/ppermute | solution.py:326
  27.7 21.6 %copy-start.1 = (f32[48,4096]{1,0:T(8,128)}, f32[48,4096]{1,0:T(8,128)S(1)}, u32[]{:S(2)}) copy-start(f32[48,4096]{1,0:T(8,128)S(1)} %get-tuple-element.56.pooled) | copy-start | bytes 2359300
  49.4 4.6 %collective-permute-start.7 = (bf16[768,128]{1,0:T(8,128)(2,1)S(1)}, bf16[768,128]{1,0:T(8,128)(2,1)S(1)}, u32[]{:S(2)}, u32[]{:S(2)}) collective-permute-start(bf16[768,128]{1,0:T(8,128)(2,1)S(1)} %bitcast.40), channel_id=1, source_target_pairs={{0,64},{64,0},{1,65},{65,1},{2,66},{66,2},{3,67},{67,3},{4,68},{68... | collective-permute-start | bytes 589832 | tf_op jit(solution)/shard_map/ppermute | solution.py:26
  49.8 8.1 %collective-permute-start.6 = (bf16[768,128]{1,0:T(8,128)(2,1)S(1)}, bf16[768,128]{1,0:T(8,128)(2,1)S(1)}, u32[]{:S(2)}, u32[]{:S(2)}) collective-permute-start(bf16[768,128]{1,0:T(8,128)(2,1)S(1)} %bitcast.41), channel_id=1, source_target_pairs={{0,32},{32,0},{1,33},{33,1},{2,34},{34,2},{3,35},{35,3},{4,36},{36... | collective-permute-start | bytes 589832 | tf_op jit(solution)/shard_map/ppermute | solution.py:22
  54.0 4.4 %collective-permute-start.8 = (bf16[768,128]{1,0:T(8,128)(2,1)S(1)}, bf16[768,128]{1,0:T(8,128)(2,1)S(1)}, u32[]{:S(2)}, u32[]{:S(2)}) collective-permute-start(bf16[768,128]{1,0:T(8,128)(2,1)S(1)} %collective-permute-done.7), channel_id=1, source_target_pairs={{0,32},{32,0},{1,33},{33,1},{2,34},{34,2},{3,35},{35,3},{4,36},{36... | collective-permute-start | bytes 589832 | tf_op jit(solution)/shard_map/ppermute | solution.py:22
  66.1 24.9 %all-to-all-start.1 = ((f16[32,24,896]{2,1,0:T(8,128)(2,1)}), f16[32,24,896]{2,1,0:T(8,128)(2,1)}, u32[]{:S(2)}, u32[]{:S(2)}) async-start(f16[32,24,896]{2,1,0:T(8,128)(2,1)} %pad_maximum_fusion), calls=%async_computation.1 | async-start | bytes 2752512 | tf_op jit(solution)/shard_map/all_to_all | solution.py:51
  108.9 22.2 %all-to-all-start.2 = ((bf16[32,24,768]{2,1,0:T(8,128)(2,1)}), bf16[32,24,768]{2,1,0:T(8,128)(2,1)S(1)}, u32[]{:S(2)}, u32[]{:S(2)}) async-start(bf16[32,24,768]{2,1,0:T(8,128)(2,1)} %copy-done), calls=%async_computation.2 | async-start | bytes 2359296 | tf_op jit(solution)/shard_map/all_to_all | solution.py:51
  121.1 3.6 %collective-permute-start.9 = (bf16[2,768,128]{2,1,0:T(8,128)(2,1)S(1)}, bf16[2,768,128]{2,1,0:T(8,128)(2,1)S(1)}, u32[]{:S(2)}, u32[]{:S(2)}) collective-permute-start(bf16[2,768,128]{2,1,0:T(8,128)(2,1)S(1)} %pad_maximum_fusion.2), channel_id=1, source_target_pairs={{0,32},{32,0},{1,33},{33,1},{2,34},{34,2},{3,35},{35,3},{4,36},{36... | collective-permute-start | bytes 1179656 | tf_op jit(solution)/shard_map/ppermute | solution.py:22
  124.7 6.4 %collective-permute-start.10 = (bf16[768,128]{1,0:T(8,128)(2,1)S(1)}, bf16[768,128]{1,0:T(8,128)(2,1)S(1)}, u32[]{:S(2)}, u32[]{:S(2)}) collective-permute-start(bf16[768,128]{1,0:T(8,128)(2,1)S(1)} %fusion.1), channel_id=1, source_target_pairs={{0,64},{64,0},{1,65},{65,1},{2,66},{66,2},{3,67},{67,3},{4,68},{68... | collective-permute-start | bytes 589832 | tf_op jit(solution)/shard_map/ppermute | solution.py:26
  131.1 20.1 %copy-start.2 = (f32[48,4096]{1,0:T(8,128)S(1)}, f32[48,4096]{1,0:T(8,128)}, u32[]{:S(2)}) copy-start(f32[48,4096]{1,0:T(8,128)} %copy-done.1) | copy-start | bytes 2359300
  152.2 10.6 %collective-permute-start.12 = (bf16[48,1024]{1,0:T(8,128)(2,1)S(1)}, bf16[48,1024]{1,0:T(8,128)(2,1)S(1)}, u32[]{:S(2)}, u32[]{:S(2)}) collective-permute-start(bf16[48,1024]{1,0:T(8,128)(2,1)S(1)} %get-tuple-element.61), channel_id=1, source_target_pairs={{0,32},{32,0},{1,33},{33,1},{2,34},{34,2},{3,35},{35,3},{4,36},{36... | collective-permute-start | bytes 294920 | tf_op jit(solution)/shard_map/ppermute | solution.py:22
  155.0 7.8 %collective-permute-start.13 = (bf16[48,1024]{1,0:T(8,128)(2,1)S(1)}, bf16[48,1024]{1,0:T(8,128)(2,1)S(1)}, u32[]{:S(2)}, u32[]{:S(2)}) collective-permute-start(bf16[48,1024]{1,0:T(8,128)(2,1)S(1)} %get-tuple-element.62), channel_id=1, source_target_pairs={{0,64},{64,0},{1,65},{65,1},{2,66},{66,2},{3,67},{67,3},{4,68},{68... | collective-permute-start | bytes 294920 | tf_op jit(solution)/shard_map/ppermute | solution.py:26
  155.4 7.4 %collective-permute-start.14 = (bf16[48,1024]{1,0:T(8,128)(2,1)S(1)}, bf16[48,1024]{1,0:T(8,128)(2,1)S(1)}, u32[]{:S(2)}, u32[]{:S(2)}) collective-permute-start(bf16[48,1024]{1,0:T(8,128)(2,1)S(1)} %get-tuple-element.63), channel_id=1, source_target_pairs={{0,96},{32,64},{64,32},{96,0},{1,97},{33,65},{65,33},{97,1},{2,98}... | collective-permute-start | bytes 294920 | tf_op jit(solution)/shard_map/ppermute | solution.py:435
  156.8 6.0 %collective-permute-start.11 = (f32[104,128]{1,0:T(8,128)S(1)}, f32[104,128]{1,0:T(8,128)S(1)}, u32[]{:S(2)}, u32[]{:S(2)}) collective-permute-start(f32[104,128]{1,0:T(8,128)S(1)} %get-tuple-element.59), channel_id=1, source_target_pairs={{16,0},{0,16},{17,1},{1,17},{18,2},{2,18},{19,3},{3,19},{20,4},{4,... | collective-permute-start | bytes 159752 | tf_op jit(solution)/shard_map/ppermute | solution.py:31
  168.2 5.7 %collective-permute-start.15 = (bf16[2,48,4096]{2,1,0:T(8,128)(2,1)S(1)}, bf16[2,48,4096]{2,1,0:T(8,128)(2,1)S(1)}, u32[]{:S(2)}, u32[]{:S(2)}) collective-permute-start(bf16[2,48,4096]{2,1,0:T(8,128)(2,1)S(1)} %get-tuple-element.72), channel_id=1, source_target_pairs={{0,32},{32,0},{1,33},{33,1},{2,34},{34,2},{3,35},{35,3},{4,36},{36... | collective-permute-start | bytes 2359304 | tf_op jit(solution)/shard_map/ppermute | solution.py:22
  169.1 3.4 %collective-permute-start.16 = (f32[104,128]{1,0:T(8,128)S(1)}, f32[104,128]{1,0:T(8,128)S(1)}, u32[]{:S(2)}, u32[]{:S(2)}) collective-permute-start(f32[104,128]{1,0:T(8,128)S(1)} %add.67), channel_id=1, source_target_pairs={{0,4},{4,0},{8,12},{12,8},{1,5},{5,1},{9,13},{13,9},{2,6},{6,2},{1... | collective-permute-start | bytes 159752 | tf_op jit(solution)/shard_map/ppermute | solution.py:38
  172.5 4.6 %collective-permute-start.17 = (f32[104,128]{1,0:T(8,128)S(1)}, f32[104,128]{1,0:T(8,128)S(1)}, u32[]{:S(2)}, u32[]{:S(2)}) collective-permute-start(f32[104,128]{1,0:T(8,128)S(1)} %add.70), channel_id=1, source_target_pairs={{0,8},{4,12},{8,0},{12,4},{1,9},{5,13},{9,1},{13,5},{2,10},{6,14},... | collective-permute-start | bytes 159752 | tf_op jit(solution)/shard_map/ppermute | solution.py:38
  174.0 10.5 %collective-permute-start.21 = (bf16[48,4096]{1,0:T(8,128)(2,1)S(1)}, bf16[48,4096]{1,0:T(8,128)(2,1)S(1)}, u32[]{:S(2)}, u32[]{:S(2)}) collective-permute-start(bf16[48,4096]{1,0:T(8,128)(2,1)S(1)} %fusion), channel_id=1, source_target_pairs={{0,64},{64,0},{1,65},{65,1},{2,66},{66,2},{3,67},{67,3},{4,68},{68... | collective-permute-start | bytes 1179656 | tf_op jit(solution)/shard_map/ppermute | solution.py:26
  177.1 4.3 %collective-permute-start.20 = (f32[104,128]{1,0:T(8,128)S(1)}, f32[104,128]{1,0:T(8,128)S(1)}, u32[]{:S(2)}, u32[]{:S(2)}) collective-permute-start(f32[104,128]{1,0:T(8,128)S(1)} %add.71), channel_id=1, source_target_pairs={{3,0},{0,1},{1,2},{2,3},{7,4},{4,5},{5,6},{6,7},{11,8},{8,9},{9,10... | collective-permute-start | bytes 159752 | tf_op jit(solution)/shard_map/ppermute | solution.py:31
  177.2 4.2 %collective-permute-start.19 = (f32[104,128]{1,0:T(8,128)S(1)}, f32[104,128]{1,0:T(8,128)S(1)}, u32[]{:S(2)}, u32[]{:S(2)}) collective-permute-start(f32[104,128]{1,0:T(8,128)S(1)} %add.71), channel_id=1, source_target_pairs={{1,0},{2,1},{3,2},{0,3},{5,4},{6,5},{7,6},{4,7},{9,8},{10,9},{11,1... | collective-permute-start | bytes 159752 | tf_op jit(solution)/shard_map/ppermute | solution.py:31
  179.8 4.6 %collective-permute-start.18 = (f32[104,128]{1,0:T(8,128)S(1)}, f32[104,128]{1,0:T(8,128)S(1)}, u32[]{:S(2)}, u32[]{:S(2)}) collective-permute-start(f32[104,128]{1,0:T(8,128)S(1)} %add.71), channel_id=1, source_target_pairs={{2,0},{3,1},{0,2},{1,3},{6,4},{7,5},{4,6},{5,7},{10,8},{11,9},{8,1... | collective-permute-start | bytes 159752 | tf_op jit(solution)/shard_map/ppermute | solution.py:31
  184.4 6.1 %collective-permute-start.24 = (f32[104,128]{1,0:T(8,128)S(1)}, f32[104,128]{1,0:T(8,128)S(1)}, u32[]{:S(2)}, u32[]{:S(2)}) collective-permute-start(f32[104,128]{1,0:T(8,128)S(1)} %add_add_fusion.refs_0_), channel_id=1, source_target_pairs={{0,96},{32,64},{64,32},{96,0},{1,97},{33,65},{65,33},{97,1},{2,98}... | collective-permute-start | bytes 159752 | tf_op jit(solution)/shard_map/ppermute | solution.py:460
  188.0 4.4 %collective-permute-start.23 = (f32[104,128]{1,0:T(8,128)S(1)}, f32[104,128]{1,0:T(8,128)S(1)}, u32[]{:S(2)}, u32[]{:S(2)}) collective-permute-start(f32[104,128]{1,0:T(8,128)S(1)} %add_add_fusion.refs_0_), channel_id=1, source_target_pairs={{0,64},{64,0},{1,65},{65,1},{2,66},{66,2},{3,67},{67,3},{4,68},{68... | collective-permute-start | bytes 159752 | tf_op jit(solution)/shard_map/ppermute | solution.py:26
  189.5 2.9 %collective-permute-start.22 = (f32[104,128]{1,0:T(8,128)S(1)}, f32[104,128]{1,0:T(8,128)S(1)}, u32[]{:S(2)}, u32[]{:S(2)}) collective-permute-start(f32[104,128]{1,0:T(8,128)S(1)} %add_add_fusion.refs_0_), channel_id=1, source_target_pairs={{0,32},{32,0},{1,33},{33,1},{2,34},{34,2},{3,35},{35,3},{4,36},{36... | collective-permute-start | bytes 159752 | tf_op jit(solution)/shard_map/ppermute | solution.py:22
  (3 other events, 3.0 us)
